TPU v7x, 32 devices: a whole 2x2x4 slice. The times are simulated.
32 devices in a mesh: grp: 2 (over x), row: 4 (over z), col: 4 (over y, core).
Axes of the slice: x: 2, y: 2, z: 4, core: 2. Of those that a mesh axis runs over, the one named last changes fastest.
Arguments:
- right_side: float32 [2, 16, 12288], P(None, None, 'row'), may hold values from -6 to 6
- near_tiles: bfloat16 [2, 256, 256, 256], P(None, ('grp', 'row', 'col')), may hold values from -0.078125 to 0.078125
- tile_pairs: int32 [256], P(('grp', 'row', 'col')), may hold values from 0 to 59, as said below
- tile_count: int32 [32], P(('grp', 'row', 'col')), may hold values from 1 to 8, as said below
- panel_expansions: bfloat16 [2, 12288, 441], P(None, 'row'), may hold values from -0.125 to 0.125
- leaf_of_panel: int32 [4, 3072], P('row'), may hold values from 0 to 23, never falling along the last dimension, each value on 1 to 256 neighbouring positions
- far_pick: int32 [4, 4, 2], replicated, may hold values from 0 to 23, as said below
- far_target: int32 [4, 8], P('row'), may hold values from 0 to 23
- far_offset: int32 [4, 8], P('row'), may hold values from 0 to 3
- translations: bfloat16 [4, 2, 441, 441], replicated, may hold values from -0.375 to 0.375
Outputs:
- solution: float32 [2, 16, 12288], P(None, None, 'row')
Inputs may be any that keep to these rules, and one draw needn't show every extreme that they name: `tile_pairs`: within one device's 8 slots the codes are distinct, and over the live slots of all devices with the same row index they are distinct too. `tile_count`: some device has all 8 slots live. far_pick[d, r] holds 2 distinct leaves.
All inputs are finite; a program needn't handle non-finite values.
Results may differ from a plain program's by a relative error of at most 0.0016.
Values may be sent and summed in bfloat16 or wider, within the bound.
No kernel may reach another device: no remote copies, remote signals or barrier semaphores. Data moves between devices by JAX's collectives and lax.ppermute only.
A program may use at most 64 MiB of HBM per device.

v0:
```python
import jax
import jax.numpy as jnp
from jax import lax
from jax.sharding import PartitionSpec as P

REACH = 2
OFFSETS = 4
LEAF_DEV = 24


EPSILON = 1e-06
HIGHEST = lax.Precision.HIGHEST


def extended_2(array, sides, width):
    for axis, dim in sides:
        count, length = (lax.axis_size(axis), array.shape[dim])
        up = [(i, (i + 1) % count) for i in range(count)]
        down = [(j, i) for i, j in up]
        last = lax.slice_in_dim(array, length - width, length, axis=dim)
        leading = lax.slice_in_dim(array, 0, width, axis=dim)
        before = lax.ppermute(last, axis, up)
        after = lax.ppermute(leading, axis, down)
        array = jnp.concatenate([before, array, after], axis=dim)
    return array


def complex_mix(products):
    return jnp.stack([products[0, 0] - products[1, 1], products[0, 1] + products[1, 0]])


def inner_local(left, right):
    real_part = jnp.sum(left[0] * right[0] + left[1] * right[1], axis=-1)
    imag_part = jnp.sum(left[0] * right[1] - left[1] * right[0], axis=-1)
    return jnp.stack([real_part, imag_part])


def scaled_vector(coeff, vector):
    real_coeff = coeff[0][:, None]
    imag_coeff = coeff[1][:, None]
    return jnp.stack(
        [
            real_coeff * vector[0] - imag_coeff * vector[1],
            real_coeff * vector[1] + imag_coeff * vector[0],
        ]
    )


def complex_times(left, right):
    return jnp.stack(
        [left[0] * right[0] - left[1] * right[1], left[0] * right[1] + left[1] * right[0]]
    )


def conjugate(value):
    return jnp.stack([value[0], -value[1]])


def small_solve(beta_norm, h_first, h_sub, h_upper, h_middle, h_last):
    radius = jnp.sqrt(h_first[0] * h_first[0] + h_first[1] * h_first[1] + h_sub * h_sub)
    cosine = h_first / radius
    sine_one = h_sub / radius
    upper_row = complex_times(conjugate(cosine), h_upper) + sine_one * h_middle
    lower_row = complex_times(cosine, h_middle) - sine_one * h_upper
    radius_two = jnp.sqrt(
        lower_row[0] * lower_row[0] + lower_row[1] * lower_row[1] + h_last * h_last
    )
    cosine_two = lower_row / radius_two
    goal_top = conjugate(cosine) * beta_norm
    goal_mid = -sine_one * beta_norm
    weight_two = conjugate(cosine_two) * (goal_mid / radius_two)
    weight_one = (goal_top - complex_times(upper_row, weight_two)) / radius
    return (weight_one, weight_two)


def row_total(partial_value):
    return lax.psum(partial_value, "row")


def near_part(vector_low, near_tiles, tile_pairs, tile_count):
    fields = vector_low.shape[1]
    panels = vector_low.shape[2]
    tile_size = near_tiles.shape[2]
    blocks_here = panels // tile_size
    span_count = 2 * REACH + 1
    extended = extended_2(vector_low, (("row", 2),), REACH * tile_size)
    blocks = extended.reshape(2, fields, blocks_here + 2 * REACH, tile_size)
    target = tile_pairs // span_count
    source = target + tile_pairs % span_count
    source_rows = jnp.take(blocks, source, axis=2)
    values = complex_mix(
        jnp.einsum("xstj,ytij->xysti", source_rows, near_tiles, preferred_element_type=jnp.float32)
    )
    live_mask = (jnp.arange(tile_pairs.shape[0], dtype=jnp.int32) < tile_count[0]).astype(
        jnp.float32
    )
    placing = (target[:, None] == jnp.arange(blocks_here, dtype=jnp.int32)[None, :]).astype(
        jnp.float32
    ) * live_mask[:, None]
    summed = jnp.einsum("xsti,tb->xsbi", values, placing, precision=HIGHEST)
    return summed.reshape(2, fields, panels)


def local(
    right_side,
    near_tiles,
    tile_pairs,
    tile_count,
    panel_expansions,
    leaf_of_panel,
    far_pick,
    far_target,
    far_offset,
    translations,
):
    fields = right_side.shape[1]
    coefs = panel_expansions.shape[2]
    share_count = fields // (lax.axis_size("grp") * lax.axis_size("col"))
    own_index = lax.axis_index("grp") * lax.axis_size("col") + lax.axis_index("col")
    row_here = lax.axis_index("row")
    row_count = lax.axis_size("row")
    leaf_ids = jnp.arange(LEAF_DEV, dtype=jnp.int32)
    member_lp = (leaf_of_panel[0][None, :] == leaf_ids[:, None]).astype(jnp.bfloat16)
    member_wide = (leaf_of_panel[0][:, None] == leaf_ids[None, :]).astype(jnp.float32)
    item_keys = far_offset[0] * LEAF_DEV + far_target[0]
    selector = (
        jnp.arange(OFFSETS * LEAF_DEV, dtype=jnp.int32)[:, None] == item_keys[None, :]
    ).astype(jnp.bfloat16)

    def translate(gathered):
        rows_now = gathered.shape[1]
        gathered_low = gathered.astype(jnp.bfloat16).reshape(2, rows_now, OFFSETS, LEAF_DEV, coefs)
        local_field = complex_mix(
            jnp.einsum(
                "xsolk,oykj->xyslj", gathered_low, translations, preferred_element_type=jnp.float32
            )
        )
        return local_field.astype(jnp.bfloat16)

    def far_part(vector_mine):
        weighted = member_lp[None, None] * vector_mine[:, :, None, :]
        multipoles = complex_mix(
            jnp.einsum(
                "xslp,ypk->xyslk", weighted, panel_expansions, preferred_element_type=jnp.float32
            )
        ).astype(jnp.bfloat16)
        pick_codes = lax.dynamic_index_in_dim(far_pick, row_here, 0, keepdims=False)
        chosen = (jnp.arange(row_count, dtype=jnp.int32)[:, None] * LEAF_DEV + pick_codes).reshape(
            -1
        )
        piece = lax.all_gather(multipoles, "row", axis=2, tiled=True)
        piece_count = piece.shape[2]
        hit_table = (chosen[:, None] == jnp.arange(piece_count, dtype=jnp.int32)[None, :]).astype(
            jnp.bfloat16
        )
        weights = jnp.dot(selector, hit_table, preferred_element_type=jnp.float32).astype(
            jnp.bfloat16
        )
        gathered = jnp.einsum("an,xsnk->xsak", weights, piece, preferred_element_type=jnp.float32)
        local_field = translate(gathered)
        per_leaf = jnp.einsum(
            "ypk,xslk->xyspl", panel_expansions, local_field, preferred_element_type=jnp.float32
        )
        picked = jnp.sum(per_leaf * member_wide[None, None, None], axis=-1)
        return complex_mix(picked)

    def apply_operator(vector):
        vector_low = vector.astype(jnp.bfloat16)
        near_image = near_part(vector_low, near_tiles, tile_pairs, tile_count)
        vector_mine = lax.dynamic_slice_in_dim(vector_low, own_index * share_count, share_count, 1)
        far_image = far_part(vector_mine)
        near_all = lax.psum(near_image, ("grp", "col"))
        far_all = lax.all_gather(far_image, ("grp", "col"), axis=1, tiled=True)
        return 0.5 * vector + near_all + far_all

    beta_norm = jnp.sqrt(row_total(jnp.sum(right_side * right_side, axis=(0, 2))) + EPSILON)
    first_basis = right_side / beta_norm[None, :, None]
    image_one = apply_operator(first_basis)
    h_first = row_total(inner_local(first_basis, image_one))
    residue = image_one - scaled_vector(h_first, first_basis)
    h_sub = jnp.sqrt(row_total(jnp.sum(residue * residue, axis=(0, 2))) + EPSILON)
    second_basis = residue / h_sub[None, :, None]
    image_two = apply_operator(second_basis)
    both_products = row_total(
        jnp.stack([inner_local(first_basis, image_two), inner_local(second_basis, image_two)])
    )
    h_upper = both_products[0]
    h_middle = both_products[1]
    remainder = (
        image_two - scaled_vector(h_upper, first_basis) - scaled_vector(h_middle, second_basis)
    )
    h_last = jnp.sqrt(row_total(jnp.sum(remainder * remainder, axis=(0, 2))) + EPSILON)
    weight_one, weight_two = small_solve(beta_norm, h_first, h_sub, h_upper, h_middle, h_last)
    return scaled_vector(weight_one, first_basis) + scaled_vector(weight_two, second_basis)


def solution(mesh):
    return jax.shard_map(
        local,
        mesh=mesh,
        in_specs=(
            P(None, None, "row"),
            P(None, ("grp", "row", "col"), None, None),
            P(("grp", "row", "col")),
            P(("grp", "row", "col")),
            P(None, "row", None),
            P("row", None),
            P(),
            P("row", None),
            P("row", None),
            P(),
        ),
        out_specs=P(None, None, "row"),
        check_vma=False,
    )
```

profile of v0, /device:TPU:0, one launch (start us, length us, event | category | flops | bytes accessed | tf_op | source)
XLA Modules:
  0.0 257.4 jit_solution(8155005641351651952)
XLA Ops:
  6.5 1.3 multiply_reduce_fusion.1
  7.8 13.5 %psum.49 = f32[16]{0:T(128)S(1)} all-reduce(f32[16]{0:T(128)S(1)} %multiply_reduce_fusion.1), channel_id=1, replica_groups=mesh['grp'=2,'row'=4,'col'=4] {'row'}, use_global_device_ids=true, to_apply=%region_1.0 | all-reduce | flops 16 | bytes 128 | tf_op jit(solution)/shard_map/psum | solution.py:77
  21.3 1.1 fusion.133
  22.5 3.8 %collective-permute-start.1 = (bf16[2,16,512]{2,1,0:T(8,128)(2,1)S(1)}, bf16[2,16,512]{2,1,0:T(8,128)(2,1)S(1)}, u32[]{:S(2)}, u32[]{:S(2)}) collective-permute-start(bf16[2,16,512]{2,1,0:T(8,128)(2,1)S(1)} %get-tuple-element.38), channel_id=1, source_target_pairs={{4,0},{8,4},{12,8},{0,12},{5,1},{9,5},{13,9},{1,13},{6,2},{10,6},{... | collective-permute-start | bytes 98312 | tf_op jit(solution)/shard_map/ppermute | solution.py:23
  26.3 0.7 fusion.52
  27.1 0.8 fusion.53
  27.9 4.5 %fusion.28 = f32[2,2,2,24,441]{4,3,1,2,0:T(8,128)S(1)} fusion(bf16[2,3072,441,1,1]{1,0,2,4,3:T(2,128)(2,1)} %bitcast.349, bf16[2,2,3072]{2,1,0:T(2,128)(2,1)S(1)} %constant_dynamic-slice_fusion.2, bf16[24,3072]{1,0:T(8,128)(2,1)S(1)} %fusion.52), kind=kOutput, calls=%fused_computation.28 | convolution fusion | flops 521404416 | bytes 5929728 | tf_op jit(solution)/shard_map/xslp,ypk->xyslk/dot_general | solution.py:143
  33.5 14.4 %all_gather.12 = bf16[2,2,96,441]{3,2,1,0:T(8,128)(2,1)S(1)} all-gather(bf16[2,2,24,441]{3,2,1,0:T(8,128)(2,1)S(1)} %pad_maximum_fusion.4), channel_id=1, replica_groups=mesh['grp'=2,'row'=4,'col'=4] {'row'}, dimensions={2}, use_global_device_ids=true | all-gather | bytes 423360 | tf_op jit(solution)/shard_map/all_gather | solution.py:151
  48.3 2.8 %fusion.34 = f32[2,2,2,24,441]{4,3,1,2,0:T(8,128)S(1)} fusion(bf16[2,2,4,24,441,1]{4,3,2,5,1,0:T(8,128)(2,1)S(1)} %bitcast.340, bf16[4,2,441,441,1,1]{3,1,2,0,5,4:T(2,128)(2,1)} %bitcast.355), kind=kOutput, calls=%fused_computation.30 | convolution fusion | flops 298722816 | bytes 3789072 | tf_op jit(solution)/shard_map/xsolk,oykj->xyslj/dot_general | solution.py:134
  51.2 4.6 %fusion.19 = f32[2,2,2,3072]{3,1,2,0:T(2,128)S(1)} fusion(bf16[2,3072,441,1,1]{1,0,2,4,3:T(2,128)(2,1)} %bitcast.350, f32[3072,24]{0,1:T(8,128)S(1)} %fusion.53, bf16[1,2,24,441]{3,2,1,0:T(8,128)(2,1)S(1)} %fusion.89, bf16[1,2,24,441]{3,2,1,0:T(8,128)(2,1)S(1)} %fusion.88), kind=kOutput, calls=%fused_computation.21 | convolution fusion | flops 521549184 | bytes 5896896 | tf_op jit(solution)/shard_map/ypk,xslk->xyspl/dot_general | solution.py:161
  58.0 0.7 convolution_bitcast_fusion.3
  58.8 0.8 reshape.574
  59.7 9.9 %all_gather.13 = f32[2,16,3072]{2,0,1:T(2,128)S(1)} all-gather(f32[2,2,3072]{2,0,1:T(2,128)S(1)} %pad_maximum_fusion.6), channel_id=1, replica_groups=mesh['grp'=2,'row'=4,'col'=4] {'grp','col'}, dimensions={1}, use_global_device_ids=true | all-gather | bytes 442368 | tf_op jit(solution)/shard_map/all_gather | solution.py:173
  69.7 42.6 %all-reduce.3.cloned.1.call-done = f32[2,16,3072]{2,1,0:T(8,128)} async-done(((f32[2,16,3072]{2,1,0:T(8,128)}), f32[2,16,3072]{2,1,0:T(8,128)}) %all-reduce.3.cloned.1.call-update) | async-done | bytes 393232 | tf_op jit(solution)/shard_map/psum | solution.py:172
  112.2 1.2 copy_add_fusion.1
  113.6 11.6 %psum.51 = f32[2,16]{1,0:T(2,128)S(1)} all-reduce(f32[2,16]{1,0:T(2,128)S(1)} %pad_maximum_fusion.9), channel_id=1, replica_groups=mesh['grp'=2,'row'=4,'col'=4] {'row'}, use_global_device_ids=true, to_apply=%region_6.8 | all-reduce | flops 32 | bytes 256 | tf_op jit(solution)/shard_map/psum | solution.py:77
  126.2 8.4 %psum.52 = f32[16]{0:T(128)S(1)} all-reduce(f32[16]{0:T(128)S(1)} %multiply_reduce_fusion), channel_id=1, replica_groups=mesh['grp'=2,'row'=4,'col'=4] {'row'}, use_global_device_ids=true, to_apply=%region_8.10 | all-reduce | flops 16 | bytes 128 | tf_op jit(solution)/shard_map/psum | solution.py:77
  134.6 1.2 fusion.132
  135.9 4.6 %fusion.31 = f32[2,2,2,24,441]{4,3,1,2,0:T(8,128)S(1)} fusion(bf16[2,3072,441,1,1]{1,0,2,4,3:T(2,128)(2,1)} %bitcast.351, bf16[2,2,3072]{2,1,0:T(2,128)(2,1)S(1)} %constant_dynamic-slice_fusion, bf16[24,3072]{1,0:T(8,128)(2,1)} %copy-done.4), kind=kOutput, calls=%fused_computation.29 | convolution fusion | flops 521404416 | bytes 5929728 | tf_op jit(solution)/shard_map/xslp,ypk->xyslk/dot_general | solution.py:143
  140.6 15.3 %all_gather.14 = bf16[2,2,96,441]{3,2,1,0:T(8,128)(2,1)S(1)} all-gather(bf16[2,2,24,441]{3,2,1,0:T(8,128)(2,1)S(1)} %pad_maximum_fusion.5), channel_id=1, replica_groups=mesh['grp'=2,'row'=4,'col'=4] {'row'}, dimensions={2}, use_global_device_ids=true | all-gather | bytes 423360 | tf_op jit(solution)/shard_map/all_gather | solution.py:151
  156.1 0.7 fusion.37
  157.1 2.1 fusion.16
  159.3 3.8 %collective-permute-start.3 = (bf16[2,16,512]{2,1,0:T(8,128)(2,1)S(1)}, bf16[2,16,512]{2,1,0:T(8,128)(2,1)S(1)}, u32[]{:S(2)}, u32[]{:S(2)}) collective-permute-start(bf16[2,16,512]{2,1,0:T(8,128)(2,1)S(1)} %get-tuple-element.36), channel_id=1, source_target_pairs={{4,0},{8,4},{12,8},{0,12},{5,1},{9,5},{13,9},{1,13},{6,2},{10,6},{... | collective-permute-start | bytes 98312 | tf_op jit(solution)/shard_map/ppermute | solution.py:23
  163.2 9.7 %all_gather.15 = f32[2,16,3072]{2,0,1:T(2,128)} all-gather(f32[2,2,3072]{2,0,1:T(2,128)S(1)} %pad_maximum_fusion.7), channel_id=1, replica_groups=mesh['grp'=2,'row'=4,'col'=4] {'grp','col'}, dimensions={1}, use_global_device_ids=true | all-gather | bytes 442368 | tf_op jit(solution)/shard_map/all_gather | solution.py:173
  173.6 0.7 fusion.25
  174.3 0.7 convolution_bitcast_fusion.2
  175.1 0.8 reshape.577
  175.9 51.6 %all-reduce.5.cloned.1.call-done = f32[2,16,3072]{2,1,0:T(8,128)} async-done(((f32[2,16,3072]{2,1,0:T(8,128)}), f32[2,16,3072]{2,1,0:T(8,128)}) %all-reduce.5.cloned.1.call-update) | async-done | bytes 393232 | tf_op jit(solution)/shard_map/psum | solution.py:172
  227.5 1.3 copy_add_fusion
  229.0 11.6 %psum.54 = f32[2,2,16]{2,1,0:T(2,128)S(1)} all-reduce(f32[2,2,16]{2,1,0:T(2,128)S(1)} %pad_maximum_fusion.8), channel_id=1, replica_groups=mesh['grp'=2,'row'=4,'col'=4] {'row'}, use_global_device_ids=true, to_apply=%region_15.17 | all-reduce | flops 64 | bytes 512 | tf_op jit(solution)/shard_map/psum | solution.py:77
  241.1 8.4 %psum.55 = f32[16]{0:T(128)S(1)} all-reduce(f32[16]{0:T(128)S(1)} %fusion.47), channel_id=1, replica_groups=mesh['grp'=2,'row'=4,'col'=4] {'row'}, use_global_device_ids=true, to_apply=%region_17.19 | all-reduce | flops 16 | bytes 128 | tf_op jit(solution)/shard_map/psum | solution.py:77
  249.8 0.8 maximum_add_fusion
  (106 shorter events, 6.9 us)
Async XLA Ops:
  6.5 50.7 %copy-start = (bf16[2,8,256,256]{3,2,1,0:T(8,128)(2,1)S(1)}, bf16[2,8,256,256]{3,2,1,0:T(8,128)(2,1)}, u32[]{:S(2)}) copy-start(bf16[2,8,256,256]{3,2,1,0:T(8,128)(2,1)} %param.13) | copy-start | bytes 6291460
  6.5 105.7 %all-reduce.3.cloned.1.call-start = ((), (), s32[]{:S(2)}) async-start(), calls=%async_computation | async-start | bytes 786432 | tf_op jit(solution)/shard_map/psum | solution.py:172
  22.4 34.2 %collective-permute-start = (bf16[2,16,512]{2,1,0:T(8,128)(2,1)S(1)}, bf16[2,16,512]{2,1,0:T(8,128)(2,1)S(1)}, u32[]{:S(2)}, u32[]{:S(2)}) collective-permute-start(bf16[2,16,512]{2,1,0:T(8,128)(2,1)S(1)} %get-tuple-element.37), channel_id=1, source_target_pairs={{0,4},{4,8},{8,12},{12,0},{1,5},{5,9},{9,13},{13,1},{2,6},{6,10},{... | collective-permute-start | bytes 98312 | tf_op jit(solution)/shard_map/ppermute | solution.py:22
  22.5 34.1 %collective-permute-start.1 = (bf16[2,16,512]{2,1,0:T(8,128)(2,1)S(1)}, bf16[2,16,512]{2,1,0:T(8,128)(2,1)S(1)}, u32[]{:S(2)}, u32[]{:S(2)}) collective-permute-start(bf16[2,16,512]{2,1,0:T(8,128)(2,1)S(1)} %get-tuple-element.38), channel_id=1, source_target_pairs={{4,0},{8,4},{12,8},{0,12},{5,1},{9,5},{13,9},{1,13},{6,2},{10,6},{... | collective-permute-start | bytes 98312 | tf_op jit(solution)/shard_map/ppermute | solution.py:23
  27.1 0.8 copy-start.4
  27.8 23.3 %copy-start.2 = (f32[3072,24]{0,1:T(8,128)}, f32[3072,24]{0,1:T(8,128)S(1)}, u32[]{:S(2)}) copy-start(f32[3072,24]{0,1:T(8,128)S(1)} %fusion.53) | copy-start | bytes 884740
  27.9 19.9 %copy-start.7 = (s32[1,8]{1,0:T(1,128)S(1)}, s32[1,8]{1,0:T(1,128)}, u32[]{:S(2)}) copy-start(s32[1,8]{1,0:T(1,128)} %param.19) | copy-start | bytes 100
  27.9 19.9 %copy-start.8 = (s32[1,8]{1,0:T(1,128)S(1)}, s32[1,8]{1,0:T(1,128)}, u32[]{:S(2)}) copy-start(s32[1,8]{1,0:T(1,128)} %param.20) | copy-start | bytes 100
  51.1 5.4 %copy-start.5 = (s32[8]{0:T(128)S(1)}, s32[8]{0:T(128)}, u32[]{:S(2)}) copy-start(s32[8]{0:T(128)} %param.14) | copy-start | bytes 100
  59.6 167.9 %all-reduce.5.cloned.1.call-start = ((), (), s32[]{:S(2)}) async-start(), calls=%async_computation.1 | async-start | bytes 786432 | tf_op jit(solution)/shard_map/psum | solution.py:172
  125.3 0.7 copy-start.1
  134.6 22.4 %slice-start = ((s8[5419008]{0:T(1024)(128)(4,1)}), s8[4194304]{0:T(1024)(128)(4,1)S(1)}, s32[]{:S(2)}) async-start(s8[5419008]{0:T(1024)(128)(4,1)} %bitcast.352), calls=%async_computation.2 | async-start | bytes 8388608
  135.8 20.3 %copy-start.6 = (bf16[4,2,441,441]{3,1,2,0:T(2,128)(2,1)S(1)}, bf16[4,2,441,441]{3,1,2,0:T(2,128)(2,1)}, u32[]{:S(2)}) copy-start(bf16[4,2,441,441]{3,1,2,0:T(2,128)(2,1)} %param.21) | copy-start | bytes 9335092
  135.8 21.1 %slice-start.1 = ((s8[5419008]{0:T(1024)(128)(4,1)}), s8[1224704]{0:T(1024)(128)(4,1)S(1)}, s32[]{:S(2)}) async-start(s8[5419008]{0:T(1024)(128)(4,1)} %bitcast.352), calls=%async_computation.3 | async-start | bytes 2449408
  156.1 1.0 copy-start.3
  159.3 13.7 %collective-permute-start.2 = (bf16[2,16,512]{2,1,0:T(8,128)(2,1)S(1)}, bf16[2,16,512]{2,1,0:T(8,128)(2,1)S(1)}, u32[]{:S(2)}, u32[]{:S(2)}) collective-permute-start(bf16[2,16,512]{2,1,0:T(8,128)(2,1)S(1)} %get-tuple-element.35), channel_id=1, source_target_pairs={{0,4},{4,8},{8,12},{12,0},{1,5},{5,9},{9,13},{13,1},{2,6},{6,10},{... | collective-permute-start | bytes 98312 | tf_op jit(solution)/shard_map/ppermute | solution.py:22
  159.3 13.6 %collective-permute-start.3 = (bf16[2,16,512]{2,1,0:T(8,128)(2,1)S(1)}, bf16[2,16,512]{2,1,0:T(8,128)(2,1)S(1)}, u32[]{:S(2)}, u32[]{:S(2)}) collective-permute-start(bf16[2,16,512]{2,1,0:T(8,128)(2,1)S(1)} %get-tuple-element.36), channel_id=1, source_target_pairs={{4,0},{8,4},{12,8},{0,12},{5,1},{9,5},{13,9},{1,13},{6,2},{10,6},{... | collective-permute-start | bytes 98312 | tf_op jit(solution)/shard_map/ppermute | solution.py:23
Sparse Core Ops, SparseCore 0:
  59.7 52.4 all-reduce.2
  176.0 51.4 all-reduce.4
where the time goes:
time: 258 us; the launch traced here: 257 us
  blocking collectives  103 us (40%)
  waiting for transfers between devices  94.2 us (37%)
  matrix products  22.9 us (9%)
  between operations  14.7 us (6%)
  other arithmetic  10.5 us (4%)
  starting transfers between devices  7.78 us (3%)
  local copies, waits for them, and re-layouts  4.78 us (2%)
    psum x2, waiting for transfers between devices, apply_operator(): near_all = lax.psum(near_image, ('grp', 'col'))  94.1 us
    psum x5, blocking collectives, row_total(): return lax.psum(partial_value, 'row')  53.4 us
    all_gather x2, blocking collectives, far_part(): piece = lax.all_gather(multipoles, 'row', axis=2, tiled=True)  29.6 us
    all_gather x2, blocking collectives, apply_operator(): far_all = lax.all_gather(far_image, ('grp', 'col'), axis=1, tiled=True)  19.7 us
    dot_general x2, matrix products, far_part(): jnp.einsum('xslp,ypk->xyslk', weighted, panel_expansions, preferred_eleme...  9.08 us
    ppermute x2, starting transfers between devices, extended_2(): after = lax.ppermute(leading, axis, down)  7.62 us
    dot_general x2, matrix products, far_part(): jnp.einsum('ypk,xslk->xyspl', panel_expansions, local_field, preferred_el...  6.73 us
  transfers between devices with their start and end apart: 6, of which 2 were waited for; matrix products, arithmetic and copies ran while one was open for 6% of the time, Pallas kernels for 0%

commit v1 on v0

v1 whole, which is shorter than its diff:
```python
import functools

import jax
import jax.numpy as jnp
from jax import lax
from jax.experimental import pallas as pl
from jax.experimental.pallas import tpu as pltpu
from jax.sharding import PartitionSpec as P

REACH = 2
SPAN = 2 * REACH + 1
LANES = 128
EPSILON = 1e-06
GROUP = ("grp", "col")
EVERY = ("grp", "row", "col")

F32 = jnp.float32
BF16 = jnp.bfloat16
SMEM = pl.BlockSpec(memory_space=pltpu.SMEM)
VMEM = pl.BlockSpec(memory_space=pltpu.VMEM)
ANY = pl.BlockSpec(memory_space=pl.ANY)


def dot_nn(left, right):
    return lax.dot_general(left, right, (((1,), (0,)), ((), ())), preferred_element_type=F32)


def dot_nt(left, right):
    return lax.dot_general(left, right, (((1,), (1,)), ((), ())), preferred_element_type=F32)


def mixed(real_side, imag_side, fields):
    real_part = real_side[:fields] - imag_side[fields:]
    imag_part = real_side[fields:] + imag_side[:fields]
    return jnp.concatenate([real_part, imag_part], axis=0)


def complex_dot(dot, rows, real_matrix, imag_matrix, fields):
    if rows.dtype == F32:
        high = rows.astype(BF16)
        rest = (rows - high.astype(F32)).astype(BF16)
        both = jnp.concatenate([high, rest], axis=0)
        real_side = dot(both, real_matrix)
        imag_side = dot(both, imag_matrix)
        real_side = real_side[: 2 * fields] + real_side[2 * fields :]
        imag_side = imag_side[: 2 * fields] + imag_side[2 * fields :]
    else:
        real_side = dot(rows, real_matrix)
        imag_side = dot(rows, imag_matrix)
    return mixed(real_side, imag_side, fields)


def lower_bound(leaf_ref, value, count):
    def halve(_, bounds):
        low, high = bounds
        middle = lax.div(low + high, 2)
        below = leaf_ref[0, jnp.minimum(middle, count - 1)] < value
        go_up = jnp.logical_and(below, low < high)
        return (jnp.where(go_up, middle + 1, low), jnp.where(go_up, high, jnp.minimum(middle, high)))

    low, _ = lax.fori_loop(0, count.bit_length(), halve, (jnp.int32(0), jnp.int32(count)))
    return low


def leaf_window(leaf_ref, leaf, count, width):
    start = lower_bound(leaf_ref, leaf, count)
    end = lower_bound(leaf_ref, leaf + 1, count)
    unit = jnp.minimum(lax.div(start, LANES), count // LANES - width)
    return start, end, unit


def window_mask(start, end, unit, rows, width):
    lane = lax.broadcasted_iota(jnp.int32, (rows, width * LANES), 1) + unit * LANES
    return jnp.logical_and(lane >= start, lane < end)


def multi_kernel(fields, items, width, pick_ref, leaf_ref, low_ref, exp_ref, out_ref, buf, sem):
    count = leaf_ref.shape[1]
    windows, copies = [], []
    for i in range(items):
        start, end, unit = leaf_window(leaf_ref, pick_ref[i], count, width)
        first = pl.multiple_of(unit * LANES, LANES)
        copy = pltpu.make_async_copy(
            exp_ref.at[:, pl.ds(first, width * LANES), :], buf.at[i], sem.at[i]
        )
        copy.start()
        windows.append((start, end, unit))
        copies.append(copy)
    for i in range(items):
        start, end, unit = windows[i]
        if len(low_ref.shape) == 2:
            first = pl.multiple_of(unit * LANES, LANES)
            rows = low_ref[:, pl.ds(first, width * LANES)]
        else:
            rows = jnp.concatenate([low_ref[unit + k] for k in range(width)], axis=-1)
        mask = window_mask(start, end, unit, 2 * fields, width)
        kept = jnp.where(mask, rows.astype(F32), 0.0).astype(rows.dtype)
        copies[i].wait()
        out_ref[i] = complex_dot(dot_nn, kept, buf[i, 0], buf[i, 1], fields).astype(BF16)


def near_kernel(fields, pairs_ref, count_ref, before_ref, here_ref, after_ref, tiles_ref, out_ref, ext):
    units = out_ref.shape[0]
    slots, tile = tiles_ref.shape[1], tiles_ref.shape[2]
    per = tile // LANES
    edge = REACH * per
    if len(here_ref.shape) == 2:
        for k in range(edge):
            ext[k] = before_ref[:, k * LANES : (k + 1) * LANES]
            ext[edge + units + k] = after_ref[:, k * LANES : (k + 1) * LANES]
        for k in range(units):
            ext[edge + k] = here_ref[:, k * LANES : (k + 1) * LANES]
    else:
        ext[0:edge] = before_ref[...]
        ext[edge + units : 2 * edge + units] = after_ref[...]
        ext[edge : edge + units] = here_ref[...]
    out_ref[...] = jnp.zeros_like(out_ref)
    for s in range(slots):

        @pl.when(s < count_ref[0])
        def _(s=s):
            code = pairs_ref[s]
            target = lax.div(code, SPAN)
            source = target + lax.rem(code, SPAN)
            rows = jnp.concatenate([ext[source * per + k] for k in range(per)], axis=-1)
            value = complex_dot(dot_nt, rows, tiles_ref[0, s], tiles_ref[1, s], fields)
            for k in range(per):
                out_ref[target * per + k] += value[:, k * LANES : (k + 1) * LANES]


def far_kernel(
    fields, items, width, target_ref, offset_ref, leaf_ref, item_ref, partial_ref, exp_ref, trans_ref,
    out_ref, total, exp_buf, trans_buf, sem,
):
    count = leaf_ref.shape[1]
    windows, copies = [], []
    for i in range(items):
        trans_copy = pltpu.make_async_copy(trans_ref.at[offset_ref[i]], trans_buf.at[i], sem.at[i, 0])
        trans_copy.start()
        start, end, unit = leaf_window(leaf_ref, target_ref[i], count, width)
        first = pl.multiple_of(unit * LANES, LANES)
        exp_copy = pltpu.make_async_copy(
            exp_ref.at[:, pl.ds(first, width * LANES), :], exp_buf.at[i], sem.at[i, 1]
        )
        exp_copy.start()
        windows.append((start, end, unit))
        copies.append((trans_copy, exp_copy))
    total[...] = partial_ref[...]
    for i in range(items):
        start, end, unit = windows[i]
        copies[i][0].wait()
        local_field = complex_dot(dot_nn, item_ref[i], trans_buf[i, 0], trans_buf[i, 1], fields)
        copies[i][1].wait()
        image = complex_dot(dot_nt, local_field.astype(BF16), exp_buf[i, 0], exp_buf[i, 1], fields)
        image = jnp.where(window_mask(start, end, unit, 2 * fields, width), image, 0.0)
        for k in range(width):
            total[unit + k] += image[:, k * LANES : (k + 1) * LANES]
    out_ref[...] = total[...].astype(out_ref.dtype)


def final_kernel(fields, coef_ref, right_ref, image_ref, out_ref):
    units = image_ref.shape[0]
    a_real, a_imag, b_real, b_imag = [coef_ref[:, k : k + 1] for k in range(4)]
    for k in range(units):
        lanes = slice(k * LANES, (k + 1) * LANES)
        r_real, r_imag = right_ref[:fields, lanes], right_ref[fields:, lanes]
        z_real = image_ref[k, :fields].astype(F32)
        z_imag = image_ref[k, fields:].astype(F32)
        out_ref[:fields, lanes] = a_real * r_real - a_imag * r_imag + b_real * z_real - b_imag * z_imag
        out_ref[fields:, lanes] = a_real * r_imag + a_imag * r_real + b_real * z_imag + b_imag * z_real


def params():
    return pltpu.CompilerParams(vmem_limit_bytes=16 * 1024 * 1024)


def item_route(rows, group, columns, send):
    items = rows * send // group

    def flat(r, g):
        return (g // columns * rows + r) * columns + g % columns

    if items >= send:
        steps = items // send
        routes = []
        for t in range(steps):
            pairs = []
            for r in range(rows):
                for g in range(group):
                    d = g * steps + (t + r) % steps
                    pairs.append((flat(r, g), flat(d, r // steps)))
            routes.append(pairs)
        return items, steps, routes
    pairs = []
    for r in range(rows):
        for g in range(group):
            d, j = g // send, g % send
            pairs.append((flat(r, g), flat(d, r * send + j)))
    return items, 1, [pairs]


def local(
    right_side,
    near_tiles,
    tile_pairs,
    tile_count,
    panel_expansions,
    leaf_of_panel,
    far_pick,
    far_target,
    far_offset,
    translations,
):
    fields, panels = right_side.shape[1:]
    coefs = panel_expansions.shape[2]
    tile = near_tiles.shape[2]
    send = far_pick.shape[2]
    rows = lax.axis_size("row")
    group = lax.axis_size("grp") * lax.axis_size("col")
    row_here = lax.axis_index("row")
    own = lax.axis_index("grp") * lax.axis_size("col") + lax.axis_index("col")
    both = 2 * fields
    units = panels // LANES
    share = -(-units // group)
    edge = REACH * tile
    edge_units = edge // LANES
    width = tile // LANES + 1
    items, steps, routes = item_route(rows, group, lax.axis_size("col"), send)

    right = right_side.reshape(both, panels)
    picks = lax.dynamic_slice_in_dim(
        lax.dynamic_index_in_dim(far_pick, row_here, 1, keepdims=False).reshape(-1), own * items, items
    )
    targets = lax.dynamic_slice_in_dim(far_target[0], own * items, items)
    offsets = lax.dynamic_slice_in_dim(far_offset[0], own * items, items)
    up = [(i, (i + 1) % rows) for i in range(rows)]
    down = [(j, i) for i, j in up]

    def multipoles(low):
        return pl.pallas_call(
            functools.partial(multi_kernel, fields, items, width),
            out_shape=jax.ShapeDtypeStruct((items, both, coefs), BF16),
            in_specs=[SMEM, SMEM, VMEM, ANY],
            out_specs=VMEM,
            scratch_shapes=[
                pltpu.VMEM((items, 2, width * LANES, coefs), BF16),
                pltpu.SemaphoreType.DMA((items,)),
            ],
            compiler_params=params(),
            cost_estimate=pl.CostEstimate(
                flops=8 * items * fields * width * LANES * coefs,
                bytes_accessed=4 * items * width * LANES * coefs,
                transcendentals=0,
            ),
            name="multi",
        )(picks, leaf_of_panel, low, panel_expansions)

    def exchanged(made):
        if items < send:
            return lax.ppermute(made, EVERY, routes[0])
        taken = jnp.zeros_like(made)
        for t in range(steps):
            outgoing = lax.dynamic_slice_in_dim(made, lax.rem(t + row_here, steps) * send, send)
            arrived = lax.ppermute(outgoing, EVERY, routes[t])
            place = lax.rem(row_here - t + steps, steps) * send
            taken = lax.dynamic_update_slice_in_dim(taken, arrived, place, 0)
        return taken

    def near(before, low, after):
        low_units = (units + 2 * edge_units, both, LANES)
        return pl.pallas_call(
            functools.partial(near_kernel, fields),
            out_shape=jax.ShapeDtypeStruct((units, both, LANES), F32),
            in_specs=[SMEM, SMEM, VMEM, VMEM, VMEM, VMEM],
            out_specs=VMEM,
            scratch_shapes=[pltpu.VMEM(low_units, low.dtype)],
            compiler_params=params(),
            cost_estimate=pl.CostEstimate(
                flops=8 * fields * near_tiles.size // 2,
                bytes_accessed=2 * near_tiles.size,
                transcendentals=0,
            ),
            name="near",
        )(tile_pairs, tile_count, before, low, after, near_tiles)

    def far_added(taken, partial, dtype):
        return pl.pallas_call(
            functools.partial(far_kernel, fields, items, width),
            out_shape=jax.ShapeDtypeStruct((units, both, LANES), dtype),
            in_specs=[SMEM, SMEM, SMEM, VMEM, VMEM, ANY, ANY],
            out_specs=VMEM,
            scratch_shapes=[
                pltpu.VMEM((units, both, LANES), F32),
                pltpu.VMEM((items, 2, width * LANES, coefs), BF16),
                pltpu.VMEM((items, 2, coefs, coefs), BF16),
                pltpu.SemaphoreType.DMA((items, 2)),
            ],
            compiler_params=params(),
            name="far",
        )(targets, offsets, leaf_of_panel, taken, partial, panel_expansions, translations)

    def image_share(low, first, last, dtype):
        before = lax.ppermute(last, "row", up)
        after = lax.ppermute(first, "row", down)
        taken = exchanged(multipoles(low))
        partial = near(before, low, after)
        summands = far_added(taken, partial, dtype)
        summands = jnp.pad(summands, ((0, share * group - units), (0, 0), (0, 0)))
        parts = lax.all_to_all(summands, GROUP, 0, 0, tiled=True)
        return jnp.sum(parts.reshape(group, share, both, LANES).astype(F32), axis=0)

    def inner(left, right_one):
        l_real, l_imag = left[:, :fields], left[:, fields:]
        r_real, r_imag = right_one[:, :fields], right_one[:, fields:]
        real_part = jnp.sum(l_real * r_real + l_imag * r_imag, axis=(0, 2))
        imag_part = jnp.sum(l_real * r_imag - l_imag * r_real, axis=(0, 2))
        return real_part, imag_part

    z_share = image_share(right, right[:, :edge], right[:, panels - edge :], F32)
    z_low = z_share.astype(BF16)
    spread = jnp.broadcast_to(z_low[None], (group, share, both, LANES)).reshape(group * share, both, LANES)
    z_all = lax.all_to_all(spread, GROUP, 0, 0, tiled=True)[:units]
    q_share = image_share(z_all, z_all[:edge_units], z_all[units - edge_units :], BF16)

    right_units = jnp.pad(
        right.reshape(both, units, LANES), ((0, 0), (0, share * group - units), (0, 0))
    )
    r_share = lax.dynamic_slice_in_dim(right_units, own * share, share, 1).transpose(1, 0, 2)
    rr, _ = inner(r_share, r_share)
    rz_real, rz_imag = inner(r_share, z_share)
    zz, _ = inner(z_share, z_share)
    rq_real, rq_imag = inner(r_share, q_share)
    zq_real, zq_imag = inner(z_share, q_share)
    qq, _ = inner(q_share, q_share)
    sums = jnp.stack([rr, rz_real, rz_imag, zz, rq_real, rq_imag, zq_real, zq_imag, qq])
    devices = group * rows
    sums = jnp.broadcast_to(sums.reshape(1, -1), (devices, sums.size))
    sums = jnp.sum(lax.all_to_all(sums, EVERY, 0, 0, tiled=True), axis=0).reshape(9, fields)
    coef = krylov_coefficients(sums)
    coef = jnp.stack(coef, axis=1)
    out = pl.pallas_call(
        functools.partial(final_kernel, fields),
        out_shape=jax.ShapeDtypeStruct((both, panels), F32),
        in_specs=[VMEM, VMEM, VMEM],
        out_specs=VMEM,
        compiler_params=params(),
        name="combine",
    )(coef, right, z_all)
    return out.reshape(right_side.shape)


def krylov_coefficients(sums):
    rr, rz_real, rz_imag, zz, rq_real, rq_imag, zq_real, zq_imag, qq = [sums[k] for k in range(9)]

    def times(left, right):
        return left[0] * right[0] - left[1] * right[1], left[0] * right[1] + left[1] * right[0]

    def conj_times(left, right):
        return left[0] * right[0] + left[1] * right[1], left[0] * right[1] - left[1] * right[0]

    def scale(factor, value):
        return factor * value[0], factor * value[1]

    def plus(*values):
        return sum(v[0] for v in values), sum(v[1] for v in values)

    def size(value):
        return value[0] * value[0] + value[1] * value[1]

    rz, rq, zq = (rz_real, rz_imag), (rq_real, rq_imag), (zq_real, zq_imag)
    beta = jnp.sqrt(rr + EPSILON)
    inv = 1.0 / beta
    norm_one = rr * inv * inv
    product = scale(inv * inv, rz)
    h_first = (0.5 * norm_one + product[0], product[1])
    shift = (h_first[0] - 0.5, h_first[1])
    residue = zz * inv * inv - 2.0 * conj_times(shift, product)[0] + size(shift) * norm_one
    residue = jnp.maximum(residue, 0.0)
    h_sub = jnp.sqrt(residue + EPSILON)
    alpha = inv / h_sub
    gamma = scale(-alpha, shift)
    h_upper = scale(
        inv,
        plus(
            scale(0.5, plus(scale(alpha, rz), scale(rr, gamma))), scale(alpha, rq), times(gamma, rz)
        ),
    )
    second = plus(
        scale(alpha * alpha, zq),
        scale(alpha * zz, gamma),
        scale(alpha, conj_times(gamma, rq)),
        scale(size(gamma), rz),
    )
    h_middle = (0.5 * residue / (h_sub * h_sub) + second[0], second[1])
    keep = (h_middle[0] - 0.5, h_middle[1])
    on_z = plus(gamma, scale(-alpha, keep))
    on_r = plus(scale(-inv, h_upper), scale(-1.0, times(keep, gamma)))
    last = (
        alpha * alpha * qq
        + size(on_z) * zz
        + size(on_r) * rr
        + 2.0
        * (
            conj_times(on_r, times(on_z, rz))[0]
            + alpha * conj_times(on_r, rq)[0]
            + alpha * conj_times(on_z, zq)[0]
        )
    )
    h_last = jnp.sqrt(jnp.maximum(last, 0.0) + EPSILON)
    radius = jnp.sqrt(size(h_first) + h_sub * h_sub)
    cosine = scale(1.0 / radius, h_first)
    sine = h_sub / radius
    upper = plus(conj_times(cosine, h_upper), scale(sine, h_middle))
    lower = plus(times(cosine, h_middle), scale(-sine, h_upper))
    radius_two = jnp.sqrt(size(lower) + h_last * h_last)
    cosine_two = scale(1.0 / radius_two, lower)
    weight_two = scale(-sine * beta / radius_two, (cosine_two[0], -cosine_two[1]))
    goal = scale(beta, (cosine[0], -cosine[1]))
    weight_one = scale(1.0 / radius, plus(goal, scale(-1.0, times(upper, weight_two))))
    on_right = plus(scale(inv, weight_one), times(weight_two, gamma))
    on_image = scale(alpha, weight_two)
    return on_right[0], on_right[1], on_image[0], on_image[1]


def solution(mesh):
    return jax.shard_map(
        local,
        mesh=mesh,
        in_specs=(
            P(None, None, "row"),
            P(None, ("grp", "row", "col"), None, None),
            P(("grp", "row", "col")),
            P(("grp", "row", "col")),
            P(None, "row", None),
            P("row", None),
            P(),
            P("row", None),
            P("row", None),
            P(),
        ),
        out_specs=P(None, None, "row"),
        check_vma=False,
    )
```

time: 258 us -> 107 us (0.41)
  waiting for transfers between devices: 94.2 us -> 5.59 us
  blocking collectives: 103 us -> 34 us
  local copies, waits for them, and re-layouts: 4.78 us -> 30.2 us
  matrix products: 22.9 us -> 0 us
  between operations: 14.7 us -> 0.94 us
  Pallas kernels: 0 us -> 13.7 us
  starting transfers between devices: 7.78 us -> 20.8 us
  other arithmetic: 10.5 us -> 0.77 us
    psum x2 -> x0, waiting for transfers between devices: 94.1 us -> none  [apply_operator(): near_all = lax.psum(near_image, ('grp', 'col'))]
    psum x5 -> x0, blocking collectives: 53.4 us -> none  [row_total(): return lax.psum(partial_value, 'row')]
    all_gather x4 -> x0, blocking collectives: 49.3 us -> none  [the longest x2 29.6 us: far_part(): piece = lax.all_gather(multipoles, 'row', axis=2, tiled=True)]
    all_to_all x0 -> x3, blocking collectives: none -> 34 us  [the longest x1 15.3 us: image_share(): parts = lax.all_to_all(summands, GROUP, 0, 0, tiled=True)]
    unnamed x22 -> x32, local copies, waits for them, and re-layouts: 0.87 us -> 27.4 us
    dot_general x13 -> x0, matrix products: 22.9 us -> none  [the longest x2 9.08 us: far_part(): jnp.einsum('xslp,ypk->xyslk', weighted, panel_expansions, preferred_eleme...]
    pallas_call x0 -> x7, Pallas kernels: none -> 13.7 us  [the longest x2 6.92 us: far_added(): pl.pallas_call(functools.partial(far_kernel, fields, items, width), out_s...]
    all_to_all x0 -> x1, starting transfers between devices: none -> 10.4 us  [image_share(): parts = lax.all_to_all(summands, GROUP, 0, 0, tiled=True)]
  transfers between devices with their start and end apart: 6 -> 7, of which waited for: 2 -> 1; matrix products, arithmetic and copies ran while one was open for 6% -> 19% of each run, Pallas kernels for 0% -> 5%
where the time goes in v1:
time: 107 us; the launch traced here: 106 us
  blocking collectives  34 us (32%)
  local copies, waits for them, and re-layouts  30.2 us (28%)
  starting transfers between devices  20.8 us (19%)
  Pallas kernels  13.7 us (13%)
  waiting for transfers between devices  5.59 us (5%)
    unnamed x32, local copies, waits for them, and re-layouts  27.4 us
    all_to_all x1, blocking collectives, image_share(): parts = lax.all_to_all(summands, GROUP, 0, 0, tiled=True)  15.3 us
    all_to_all x1, blocking collectives, local(): lax.all_to_all(sums, EVERY, 0, 0, tiled=True)  10.6 us
    all_to_all x1, starting transfers between devices, image_share(): parts = lax.all_to_all(summands, GROUP, 0, 0, tiled=True)  10.4 us
    all_to_all x1, blocking collectives, local(): z_all = lax.all_to_all(spread, GROUP, 0, 0, tiled=True)[:units]  8.05 us
    pallas_call x2, Pallas kernels, far_added(): pl.pallas_call(functools.partial(far_kernel, fields, items, width), out_s...  6.92 us
    all_to_all x1, waiting for transfers between devices, image_share(): parts = lax.all_to_all(summands, GROUP, 0, 0, tiled=True)  5.53 us
    ppermute x2, starting transfers between devices, image_share(): after = lax.ppermute(first, 'row', down)  5.33 us
  transfers between devices with their start and end apart: 7, of which 1 were waited for; matrix products, arithmetic and copies ran while one was open for 19% of the time, Pallas kernels for 5%

profile of v1, /device:TPU:0, one launch (start us, length us, event | category | flops | bytes accessed | tf_op | source)
XLA Modules:
  0.0 106.0 jit_solution(17318668933873424588)
XLA Ops:
  0.0 0.9 fusion.8
  0.9 3.1 %collective-permute-start.1 = (f32[32,512]{1,0:T(8,128)S(1)}, f32[32,512]{1,0:T(8,128)S(1)}, u32[]{:S(2)}, u32[]{:S(2)}) collective-permute-start(f32[32,512]{1,0:T(8,128)S(1)} %get-tuple-element.39), channel_id=1, source_target_pairs={{0,4},{4,8},{8,12},{12,0},{1,5},{5,9},{9,13},{13,1},{2,6},{6,10},{... | collective-permute-start | bytes 196616 | tf_op jit(solution)/shard_map/ppermute | solution.py:303
  4.0 2.1 %collective-permute-start.2 = (f32[32,512]{1,0:T(8,128)S(1)}, f32[32,512]{1,0:T(8,128)S(1)}, u32[]{:S(2)}, u32[]{:S(2)}) collective-permute-start(f32[32,512]{1,0:T(8,128)S(1)} %get-tuple-element.38), channel_id=1, source_target_pairs={{4,0},{8,4},{12,8},{0,12},{5,1},{9,5},{13,9},{1,13},{6,2},{10,6},{... | collective-permute-start | bytes 196616 | tf_op jit(solution)/shard_map/ppermute | solution.py:304
  6.1 0.2 dynamic-slice_reduce_fusion
  6.3 0.1 reshape.52
  6.4 16.1 %copy.57.exp_ref = bf16[2,3072,441]{2,1,0:T(8,128)(2,1)} copy(bf16[2,3072,441]{1,0,2:T(2,128)(2,1)} %param.14) | data formatting | bytes 10838016 | tf_op args[4]
  22.5 0.6 dynamic_slice.26.pick_ref
  23.1 2.8 %copy-done.1 = bf16[2,3072,441]{2,1,0:T(8,128)(2,1)S(1)} copy-done((bf16[2,3072,441]{2,1,0:T(8,128)(2,1)S(1)}, bf16[2,3072,441]{2,1,0:T(8,128)(2,1)}, u32[]{:S(2)}) %copy-start.1) | copy-done | bytes 5419032
  25.9 2.2 %multi.2 = bf16[1,32,441]{2,1,0:T(8,128)(2,1)S(1)} custom-call(s32[1]{0:T(128)} %dynamic_slice.26.pick_ref, s32[1,3072]{1,0:T(1,128)S(1)} %copy-done.8, f32[32,3072]{1,0:T(8,128)S(1)} %bitcast.34, bf16[2,3072,441]{2,1,0:T(8,128)(2,1)S(1)} %copy-done.1), custom_call_target="tpu_custom_call" | custom-call | flops 21676032 | bytes 677376 | tf_op jit(solution)/shard_map/multi/pallas_call | solution.py:240
  28.1 0.8 collective-permute-start
  29.6 2.8 %copy.59.trans_ref = bf16[4,2,441,441]{3,2,1,0:T(8,128)(2,1)S(1)} copy(bf16[4,2,441,441]{3,1,2,0:T(2,128)(2,1)} %param.19) | data formatting | bytes 6223392 | tf_op args[9]
  32.4 0.7 constant_dynamic-slice_fusion
  33.2 0.8 near.2.partial_ref
  34.0 3.1 %far.2 = f32[24,32,128]{2,1,0:T(8,128)S(1)} custom-call(s32[1]{0:T(128)} %bitcast.2.target_ref, s32[1]{0:T(128)} %bitcast.3.offset_ref, s32[1,3072]{1,0:T(1,128)S(1)} %copy-done.8, bf16[1,32,441]{2,1,0:T(8,128)(2,1)S(1)} %collective-permute-done.item_ref, f32[24,32,128]{2,1,0:T(8,128)S(1)} %near.2.partial_ref, bf16[2,3072,441]{2,1,0:T(8,128)(2,1)S(1)} %bitcast.32, ...), custom_call_target="tpu_custom_call" | custom-call | tf_op jit(solution)/shard_map/far/pallas_call | solution.py:287
  37.1 15.3 %all_to_all.21 = f32[24,32,128]{2,1,0:T(8,128)S(1)} all-to-all(f32[24,32,128]{2,1,0:T(8,128)S(1)} %far.2), channel_id=1, replica_groups=mesh['grp'=2,'row'=4,'col'=4] {'grp','col'}, dimensions={0} | all-to-all | bytes 786432 | tf_op jit(solution)/shard_map/all_to_all | solution.py:309
  52.6 8.1 %all_to_all.22.low_ref.here_ref.image_ref = bf16[24,32,128]{2,1,0:T(8,128)(2,1)S(1)} all-to-all(bf16[24,32,128]{2,1,0:T(8,128)(2,1)S(1)} %bitcast.39), channel_id=1, replica_groups=mesh['grp'=2,'row'=4,'col'=4] {'grp','col'}, dimensions={0} | all-to-all | bytes 393216 | tf_op jit(solution)/shard_map/all_to_all | solution.py:322
  60.6 0.6 collective-permute-start.4
  61.2 3.2 %collective-permute-start.5 = (bf16[4,32,128]{2,1,0:T(8,128)(2,1)S(1)}, bf16[4,32,128]{2,1,0:T(8,128)(2,1)S(1)}, u32[]{:S(2)}, u32[]{:S(2)}) collective-permute-start(bf16[4,32,128]{2,1,0:T(8,128)(2,1)S(1)} %get-tuple-element.40), channel_id=1, source_target_pairs={{4,0},{8,4},{12,8},{0,12},{5,1},{9,5},{13,9},{1,13},{6,2},{10,6},{... | collective-permute-start | bytes 98312 | tf_op jit(solution)/shard_map/ppermute | solution.py:304
  64.5 2.8 %copy-done.2 = bf16[2,3072,441]{2,1,0:T(8,128)(2,1)S(1)} copy-done((bf16[2,3072,441]{2,1,0:T(8,128)(2,1)S(1)}, bf16[2,3072,441]{2,1,0:T(8,128)(2,1)}, u32[]{:S(2)}) %copy-start.2) | copy-done | bytes 5419032
  67.2 2.2 %multi.3 = bf16[1,32,441]{2,1,0:T(8,128)(2,1)S(1)} custom-call(s32[1]{0:T(128)} %dynamic_slice.26.pick_ref, s32[1,3072]{1,0:T(1,128)S(1)} %copy-done.8, bf16[24,32,128]{2,1,0:T(8,128)(2,1)S(1)} %all_to_all.22.low_ref.here_ref.image_ref, bf16[2,3072,441]{2,1,0:T(8,128)(2,1)S(1)} %copy-done.2), custom_call_target="tpu_custom_call" | custom-call | flops 21676032 | bytes 677376 | tf_op jit(solution)/shard_map/multi/pallas_call | solution.py:240
  69.4 0.7 collective-permute-start.3
  70.1 0.7 near.3.partial_ref
  70.9 2.8 %copy-done.3 = bf16[2,3072,441]{2,1,0:T(8,128)(2,1)S(1)} copy-done((bf16[2,3072,441]{2,1,0:T(8,128)(2,1)S(1)}, bf16[2,3072,441]{2,1,0:T(8,128)(2,1)}, u32[]{:S(2)}) %copy-start.3) | copy-done | bytes 5419032
  73.7 3.8 %far.3 = bf16[24,32,128]{2,1,0:T(8,128)(2,1)} custom-call(s32[1]{0:T(128)} %bitcast.2.target_ref, s32[1]{0:T(128)} %bitcast.3.offset_ref, s32[1,3072]{1,0:T(1,128)S(1)} %copy-done.8, bf16[1,32,441]{2,1,0:T(8,128)(2,1)S(1)} %collective-permute-done.3.item_ref, f32[24,32,128]{2,1,0:T(8,128)S(1)} %near.3.partial_ref, bf16[2,3072,441]{2,1,0:T(8,128)(2,1)S(1)} %copy-done.3, ...), custom_call_target="tpu_custom_call" | custom-call | tf_op jit(solution)/shard_map/far/pallas_call | solution.py:287
  77.5 10.4 %all-to-all-start.2 = ((bf16[24,32,128]{2,1,0:T(8,128)(2,1)}), bf16[24,32,128]{2,1,0:T(8,128)(2,1)S(1)}, u32[]{:S(2)}, u32[]{:S(2)}) async-start(bf16[24,32,128]{2,1,0:T(8,128)(2,1)} %far.3), calls=%async_computation.2 | async-start | bytes 393216 | tf_op jit(solution)/shard_map/all_to_all | solution.py:309
  87.9 5.5 %all-to-all-done.2 = bf16[24,32,128]{2,1,0:T(8,128)(2,1)S(1)} async-done(((bf16[24,32,128]{2,1,0:T(8,128)(2,1)}), bf16[24,32,128]{2,1,0:T(8,128)(2,1)S(1)}, u32[]{:S(2)}, u32[]{:S(2)}) %all-to-all-start.2) | async-done | bytes 196640 | tf_op jit(solution)/shard_map/all_to_all | solution.py:309
  93.5 0.3 subtract_reduce_fusion
  93.9 10.6 %all_to_all.23 = f32[32,1,144]{2,1,0:T(1,128)S(1)} all-to-all(f32[32,1,144]{2,1,0:T(1,128)S(1)} %broadcast_in_dim.15), channel_id=1, replica_groups=mesh['grp'=2,'row'=4,'col'=4] {'grp','row','col'}, dimensions={0} | all-to-all | bytes 36864 | tf_op jit(solution)/shard_map/all_to_all | solution.py:338
  104.6 0.1 add_sqrt_fusion.1
  104.6 0.1 broadcast_divide_fusion
  104.8 0.1 add_bitcast_fusion.1
  105.0 0.9 combine.1
  (47 shorter events, 0.7 us)
Async XLA Ops:
  0.0 6.1 %copy-start = (s32[4,4,2]{1,2,0:T(2,128)S(1)}, s32[4,4,2]{1,2,0:T(2,128)}, u32[]{:S(2)}) copy-start(s32[4,4,2]{1,2,0:T(2,128)} %param.16) | copy-start | bytes 388
  0.9 32.2 %collective-permute-start.1 = (f32[32,512]{1,0:T(8,128)S(1)}, f32[32,512]{1,0:T(8,128)S(1)}, u32[]{:S(2)}, u32[]{:S(2)}) collective-permute-start(f32[32,512]{1,0:T(8,128)S(1)} %get-tuple-element.39), channel_id=1, source_target_pairs={{0,4},{4,8},{8,12},{12,0},{1,5},{5,9},{9,13},{13,1},{2,6},{6,10},{... | collective-permute-start | bytes 196616 | tf_op jit(solution)/shard_map/ppermute | solution.py:303
  4.0 29.2 %collective-permute-start.2 = (f32[32,512]{1,0:T(8,128)S(1)}, f32[32,512]{1,0:T(8,128)S(1)}, u32[]{:S(2)}, u32[]{:S(2)}) collective-permute-start(f32[32,512]{1,0:T(8,128)S(1)} %get-tuple-element.38), channel_id=1, source_target_pairs={{4,0},{8,4},{12,8},{0,12},{5,1},{9,5},{13,9},{1,13},{6,2},{10,6},{... | collective-permute-start | bytes 196616 | tf_op jit(solution)/shard_map/ppermute | solution.py:304
  6.4 16.7 %copy-start.7 = (f32[2,16,3072]{2,1,0:T(8,128)S(1)}, f32[2,16,3072]{2,1,0:T(8,128)}, u32[]{:S(2)}) copy-start(f32[2,16,3072]{2,1,0:T(8,128)} %param.10) | copy-start | bytes 1179652
  6.4 16.7 %copy-start.8 = (s32[1,3072]{1,0:T(1,128)S(1)}, s32[1,3072]{1,0:T(1,128)}, u32[]{:S(2)}) copy-start(s32[1,3072]{1,0:T(1,128)} %leaf_ref.7) | copy-start | bytes 36868
  23.1 2.8 %copy-start.1 = (bf16[2,3072,441]{2,1,0:T(8,128)(2,1)S(1)}, bf16[2,3072,441]{2,1,0:T(8,128)(2,1)}, u32[]{:S(2)}) copy-start(bf16[2,3072,441]{2,1,0:T(8,128)(2,1)} %copy.57.exp_ref) | copy-start | bytes 16257028
  25.9 8.1 %slice-start = ((s8[6291456]{0:T(1024)(128)(4,1)}), s8[4194304]{0:T(1024)(128)(4,1)S(1)}, s32[]{:S(2)}) async-start(s8[6291456]{0:T(1024)(128)(4,1)} %bitcast.31), calls=%async_computation.4 | async-start | bytes 8388608
  28.0 4.3 %copy-start.10 = (s32[1,8]{1,0:T(1,128)S(1)}, s32[1,8]{1,0:T(1,128)}, u32[]{:S(2)}) copy-start(s32[1,8]{1,0:T(1,128)} %param.18) | copy-start | bytes 100
  28.1 4.3 %copy-start.11 = (s32[1,8]{1,0:T(1,128)S(1)}, s32[1,8]{1,0:T(1,128)}, u32[]{:S(2)}) copy-start(s32[1,8]{1,0:T(1,128)} %param.17) | copy-start | bytes 100
  28.1 5.1 %copy-start.6 = (bf16[2,8,256,256]{3,2,1,0:T(8,128)(2,1)S(1)}, bf16[2,8,256,256]{3,2,1,0:T(8,128)(2,1)}, u32[]{:S(2)}) copy-start(bf16[2,8,256,256]{3,2,1,0:T(8,128)(2,1)} %tiles_ref.3) | copy-start | bytes 6291460
  28.1 5.1 %copy-start.9 = (s32[8]{0:T(128)S(1)}, s32[8]{0:T(128)}, u32[]{:S(2)}) copy-start(s32[8]{0:T(128)} %pairs_ref.3) | copy-start | bytes 100
  28.1 5.9 %collective-permute-start = (bf16[1,32,441]{2,1,0:T(8,128)(2,1)S(1)}, bf16[1,32,441]{2,1,0:T(8,128)(2,1)S(1)}, u32[]{:S(2)}, u32[]{:S(2)}) collective-permute-start(bf16[1,32,441]{2,1,0:T(8,128)(2,1)S(1)} %multi.2), channel_id=1, source_target_pairs={{0,0},{1,1},{2,4},{3,5},{16,8},{17,9},{18,12},{19,13},{4,2},{5,3},... | collective-permute-start | bytes 84680 | tf_op jit(solution)/shard_map/ppermute | solution.py:260
  29.5 4.4 %slice-start.1 = ((s8[6291456]{0:T(1024)(128)(4,1)}), s8[2097152]{0:T(1024)(128)(4,1)S(1)}, s32[]{:S(2)}) async-start(s8[6291456]{0:T(1024)(128)(4,1)} %bitcast.31), calls=%async_computation.5 | async-start | bytes 4194304
  32.4 4.7 %copy-start.4 = (bf16[4,2,441,441]{3,2,1,0:T(8,128)(2,1)}, bf16[4,2,441,441]{3,2,1,0:T(8,128)(2,1)S(1)}, u32[]{:S(2)}) copy-start(bf16[4,2,441,441]{3,2,1,0:T(8,128)(2,1)S(1)} %copy.59.trans_ref) | copy-start | bytes 9335092
  60.6 9.4 %collective-permute-start.4 = (bf16[4,32,128]{2,1,0:T(8,128)(2,1)S(1)}, bf16[4,32,128]{2,1,0:T(8,128)(2,1)S(1)}, u32[]{:S(2)}, u32[]{:S(2)}) collective-permute-start(bf16[4,32,128]{2,1,0:T(8,128)(2,1)S(1)} %get-tuple-element.41), channel_id=1, source_target_pairs={{0,4},{4,8},{8,12},{12,0},{1,5},{5,9},{9,13},{13,1},{2,6},{6,10},{... | collective-permute-start | bytes 98312 | tf_op jit(solution)/shard_map/ppermute | solution.py:303
  61.2 8.9 %collective-permute-start.5 = (bf16[4,32,128]{2,1,0:T(8,128)(2,1)S(1)}, bf16[4,32,128]{2,1,0:T(8,128)(2,1)S(1)}, u32[]{:S(2)}, u32[]{:S(2)}) collective-permute-start(bf16[4,32,128]{2,1,0:T(8,128)(2,1)S(1)} %get-tuple-element.40), channel_id=1, source_target_pairs={{4,0},{8,4},{12,8},{0,12},{5,1},{9,5},{13,9},{1,13},{6,2},{10,6},{... | collective-permute-start | bytes 98312 | tf_op jit(solution)/shard_map/ppermute | solution.py:304
  64.5 2.8 %copy-start.2 = (bf16[2,3072,441]{2,1,0:T(8,128)(2,1)S(1)}, bf16[2,3072,441]{2,1,0:T(8,128)(2,1)}, u32[]{:S(2)}) copy-start(bf16[2,3072,441]{2,1,0:T(8,128)(2,1)} %copy.57.exp_ref) | copy-start | bytes 16257028
  67.2 3.6 %copy-start.5 = (bf16[4,2,441,441]{3,2,1,0:T(8,128)(2,1)S(1)}, bf16[4,2,441,441]{3,2,1,0:T(8,128)(2,1)}, u32[]{:S(2)}) copy-start(bf16[4,2,441,441]{3,2,1,0:T(8,128)(2,1)} %copy-done.4) | copy-start | bytes 9335092
  69.4 1.5 %collective-permute-start.3 = (bf16[1,32,441]{2,1,0:T(8,128)(2,1)S(1)}, bf16[1,32,441]{2,1,0:T(8,128)(2,1)S(1)}, u32[]{:S(2)}, u32[]{:S(2)}) collective-permute-start(bf16[1,32,441]{2,1,0:T(8,128)(2,1)S(1)} %multi.3), channel_id=1, source_target_pairs={{0,0},{1,1},{2,4},{3,5},{16,8},{17,9},{18,12},{19,13},{4,2},{5,3},... | collective-permute-start | bytes 84680 | tf_op jit(solution)/shard_map/ppermute | solution.py:260
  70.9 2.8 %copy-start.3 = (bf16[2,3072,441]{2,1,0:T(8,128)(2,1)S(1)}, bf16[2,3072,441]{2,1,0:T(8,128)(2,1)}, u32[]{:S(2)}) copy-start(bf16[2,3072,441]{2,1,0:T(8,128)(2,1)} %copy.57.exp_ref) | copy-start | bytes 16257028
  77.5 16.0 %all-to-all-start.2 = ((bf16[24,32,128]{2,1,0:T(8,128)(2,1)}), bf16[24,32,128]{2,1,0:T(8,128)(2,1)S(1)}, u32[]{:S(2)}, u32[]{:S(2)}) async-start(bf16[24,32,128]{2,1,0:T(8,128)(2,1)} %far.3), calls=%async_computation.2 | async-start | bytes 393216 | tf_op jit(solution)/shard_map/all_to_all | solution.py:309

commit v2 on v1

--- a/solution.py
+++ b/solution.py
@@ -18,7 +18,7 @@
 BF16 = jnp.bfloat16
 SMEM = pl.BlockSpec(memory_space=pltpu.SMEM)
 VMEM = pl.BlockSpec(memory_space=pltpu.VMEM)
-ANY = pl.BlockSpec(memory_space=pl.ANY)
+HBM = pl.BlockSpec(memory_space=pltpu.HBM)
 
 
 def dot_nn(left, right):
@@ -29,25 +29,27 @@
     return lax.dot_general(left, right, (((1,), (1,)), ((), ())), preferred_element_type=F32)
 
 
-def mixed(real_side, imag_side, fields):
-    real_part = real_side[:fields] - imag_side[fields:]
-    imag_part = real_side[fields:] + imag_side[:fields]
-    return jnp.concatenate([real_part, imag_part], axis=0)
-
-
-def complex_dot(dot, rows, real_matrix, imag_matrix, fields):
-    if rows.dtype == F32:
-        high = rows.astype(BF16)
-        rest = (rows - high.astype(F32)).astype(BF16)
-        both = jnp.concatenate([high, rest], axis=0)
-        real_side = dot(both, real_matrix)
-        imag_side = dot(both, imag_matrix)
-        real_side = real_side[: 2 * fields] + real_side[2 * fields :]
-        imag_side = imag_side[: 2 * fields] + imag_side[2 * fields :]
-    else:
-        real_side = dot(rows, real_matrix)
-        imag_side = dot(rows, imag_matrix)
-    return mixed(real_side, imag_side, fields)
+def halves(rows):
+    if rows.dtype != F32:
+        return rows
+    high = rows.astype(BF16)
+    return jnp.concatenate([high, (rows - high.astype(F32)).astype(BF16)], axis=0)
+
+
+def joined(sums, count):
+    return sums if sums.shape[0] == count else sums[:count] + sums[count:]
+
+
+def odd_lanes(shape):
+    return lax.rem(lax.broadcasted_iota(jnp.int32, shape, 1), 2) == 1
+
+
+def from_left(value):
+    return pltpu.roll(value, 1, 1)
+
+
+def from_right(value):
+    return pltpu.roll(value, value.shape[1] - 1, 1)
 
 
 def lower_bound(leaf_ref, value, count):
@@ -74,29 +76,72 @@
     return jnp.logical_and(lane >= start, lane < end)
 
 
-def multi_kernel(fields, items, width, pick_ref, leaf_ref, low_ref, exp_ref, out_ref, buf, sem):
+def multi_rows(fields, width, item, range_ref, low_ref, window_ref):
+    start, end, unit = range_ref[item, 0], range_ref[item, 1], range_ref[item, 2]
+    if len(low_ref.shape) == 2:
+        first = pl.multiple_of(unit * LANES, LANES)
+        rows = low_ref[:, pl.ds(first, width * LANES)]
+    else:
+        rows = jnp.concatenate([low_ref[unit + k] for k in range(width)], axis=-1)
+    mask = window_mask(start, end, unit, 2 * fields, width)
+    rows = halves(jnp.where(mask, rows.astype(F32), 0.0).astype(rows.dtype))
+    total = None
+    for k in range(width):
+        part = dot_nt(rows[:, k * LANES : (k + 1) * LANES], as_rows(window_ref.at[item, k]))
+        total = part if total is None else total + part
+    total = joined(total, 2 * fields)
+    on_real, on_imag = total[:fields], total[fields:]
+    odd = odd_lanes(on_real.shape)
+    other = jnp.where(odd, from_left(on_imag), from_right(on_imag))
+    return jnp.where(odd, -on_real, on_real) - other
+
+
+def as_rows(ref):
+    return ref.reshape(ref.shape[0] * 2, ref.shape[2])[...]
+
+
+def first_multi_kernel(
+    fields, items, width, pick_ref, target_ref, leaf_ref, low_ref, exp_ref,
+    out_ref, range_ref, target_range_ref, window_ref, target_window_ref, spread_ref, sem,
+):
     count = leaf_ref.shape[1]
-    windows, copies = [], []
+    coefs = exp_ref.shape[0]
+    copies = []
     for i in range(items):
-        start, end, unit = leaf_window(leaf_ref, pick_ref[i], count, width)
-        first = pl.multiple_of(unit * LANES, LANES)
-        copy = pltpu.make_async_copy(
-            exp_ref.at[:, pl.ds(first, width * LANES), :], buf.at[i], sem.at[i]
-        )
-        copy.start()
-        windows.append((start, end, unit))
-        copies.append(copy)
+        for which, leaf, ranges, window in (
+            (0, pick_ref[i], range_ref, window_ref),
+            (1, target_ref[i], target_range_ref, target_window_ref),
+        ):
+            start, end, unit = leaf_window(leaf_ref, leaf, count, width)
+            ranges[i, 0], ranges[i, 1], ranges[i, 2] = start, end, unit
+            for k in range(width):
+                first = pl.multiple_of((unit + k) * LANES, LANES)
+                copy = pltpu.make_async_copy(
+                    exp_ref.at[:, :, pl.ds(first, LANES)],
+                    window.at[i, k, pl.ds(0, coefs)],
+                    sem.at[i, which, k],
+                )
+                copy.start()
+                copies.append((which, copy))
+                rest = window.shape[2] - coefs
+                window[i, k, pl.ds(coefs, rest)] = jnp.zeros((rest, 2, LANES), BF16)
+    shape = spread_ref.shape
+    row = lax.broadcasted_iota(jnp.int32, shape, 0)
+    column = lax.broadcasted_iota(jnp.int32, shape, 1)
+    spread_ref[...] = jnp.where(column == 2 * row, 1.0, 0.0).astype(BF16)
+    for which, copy in copies:
+        if which == 0:
+            copy.wait()
     for i in range(items):
-        start, end, unit = windows[i]
-        if len(low_ref.shape) == 2:
-            first = pl.multiple_of(unit * LANES, LANES)
-            rows = low_ref[:, pl.ds(first, width * LANES)]
-        else:
-            rows = jnp.concatenate([low_ref[unit + k] for k in range(width)], axis=-1)
-        mask = window_mask(start, end, unit, 2 * fields, width)
-        kept = jnp.where(mask, rows.astype(F32), 0.0).astype(rows.dtype)
-        copies[i].wait()
-        out_ref[i] = complex_dot(dot_nn, kept, buf[i, 0], buf[i, 1], fields).astype(BF16)
+        out_ref[i] = multi_rows(fields, width, i, range_ref, low_ref, window_ref).astype(BF16)
+    for which, copy in copies:
+        if which == 1:
+            copy.wait()
+
+
+def multi_kernel(fields, items, width, range_ref, low_ref, window_ref, out_ref):
+    for i in range(items):
+        out_ref[i] = multi_rows(fields, width, i, range_ref, low_ref, window_ref).astype(BF16)
 
 
 def near_kernel(fields, pairs_ref, count_ref, before_ref, here_ref, after_ref, tiles_ref, out_ref, ext):
@@ -116,46 +161,68 @@
         ext[edge : edge + units] = here_ref[...]
     out_ref[...] = jnp.zeros_like(out_ref)
     for s in range(slots):
-
-        @pl.when(s < count_ref[0])
-        def _(s=s):
-            code = pairs_ref[s]
-            target = lax.div(code, SPAN)
-            source = target + lax.rem(code, SPAN)
-            rows = jnp.concatenate([ext[source * per + k] for k in range(per)], axis=-1)
-            value = complex_dot(dot_nt, rows, tiles_ref[0, s], tiles_ref[1, s], fields)
-            for k in range(per):
-                out_ref[target * per + k] += value[:, k * LANES : (k + 1) * LANES]
+        code = pairs_ref[s]
+        target = lax.div(code, SPAN)
+        source = target + lax.rem(code, SPAN)
+        rows = halves(jnp.concatenate([ext[source * per + k] for k in range(per)], axis=-1))
+        on_real = joined(dot_nt(rows, tiles_ref[0, s]), 2 * fields)
+        on_imag = joined(dot_nt(rows, tiles_ref[1, s]), 2 * fields)
+        value = jnp.concatenate(
+            [on_real[:fields] - on_imag[fields:], on_real[fields:] + on_imag[:fields]], axis=0
+        )
+        value = jnp.where(s < count_ref[0], value, 0.0)
+        for k in range(per):
+            out_ref[target * per + k] += value[:, k * LANES : (k + 1) * LANES]
 
 
 def far_kernel(
-    fields, items, width, target_ref, offset_ref, leaf_ref, item_ref, partial_ref, exp_ref, trans_ref,
-    out_ref, total, exp_buf, trans_buf, sem,
+    fields, items, width, core_ref, range_ref, item_ref, partial_ref, trans_ref, spread_ref, window_ref,
+    keep_ref, give_ref, total,
 ):
-    count = leaf_ref.shape[1]
-    windows, copies = [], []
+    units = partial_ref.shape[0]
+    total[0:units] = partial_ref[...]
+    if total.shape[0] > units:
+        total[units:] = jnp.zeros((total.shape[0] - units, *total.shape[1:]), F32)
     for i in range(items):
-        trans_copy = pltpu.make_async_copy(trans_ref.at[offset_ref[i]], trans_buf.at[i], sem.at[i, 0])
-        trans_copy.start()
-        start, end, unit = leaf_window(leaf_ref, target_ref[i], count, width)
-        first = pl.multiple_of(unit * LANES, LANES)
-        exp_copy = pltpu.make_async_copy(
-            exp_ref.at[:, pl.ds(first, width * LANES), :], exp_buf.at[i], sem.at[i, 1]
-        )
-        exp_copy.start()
-        windows.append((start, end, unit))
-        copies.append((trans_copy, exp_copy))
-    total[...] = partial_ref[...]
-    for i in range(items):
-        start, end, unit = windows[i]
-        copies[i][0].wait()
-        local_field = complex_dot(dot_nn, item_ref[i], trans_buf[i, 0], trans_buf[i, 1], fields)
-        copies[i][1].wait()
-        image = complex_dot(dot_nt, local_field.astype(BF16), exp_buf[i, 0], exp_buf[i, 1], fields)
-        image = jnp.where(window_mask(start, end, unit, 2 * fields, width), image, 0.0)
+        start, end, unit = range_ref[i, 0], range_ref[i, 1], range_ref[i, 2]
+        plain = item_ref[i].astype(F32)
+        odd = odd_lanes(plain.shape)
+        turned = jnp.where(odd, from_left(plain), -from_right(plain))
+        rows = jnp.concatenate([plain, turned], axis=0).astype(BF16)
+        local_field = dot_nn(rows, trans_ref[i]).astype(BF16)
+        apart = dot_nn(local_field, spread_ref[...])
+        local_real, local_imag = apart[:fields], apart[fields:]
+        rows = jnp.concatenate(
+            [local_real - from_left(local_imag), local_imag + from_left(local_real)], axis=0
+        ).astype(BF16)
+        mask = window_mask(start, end, unit, 2 * fields, width)
         for k in range(width):
-            total[unit + k] += image[:, k * LANES : (k + 1) * LANES]
-    out_ref[...] = total[...].astype(out_ref.dtype)
+            image = dot_nn(rows, as_rows(window_ref.at[i, k]))
+            total[unit + k] += jnp.where(mask[:, k * LANES : (k + 1) * LANES], image, 0.0)
+    chips, share = keep_ref.shape[:2]
+    core = core_ref[0]
+    for c in range(chips):
+        keep_ref[c] = total[pl.ds((2 * c + core) * share, share)].astype(keep_ref.dtype)
+        give_ref[c] = total[pl.ds((2 * c + 1 - core) * share, share)].astype(give_ref.dtype)
+
+
+def fold_kernel(chip_ref, keep_ref, got_ref, own_ref, *out_refs):
+    for step, out_ref in enumerate((own_ref,) + out_refs):
+        chip = lax.bitwise_xor(chip_ref[0], step)
+        out_ref[...] = (keep_ref[chip].astype(F32) + got_ref[chip].astype(F32)).astype(out_ref.dtype)
+
+
+def assemble_kernel(core_ref, chip_ref, mine_ref, theirs_ref, out_ref, first_ref, last_ref, whole):
+    chips, share = mine_ref.shape[:2]
+    units, edge = out_ref.shape[0], first_ref.shape[0]
+    core = core_ref[0]
+    for step in range(chips):
+        chip = lax.bitwise_xor(chip_ref[0], step)
+        whole[pl.ds((2 * chip + core) * share, share)] = mine_ref[step]
+        whole[pl.ds((2 * chip + 1 - core) * share, share)] = theirs_ref[step]
+    out_ref[...] = whole[0:units]
+    first_ref[...] = whole[0:edge]
+    last_ref[...] = whole[units - edge : units]
 
 
 def final_kernel(fields, coef_ref, right_ref, image_ref, out_ref):
@@ -170,8 +237,8 @@
         out_ref[fields:, lanes] = a_real * r_imag + a_imag * r_real + b_real * z_imag + b_imag * z_real
 
 
-def params():
-    return pltpu.CompilerParams(vmem_limit_bytes=16 * 1024 * 1024)
+def params(mebibytes=16):
+    return pltpu.CompilerParams(vmem_limit_bytes=mebibytes * 1024 * 1024)
 
 
 def item_route(rows, group, columns, send):
@@ -236,24 +303,43 @@
     up = [(i, (i + 1) % rows) for i in range(rows)]
     down = [(j, i) for i, j in up]
 
-    def multipoles(low):
+    pad_coefs = -(-coefs // 8) * 8
+    core, chip = lax.rem(own, 2).reshape(1), lax.div(own, 2).reshape(1)
+    chips = group // 2
+    steps_between = range(1, chips)
+    assert group == 2 * chips and chips & (chips - 1) == 0
+    window_shape = jax.ShapeDtypeStruct((items, width, pad_coefs, 2, LANES), BF16)
+    item_shape = jax.ShapeDtypeStruct((items, fields, 2 * pad_coefs), BF16)
+    range_shape = jax.ShapeDtypeStruct((items, 3), jnp.int32)
+    part_shape = (share, both, LANES)
+
+    def first_multipoles(low):
+        return pl.pallas_call(
+            functools.partial(first_multi_kernel, fields, items, width),
+            out_shape=(
+                item_shape,
+                range_shape,
+                range_shape,
+                window_shape,
+                window_shape,
+                jax.ShapeDtypeStruct((coefs, 2 * pad_coefs), BF16),
+            ),
+            in_specs=[SMEM, SMEM, SMEM, VMEM, HBM],
+            out_specs=(VMEM, SMEM, SMEM, VMEM, VMEM, VMEM),
+            scratch_shapes=[pltpu.SemaphoreType.DMA((items, 2, width))],
+            compiler_params=params(58),
+            name="first_multi",
+        )(picks, targets, leaf_of_panel, low, panel_expansions.transpose(2, 0, 1))
+
+    def multipoles(low, ranges, windows):
         return pl.pallas_call(
             functools.partial(multi_kernel, fields, items, width),
-            out_shape=jax.ShapeDtypeStruct((items, both, coefs), BF16),
-            in_specs=[SMEM, SMEM, VMEM, ANY],
+            out_shape=item_shape,
+            in_specs=[SMEM, VMEM, VMEM],
             out_specs=VMEM,
-            scratch_shapes=[
-                pltpu.VMEM((items, 2, width * LANES, coefs), BF16),
-                pltpu.SemaphoreType.DMA((items,)),
-            ],
             compiler_params=params(),
-            cost_estimate=pl.CostEstimate(
-                flops=8 * items * fields * width * LANES * coefs,
-                bytes_accessed=4 * items * width * LANES * coefs,
-                transcendentals=0,
-            ),
             name="multi",
-        )(picks, leaf_of_panel, low, panel_expansions)
+        )(ranges, low, windows)
 
     def exchanged(made):
         if items < send:
@@ -283,31 +369,48 @@
             name="near",
         )(tile_pairs, tile_count, before, low, after, near_tiles)
 
-    def far_added(taken, partial, dtype):
-        return pl.pallas_call(
+    def swapped(value, step):
+        return lax.ppermute(value, GROUP, [(g, g ^ step) for g in range(group)])
+
+    def reduced_share(taken, partial, dtype):
+        half_shape = jax.ShapeDtypeStruct((chips, *part_shape), dtype)
+        keep, give = pl.pallas_call(
             functools.partial(far_kernel, fields, items, width),
-            out_shape=jax.ShapeDtypeStruct((units, both, LANES), dtype),
-            in_specs=[SMEM, SMEM, SMEM, VMEM, VMEM, ANY, ANY],
-            out_specs=VMEM,
-            scratch_shapes=[
-                pltpu.VMEM((units, both, LANES), F32),
-                pltpu.VMEM((items, 2, width * LANES, coefs), BF16),
-                pltpu.VMEM((items, 2, coefs, coefs), BF16),
-                pltpu.SemaphoreType.DMA((items, 2)),
-            ],
+            out_shape=(half_shape, half_shape),
+            in_specs=[SMEM, SMEM, VMEM, VMEM, VMEM, VMEM, VMEM],
+            out_specs=(VMEM, VMEM),
+            scratch_shapes=[pltpu.VMEM((share * group, both, LANES), F32)],
             compiler_params=params(),
             name="far",
-        )(targets, offsets, leaf_of_panel, taken, partial, panel_expansions, translations)
-
-    def image_share(low, first, last, dtype):
-        before = lax.ppermute(last, "row", up)
-        after = lax.ppermute(first, "row", down)
-        taken = exchanged(multipoles(low))
-        partial = near(before, low, after)
-        summands = far_added(taken, partial, dtype)
-        summands = jnp.pad(summands, ((0, share * group - units), (0, 0), (0, 0)))
-        parts = lax.all_to_all(summands, GROUP, 0, 0, tiled=True)
-        return jnp.sum(parts.reshape(group, share, both, LANES).astype(F32), axis=0)
+        )(core, target_ranges, taken, partial, moved, spread, target_windows)
+        got = swapped(give, 1)
+        pieces = pl.pallas_call(
+            fold_kernel,
+            out_shape=(jax.ShapeDtypeStruct(part_shape, F32),)
+            + (jax.ShapeDtypeStruct(part_shape, dtype),) * (chips - 1),
+            in_specs=[SMEM, VMEM, VMEM],
+            out_specs=(VMEM,) * chips,
+            compiler_params=params(),
+            name="fold",
+        )(chip, keep, got)
+        total = pieces[0]
+        for step in steps_between:
+            total = total + swapped(pieces[step], 2 * step).astype(F32)
+        return total
+
+    def gathered(low):
+        mine = jnp.stack([low] + [swapped(low, 2 * step) for step in steps_between])
+        theirs = swapped(mine, 1)
+        edge_shape = jax.ShapeDtypeStruct((edge_units, both, LANES), BF16)
+        return pl.pallas_call(
+            assemble_kernel,
+            out_shape=(jax.ShapeDtypeStruct((units, both, LANES), BF16), edge_shape, edge_shape),
+            in_specs=[SMEM, SMEM, VMEM, VMEM],
+            out_specs=(VMEM, VMEM, VMEM),
+            scratch_shapes=[pltpu.VMEM((share * group, both, LANES), BF16)],
+            compiler_params=params(),
+            name="assemble",
+        )(core, chip, mine, theirs)
 
     def inner(left, right_one):
         l_real, l_imag = left[:, :fields], left[:, fields:]
@@ -316,11 +419,21 @@
         imag_part = jnp.sum(l_real * r_imag - l_imag * r_real, axis=(0, 2))
         return real_part, imag_part
 
-    z_share = image_share(right, right[:, :edge], right[:, panels - edge :], F32)
-    z_low = z_share.astype(BF16)
-    spread = jnp.broadcast_to(z_low[None], (group, share, both, LANES)).reshape(group * share, both, LANES)
-    z_all = lax.all_to_all(spread, GROUP, 0, 0, tiled=True)[:units]
-    q_share = image_share(z_all, z_all[:edge_units], z_all[units - edge_units :], BF16)
+    moved = translations.transpose(0, 2, 1, 3)
+    moved = [lax.dynamic_index_in_dim(moved, offsets[i], 0, keepdims=False) for i in range(items)]
+    moved = jnp.pad(jnp.stack(moved), ((0, 0), (0, pad_coefs - coefs), (0, 0), (0, 0)))
+    moved = moved.reshape(items, 2 * pad_coefs, coefs)
+
+    before = lax.ppermute(right[:, panels - edge :], "row", up)
+    after = lax.ppermute(right[:, :edge], "row", down)
+    made, ranges, target_ranges, windows, target_windows, spread = first_multipoles(right)
+    taken = exchanged(made)
+    z_share = reduced_share(taken, near(before, right, after), F32)
+    z_all, first, last = gathered(z_share.astype(BF16))
+    before = lax.ppermute(last, "row", up)
+    after = lax.ppermute(first, "row", down)
+    taken = exchanged(multipoles(z_all, ranges, windows))
+    q_share = reduced_share(taken, near(before, z_all, after), BF16)
 
     right_units = jnp.pad(
         right.reshape(both, units, LANES), ((0, 0), (0, share * group - units), (0, 0))

time: 107 us -> 93 us (0.87)
  blocking collectives: 34 us -> 8.94 us
  local copies, waits for them, and re-layouts: 30.2 us -> 15.8 us
  starting transfers between devices: 20.8 us -> 32.5 us
  waiting for transfers between devices: 5.59 us -> 16.3 us
  between operations: 0.94 us -> 2.87 us
  Pallas kernels: 13.7 us -> 15.2 us
    all_to_all x2 -> x0, blocking collectives: 23.4 us -> none  [the longest x1 15.3 us: image_share(): parts = lax.all_to_all(summands, GROUP, 0, 0, tiled=True)]
    ppermute x4 -> x16, starting transfers between devices: 8.99 us -> 29.7 us  [the longest x12 18.8 us: swapped(): return lax.ppermute(value, GROUP, [(g, g ^ step) for g in range(group)])]
    unnamed x32, local copies, waits for them, and re-layouts: 27.4 us -> 6.67 us
    ppermute x4 -> x16, waiting for transfers between devices: 0.01 us -> 16.3 us  [the longest x12 16.3 us: swapped(): return lax.ppermute(value, GROUP, [(g, g ^ step) for g in range(group)])]
    all_to_all x1 -> x0, starting transfers between devices: 10.4 us -> none  [image_share(): parts = lax.all_to_all(summands, GROUP, 0, 0, tiled=True)]
    all_to_all x1 -> x0, waiting for transfers between devices: 5.53 us -> none  [image_share(): parts = lax.all_to_all(summands, GROUP, 0, 0, tiled=True)]
    pallas_call x2 -> x6, Pallas kernels: 6.92 us -> 10.7 us  [the longest x1 5.83 us: first_multipoles(): pl.pallas_call(functools.partial(first_multi_kernel, fields, items, width...]
    pallas_call x2 -> x1, Pallas kernels: 4.33 us -> 1.07 us  [multipoles(): pl.pallas_call(functools.partial(multi_kernel, fields, items, width), out...]
  transfers between devices with their start and end apart: 7 -> 18, of which waited for: 1 -> 10; matrix products, arithmetic and copies ran while one was open for 19% -> 7% of each run, Pallas kernels for 5% -> 4%
where the time goes in v2:
time: 93 us; the launch traced here: 92.4 us
  starting transfers between devices  32.5 us (35%)
  waiting for transfers between devices  16.3 us (18%)
  local copies, waits for them, and re-layouts  15.8 us (17%)
  Pallas kernels  15.2 us (16%)
  blocking collectives  8.94 us (10%)
  between operations  2.87 us (3%)
    ppermute x12, starting transfers between devices, swapped(): return lax.ppermute(value, GROUP, [(g, g ^ step) for g in range(group)])  18.8 us
    ppermute x12, waiting for transfers between devices, swapped(): return lax.ppermute(value, GROUP, [(g, g ^ step) for g in range(group)])  16.3 us
    all_to_all x1, blocking collectives, local(): lax.all_to_all(sums, EVERY, 0, 0, tiled=True)  8.94 us
    unnamed x32, local copies, waits for them, and re-layouts  6.67 us
    pallas_call x1, Pallas kernels, first_multipoles(): pl.pallas_call(functools.partial(first_multi_kernel, fields, items, width...  5.83 us
    ppermute x1, starting transfers between devices, local(): before = lax.ppermute(right[:, panels - edge:], 'row', up)  4.35 us
    ppermute x1, starting transfers between devices, local(): after = lax.ppermute(first, 'row', down)  3.81 us
    pallas_call x2, Pallas kernels, reduced_share(): pl.pallas_call(functools.partial(far_kernel, fields, items, width), out_s...  3.81 us
  transfers between devices with their start and end apart: 18, of which 10 were waited for; matrix products, arithmetic and copies ran while one was open for 7% of the time, Pallas kernels for 4%

profile of v2, /device:TPU:0, one launch (start us, length us, event | category | flops | bytes accessed | tf_op | source)
XLA Modules:
  0.0 92.4 jit_solution(17996386384703699175)
XLA Ops:
  1.6 1.3 %constant_dynamic-slice_fusion = (s32[1,1]{1,0:T(1,128)}, s32[1,1]{1,0:T(1,128)}) fusion(s32[1,8]{1,0:T(1,128)} %param.18, s32[]{:T(128)S(6)} %select_n.18, s32[1,8]{1,0:T(1,128)} %param.17), kind=kLoop, calls=%fused_computation.16 | loop fusion | bytes 20 | tf_op jit(solution)/shard_map/dynamic_slice | solution.py:302
  2.9 5.8 %first_multi.1 = (bf16[1,16,896]{2,1,0:T(8,128)(2,1)}, s32[1,3]{1,0:T(1,128)}, s32[1,3]{1,0:T(1,128)}, bf16[1,3,448,2,128]{4,3,2,1,0:T(2,128)(2,1)}, bf16[1,3,44...) custom-call(s32[1]{0:T(128)} %dynamic_slice.24.pick_ref, s32[1]{0:T(128)} %bitcast.4.target_ref, s32[1,3072]{1,0:T(1,128)} %leaf_ref.1, ...), custom_call_target="tpu_custom_call" | custom-call | tf_op jit(solution)/shard_map/first_multi/pallas_call | solution.py:317
  8.8 2.1 %collective-permute-start = (bf16[1,16,896]{2,1,0:T(8,128)(2,1)}, bf16[1,16,896]{2,1,0:T(8,128)(2,1)}, u32[]{:S(2)}, u32[]{:S(2)}) collective-permute-start(bf16[1,16,896]{2,1,0:T(8,128)(2,1)} %get-tuple-element.27), channel_id=1, source_target_pairs={{0,0},{1,1},{2,4},{3,5},{16,8},{17,9},{18,12},{19,13},{4,2},{5,3},... | collective-permute-start | bytes 86024 | tf_op jit(solution)/shard_map/ppermute | solution.py:346
  11.6 4.3 %collective-permute-start.1 = (f32[32,512]{1,0:T(8,128)}, f32[32,512]{1,0:T(8,128)S(1)}, u32[]{:S(2)}, u32[]{:S(2)}) collective-permute-start(f32[32,512]{1,0:T(8,128)} %get-tuple-element.83), channel_id=1, source_target_pairs={{0,4},{4,8},{8,12},{12,0},{1,5},{5,9},{9,13},{13,1},{2,6},{6,10},{... | collective-permute-start | bytes 196616 | tf_op jit(solution)/shard_map/ppermute | solution.py:427
  15.9 2.7 %collective-permute-start.2 = (f32[32,512]{1,0:T(8,128)}, f32[32,512]{1,0:T(8,128)S(1)}, u32[]{:S(2)}, u32[]{:S(2)}) collective-permute-start(f32[32,512]{1,0:T(8,128)} %get-tuple-element.82), channel_id=1, source_target_pairs={{4,0},{8,4},{12,8},{0,12},{5,1},{9,5},{13,9},{1,13},{6,2},{10,6},{... | collective-permute-start | bytes 196616 | tf_op jit(solution)/shard_map/ppermute | solution.py:428
  20.5 1.8 %dynamic-slice_bitcast_fusion = bf16[1,441,2,441]{3,2,1,0:T(2,128)(2,1)S(1)} fusion(bf16[4,2,441,441]{3,1,2,0:T(2,128)(2,1)} %param.19, s32[]{:T(128)S(6)} %select_n.19), kind=kLoop, calls=%fused_computation | loop fusion | bytes 1555852 | tf_op jit(solution)/shard_map/jit(dynamic_index_in_dim)/dynamic_slice | solution.py:423
  22.4 1.7 %pad.4 = bf16[1,448,2,441]{3,2,1,0:T(2,128)(2,1)} pad(bf16[1,441,2,441]{3,2,1,0:T(2,128)(2,1)S(1)} %dynamic-slice_bitcast_fusion, bf16[]{:T(256)} %constant.51.clone.1), padding=0_0x0_7x0_0x0_0 | pad | bytes 1568198 | tf_op jit(solution)/shard_map/jit(_pad)/pad | solution.py:424
  24.0 2.5 %reshape.54.trans_ref = bf16[1,896,441]{2,1,0:T(8,128)(2,1)S(1)} reshape(bf16[1,448,2,441]{3,2,1,0:T(2,128)(2,1)} %pad.4) | data formatting | bytes 1580544 | tf_op jit(solution)/shard_map/reshape | solution.py:425
  27.3 1.3 %near.2.partial_ref = f32[24,32,128]{2,1,0:T(8,128)S(1)} custom-call(s32[8]{0:T(128)S(1)} %copy-done.13, s32[1]{0:T(128)S(6)} %copy.41.count_ref, f32[32,512]{1,0:T(8,128)S(1)} %collective-permute-done.1.before_ref, f32[32,3072]{1,0:T(8,128)S(1)} %bitcast.38, f32[32,512]{1,0:T(8,128)S(1)} %collective-permute-done.2.after_ref, ...), custom_call_target="tpu_custom_call" | custom-call | flops 67108864 | bytes 2097152 | tf_op jit(solution)/shard_map/near/pallas_call | solution.py:357
  28.6 1.1 %copy-done.3 = bf16[441,896]{1,0:T(8,128)(2,1)S(1)} copy-done((bf16[441,896]{1,0:T(8,128)(2,1)S(1)}, bf16[441,896]{1,0:T(8,128)(2,1)}, u32[]{:S(2)}) %copy-start.3) | copy-done | bytes 790296
  29.7 1.1 %copy-done.5 = bf16[1,3,448,2,128]{4,3,2,1,0:T(2,128)(2,1)S(1)} copy-done((bf16[1,3,448,2,128]{4,3,2,1,0:T(2,128)(2,1)S(1)}, bf16[1,3,448,2,128]{4,3,2,1,0:T(2,128)(2,1)}, u32[]{:S(2)}) %copy-start.5) | copy-done | bytes 688152
  30.8 2.4 %far.2 = (f32[4,3,32,128]{3,2,1,0:T(8,128)S(1)}, f32[4,3,32,128]{3,2,1,0:T(8,128)}) custom-call(s32[1]{0:T(128)} %bitcast.3.core_ref, s32[1,3]{1,0:T(1,128)S(1)} %copy-done.12, bf16[1,16,896]{2,1,0:T(8,128)(2,1)} %collective-permute-done.item_ref, f32[24,32,128]{2,1,0:T(8,128)S(1)} %near.2.partial_ref, bf16[1,896,441]{2,1,0:T(8,128)(2,1)S(1)} %reshape.54.trans_ref, ...), custom_call_target="tpu_custom_call" | custom-call | tf_op jit(solution)/shard_map/far/pallas_call | solution.py:377
  33.9 1.8 %collective-permute-done.3.got_ref = f32[4,3,32,128]{3,2,1,0:T(8,128)} collective-permute-done((f32[4,3,32,128]{3,2,1,0:T(8,128)}, f32[4,3,32,128]{3,2,1,0:T(8,128)}, u32[]{:S(2)}, u32[]{:S(2)}) %collective-permute-start.3) | collective-permute-done | bytes 196640 | tf_op jit(solution)/shard_map/ppermute | solution.py:373
  37.5 1.2 %collective-permute-start.4 = (f32[3,32,128]{2,1,0:T(8,128)S(1)}, f32[3,32,128]{2,1,0:T(8,128)S(1)}, u32[]{:S(2)}, u32[]{:S(2)}) collective-permute-start(f32[3,32,128]{2,1,0:T(8,128)S(1)} %get-tuple-element.33), channel_id=1, source_target_pairs={{0,2},{1,3},{2,0},{3,1},{16,18},{17,19},{18,16},{19,17},{4,6},{5,7... | collective-permute-start | bytes 147464 | tf_op jit(solution)/shard_map/ppermute | solution.py:373
  38.8 3.5 %collective-permute-start.5 = (f32[3,32,128]{2,1,0:T(8,128)S(1)}, f32[3,32,128]{2,1,0:T(8,128)S(1)}, u32[]{:S(2)}, u32[]{:S(2)}) collective-permute-start(f32[3,32,128]{2,1,0:T(8,128)S(1)} %get-tuple-element.34), channel_id=1, source_target_pairs={{0,16},{1,17},{2,18},{3,19},{16,0},{17,1},{18,2},{19,3},{4,20},{5,... | collective-permute-start | bytes 147464 | tf_op jit(solution)/shard_map/ppermute | solution.py:373
  42.2 2.2 %collective-permute-done.5 = f32[3,32,128]{2,1,0:T(8,128)S(1)} collective-permute-done((f32[3,32,128]{2,1,0:T(8,128)S(1)}, f32[3,32,128]{2,1,0:T(8,128)S(1)}, u32[]{:S(2)}, u32[]{:S(2)}) %collective-permute-start.5) | collective-permute-done | bytes 49184 | tf_op jit(solution)/shard_map/ppermute | solution.py:373
  44.5 2.7 %collective-permute-done.6 = f32[3,32,128]{2,1,0:T(8,128)S(1)} collective-permute-done((f32[3,32,128]{2,1,0:T(8,128)S(1)}, f32[3,32,128]{2,1,0:T(8,128)S(1)}, u32[]{:S(2)}, u32[]{:S(2)}) %collective-permute-start.6) | collective-permute-done | bytes 49184 | tf_op jit(solution)/shard_map/ppermute | solution.py:373
  47.4 1.0 %collective-permute-start.8 = (bf16[3,32,128]{2,1,0:T(8,128)(2,1)S(1)}, bf16[3,32,128]{2,1,0:T(8,128)(2,1)S(1)}, u32[]{:S(2)}, u32[]{:S(2)}) collective-permute-start(bf16[3,32,128]{2,1,0:T(8,128)(2,1)S(1)} %get-tuple-element.80), channel_id=1, source_target_pairs={{0,16},{1,17},{2,18},{3,19},{16,0},{17,1},{18,2},{19,3},{4,20},{5,... | collective-permute-start | bytes 73736 | tf_op jit(solution)/shard_map/ppermute | solution.py:373
  48.4 2.4 %collective-permute-start.9 = (bf16[3,32,128]{2,1,0:T(8,128)(2,1)S(1)}, bf16[3,32,128]{2,1,0:T(8,128)(2,1)S(1)}, u32[]{:S(2)}, u32[]{:S(2)}) collective-permute-start(bf16[3,32,128]{2,1,0:T(8,128)(2,1)S(1)} %get-tuple-element.80), channel_id=1, source_target_pairs={{0,18},{1,19},{2,16},{3,17},{16,2},{17,3},{18,0},{19,1},{4,22},{5,... | collective-permute-start | bytes 73736 | tf_op jit(solution)/shard_map/ppermute | solution.py:373
  51.2 1.9 %collective-permute-done.9 = bf16[3,32,128]{2,1,0:T(8,128)(2,1)S(1)} collective-permute-done((bf16[3,32,128]{2,1,0:T(8,128)(2,1)S(1)}, bf16[3,32,128]{2,1,0:T(8,128)(2,1)S(1)}, u32[]{:S(2)}, u32[]{:S(2)}) %collective-permute-start.9) | collective-permute-done | bytes 24608 | tf_op jit(solution)/shard_map/ppermute | solution.py:373
  53.2 1.3 %collective-permute-done.10.theirs_ref = bf16[4,3,32,128]{3,2,1,0:T(8,128)(2,1)S(1)} collective-permute-done((bf16[4,3,32,128]{3,2,1,0:T(8,128)(2,1)S(1)}, bf16[4,3,32,128]{3,2,1,0:T(8,128)(2,1)S(1)}, u32[]{:S(2)}, u32[]{:S(2)}) %collective-permute-start.10) | collective-permute-done | bytes 98336 | tf_op jit(solution)/shard_map/ppermute | solution.py:373
  54.6 3.8 %collective-permute-start.13 = (bf16[4,32,128]{2,1,0:T(8,128)(2,1)S(1)}, bf16[4,32,128]{2,1,0:T(8,128)(2,1)S(1)}, u32[]{:S(2)}, u32[]{:S(2)}) collective-permute-start(bf16[4,32,128]{2,1,0:T(8,128)(2,1)S(1)} %get-tuple-element.40), channel_id=1, source_target_pairs={{4,0},{8,4},{12,8},{0,12},{5,1},{9,5},{13,9},{1,13},{6,2},{10,6},{... | collective-permute-start | bytes 98312 | tf_op jit(solution)/shard_map/ppermute | solution.py:434
  58.5 1.1 %copy-done.9 = bf16[1,3,448,2,128]{4,3,2,1,0:T(2,128)(2,1)S(1)} copy-done((bf16[1,3,448,2,128]{4,3,2,1,0:T(2,128)(2,1)S(1)}, bf16[1,3,448,2,128]{4,3,2,1,0:T(2,128)(2,1)}, u32[]{:S(2)}) %copy-start.9) | copy-done | bytes 688152
  59.6 1.1 %multi.1 = bf16[1,16,896]{2,1,0:T(8,128)(2,1)S(1)} custom-call(s32[1,3]{1,0:T(1,128)S(1)} %copy-done.14, bf16[24,32,128]{2,1,0:T(8,128)(2,1)S(1)} %get-tuple-element.37.low_ref.here_ref.image_ref, bf16[1,3,448,2,128]{4,3,2,1,0:T(2,128)(2,1)S(1)} %copy-done.9), custom_call_target="tpu_custom_call" | custom-call | tf_op jit(solution)/shard_map/multi/pallas_call | solution.py:335
  61.3 1.3 %near.3.partial_ref = f32[24,32,128]{2,1,0:T(8,128)S(1)} custom-call(s32[8]{0:T(128)S(1)} %copy-done.13, s32[1]{0:T(128)S(6)} %copy.41.count_ref, bf16[4,32,128]{2,1,0:T(8,128)(2,1)S(1)} %collective-permute-done.12.before_ref, bf16[24,32,128]{2,1,0:T(8,128)(2,1)S(1)} %get-tuple-element.37.low_ref.here_ref.image_ref, ...), custom_call_target="tpu_custom_call" | custom-call | flops 67108864 | bytes 2097152 | tf_op jit(solution)/shard_map/near/pallas_call | solution.py:357
  62.6 1.5 %far.3 = (bf16[4,3,32,128]{3,2,1,0:T(8,128)(2,1)S(1)}, bf16[4,3,32,128]{3,2,1,0:T(8,128)(2,1)S(1)}) custom-call(s32[1]{0:T(128)} %bitcast.3.core_ref, s32[1,3]{1,0:T(1,128)S(1)} %copy-done.12, bf16[1,16,896]{2,1,0:T(8,128)(2,1)S(1)} %collective-permute-done.11.item_ref, f32[24,32,128]{2,1,0:T(8,128)S(1)} %near.3.partial_ref, ...), custom_call_target="tpu_custom_call" | custom-call | tf_op jit(solution)/shard_map/far/pallas_call | solution.py:377
  64.2 1.2 %collective-permute-done.14.got_ref = bf16[4,3,32,128]{3,2,1,0:T(8,128)(2,1)S(1)} collective-permute-done((bf16[4,3,32,128]{3,2,1,0:T(8,128)(2,1)S(1)}, bf16[4,3,32,128]{3,2,1,0:T(8,128)(2,1)S(1)}, u32[]{:S(2)}, u32[]{:S(2)}) %collective-permute-start.14) | collective-permute-done | bytes 98336 | tf_op jit(solution)/shard_map/ppermute | solution.py:373
  65.5 5.7 %collective-permute-start.15 = (bf16[3,32,128]{2,1,0:T(8,128)(2,1)S(1)}, bf16[3,32,128]{2,1,0:T(8,128)(2,1)S(1)}, u32[]{:S(2)}, u32[]{:S(2)}) collective-permute-start(bf16[3,32,128]{2,1,0:T(8,128)(2,1)S(1)} %get-tuple-element.44), channel_id=1, source_target_pairs={{0,2},{1,3},{2,0},{3,1},{16,18},{17,19},{18,16},{19,17},{4,6},{5,7... | collective-permute-start | bytes 73736 | tf_op jit(solution)/shard_map/ppermute | solution.py:373
  71.2 4.7 %collective-permute-start.16 = (bf16[3,32,128]{2,1,0:T(8,128)(2,1)S(1)}, bf16[3,32,128]{2,1,0:T(8,128)(2,1)S(1)}, u32[]{:S(2)}, u32[]{:S(2)}) collective-permute-start(bf16[3,32,128]{2,1,0:T(8,128)(2,1)S(1)} %get-tuple-element.45), channel_id=1, source_target_pairs={{0,16},{1,17},{2,18},{3,19},{16,0},{17,1},{18,2},{19,3},{4,20},{5,... | collective-permute-start | bytes 73736 | tf_op jit(solution)/shard_map/ppermute | solution.py:373
  75.9 1.8 %collective-permute-done.16 = bf16[3,32,128]{2,1,0:T(8,128)(2,1)S(1)} collective-permute-done((bf16[3,32,128]{2,1,0:T(8,128)(2,1)S(1)}, bf16[3,32,128]{2,1,0:T(8,128)(2,1)S(1)}, u32[]{:S(2)}, u32[]{:S(2)}) %collective-permute-start.16) | collective-permute-done | bytes 24608 | tf_op jit(solution)/shard_map/ppermute | solution.py:373
  77.7 2.9 %collective-permute-done.17 = bf16[3,32,128]{2,1,0:T(8,128)(2,1)S(1)} collective-permute-done((bf16[3,32,128]{2,1,0:T(8,128)(2,1)S(1)}, bf16[3,32,128]{2,1,0:T(8,128)(2,1)S(1)}, u32[]{:S(2)}, u32[]{:S(2)}) %collective-permute-start.17) | collective-permute-done | bytes 24608 | tf_op jit(solution)/shard_map/ppermute | solution.py:373
  81.0 8.9 %all_to_all.6 = f32[32,1,144]{2,1,0:T(1,128)S(1)} all-to-all(f32[32,1,144]{2,1,0:T(1,128)S(1)} %broadcast_in_dim.8), channel_id=1, replica_groups=mesh['grp'=2,'row'=4,'col'=4] {'grp','row','col'}, dimensions={0} | all-to-all | bytes 36864 | tf_op jit(solution)/shard_map/all_to_all | solution.py:451
  (70 shorter events, 9.3 us)
Async XLA Ops:
  0.0 0.7 copy-start
  0.0 10.9 %copy-start.2 = (f32[2,16,3072]{2,1,0:T(8,128)S(1)}, f32[2,16,3072]{2,1,0:T(8,128)}, u32[]{:S(2)}) copy-start(f32[2,16,3072]{2,1,0:T(8,128)} %param.10) | copy-start | bytes 1179652
  8.8 18.5 %copy-start.1 = (bf16[2,8,256,256]{3,2,1,0:T(8,128)(2,1)S(1)}, bf16[2,8,256,256]{3,2,1,0:T(8,128)(2,1)}, u32[]{:S(2)}) copy-start(bf16[2,8,256,256]{3,2,1,0:T(8,128)(2,1)} %tiles_ref.3) | copy-start | bytes 6291460
  8.8 18.5 %copy-start.13 = (s32[8]{0:T(128)S(1)}, s32[8]{0:T(128)}, u32[]{:S(2)}) copy-start(s32[8]{0:T(128)} %pairs_ref.3) | copy-start | bytes 100
  8.8 19.8 %collective-permute-start = (bf16[1,16,896]{2,1,0:T(8,128)(2,1)}, bf16[1,16,896]{2,1,0:T(8,128)(2,1)}, u32[]{:S(2)}, u32[]{:S(2)}) collective-permute-start(bf16[1,16,896]{2,1,0:T(8,128)(2,1)} %get-tuple-element.27), channel_id=1, source_target_pairs={{0,0},{1,1},{2,4},{3,5},{16,8},{17,9},{18,12},{19,13},{4,2},{5,3},... | collective-permute-start | bytes 86024 | tf_op jit(solution)/shard_map/ppermute | solution.py:346
  11.6 15.7 %collective-permute-start.1 = (f32[32,512]{1,0:T(8,128)}, f32[32,512]{1,0:T(8,128)S(1)}, u32[]{:S(2)}, u32[]{:S(2)}) collective-permute-start(f32[32,512]{1,0:T(8,128)} %get-tuple-element.83), channel_id=1, source_target_pairs={{0,4},{4,8},{8,12},{12,0},{1,5},{5,9},{9,13},{13,1},{2,6},{6,10},{... | collective-permute-start | bytes 196616 | tf_op jit(solution)/shard_map/ppermute | solution.py:427
  15.9 11.3 %collective-permute-start.2 = (f32[32,512]{1,0:T(8,128)}, f32[32,512]{1,0:T(8,128)S(1)}, u32[]{:S(2)}, u32[]{:S(2)}) collective-permute-start(f32[32,512]{1,0:T(8,128)} %get-tuple-element.82), channel_id=1, source_target_pairs={{4,0},{8,4},{12,8},{0,12},{5,1},{9,5},{13,9},{1,13},{6,2},{10,6},{... | collective-permute-start | bytes 196616 | tf_op jit(solution)/shard_map/ppermute | solution.py:428
  22.3 6.2 %copy-start.12 = (s32[1,3]{1,0:T(1,128)S(1)}, s32[1,3]{1,0:T(1,128)}, u32[]{:S(2)}) copy-start(s32[1,3]{1,0:T(1,128)} %get-tuple-element.26.range_ref) | copy-start | bytes 40
  26.6 31.9 %copy-start.14 = (s32[1,3]{1,0:T(1,128)S(1)}, s32[1,3]{1,0:T(1,128)}, u32[]{:S(2)}) copy-start(s32[1,3]{1,0:T(1,128)} %get-tuple-element.36.range_ref) | copy-start | bytes 40
  28.6 1.1 %copy-start.3 = (bf16[441,896]{1,0:T(8,128)(2,1)S(1)}, bf16[441,896]{1,0:T(8,128)(2,1)}, u32[]{:S(2)}) copy-start(bf16[441,896]{1,0:T(8,128)(2,1)} %get-tuple-element.28.spread_ref) | copy-start | bytes 2370820
  29.7 1.1 %copy-start.5 = (bf16[1,3,448,2,128]{4,3,2,1,0:T(2,128)(2,1)S(1)}, bf16[1,3,448,2,128]{4,3,2,1,0:T(2,128)(2,1)}, u32[]{:S(2)}) copy-start(bf16[1,3,448,2,128]{4,3,2,1,0:T(2,128)(2,1)} %get-tuple-element.29.window_ref) | copy-start | bytes 2064388
  33.9 1.8 %collective-permute-start.3 = (f32[4,3,32,128]{3,2,1,0:T(8,128)}, f32[4,3,32,128]{3,2,1,0:T(8,128)}, u32[]{:S(2)}, u32[]{:S(2)}) collective-permute-start(f32[4,3,32,128]{3,2,1,0:T(8,128)} %get-tuple-element.31), channel_id=1, source_target_pairs={{0,1},{1,0},{2,3},{3,2},{16,17},{17,16},{18,19},{19,18},{4,5},{5,4... | collective-permute-start | bytes 589832 | tf_op jit(solution)/shard_map/ppermute | solution.py:373
  33.9 28.7 %copy-start.4 = (bf16[441,896]{1,0:T(8,128)(2,1)S(1)}, bf16[441,896]{1,0:T(8,128)(2,1)}, u32[]{:S(2)}) copy-start(bf16[441,896]{1,0:T(8,128)(2,1)} %get-tuple-element.28.spread_ref) | copy-start | bytes 2370820
  33.9 28.7 %copy-start.6 = (bf16[1,3,448,2,128]{4,3,2,1,0:T(2,128)(2,1)S(1)}, bf16[1,3,448,2,128]{4,3,2,1,0:T(2,128)(2,1)}, u32[]{:S(2)}) copy-start(bf16[1,3,448,2,128]{4,3,2,1,0:T(2,128)(2,1)} %get-tuple-element.29.window_ref) | copy-start | bytes 2064388
  35.7 0.9 %copy-start.11 = (f32[4,3,32,128]{3,2,1,0:T(8,128)S(1)}, f32[4,3,32,128]{3,2,1,0:T(8,128)}, u32[]{:S(2)}) copy-start(f32[4,3,32,128]{3,2,1,0:T(8,128)} %copy-done.10) | copy-start | bytes 589828
  37.5 4.7 %collective-permute-start.4 = (f32[3,32,128]{2,1,0:T(8,128)S(1)}, f32[3,32,128]{2,1,0:T(8,128)S(1)}, u32[]{:S(2)}, u32[]{:S(2)}) collective-permute-start(f32[3,32,128]{2,1,0:T(8,128)S(1)} %get-tuple-element.33), channel_id=1, source_target_pairs={{0,2},{1,3},{2,0},{3,1},{16,18},{17,19},{18,16},{19,17},{4,6},{5,7... | collective-permute-start | bytes 147464 | tf_op jit(solution)/shard_map/ppermute | solution.py:373
  38.8 5.7 %collective-permute-start.5 = (f32[3,32,128]{2,1,0:T(8,128)S(1)}, f32[3,32,128]{2,1,0:T(8,128)S(1)}, u32[]{:S(2)}, u32[]{:S(2)}) collective-permute-start(f32[3,32,128]{2,1,0:T(8,128)S(1)} %get-tuple-element.34), channel_id=1, source_target_pairs={{0,16},{1,17},{2,18},{3,19},{16,0},{17,1},{18,2},{19,3},{4,20},{5,... | collective-permute-start | bytes 147464 | tf_op jit(solution)/shard_map/ppermute | solution.py:373
  42.2 5.0 %collective-permute-start.6 = (f32[3,32,128]{2,1,0:T(8,128)S(1)}, f32[3,32,128]{2,1,0:T(8,128)S(1)}, u32[]{:S(2)}, u32[]{:S(2)}) collective-permute-start(f32[3,32,128]{2,1,0:T(8,128)S(1)} %get-tuple-element.35), channel_id=1, source_target_pairs={{0,18},{1,19},{2,16},{3,17},{16,2},{17,3},{18,0},{19,1},{4,22},{5,... | collective-permute-start | bytes 147464 | tf_op jit(solution)/shard_map/ppermute | solution.py:373
  47.2 3.9 %collective-permute-start.7 = (bf16[3,32,128]{2,1,0:T(8,128)(2,1)S(1)}, bf16[3,32,128]{2,1,0:T(8,128)(2,1)S(1)}, u32[]{:S(2)}, u32[]{:S(2)}) collective-permute-start(bf16[3,32,128]{2,1,0:T(8,128)(2,1)S(1)} %get-tuple-element.80), channel_id=1, source_target_pairs={{0,2},{1,3},{2,0},{3,1},{16,18},{17,19},{18,16},{19,17},{4,6},{5,7... | collective-permute-start | bytes 73736 | tf_op jit(solution)/shard_map/ppermute | solution.py:373
  47.4 3.8 %collective-permute-start.8 = (bf16[3,32,128]{2,1,0:T(8,128)(2,1)S(1)}, bf16[3,32,128]{2,1,0:T(8,128)(2,1)S(1)}, u32[]{:S(2)}, u32[]{:S(2)}) collective-permute-start(bf16[3,32,128]{2,1,0:T(8,128)(2,1)S(1)} %get-tuple-element.80), channel_id=1, source_target_pairs={{0,16},{1,17},{2,18},{3,19},{16,0},{17,1},{18,2},{19,3},{4,20},{5,... | collective-permute-start | bytes 73736 | tf_op jit(solution)/shard_map/ppermute | solution.py:373
  48.4 4.7 %collective-permute-start.9 = (bf16[3,32,128]{2,1,0:T(8,128)(2,1)S(1)}, bf16[3,32,128]{2,1,0:T(8,128)(2,1)S(1)}, u32[]{:S(2)}, u32[]{:S(2)}) collective-permute-start(bf16[3,32,128]{2,1,0:T(8,128)(2,1)S(1)} %get-tuple-element.80), channel_id=1, source_target_pairs={{0,18},{1,19},{2,16},{3,17},{16,2},{17,3},{18,0},{19,1},{4,22},{5,... | collective-permute-start | bytes 73736 | tf_op jit(solution)/shard_map/ppermute | solution.py:373
  53.1 1.4 %collective-permute-start.10 = (bf16[4,3,32,128]{3,2,1,0:T(8,128)(2,1)S(1)}, bf16[4,3,32,128]{3,2,1,0:T(8,128)(2,1)S(1)}, u32[]{:S(2)}, u32[]{:S(2)}) collective-permute-start(bf16[4,3,32,128]{3,2,1,0:T(8,128)(2,1)S(1)} %pad_maximum_fusion.mine_ref), channel_id=1, source_target_pairs={{0,1},{1,0},{2,3},{3,2},{16,17},{17,16},{18,19},{19,18},{4,5},{5,4... | collective-permute-start | bytes 294920 | tf_op jit(solution)/shard_map/ppermute | solution.py:373
  54.6 9.5 %copy-start.7 = (bf16[24,32,128]{2,1,0:T(8,128)(2,1)}, bf16[24,32,128]{2,1,0:T(8,128)(2,1)S(1)}, u32[]{:S(2)}) copy-start(bf16[24,32,128]{2,1,0:T(8,128)(2,1)S(1)} %get-tuple-element.37.low_ref.here_ref.image_ref) | copy-start | bytes 589828
  54.6 6.7 %collective-permute-start.12 = (bf16[4,32,128]{2,1,0:T(8,128)(2,1)S(1)}, bf16[4,32,128]{2,1,0:T(8,128)(2,1)S(1)}, u32[]{:S(2)}, u32[]{:S(2)}) collective-permute-start(bf16[4,32,128]{2,1,0:T(8,128)(2,1)S(1)} %get-tuple-element.39), channel_id=1, source_target_pairs={{0,4},{4,8},{8,12},{12,0},{1,5},{5,9},{9,13},{13,1},{2,6},{6,10},{... | collective-permute-start | bytes 98312 | tf_op jit(solution)/shard_map/ppermute | solution.py:433
  54.6 6.7 %collective-permute-start.13 = (bf16[4,32,128]{2,1,0:T(8,128)(2,1)S(1)}, bf16[4,32,128]{2,1,0:T(8,128)(2,1)S(1)}, u32[]{:S(2)}, u32[]{:S(2)}) collective-permute-start(bf16[4,32,128]{2,1,0:T(8,128)(2,1)S(1)} %get-tuple-element.40), channel_id=1, source_target_pairs={{4,0},{8,4},{12,8},{0,12},{5,1},{9,5},{13,9},{1,13},{6,2},{10,6},{... | collective-permute-start | bytes 98312 | tf_op jit(solution)/shard_map/ppermute | solution.py:434
  58.5 1.1 %copy-start.9 = (bf16[1,3,448,2,128]{4,3,2,1,0:T(2,128)(2,1)S(1)}, bf16[1,3,448,2,128]{4,3,2,1,0:T(2,128)(2,1)}, u32[]{:S(2)}) copy-start(bf16[1,3,448,2,128]{4,3,2,1,0:T(2,128)(2,1)} %get-tuple-element.38.window_ref) | copy-start | bytes 2064388
  60.6 2.0 %collective-permute-start.11 = (bf16[1,16,896]{2,1,0:T(8,128)(2,1)S(1)}, bf16[1,16,896]{2,1,0:T(8,128)(2,1)S(1)}, u32[]{:S(2)}, u32[]{:S(2)}) collective-permute-start(bf16[1,16,896]{2,1,0:T(8,128)(2,1)S(1)} %multi.1), channel_id=1, source_target_pairs={{0,0},{1,1},{2,4},{3,5},{16,8},{17,9},{18,12},{19,13},{4,2},{5,3},... | collective-permute-start | bytes 86024 | tf_op jit(solution)/shard_map/ppermute | solution.py:346
  64.1 1.4 %collective-permute-start.14 = (bf16[4,3,32,128]{3,2,1,0:T(8,128)(2,1)S(1)}, bf16[4,3,32,128]{3,2,1,0:T(8,128)(2,1)S(1)}, u32[]{:S(2)}, u32[]{:S(2)}) collective-permute-start(bf16[4,3,32,128]{3,2,1,0:T(8,128)(2,1)S(1)} %get-tuple-element.42), channel_id=1, source_target_pairs={{0,1},{1,0},{2,3},{3,2},{16,17},{17,16},{18,19},{19,18},{4,5},{5,4... | collective-permute-start | bytes 294920 | tf_op jit(solution)/shard_map/ppermute | solution.py:373
  65.5 10.4 %collective-permute-start.15 = (bf16[3,32,128]{2,1,0:T(8,128)(2,1)S(1)}, bf16[3,32,128]{2,1,0:T(8,128)(2,1)S(1)}, u32[]{:S(2)}, u32[]{:S(2)}) collective-permute-start(bf16[3,32,128]{2,1,0:T(8,128)(2,1)S(1)} %get-tuple-element.44), channel_id=1, source_target_pairs={{0,2},{1,3},{2,0},{3,1},{16,18},{17,19},{18,16},{19,17},{4,6},{5,7... | collective-permute-start | bytes 73736 | tf_op jit(solution)/shard_map/ppermute | solution.py:373
  71.2 6.5 %collective-permute-start.16 = (bf16[3,32,128]{2,1,0:T(8,128)(2,1)S(1)}, bf16[3,32,128]{2,1,0:T(8,128)(2,1)S(1)}, u32[]{:S(2)}, u32[]{:S(2)}) collective-permute-start(bf16[3,32,128]{2,1,0:T(8,128)(2,1)S(1)} %get-tuple-element.45), channel_id=1, source_target_pairs={{0,16},{1,17},{2,18},{3,19},{16,0},{17,1},{18,2},{19,3},{4,20},{5,... | collective-permute-start | bytes 73736 | tf_op jit(solution)/shard_map/ppermute | solution.py:373
  75.9 4.7 %collective-permute-start.17 = (bf16[3,32,128]{2,1,0:T(8,128)(2,1)S(1)}, bf16[3,32,128]{2,1,0:T(8,128)(2,1)S(1)}, u32[]{:S(2)}, u32[]{:S(2)}) collective-permute-start(bf16[3,32,128]{2,1,0:T(8,128)(2,1)S(1)} %get-tuple-element.46), channel_id=1, source_target_pairs={{0,18},{1,19},{2,16},{3,17},{16,2},{17,3},{18,0},{19,1},{4,22},{5,... | collective-permute-start | bytes 73736 | tf_op jit(solution)/shard_map/ppermute | solution.py:373
  90.5 0.9 %copy-start.8 = (bf16[24,32,128]{2,1,0:T(8,128)(2,1)S(1)}, bf16[24,32,128]{2,1,0:T(8,128)(2,1)}, u32[]{:S(2)}) copy-start(bf16[24,32,128]{2,1,0:T(8,128)(2,1)} %copy-done.7) | copy-start | bytes 589828
  (1 other events, 0.7 us)

commit v3 on v2

v3 whole, which is shorter than its diff:
```python
import functools

import jax
import jax.numpy as jnp
from jax import lax
from jax.experimental import pallas as pl
from jax.experimental.pallas import tpu as pltpu
from jax.sharding import PartitionSpec as P

REACH = 2
SPAN = 2 * REACH + 1
LANES = 128
EPSILON = 1e-06
GROUP = ("grp", "col")
CORE, CHIP, OWN, COUNT, CODES = range(5)
PER_ITEM = 5
EVERY = ("grp", "row", "col")

F32 = jnp.float32
BF16 = jnp.bfloat16
SMEM = pl.BlockSpec(memory_space=pltpu.SMEM)
VMEM = pl.BlockSpec(memory_space=pltpu.VMEM)
HBM = pl.BlockSpec(memory_space=pltpu.HBM)


def dot_nn(left, right):
    return lax.dot_general(left, right, (((1,), (0,)), ((), ())), preferred_element_type=F32)


def dot_nt(left, right):
    return lax.dot_general(left, right, (((1,), (1,)), ((), ())), preferred_element_type=F32)


def halves(rows):
    if rows.dtype != F32:
        return rows
    high = rows.astype(BF16)
    return jnp.concatenate([high, (rows - high.astype(F32)).astype(BF16)], axis=0)


def joined(sums, count):
    return sums if sums.shape[0] == count else sums[:count] + sums[count:]


def odd_lanes(shape):
    return lax.rem(lax.broadcasted_iota(jnp.int32, shape, 1), 2) == 1


def from_left(value):
    return pltpu.roll(value, 1, 1)


def from_right(value):
    return pltpu.roll(value, value.shape[1] - 1, 1)


def item_place(slots, item):
    return CODES + slots + PER_ITEM * item


def window_start(leaf_ref, leaf, width):
    units = leaf_ref.shape[1] // LANES
    before = jnp.int32(0)
    for k in range(units):
        before = before + (leaf_ref[0, k * LANES] < leaf).astype(jnp.int32)
    return jnp.clip(before - 1, 0, units - width)


def window_mask(leaves_ref, leaf, unit, rows, width):
    leaves = jnp.concatenate([leaves_ref[unit + k] for k in range(width)], axis=-1)
    return jnp.broadcast_to(leaves, (rows, width * LANES)) == leaf


def window_copies(exp_ref, unit, window_ref, sem, width):
    coefs = exp_ref.shape[0]
    return [
        pltpu.make_async_copy(exp_ref.at[:, unit + k], window_ref.at[k, pl.ds(0, coefs)], sem.at[k])
        for k in range(width)
    ]


def clear_rest(window_ref, coefs, width):
    rest = window_ref.shape[1] - coefs
    for k in range(width):
        window_ref[k, pl.ds(coefs, rest)] = jnp.zeros((rest, 2, LANES), BF16)


def multi_rows(fields, width, leaf, unit, leaves_ref, low_ref, window_ref):
    if len(low_ref.shape) == 2:
        first = pl.multiple_of(unit * LANES, LANES)
        rows = low_ref[:, pl.ds(first, width * LANES)]
    else:
        rows = jnp.concatenate([low_ref[unit + k] for k in range(width)], axis=-1)
    mask = window_mask(leaves_ref, leaf, unit, 2 * fields, width)
    rows = halves(jnp.where(mask, rows.astype(F32), 0.0).astype(rows.dtype))
    total = None
    for k in range(width):
        part = dot_nt(rows[:, k * LANES : (k + 1) * LANES], as_rows(window_ref.at[k]))
        total = part if total is None else total + part
    total = joined(total, 2 * fields)
    on_real, on_imag = total[:fields], total[fields:]
    odd = odd_lanes(on_real.shape)
    other = jnp.where(odd, from_left(on_imag), from_right(on_imag))
    return jnp.where(odd, -on_real, on_real) - other


def as_rows(ref):
    return ref.reshape(ref.shape[0] * 2, ref.shape[2])[...]


def begin_kernel(
    fields, items, width, send, edge, row_ref, own_ref, count_ref, pick_hbm, leaf_hbm, leaves_hbm, target_hbm,
    offset_hbm, pairs_hbm, right_hbm, exp_ref,
    plan_ref, out_ref, window_ref, leaves_ref, right_ref, first_ref, last_ref,
    pick_ref, leaf_ref, target_ref, offset_ref, pairs_ref, sem, window_sem,
):
    panels = right_ref.shape[1]
    loads = [
        pltpu.make_async_copy(source, place, sem.at[k])
        for k, (source, place) in enumerate(
            (
                (leaf_hbm, leaf_ref),
                (pick_hbm, pick_ref),
                (target_hbm, target_ref),
                (offset_hbm, offset_ref),
                (pairs_hbm, pairs_ref),
                (leaves_hbm, leaves_ref),
                (right_hbm, right_ref),
            )
        )
    ]
    for load in loads:
        load.start()
    for i in range(items):
        clear_rest(window_ref.at[i], exp_ref.shape[0], width)
    slots = pairs_ref.shape[0]
    own = own_ref[0]
    loads[0].wait()
    loads[1].wait()
    for i in range(items):
        outgoing = own * items + i
        leaf = pick_ref[lax.div(outgoing, send), lax.rem(outgoing, send), row_ref[0]]
        unit = window_start(leaf_ref, leaf, width)
        place = item_place(slots, i)
        plan_ref[place], plan_ref[place + 1] = leaf, unit
        for copy in window_copies(exp_ref, unit, window_ref.at[i], window_sem.at[i], width):
            copy.start()
    for load in loads[2:]:
        load.wait()
    first_ref[...] = right_ref[:, :edge]
    last_ref[...] = right_ref[:, panels - edge :]
    plan_ref[CORE], plan_ref[CHIP], plan_ref[OWN] = lax.rem(own, 2), lax.div(own, 2), own
    plan_ref[COUNT] = count_ref[0]
    for s in range(slots):
        plan_ref[CODES + s] = pairs_ref[s]
    for i in range(items):
        place = item_place(slots, i)
        leaf = target_ref[0, own * items + i]
        plan_ref[place + 2], plan_ref[place + 3] = leaf, window_start(leaf_ref, leaf, width)
        plan_ref[place + 4] = offset_ref[0, own * items + i]
    for i in range(items):
        place = item_place(slots, i)
        leaf, unit = plan_ref[place], plan_ref[place + 1]
        for copy in window_copies(exp_ref, unit, window_ref.at[i], window_sem.at[i], width):
            copy.wait()
        out_ref[i] = multi_rows(fields, width, leaf, unit, leaves_ref, right_ref, window_ref.at[i]).astype(BF16)


def multi_kernel(fields, items, width, slots, plan_ref, leaves_ref, low_ref, window_ref, out_ref):
    for i in range(items):
        place = item_place(slots, i)
        out_ref[i] = multi_rows(
            fields, width, plan_ref[place], plan_ref[place + 1], leaves_ref, low_ref, window_ref.at[i]
        ).astype(BF16)


def first_near_kernel(
    fields, items, width, plan_ref, exp_ref, trans_ref, before_ref, here_ref, after_ref, tiles_ref,
    out_ref, window_ref, moved_ref, spread_ref, ext, trans_buf, sem, trans_sem,
):
    coefs = trans_ref.shape[3]
    slots = tiles_ref.shape[1]

    def trans_copy(i):
        offset = plan_ref[item_place(slots, i) + 4]
        return pltpu.make_async_copy(trans_ref.at[offset], trans_buf.at[i], trans_sem.at[i])

    def exp_copies(i):
        unit = plan_ref[item_place(slots, i) + 3]
        return window_copies(exp_ref, unit, window_ref.at[i], sem.at[i], width)

    for i in range(items):
        trans_copy(i).start()
        for copy in exp_copies(i):
            copy.start()
        clear_rest(window_ref.at[i], coefs, width)
    shape = spread_ref.shape
    row = lax.broadcasted_iota(jnp.int32, shape, 0)
    column = lax.broadcasted_iota(jnp.int32, shape, 1)
    spread_ref[...] = jnp.where(column == 2 * row, 1.0, 0.0).astype(BF16)
    near_kernel(fields, plan_ref, before_ref, here_ref, after_ref, tiles_ref, out_ref, ext)
    rest = moved_ref.shape[1] - 2 * coefs
    for i in range(items):
        trans_copy(i).wait()
        moved_ref[i, pl.ds(0, 2 * coefs)] = trans_buf[i].reshape(2 * coefs, coefs)
        moved_ref[i, pl.ds(2 * coefs, rest)] = jnp.zeros((rest, coefs), BF16)
        for copy in exp_copies(i):
            copy.wait()


def near_kernel(fields, plan_ref, before_ref, here_ref, after_ref, tiles_ref, out_ref, ext):
    units = out_ref.shape[0]
    slots, tile = tiles_ref.shape[1], tiles_ref.shape[2]
    per = tile // LANES
    edge = REACH * per
    if len(here_ref.shape) == 2:
        for k in range(edge):
            ext[k] = before_ref[:, k * LANES : (k + 1) * LANES]
            ext[edge + units + k] = after_ref[:, k * LANES : (k + 1) * LANES]
        for k in range(units):
            ext[edge + k] = here_ref[:, k * LANES : (k + 1) * LANES]
    else:
        ext[0:edge] = before_ref[...]
        ext[edge + units : 2 * edge + units] = after_ref[...]
        ext[edge : edge + units] = here_ref[...]
    out_ref[...] = jnp.zeros_like(out_ref)
    for s in range(slots):
        code = plan_ref[CODES + s]
        target = lax.div(code, SPAN)
        source = target + lax.rem(code, SPAN)
        rows = halves(jnp.concatenate([ext[source * per + k] for k in range(per)], axis=-1))
        on_real = joined(dot_nt(rows, tiles_ref[0, s]), 2 * fields)
        on_imag = joined(dot_nt(rows, tiles_ref[1, s]), 2 * fields)
        value = jnp.concatenate(
            [on_real[:fields] - on_imag[fields:], on_real[fields:] + on_imag[:fields]], axis=0
        )
        value = jnp.where(s < plan_ref[COUNT], value, 0.0)
        for k in range(per):
            out_ref[target * per + k] += value[:, k * LANES : (k + 1) * LANES]


def far_kernel(
    fields, items, width, slots, plan_ref, leaves_ref, item_ref, partial_ref, trans_ref, spread_ref, window_ref,
    keep_ref, give_ref, total,
):
    units = partial_ref.shape[0]
    total[0:units] = partial_ref[...]
    if total.shape[0] > units:
        total[units:] = jnp.zeros((total.shape[0] - units, *total.shape[1:]), F32)
    for i in range(items):
        place = item_place(slots, i)
        leaf, unit = plan_ref[place + 2], plan_ref[place + 3]
        plain = item_ref[i].astype(F32)
        odd = odd_lanes(plain.shape)
        turned = jnp.where(odd, from_left(plain), -from_right(plain))
        rows = jnp.concatenate([plain, turned], axis=0).astype(BF16)
        local_field = dot_nn(rows, trans_ref[i]).astype(BF16)
        apart = dot_nn(local_field, spread_ref[...])
        local_real, local_imag = apart[:fields], apart[fields:]
        rows = jnp.concatenate(
            [local_real - from_left(local_imag), local_imag + from_left(local_real)], axis=0
        ).astype(BF16)
        mask = window_mask(leaves_ref, leaf, unit, 2 * fields, width)
        for k in range(width):
            image = dot_nn(rows, as_rows(window_ref.at[i, k]))
            total[unit + k] += jnp.where(mask[:, k * LANES : (k + 1) * LANES], image, 0.0)
    chips, share = keep_ref.shape[:2]
    core = plan_ref[CORE]
    for c in range(chips):
        keep_ref[c] = total[pl.ds((2 * c + core) * share, share)].astype(keep_ref.dtype)
        give_ref[c] = total[pl.ds((2 * c + 1 - core) * share, share)].astype(give_ref.dtype)


def fold_kernel(plan_ref, keep_ref, got_ref, own_ref, *out_refs):
    for step, out_ref in enumerate((own_ref,) + out_refs):
        chip = lax.bitwise_xor(plan_ref[CHIP], step)
        out_ref[...] = (keep_ref[chip].astype(F32) + got_ref[chip].astype(F32)).astype(out_ref.dtype)


def pair_kernel(keep_ref, got_ref, out_ref):
    out_ref[...] = (keep_ref[...].astype(F32) + got_ref[...].astype(F32)).astype(out_ref.dtype)


def tree_sum(values):
    while len(values) > 1:
        values = [values[k] + values[k + 1] for k in range(0, len(values), 2)]
    return values[0]


def close_kernel(*refs):
    refs[-1][...] = tree_sum([ref[...].astype(F32) for ref in refs[:-1]])


def assemble_kernel(plan_ref, mine_ref, theirs_ref, out_ref, low_ref, first_ref, last_ref, whole):
    chips, share = mine_ref.shape[:2]
    units, edge = out_ref.shape[0], first_ref.shape[0]
    core = plan_ref[CORE]
    for chip in range(chips):
        whole[pl.ds((2 * chip + core) * share, share)] = mine_ref[chip]
        whole[pl.ds((2 * chip + 1 - core) * share, share)] = theirs_ref[chip]
    out_ref[...] = whole[0:units]
    low_ref[...] = whole[0:units].astype(BF16)
    first_ref[...] = whole[0:edge].astype(BF16)
    last_ref[...] = whole[units - edge : units].astype(BF16)


def flat_lines(columns, fields):
    per = LANES // fields
    lines = []
    for first in range(0, len(columns), per):
        some = columns[first : first + per]
        if len(some) < per:
            some = some + [jnp.zeros(((per - len(some)) * fields, 1), F32)]
        square = jnp.broadcast_to(jnp.concatenate(some, axis=0), (LANES, LANES))
        lines.append(jnp.transpose(square)[:1])
    return jnp.concatenate(lines, axis=0)


def columns_of(lines, count, fields):
    per = LANES // fields
    columns = []
    for k in range(lines.shape[0]):
        square = jnp.transpose(jnp.broadcast_to(lines[k : k + 1], (LANES, LANES)))
        columns += [square[j * fields : (j + 1) * fields, :1] for j in range(per)]
    return columns[:count]


def gram_kernel(fields, plan_ref, right_ref, image_ref, *refs):
    out_ref = refs[-1]
    pieces = refs[:-1]
    units = image_ref.shape[0]
    share = pieces[0].shape[0]
    totals = None
    for k in range(share):
        unit = plan_ref[OWN] * share + k
        place = jnp.minimum(unit, units - 1)
        r = right_ref[:, pl.ds(pl.multiple_of(place * LANES, LANES), LANES)]
        z = image_ref[place]
        q = tree_sum([piece[k].astype(F32) for piece in pieces])
        r = jnp.where(unit < units, r, 0.0)
        z = jnp.where(unit < units, z, 0.0)
        (rr, ri), (zr, zi), (qr, qi) = [(v[:fields], v[fields:]) for v in (r, z, q)]
        products = [
            rr * rr + ri * ri,
            rr * zr + ri * zi,
            rr * zi - ri * zr,
            zr * zr + zi * zi,
            rr * qr + ri * qi,
            rr * qi - ri * qr,
            zr * qr + zi * qi,
            zr * qi - zi * qr,
            qr * qr + qi * qi,
        ]
        totals = products if totals is None else [t + p for t, p in zip(totals, products)]
    lines = flat_lines([jnp.sum(t, axis=1, keepdims=True) for t in totals], fields)
    out_ref[...] = jnp.broadcast_to(lines[None], out_ref.shape)


def final_kernel(fields, sums_ref, right_ref, image_ref, out_ref):
    units = image_ref.shape[0]
    sums = columns_of(jnp.sum(sums_ref[...], axis=0), 9, fields)
    a_real, a_imag, b_real, b_imag = [
        jnp.broadcast_to(value, (fields, LANES)) for value in krylov_coefficients(sums)
    ]
    for k in range(units):
        lanes = slice(k * LANES, (k + 1) * LANES)
        r_real, r_imag = right_ref[:fields, lanes], right_ref[fields:, lanes]
        z_real, z_imag = image_ref[k, :fields], image_ref[k, fields:]
        out_ref[:fields, lanes] = a_real * r_real - a_imag * r_imag + b_real * z_real - b_imag * z_imag
        out_ref[fields:, lanes] = a_real * r_imag + a_imag * r_real + b_real * z_imag + b_imag * z_real


def params(mebibytes=16):
    return pltpu.CompilerParams(vmem_limit_bytes=mebibytes * 1024 * 1024)


def item_route(rows, group, columns, send):
    items = rows * send // group

    def flat(r, g):
        return (g // columns * rows + r) * columns + g % columns

    if items >= send:
        steps = items // send
        routes = []
        for t in range(steps):
            pairs = []
            for r in range(rows):
                for g in range(group):
                    d = g * steps + (t + r) % steps
                    pairs.append((flat(r, g), flat(d, r // steps)))
            routes.append(pairs)
        return items, steps, routes
    pairs = []
    for r in range(rows):
        for g in range(group):
            d, j = g // send, g % send
            pairs.append((flat(r, g), flat(d, r * send + j)))
    return items, 1, [pairs]


def local(
    right_side,
    near_tiles,
    tile_pairs,
    tile_count,
    panel_expansions,
    leaf_of_panel,
    far_pick,
    far_target,
    far_offset,
    translations,
):
    fields, panels = right_side.shape[1:]
    coefs = panel_expansions.shape[2]
    tile = near_tiles.shape[2]
    send = far_pick.shape[2]
    rows = lax.axis_size("row")
    group = lax.axis_size("grp") * lax.axis_size("col")
    row_here = lax.axis_index("row")
    own = lax.axis_index("grp") * lax.axis_size("col") + lax.axis_index("col")
    both = 2 * fields
    units = panels // LANES
    share = -(-units // group)
    edge = REACH * tile
    edge_units = edge // LANES
    width = tile // LANES + 1
    items, steps, routes = item_route(rows, group, lax.axis_size("col"), send)

    up = [(i, (i + 1) % rows) for i in range(rows)]
    down = [(j, i) for i, j in up]

    slots = near_tiles.shape[1]
    pad_coefs = -(-coefs // 8) * 8
    chips = group // 2
    steps_between = range(chips - 1, 0, -1)
    assert group == 2 * chips and chips & (chips - 1) == 0 and LANES % fields == 0
    window_shape = jax.ShapeDtypeStruct((items, width, pad_coefs, 2, LANES), BF16)
    item_shape = jax.ShapeDtypeStruct((items, fields, 2 * pad_coefs), BF16)
    plan_shape = jax.ShapeDtypeStruct((item_place(slots, items),), jnp.int32)
    part_shape = (share, both, LANES)

    def in_hbm(value):
        return pltpu.with_memory_space_constraint(value, pltpu.HBM)

    leaves = leaf_of_panel.reshape(units, 1, LANES)
    expansions = panel_expansions.transpose(2, 0, 1).reshape(coefs, 2, units, LANES).transpose(0, 2, 1, 3)
    expansions = in_hbm(expansions)
    moves = in_hbm(translations.transpose(0, 2, 1, 3))
    picks = far_pick.transpose(0, 2, 1)
    edge_shape = jax.ShapeDtypeStruct((both, edge), F32)

    plan, made, windows, leaves, right, first, last = pl.pallas_call(
        functools.partial(begin_kernel, fields, items, width, send, edge),
        out_shape=(
            plan_shape,
            item_shape,
            window_shape,
            jax.ShapeDtypeStruct(leaves.shape, jnp.int32),
            jax.ShapeDtypeStruct((both, panels), F32),
            edge_shape,
            edge_shape,
        ),
        in_specs=[SMEM] * 3 + [HBM] * 8,
        out_specs=(SMEM,) + (VMEM,) * 6,
        scratch_shapes=[
            pltpu.SMEM(value.shape, jnp.int32)
            for value in (picks, leaf_of_panel, far_target, far_offset, tile_pairs)
        ]
        + [pltpu.SemaphoreType.DMA((7,)), pltpu.SemaphoreType.DMA((items, width))],
        compiler_params=params(),
        name="begin",
    )(
        row_here.reshape(1),
        own.reshape(1),
        tile_count,
        in_hbm(picks),
        in_hbm(leaf_of_panel),
        in_hbm(leaves),
        in_hbm(far_target),
        in_hbm(far_offset),
        in_hbm(tile_pairs),
        in_hbm(right_side.reshape(both, panels)),
        expansions,
    )

    def multipoles(low):
        return pl.pallas_call(
            functools.partial(multi_kernel, fields, items, width, slots),
            out_shape=item_shape,
            in_specs=[SMEM, VMEM, VMEM, VMEM],
            out_specs=VMEM,
            compiler_params=params(),
            name="multi",
        )(plan, leaves, low, windows)

    def exchanged(made):
        if items < send:
            return lax.ppermute(made, EVERY, routes[0])
        taken = jnp.zeros_like(made)
        for t in range(steps):
            outgoing = lax.dynamic_slice_in_dim(made, lax.rem(t + row_here, steps) * send, send)
            arrived = lax.ppermute(outgoing, EVERY, routes[t])
            place = lax.rem(row_here - t + steps, steps) * send
            taken = lax.dynamic_update_slice_in_dim(taken, arrived, place, 0)
        return taken

    image_shape = jax.ShapeDtypeStruct((units, both, LANES), F32)
    near_cost = pl.CostEstimate(
        flops=8 * fields * near_tiles.size // 2, bytes_accessed=2 * near_tiles.size, transcendentals=0
    )

    def first_near(before, low, after):
        return pl.pallas_call(
            functools.partial(first_near_kernel, fields, items, width),
            out_shape=(
                image_shape,
                window_shape,
                jax.ShapeDtypeStruct((items, 2 * pad_coefs, coefs), BF16),
                jax.ShapeDtypeStruct((coefs, 2 * pad_coefs), BF16),
            ),
            in_specs=[SMEM] + [HBM] * 2 + [VMEM] * 4,
            out_specs=(VMEM, VMEM, VMEM, VMEM),
            scratch_shapes=[
                pltpu.VMEM((units + 2 * edge_units, both, LANES), low.dtype),
                pltpu.VMEM((items, coefs, 2, coefs), BF16),
                pltpu.SemaphoreType.DMA((items, width)),
                pltpu.SemaphoreType.DMA((items,)),
            ],
            compiler_params=params(24),
            cost_estimate=near_cost,
            name="first_near",
        )(plan, expansions, moves, before, low, after, near_tiles)

    def near(before, low, after):
        return pl.pallas_call(
            functools.partial(near_kernel, fields),
            out_shape=image_shape,
            in_specs=[SMEM, VMEM, VMEM, VMEM, VMEM],
            out_specs=VMEM,
            scratch_shapes=[pltpu.VMEM((units + 2 * edge_units, both, LANES), low.dtype)],
            compiler_params=params(),
            cost_estimate=near_cost,
            name="near",
        )(plan, before, low, after, near_tiles)

    def swapped(value, step):
        return lax.ppermute(value, GROUP, [(g, g ^ step) for g in range(group)])

    def core_parts(taken, partial, dtype):
        half_shape = jax.ShapeDtypeStruct((chips, *part_shape), dtype)
        keep, give = pl.pallas_call(
            functools.partial(far_kernel, fields, items, width, slots),
            out_shape=(half_shape, half_shape),
            in_specs=[SMEM] + [VMEM] * 6,
            out_specs=(VMEM, VMEM),
            scratch_shapes=[pltpu.VMEM((share * group, both, LANES), F32)],
            compiler_params=params(),
            name="far",
        )(plan, leaves, taken, partial, moved, spread, target_windows)
        return keep, swapped(give, 1)

    def whole_sum(keep, got):
        pair = pl.pallas_call(
            pair_kernel,
            out_shape=jax.ShapeDtypeStruct(keep.shape, BF16),
            in_specs=[VMEM, VMEM],
            out_specs=VMEM,
            compiler_params=params(),
            name="pair",
        )(keep, got)
        arrived = {step: swapped(pair, 2 * step) for step in steps_between}
        mine = pl.pallas_call(
            close_kernel,
            out_shape=jax.ShapeDtypeStruct(keep.shape, F32),
            in_specs=[VMEM] * chips,
            out_specs=VMEM,
            compiler_params=params(),
            name="close",
        )(pair, *[arrived[step] for step in range(1, chips)])
        theirs = swapped(mine, 1)
        low_shape = jax.ShapeDtypeStruct((units, both, LANES), BF16)
        low_edge = jax.ShapeDtypeStruct((edge_units, both, LANES), BF16)
        return pl.pallas_call(
            assemble_kernel,
            out_shape=(image_shape, low_shape, low_edge, low_edge),
            in_specs=[SMEM, VMEM, VMEM],
            out_specs=(VMEM,) * 4,
            scratch_shapes=[pltpu.VMEM((share * group, both, LANES), F32)],
            compiler_params=params(),
            name="assemble",
        )(plan, mine, theirs)

    def share_pieces(keep, got):
        pieces = pl.pallas_call(
            fold_kernel,
            out_shape=(jax.ShapeDtypeStruct(part_shape, F32),)
            + (jax.ShapeDtypeStruct(part_shape, BF16),) * (chips - 1),
            in_specs=[SMEM, VMEM, VMEM],
            out_specs=(VMEM,) * chips,
            compiler_params=params(),
            name="fold",
        )(plan, keep, got)
        arrived = {step: swapped(pieces[step], 2 * step) for step in steps_between}
        return [pieces[0]] + [arrived[step] for step in range(1, chips)]

    before = lax.ppermute(last, "row", up)
    after = lax.ppermute(first, "row", down)
    taken = exchanged(made)
    partial, target_windows, moved, spread = first_near(before, right, after)
    z_all, z_low, first, last = whole_sum(*core_parts(taken, partial, F32))
    before = lax.ppermute(last, "row", up)
    after = lax.ppermute(first, "row", down)
    taken = exchanged(multipoles(z_low))
    pieces = share_pieces(*core_parts(taken, near(before, z_low, after), BF16))

    lines = -(-9 * fields // LANES)
    sums = pl.pallas_call(
        functools.partial(gram_kernel, fields),
        out_shape=jax.ShapeDtypeStruct((group * rows, lines, LANES), F32),
        in_specs=[SMEM] + [VMEM] * (2 + chips),
        out_specs=VMEM,
        compiler_params=params(),
        name="gram",
    )(plan, right, z_all, *pieces)
    sums = lax.all_to_all(sums, EVERY, 0, 0, tiled=True)
    out = pl.pallas_call(
        functools.partial(final_kernel, fields),
        out_shape=jax.ShapeDtypeStruct((both, panels), F32),
        in_specs=[VMEM, VMEM, VMEM],
        out_specs=VMEM,
        compiler_params=params(),
        name="combine",
    )(sums, right, z_all)
    return out.reshape(right_side.shape)


def krylov_coefficients(sums):
    rr, rz_real, rz_imag, zz, rq_real, rq_imag, zq_real, zq_imag, qq = sums

    def times(left, right):
        return left[0] * right[0] - left[1] * right[1], left[0] * right[1] + left[1] * right[0]

    def conj_times(left, right):
        return left[0] * right[0] + left[1] * right[1], left[0] * right[1] - left[1] * right[0]

    def scale(factor, value):
        return factor * value[0], factor * value[1]

    def plus(*values):
        return sum(v[0] for v in values), sum(v[1] for v in values)

    def size(value):
        return value[0] * value[0] + value[1] * value[1]

    rz, rq, zq = (rz_real, rz_imag), (rq_real, rq_imag), (zq_real, zq_imag)
    beta = jnp.sqrt(rr + EPSILON)
    inv = 1.0 / beta
    norm_one = rr * inv * inv
    product = scale(inv * inv, rz)
    h_first = (0.5 * norm_one + product[0], product[1])
    shift = (h_first[0] - 0.5, h_first[1])
    residue = zz * inv * inv - 2.0 * conj_times(shift, product)[0] + size(shift) * norm_one
    residue = jnp.maximum(residue, 0.0)
    h_sub = jnp.sqrt(residue + EPSILON)
    alpha = inv / h_sub
    gamma = scale(-alpha, shift)
    h_upper = scale(
        inv,
        plus(
            scale(0.5, plus(scale(alpha, rz), scale(rr, gamma))), scale(alpha, rq), times(gamma, rz)
        ),
    )
    second = plus(
        scale(alpha * alpha, zq),
        scale(alpha * zz, gamma),
        scale(alpha, conj_times(gamma, rq)),
        scale(size(gamma), rz),
    )
    h_middle = (0.5 * residue / (h_sub * h_sub) + second[0], second[1])
    keep = (h_middle[0] - 0.5, h_middle[1])
    on_z = plus(gamma, scale(-alpha, keep))
    on_r = plus(scale(-inv, h_upper), scale(-1.0, times(keep, gamma)))
    last = (
        alpha * alpha * qq
        + size(on_z) * zz
        + size(on_r) * rr
        + 2.0
        * (
            conj_times(on_r, times(on_z, rz))[0]
            + alpha * conj_times(on_r, rq)[0]
            + alpha * conj_times(on_z, zq)[0]
        )
    )
    h_last = jnp.sqrt(jnp.maximum(last, 0.0) + EPSILON)
    radius = jnp.sqrt(size(h_first) + h_sub * h_sub)
    cosine = scale(1.0 / radius, h_first)
    sine = h_sub / radius
    upper = plus(conj_times(cosine, h_upper), scale(sine, h_middle))
    lower = plus(times(cosine, h_middle), scale(-sine, h_upper))
    radius_two = jnp.sqrt(size(lower) + h_last * h_last)
    cosine_two = scale(1.0 / radius_two, lower)
    weight_two = scale(-sine * beta / radius_two, (cosine_two[0], -cosine_two[1]))
    goal = scale(beta, (cosine[0], -cosine[1]))
    weight_one = scale(1.0 / radius, plus(goal, scale(-1.0, times(upper, weight_two))))
    on_right = plus(scale(inv, weight_one), times(weight_two, gamma))
    on_image = scale(alpha, weight_two)
    return on_right[0], on_right[1], on_image[0], on_image[1]


def solution(mesh):
    return jax.shard_map(
        local,
        mesh=mesh,
        in_specs=(
            P(None, None, "row"),
            P(None, ("grp", "row", "col"), None, None),
            P(("grp", "row", "col")),
            P(("grp", "row", "col")),
            P(None, "row", None),
            P("row", None),
            P(),
            P("row", None),
            P("row", None),
            P(),
        ),
        out_specs=P(None, None, "row"),
        check_vma=False,
    )
```

time: 93 us -> 68.1 us (0.73)
  local copies, waits for them, and re-layouts: 15.8 us -> 0.01 us
  starting transfers between devices: 32.5 us -> 27.7 us
  between operations: 2.87 us -> 0.95 us
    ppermute x2 -> x0, starting transfers between devices: 7.07 us -> none  [the longest x1 4.35 us: local(): before = lax.ppermute(right[:, panels - edge:], 'row', up)]
    unnamed x32 -> x2, local copies, waits for them, and re-layouts: 6.67 us -> 0.01 us
    dynamic_slice x5 -> x0, local copies, waits for them, and re-layouts: 3.97 us -> none  [the longest x1 1.8 us: local(): lax.dynamic_index_in_dim(moved, offsets[i], 0, keepdims=False)]
    ppermute x1 -> x2, starting transfers between devices: 0.06 us -> 3.13 us  [local(): before = lax.ppermute(last, 'row', up)]
    ppermute x12 -> x9, waiting for transfers between devices: 16.3 us -> 13.4 us  [swapped(): return lax.ppermute(value, GROUP, [(g, g ^ step) for g in range(group)])]
    reshape x2 -> x0, local copies, waits for them, and re-layouts: 2.59 us -> none  [the longest x1 2.51 us: local(): moved = moved.reshape(items, 2 * pad_coefs, coefs)]
    ppermute x1 -> x2, starting transfers between devices: 3.81 us -> 5.9 us  [local(): after = lax.ppermute(first, 'row', down)]
    ppermute x1 -> x2, waiting for transfers between devices: 0.01 us -> 1.82 us  [local(): before = lax.ppermute(last, 'row', up)]
  transfers between devices with their start and end apart: 18 -> 15, of which waited for: 10 -> 11; matrix products, arithmetic and copies ran while one was open for 7% -> 0% of each run, Pallas kernels for 4% -> 8%
where the time goes in v3:
time: 68.1 us; the launch traced here: 67.8 us
  starting transfers between devices  27.7 us (41%)
  waiting for transfers between devices  15.8 us (23%)
  Pallas kernels  14.4 us (21%)
  blocking collectives  8.94 us (13%)
  between operations  0.95 us (1%)
    ppermute x9, starting transfers between devices, swapped(): return lax.ppermute(value, GROUP, [(g, g ^ step) for g in range(group)])  17.4 us
    ppermute x9, waiting for transfers between devices, swapped(): return lax.ppermute(value, GROUP, [(g, g ^ step) for g in range(group)])  13.4 us
    all_to_all x1, blocking collectives, local(): sums = lax.all_to_all(sums, EVERY, 0, 0, tiled=True)  8.94 us
    ppermute x2, starting transfers between devices, local(): after = lax.ppermute(first, 'row', down)  5.9 us
    ppermute x2, starting transfers between devices, local(): before = lax.ppermute(last, 'row', up)  3.13 us
    pallas_call x1, Pallas kernels, first_near(): pl.pallas_call(functools.partial(first_near_kernel, fields, items, width)...  3.09 us
    pallas_call x2, Pallas kernels, core_parts(): pl.pallas_call(functools.partial(far_kernel, fields, items, width, slots)...  2.91 us
    pallas_call x1, Pallas kernels, local(): pl.pallas_call(functools.partial(begin_kernel, fields, items, width, send...  2.84 us
  transfers between devices with their start and end apart: 15, of which 11 were waited for; matrix products, arithmetic and copies ran while one was open for 0% of the time, Pallas kernels for 8%

profile of v3, /device:TPU:0, one launch (start us, length us, event | category | flops | bytes accessed | tf_op | source)
XLA Modules:
  0.0 67.8 jit_solution(5741145564486547338)
XLA Ops:
  0.8 2.8 %begin.1 = (s32[17]{0:T(128)S(1)}, bf16[1,16,896]{2,1,0:T(8,128)(2,1)S(1)}, bf16[1,3,448,2,128]{4,3,2,1,0:T(2,128)(2,1)S(1)}, s32[24,1,128]{2,1,0:T(1,128)S(1)},...) custom-call(s32[1]{0:T(128)} %bitcast.row_ref, s32[1]{0:T(128)} %bitcast.1.own_ref, ...), custom_call_target="tpu_custom_call" | custom-call | tf_op jit(solution)/shard_map/begin/pallas_call | solution.py:453
  3.7 3.1 %collective-permute-start.1 = (f32[32,512]{1,0:T(8,128)S(1)}, f32[32,512]{1,0:T(8,128)S(1)}, u32[]{:S(2)}, u32[]{:S(2)}) collective-permute-start(f32[32,512]{1,0:T(8,128)S(1)} %get-tuple-element.32), channel_id=1, source_target_pairs={{0,4},{4,8},{8,12},{12,0},{1,5},{5,9},{9,13},{13,1},{2,6},{6,10},{... | collective-permute-start | bytes 196616 | tf_op jit(solution)/shard_map/ppermute | solution.py:607
  6.7 2.1 %collective-permute-start.2 = (f32[32,512]{1,0:T(8,128)S(1)}, f32[32,512]{1,0:T(8,128)S(1)}, u32[]{:S(2)}, u32[]{:S(2)}) collective-permute-start(f32[32,512]{1,0:T(8,128)S(1)} %get-tuple-element.33), channel_id=1, source_target_pairs={{4,0},{8,4},{12,8},{0,12},{5,1},{9,5},{13,9},{1,13},{6,2},{10,6},{... | collective-permute-start | bytes 196616 | tf_op jit(solution)/shard_map/ppermute | solution.py:608
  8.8 0.7 collective-permute-start
  9.5 1.7 %collective-permute-done.1.before_ref = f32[32,512]{1,0:T(8,128)S(1)} collective-permute-done((f32[32,512]{1,0:T(8,128)S(1)}, f32[32,512]{1,0:T(8,128)S(1)}, u32[]{:S(2)}, u32[]{:S(2)}) %collective-permute-start.1) | collective-permute-done | bytes 65568 | tf_op jit(solution)/shard_map/ppermute | solution.py:607
  11.2 0.5 collective-permute-done.2.after_ref
  11.7 3.1 %first_near.1 = (f32[24,32,128]{2,1,0:T(8,128)S(1)}, bf16[1,3,448,2,128]{4,3,2,1,0:T(2,128)(2,1)S(1)}, bf16[1,896,441]{2,1,0:T(8,128)(2,1)S(1)}, bf16[441,896]{1,0:T(8,128)(2,1)S(1)}) custom-call(s32[17]{0:T(128)S(1)} %get-tuple-element.28.plan_ref, bf16[441,24,2,128]{3,2,1,0:T(2,128)(2,1)} %bitcast.13, bf16[4,441,2,441]{3,2,1,0:T(2,128)(2,1)} %bitcast.14, ...), custom_call_target="tpu_custom_call" | custom-call | flops 67108864 | bytes 2097152 | tf_op jit(solution)/shard_map/first_near/pallas_call | solution.py:514
  14.8 1.5 %far.2 = (f32[4,3,32,128]{3,2,1,0:T(8,128)S(1)}, f32[4,3,32,128]{3,2,1,0:T(8,128)S(1)}) custom-call(s32[17]{0:T(128)S(1)} %get-tuple-element.28.plan_ref, s32[24,1,128]{2,1,0:T(1,128)S(1)} %get-tuple-element.30.leaves_ref, bf16[1,16,896]{2,1,0:T(8,128)(2,1)S(1)} %collective-permute-done.item_ref, f32[24,32,128]{2,1,0:T(8,128)S(1)} %get-tuple-element.34.partial_ref, ...), custom_call_target="tpu_custom_call" | custom-call | tf_op jit(solution)/shard_map/far/pallas_call | solution.py:552
  16.4 1.4 %collective-permute-done.3.got_ref = f32[4,3,32,128]{3,2,1,0:T(8,128)S(1)} collective-permute-done((f32[4,3,32,128]{3,2,1,0:T(8,128)S(1)}, f32[4,3,32,128]{3,2,1,0:T(8,128)S(1)}, u32[]{:S(2)}, u32[]{:S(2)}) %collective-permute-start.3) | collective-permute-done | bytes 196640 | tf_op jit(solution)/shard_map/ppermute | solution.py:548
  17.8 6.0 %collective-permute-start.6 = (bf16[4,3,32,128]{3,2,1,0:T(8,128)(2,1)S(1)}, bf16[4,3,32,128]{3,2,1,0:T(8,128)(2,1)S(1)}, u32[]{:S(2)}, u32[]{:S(2)}) collective-permute-start(bf16[4,3,32,128]{3,2,1,0:T(8,128)(2,1)S(1)} %pair.1.refs_0_), channel_id=1, source_target_pairs={{0,18},{1,19},{2,16},{3,17},{16,2},{17,3},{18,0},{19,1},{4,22},{5,... | collective-permute-start | bytes 294920 | tf_op jit(solution)/shard_map/ppermute | solution.py:548
  23.8 0.6 collective-permute-start.4
  24.5 2.9 %collective-permute-done.6.refs_3_ = bf16[4,3,32,128]{3,2,1,0:T(8,128)(2,1)S(1)} collective-permute-done((bf16[4,3,32,128]{3,2,1,0:T(8,128)(2,1)S(1)}, bf16[4,3,32,128]{3,2,1,0:T(8,128)(2,1)S(1)}, u32[]{:S(2)}, u32[]{:S(2)}) %collective-permute-start.6) | collective-permute-done | bytes 98336 | tf_op jit(solution)/shard_map/ppermute | solution.py:548
  27.4 1.0 %collective-permute-done.5.refs_2_ = bf16[4,3,32,128]{3,2,1,0:T(8,128)(2,1)S(1)} collective-permute-done((bf16[4,3,32,128]{3,2,1,0:T(8,128)(2,1)S(1)}, bf16[4,3,32,128]{3,2,1,0:T(8,128)(2,1)S(1)}, u32[]{:S(2)}, u32[]{:S(2)}) %collective-permute-start.5) | collective-permute-done | bytes 98336 | tf_op jit(solution)/shard_map/ppermute | solution.py:548
  28.5 0.6 collective-permute-done.4.refs_1_
  29.1 0.1 collective-permute-start.7
  29.2 1.4 %collective-permute-done.7.theirs_ref = f32[4,3,32,128]{3,2,1,0:T(8,128)S(1)} collective-permute-done((f32[4,3,32,128]{3,2,1,0:T(8,128)S(1)}, f32[4,3,32,128]{3,2,1,0:T(8,128)S(1)}, u32[]{:S(2)}, u32[]{:S(2)}) %collective-permute-start.7) | collective-permute-done | bytes 196640 | tf_op jit(solution)/shard_map/ppermute | solution.py:548
  30.6 0.6 assemble.1
  31.3 3.8 %collective-permute-start.10 = (bf16[4,32,128]{2,1,0:T(8,128)(2,1)S(1)}, bf16[4,32,128]{2,1,0:T(8,128)(2,1)S(1)}, u32[]{:S(2)}, u32[]{:S(2)}) collective-permute-start(bf16[4,32,128]{2,1,0:T(8,128)(2,1)S(1)} %get-tuple-element.44), channel_id=1, source_target_pairs={{4,0},{8,4},{12,8},{0,12},{5,1},{9,5},{13,9},{1,13},{6,2},{10,6},{... | collective-permute-start | bytes 98312 | tf_op jit(solution)/shard_map/ppermute | solution.py:613
  35.1 1.1 %multi.1 = bf16[1,16,896]{2,1,0:T(8,128)(2,1)S(1)} custom-call(s32[17]{0:T(128)S(1)} %get-tuple-element.28.plan_ref, s32[24,1,128]{2,1,0:T(1,128)S(1)} %get-tuple-element.30.leaves_ref, bf16[24,32,128]{2,1,0:T(8,128)(2,1)S(1)} %get-tuple-element.41.low_ref.here_ref, bf16[1,3,448,2,128]{4,3,2,1,0:T(2,128)(2,1)S(1)} %get-tuple-element.42.window_ref), custom_call_target="tpu_custom_call" | custom-call | tf_op jit(solution)/shard_map/multi/pallas_call | solution.py:488
  36.2 0.7 collective-permute-start.8
  36.8 0.2 collective-permute-done.9.before_ref
  37.0 1.3 %near.1.partial_ref = f32[24,32,128]{2,1,0:T(8,128)S(1)} custom-call(s32[17]{0:T(128)S(1)} %get-tuple-element.28.plan_ref, bf16[4,32,128]{2,1,0:T(8,128)(2,1)S(1)} %collective-permute-done.9.before_ref, bf16[24,32,128]{2,1,0:T(8,128)(2,1)S(1)} %get-tuple-element.41.low_ref.here_ref, bf16[4,32,128]{2,1,0:T(8,128)(2,1)S(1)} %collective-permute-done.10.after_ref, ...), custom_call_target="tpu_custom_call" | custom-call | flops 67108864 | bytes 2097152 | tf_op jit(solution)/shard_map/near/pallas_call | solution.py:536
  38.3 1.5 %far.3 = (bf16[4,3,32,128]{3,2,1,0:T(8,128)(2,1)S(1)}, bf16[4,3,32,128]{3,2,1,0:T(8,128)(2,1)S(1)}) custom-call(s32[17]{0:T(128)S(1)} %get-tuple-element.28.plan_ref, s32[24,1,128]{2,1,0:T(1,128)S(1)} %get-tuple-element.30.leaves_ref, bf16[1,16,896]{2,1,0:T(8,128)(2,1)S(1)} %collective-permute-done.8.item_ref, f32[24,32,128]{2,1,0:T(8,128)S(1)} %near.1.partial_ref, ...), custom_call_target="tpu_custom_call" | custom-call | tf_op jit(solution)/shard_map/far/pallas_call | solution.py:552
  39.8 1.3 %collective-permute-done.11.got_ref = bf16[4,3,32,128]{3,2,1,0:T(8,128)(2,1)S(1)} collective-permute-done((bf16[4,3,32,128]{3,2,1,0:T(8,128)(2,1)S(1)}, bf16[4,3,32,128]{3,2,1,0:T(8,128)(2,1)S(1)}, u32[]{:S(2)}, u32[]{:S(2)}) %collective-permute-start.11) | collective-permute-done | bytes 98336 | tf_op jit(solution)/shard_map/ppermute | solution.py:548
  41.1 0.6 fold.1
  41.7 5.2 %collective-permute-start.12 = (bf16[3,32,128]{2,1,0:T(8,128)(2,1)S(1)}, bf16[3,32,128]{2,1,0:T(8,128)(2,1)S(1)}, u32[]{:S(2)}, u32[]{:S(2)}) collective-permute-start(bf16[3,32,128]{2,1,0:T(8,128)(2,1)S(1)} %get-tuple-element.48), channel_id=1, source_target_pairs={{0,2},{1,3},{2,0},{3,1},{16,18},{17,19},{18,16},{19,17},{4,6},{5,7... | collective-permute-start | bytes 73736 | tf_op jit(solution)/shard_map/ppermute | solution.py:548
  46.9 5.3 %collective-permute-start.13 = (bf16[3,32,128]{2,1,0:T(8,128)(2,1)S(1)}, bf16[3,32,128]{2,1,0:T(8,128)(2,1)S(1)}, u32[]{:S(2)}, u32[]{:S(2)}) collective-permute-start(bf16[3,32,128]{2,1,0:T(8,128)(2,1)S(1)} %get-tuple-element.49), channel_id=1, source_target_pairs={{0,16},{1,17},{2,18},{3,19},{16,0},{17,1},{18,2},{19,3},{4,20},{5,... | collective-permute-start | bytes 73736 | tf_op jit(solution)/shard_map/ppermute | solution.py:548
  52.2 1.8 %collective-permute-done.13.refs_2_ = bf16[3,32,128]{2,1,0:T(8,128)(2,1)S(1)} collective-permute-done((bf16[3,32,128]{2,1,0:T(8,128)(2,1)S(1)}, bf16[3,32,128]{2,1,0:T(8,128)(2,1)S(1)}, u32[]{:S(2)}, u32[]{:S(2)}) %collective-permute-start.13) | collective-permute-done | bytes 24608 | tf_op jit(solution)/shard_map/ppermute | solution.py:548
  54.0 2.9 %collective-permute-done.14.refs_3_ = bf16[3,32,128]{2,1,0:T(8,128)(2,1)S(1)} collective-permute-done((bf16[3,32,128]{2,1,0:T(8,128)(2,1)S(1)}, bf16[3,32,128]{2,1,0:T(8,128)(2,1)S(1)}, u32[]{:S(2)}, u32[]{:S(2)}) %collective-permute-start.14) | collective-permute-done | bytes 24608 | tf_op jit(solution)/shard_map/ppermute | solution.py:548
  56.9 0.8 %gram.1 = f32[32,2,128]{2,1,0:T(2,128)S(1)} custom-call(s32[17]{0:T(128)S(1)} %get-tuple-element.28.plan_ref, f32[32,3072]{1,0:T(8,128)S(1)} %get-tuple-element.29.here_ref.right_ref, f32[24,32,128]{2,1,0:T(8,128)S(1)} %get-tuple-element.40.image_ref, f32[3,32,128]{2,1,0:T(8,128)S(1)} %get-tuple-element.47.refs_0_, ...), custom_call_target="tpu_custom_call" | custom-call | tf_op jit(solution)/shard_map/gram/pallas_call | solution.py:618
  57.7 8.9 %all_to_all.5.sums_ref = f32[32,2,128]{2,1,0:T(2,128)S(1)} all-to-all(f32[32,2,128]{2,1,0:T(2,128)S(1)} %gram.1), channel_id=1, replica_groups=mesh['grp'=2,'row'=4,'col'=4] {'grp','row','col'}, dimensions={0} | all-to-all | bytes 65536 | tf_op jit(solution)/shard_map/all_to_all | solution.py:626
  66.7 1.1 %combine.1 = f32[32,3072]{1,0:T(8,128)} custom-call(f32[32,2,128]{2,1,0:T(2,128)S(1)} %all_to_all.5.sums_ref, f32[32,3072]{1,0:T(8,128)S(1)} %get-tuple-element.29.here_ref.right_ref, f32[24,32,128]{2,1,0:T(8,128)S(1)} %get-tuple-element.40.image_ref), custom_call_target="tpu_custom_call" | custom-call | tf_op jit(solution)/shard_map/combine/pallas_call | solution.py:627
  (13 shorter events, 0.3 us)
Async XLA Ops:
  0.0 11.7 %copy-start = (bf16[2,8,256,256]{3,2,1,0:T(8,128)(2,1)S(1)}, bf16[2,8,256,256]{3,2,1,0:T(8,128)(2,1)}, u32[]{:S(2)}) copy-start(bf16[2,8,256,256]{3,2,1,0:T(8,128)(2,1)} %tiles_ref.3) | copy-start | bytes 6291460
  3.7 7.5 %collective-permute-start.1 = (f32[32,512]{1,0:T(8,128)S(1)}, f32[32,512]{1,0:T(8,128)S(1)}, u32[]{:S(2)}, u32[]{:S(2)}) collective-permute-start(f32[32,512]{1,0:T(8,128)S(1)} %get-tuple-element.32), channel_id=1, source_target_pairs={{0,4},{4,8},{8,12},{12,0},{1,5},{5,9},{9,13},{13,1},{2,6},{6,10},{... | collective-permute-start | bytes 196616 | tf_op jit(solution)/shard_map/ppermute | solution.py:607
  6.7 5.0 %collective-permute-start.2 = (f32[32,512]{1,0:T(8,128)S(1)}, f32[32,512]{1,0:T(8,128)S(1)}, u32[]{:S(2)}, u32[]{:S(2)}) collective-permute-start(f32[32,512]{1,0:T(8,128)S(1)} %get-tuple-element.33), channel_id=1, source_target_pairs={{4,0},{8,4},{12,8},{0,12},{5,1},{9,5},{13,9},{1,13},{6,2},{10,6},{... | collective-permute-start | bytes 196616 | tf_op jit(solution)/shard_map/ppermute | solution.py:608
  8.8 6.0 %collective-permute-start = (bf16[1,16,896]{2,1,0:T(8,128)(2,1)S(1)}, bf16[1,16,896]{2,1,0:T(8,128)(2,1)S(1)}, u32[]{:S(2)}, u32[]{:S(2)}) collective-permute-start(bf16[1,16,896]{2,1,0:T(8,128)(2,1)S(1)} %get-tuple-element.31), channel_id=1, source_target_pairs={{0,0},{1,1},{2,4},{3,5},{16,8},{17,9},{18,12},{19,13},{4,2},{5,3},... | collective-permute-start | bytes 86024 | tf_op jit(solution)/shard_map/ppermute | solution.py:499
  16.3 1.5 %collective-permute-start.3 = (f32[4,3,32,128]{3,2,1,0:T(8,128)S(1)}, f32[4,3,32,128]{3,2,1,0:T(8,128)S(1)}, u32[]{:S(2)}, u32[]{:S(2)}) collective-permute-start(f32[4,3,32,128]{3,2,1,0:T(8,128)S(1)} %get-tuple-element.39), channel_id=1, source_target_pairs={{0,1},{1,0},{2,3},{3,2},{16,17},{17,16},{18,19},{19,18},{4,5},{5,4... | collective-permute-start | bytes 589832 | tf_op jit(solution)/shard_map/ppermute | solution.py:548
  17.8 9.6 %collective-permute-start.6 = (bf16[4,3,32,128]{3,2,1,0:T(8,128)(2,1)S(1)}, bf16[4,3,32,128]{3,2,1,0:T(8,128)(2,1)S(1)}, u32[]{:S(2)}, u32[]{:S(2)}) collective-permute-start(bf16[4,3,32,128]{3,2,1,0:T(8,128)(2,1)S(1)} %pair.1.refs_0_), channel_id=1, source_target_pairs={{0,18},{1,19},{2,16},{3,17},{16,2},{17,3},{18,0},{19,1},{4,22},{5,... | collective-permute-start | bytes 294920 | tf_op jit(solution)/shard_map/ppermute | solution.py:548
  23.8 4.6 %collective-permute-start.5 = (bf16[4,3,32,128]{3,2,1,0:T(8,128)(2,1)S(1)}, bf16[4,3,32,128]{3,2,1,0:T(8,128)(2,1)S(1)}, u32[]{:S(2)}, u32[]{:S(2)}) collective-permute-start(bf16[4,3,32,128]{3,2,1,0:T(8,128)(2,1)S(1)} %pair.1.refs_0_), channel_id=1, source_target_pairs={{0,16},{1,17},{2,18},{3,19},{16,0},{17,1},{18,2},{19,3},{4,20},{5,... | collective-permute-start | bytes 294920 | tf_op jit(solution)/shard_map/ppermute | solution.py:548
  23.8 5.2 %collective-permute-start.4 = (bf16[4,3,32,128]{3,2,1,0:T(8,128)(2,1)S(1)}, bf16[4,3,32,128]{3,2,1,0:T(8,128)(2,1)S(1)}, u32[]{:S(2)}, u32[]{:S(2)}) collective-permute-start(bf16[4,3,32,128]{3,2,1,0:T(8,128)(2,1)S(1)} %pair.1.refs_0_), channel_id=1, source_target_pairs={{0,2},{1,3},{2,0},{3,1},{16,18},{17,19},{18,16},{19,17},{4,6},{5,7... | collective-permute-start | bytes 294920 | tf_op jit(solution)/shard_map/ppermute | solution.py:548
  29.1 1.5 %collective-permute-start.7 = (f32[4,3,32,128]{3,2,1,0:T(8,128)S(1)}, f32[4,3,32,128]{3,2,1,0:T(8,128)S(1)}, u32[]{:S(2)}, u32[]{:S(2)}) collective-permute-start(f32[4,3,32,128]{3,2,1,0:T(8,128)S(1)} %close.1.mine_ref), channel_id=1, source_target_pairs={{0,1},{1,0},{2,3},{3,2},{16,17},{17,16},{18,19},{19,18},{4,5},{5,4... | collective-permute-start | bytes 589832 | tf_op jit(solution)/shard_map/ppermute | solution.py:548
  31.2 5.8 %collective-permute-start.9 = (bf16[4,32,128]{2,1,0:T(8,128)(2,1)S(1)}, bf16[4,32,128]{2,1,0:T(8,128)(2,1)S(1)}, u32[]{:S(2)}, u32[]{:S(2)}) collective-permute-start(bf16[4,32,128]{2,1,0:T(8,128)(2,1)S(1)} %get-tuple-element.43), channel_id=1, source_target_pairs={{0,4},{4,8},{8,12},{12,0},{1,5},{5,9},{9,13},{13,1},{2,6},{6,10},{... | collective-permute-start | bytes 98312 | tf_op jit(solution)/shard_map/ppermute | solution.py:612
  31.3 5.7 %collective-permute-start.10 = (bf16[4,32,128]{2,1,0:T(8,128)(2,1)S(1)}, bf16[4,32,128]{2,1,0:T(8,128)(2,1)S(1)}, u32[]{:S(2)}, u32[]{:S(2)}) collective-permute-start(bf16[4,32,128]{2,1,0:T(8,128)(2,1)S(1)} %get-tuple-element.44), channel_id=1, source_target_pairs={{4,0},{8,4},{12,8},{0,12},{5,1},{9,5},{13,9},{1,13},{6,2},{10,6},{... | collective-permute-start | bytes 98312 | tf_op jit(solution)/shard_map/ppermute | solution.py:613
  36.2 2.1 %collective-permute-start.8 = (bf16[1,16,896]{2,1,0:T(8,128)(2,1)S(1)}, bf16[1,16,896]{2,1,0:T(8,128)(2,1)S(1)}, u32[]{:S(2)}, u32[]{:S(2)}) collective-permute-start(bf16[1,16,896]{2,1,0:T(8,128)(2,1)S(1)} %multi.1), channel_id=1, source_target_pairs={{0,0},{1,1},{2,4},{3,5},{16,8},{17,9},{18,12},{19,13},{4,2},{5,3},... | collective-permute-start | bytes 86024 | tf_op jit(solution)/shard_map/ppermute | solution.py:499
  39.7 1.4 %collective-permute-start.11 = (bf16[4,3,32,128]{3,2,1,0:T(8,128)(2,1)S(1)}, bf16[4,3,32,128]{3,2,1,0:T(8,128)(2,1)S(1)}, u32[]{:S(2)}, u32[]{:S(2)}) collective-permute-start(bf16[4,3,32,128]{3,2,1,0:T(8,128)(2,1)S(1)} %get-tuple-element.46), channel_id=1, source_target_pairs={{0,1},{1,0},{2,3},{3,2},{16,17},{17,16},{18,19},{19,18},{4,5},{5,4... | collective-permute-start | bytes 294920 | tf_op jit(solution)/shard_map/ppermute | solution.py:548
  41.7 10.5 %collective-permute-start.12 = (bf16[3,32,128]{2,1,0:T(8,128)(2,1)S(1)}, bf16[3,32,128]{2,1,0:T(8,128)(2,1)S(1)}, u32[]{:S(2)}, u32[]{:S(2)}) collective-permute-start(bf16[3,32,128]{2,1,0:T(8,128)(2,1)S(1)} %get-tuple-element.48), channel_id=1, source_target_pairs={{0,2},{1,3},{2,0},{3,1},{16,18},{17,19},{18,16},{19,17},{4,6},{5,7... | collective-permute-start | bytes 73736 | tf_op jit(solution)/shard_map/ppermute | solution.py:548
  46.9 7.1 %collective-permute-start.13 = (bf16[3,32,128]{2,1,0:T(8,128)(2,1)S(1)}, bf16[3,32,128]{2,1,0:T(8,128)(2,1)S(1)}, u32[]{:S(2)}, u32[]{:S(2)}) collective-permute-start(bf16[3,32,128]{2,1,0:T(8,128)(2,1)S(1)} %get-tuple-element.49), channel_id=1, source_target_pairs={{0,16},{1,17},{2,18},{3,19},{16,0},{17,1},{18,2},{19,3},{4,20},{5,... | collective-permute-start | bytes 73736 | tf_op jit(solution)/shard_map/ppermute | solution.py:548
  52.2 4.7 %collective-permute-start.14 = (bf16[3,32,128]{2,1,0:T(8,128)(2,1)S(1)}, bf16[3,32,128]{2,1,0:T(8,128)(2,1)S(1)}, u32[]{:S(2)}, u32[]{:S(2)}) collective-permute-start(bf16[3,32,128]{2,1,0:T(8,128)(2,1)S(1)} %get-tuple-element.50), channel_id=1, source_target_pairs={{0,18},{1,19},{2,16},{3,17},{16,2},{17,3},{18,0},{19,1},{4,22},{5,... | collective-permute-start | bytes 73736 | tf_op jit(solution)/shard_map/ppermute | solution.py:548

commit v4 on v3

--- a/solution.py
+++ b/solution.py
@@ -12,7 +12,7 @@
 LANES = 128
 EPSILON = 1e-06
 GROUP = ("grp", "col")
-CORE, CHIP, OWN, COUNT, CODES = range(5)
+COUNT, CODES = range(2)
 PER_ITEM = 5
 EVERY = ("grp", "row", "col")
 
@@ -21,6 +21,7 @@
 SMEM = pl.BlockSpec(memory_space=pltpu.SMEM)
 VMEM = pl.BlockSpec(memory_space=pltpu.VMEM)
 HBM = pl.BlockSpec(memory_space=pltpu.HBM)
+ANY = pl.BlockSpec(memory_space=pl.ANY)
 
 
 def dot_nn(left, right):
@@ -108,12 +109,25 @@
     return ref.reshape(ref.shape[0] * 2, ref.shape[2])[...]
 
 
+def write_edges(row, first, last, one_ref, two_ref):
+    even = lax.rem(row, 2) == 0
+
+    @pl.when(even)
+    def _():
+        one_ref[...], two_ref[...] = last, first
+
+    @pl.when(jnp.logical_not(even))
+    def _():
+        one_ref[...], two_ref[...] = first, last
+
+
 def begin_kernel(
-    fields, items, width, send, edge, row_ref, own_ref, count_ref, pick_hbm, leaf_hbm, leaves_hbm, target_hbm,
-    offset_hbm, pairs_hbm, right_hbm, exp_ref,
-    plan_ref, out_ref, window_ref, leaves_ref, right_ref, first_ref, last_ref,
-    pick_ref, leaf_ref, target_ref, offset_ref, pairs_ref, sem, window_sem,
+    fields, items, width, send, rows, edge, row_ref, own_ref, count_ref, pick_hbm, leaf_hbm, leaves_hbm,
+    target_hbm, offset_hbm, pairs_hbm, right_hbm, exp_ref,
+    plan_ref, out_ref, window_ref, leaves_ref, right_ref, *edge_refs_and_scratch,
 ):
+    edge_refs = edge_refs_and_scratch[:2]
+    pick_ref, leaf_ref, target_ref, offset_ref, pairs_ref, sem, window_sem = edge_refs_and_scratch[2:]
     panels = right_ref.shape[1]
     loads = [
         pltpu.make_async_copy(source, place, sem.at[k])
@@ -137,9 +151,15 @@
     own = own_ref[0]
     loads[0].wait()
     loads[1].wait()
+    row = row_ref[0]
+
+    def partner(i):
+        number = own * items + i
+        return lax.rem(lax.div(number, send) - row + rows, rows), lax.rem(number, send)
+
     for i in range(items):
-        outgoing = own * items + i
-        leaf = pick_ref[lax.div(outgoing, send), lax.rem(outgoing, send), row_ref[0]]
+        other, number = partner(i)
+        leaf = pick_ref[other, number, row]
         unit = window_start(leaf_ref, leaf, width)
         place = item_place(slots, i)
         plan_ref[place], plan_ref[place + 1] = leaf, unit
@@ -147,17 +167,17 @@
             copy.start()
     for load in loads[2:]:
         load.wait()
-    first_ref[...] = right_ref[:, :edge]
-    last_ref[...] = right_ref[:, panels - edge :]
-    plan_ref[CORE], plan_ref[CHIP], plan_ref[OWN] = lax.rem(own, 2), lax.div(own, 2), own
+    edges = right_ref[:, :edge].astype(BF16), right_ref[:, panels - edge :].astype(BF16)
+    write_edges(row, *edges, *edge_refs)
     plan_ref[COUNT] = count_ref[0]
     for s in range(slots):
         plan_ref[CODES + s] = pairs_ref[s]
     for i in range(items):
         place = item_place(slots, i)
-        leaf = target_ref[0, own * items + i]
+        other, number = partner(i)
+        leaf = target_ref[0, other * send + number]
         plan_ref[place + 2], plan_ref[place + 3] = leaf, window_start(leaf_ref, leaf, width)
-        plan_ref[place + 4] = offset_ref[0, own * items + i]
+        plan_ref[place + 4] = offset_ref[0, other * send + number]
     for i in range(items):
         place = item_place(slots, i)
         leaf, unit = plan_ref[place], plan_ref[place + 1]
@@ -166,20 +186,20 @@
         out_ref[i] = multi_rows(fields, width, leaf, unit, leaves_ref, right_ref, window_ref.at[i]).astype(BF16)
 
 
-def multi_kernel(fields, items, width, slots, plan_ref, leaves_ref, low_ref, window_ref, out_ref):
-    for i in range(items):
-        place = item_place(slots, i)
-        out_ref[i] = multi_rows(
-            fields, width, plan_ref[place], plan_ref[place + 1], leaves_ref, low_ref, window_ref.at[i]
-        ).astype(BF16)
-
-
 def first_near_kernel(
-    fields, items, width, plan_ref, exp_ref, trans_ref, before_ref, here_ref, after_ref, tiles_ref,
-    out_ref, window_ref, moved_ref, spread_ref, ext, trans_buf, sem, trans_sem,
+    fields, items, width, row_ref, plan_any, exp_ref, trans_ref, one_ref, two_ref, here_ref, tiles_ref,
+    out_ref, window_ref, moved_ref, spread_ref, ext, plan_ref, plan_sem, trans_buf, sem, trans_sem,
 ):
+    plan_copy = pltpu.make_async_copy(plan_any, plan_ref, plan_sem)
+    plan_copy.start()
     coefs = trans_ref.shape[3]
     slots = tiles_ref.shape[1]
+    shape = spread_ref.shape
+    row = lax.broadcasted_iota(jnp.int32, shape, 0)
+    column = lax.broadcasted_iota(jnp.int32, shape, 1)
+    spread_ref[...] = jnp.where(column == 2 * row, 1.0, 0.0).astype(BF16)
+    near_sources(row_ref, one_ref, two_ref, here_ref, out_ref, ext)
+    plan_copy.wait()
 
     def trans_copy(i):
         offset = plan_ref[item_place(slots, i) + 4]
@@ -194,11 +214,7 @@
         for copy in exp_copies(i):
             copy.start()
         clear_rest(window_ref.at[i], coefs, width)
-    shape = spread_ref.shape
-    row = lax.broadcasted_iota(jnp.int32, shape, 0)
-    column = lax.broadcasted_iota(jnp.int32, shape, 1)
-    spread_ref[...] = jnp.where(column == 2 * row, 1.0, 0.0).astype(BF16)
-    near_kernel(fields, plan_ref, before_ref, here_ref, after_ref, tiles_ref, out_ref, ext)
+    near_slots(fields, plan_ref, tiles_ref, out_ref, ext)
     rest = moved_ref.shape[1] - 2 * coefs
     for i in range(items):
         trans_copy(i).wait()
@@ -208,22 +224,37 @@
             copy.wait()
 
 
-def near_kernel(fields, plan_ref, before_ref, here_ref, after_ref, tiles_ref, out_ref, ext):
+def near_sources(row_ref, one_ref, two_ref, here_ref, out_ref, ext):
     units = out_ref.shape[0]
-    slots, tile = tiles_ref.shape[1], tiles_ref.shape[2]
-    per = tile // LANES
-    edge = REACH * per
+    edge = (ext.shape[0] - units) // 2
+    even = lax.rem(row_ref[0], 2) == 0
+    one_at = jnp.where(even, edge + units, 0)
+    two_at = jnp.where(even, 0, edge + units)
     if len(here_ref.shape) == 2:
         for k in range(edge):
-            ext[k] = before_ref[:, k * LANES : (k + 1) * LANES]
-            ext[edge + units + k] = after_ref[:, k * LANES : (k + 1) * LANES]
+            lanes = slice(k * LANES, (k + 1) * LANES)
+            ext[one_at + k] = one_ref[:, lanes].astype(ext.dtype)
+            ext[two_at + k] = two_ref[:, lanes].astype(ext.dtype)
         for k in range(units):
             ext[edge + k] = here_ref[:, k * LANES : (k + 1) * LANES]
     else:
-        ext[0:edge] = before_ref[...]
-        ext[edge + units : 2 * edge + units] = after_ref[...]
+        ext[pl.ds(one_at, edge)] = one_ref[...]
+        ext[pl.ds(two_at, edge)] = two_ref[...]
         ext[edge : edge + units] = here_ref[...]
     out_ref[...] = jnp.zeros_like(out_ref)
+
+
+def near_kernel(fields, row_ref, plan_any, one_ref, two_ref, here_ref, tiles_ref, out_ref, ext, plan_ref, plan_sem):
+    plan_copy = pltpu.make_async_copy(plan_any, plan_ref, plan_sem)
+    plan_copy.start()
+    near_sources(row_ref, one_ref, two_ref, here_ref, out_ref, ext)
+    plan_copy.wait()
+    near_slots(fields, plan_ref, tiles_ref, out_ref, ext)
+
+
+def near_slots(fields, plan_ref, tiles_ref, out_ref, ext):
+    slots, tile = tiles_ref.shape[1], tiles_ref.shape[2]
+    per = tile // LANES
     for s in range(slots):
         code = plan_ref[CODES + s]
         target = lax.div(code, SPAN)
@@ -240,16 +271,16 @@
 
 
 def far_kernel(
-    fields, items, width, slots, plan_ref, leaves_ref, item_ref, partial_ref, trans_ref, spread_ref, window_ref,
-    keep_ref, give_ref, total,
+    fields, items, width, slots, core_ref, plan_any, leaves_ref, item_ref, partial_ref, trans_ref, spread_ref,
+    window_ref, keep_ref, give_ref, total, plan_ref, plan_sem,
 ):
+    plan_copy = pltpu.make_async_copy(plan_any, plan_ref, plan_sem)
+    plan_copy.start()
     units = partial_ref.shape[0]
     total[0:units] = partial_ref[...]
     if total.shape[0] > units:
         total[units:] = jnp.zeros((total.shape[0] - units, *total.shape[1:]), F32)
     for i in range(items):
-        place = item_place(slots, i)
-        leaf, unit = plan_ref[place + 2], plan_ref[place + 3]
         plain = item_ref[i].astype(F32)
         odd = odd_lanes(plain.shape)
         turned = jnp.where(odd, from_left(plain), -from_right(plain))
@@ -260,21 +291,26 @@
         rows = jnp.concatenate(
             [local_real - from_left(local_imag), local_imag + from_left(local_real)], axis=0
         ).astype(BF16)
+        if i == 0:
+            plan_copy.wait()
+        place = item_place(slots, i)
+        leaf, unit = plan_ref[place + 2], plan_ref[place + 3]
         mask = window_mask(leaves_ref, leaf, unit, 2 * fields, width)
         for k in range(width):
             image = dot_nn(rows, as_rows(window_ref.at[i, k]))
             total[unit + k] += jnp.where(mask[:, k * LANES : (k + 1) * LANES], image, 0.0)
     chips, share = keep_ref.shape[:2]
-    core = plan_ref[CORE]
+    core = core_ref[0]
     for c in range(chips):
         keep_ref[c] = total[pl.ds((2 * c + core) * share, share)].astype(keep_ref.dtype)
         give_ref[c] = total[pl.ds((2 * c + 1 - core) * share, share)].astype(give_ref.dtype)
 
 
-def fold_kernel(plan_ref, keep_ref, got_ref, own_ref, *out_refs):
-    for step, out_ref in enumerate((own_ref,) + out_refs):
-        chip = lax.bitwise_xor(plan_ref[CHIP], step)
-        out_ref[...] = (keep_ref[chip].astype(F32) + got_ref[chip].astype(F32)).astype(out_ref.dtype)
+def halve_kernel(level, chip_ref, mine_ref, got_ref, keep_ref, give_ref):
+    bit = lax.rem(lax.div(chip_ref[0], 1 << level), 2)
+    for k in range(keep_ref.shape[0]):
+        for out_ref, place in ((keep_ref, 2 * k + bit), (give_ref, 2 * k + 1 - bit)):
+            out_ref[k] = (mine_ref[place].astype(F32) + got_ref[place].astype(F32)).astype(out_ref.dtype)
 
 
 def pair_kernel(keep_ref, got_ref, out_ref):
@@ -291,17 +327,29 @@
     refs[-1][...] = tree_sum([ref[...].astype(F32) for ref in refs[:-1]])
 
 
-def assemble_kernel(plan_ref, mine_ref, theirs_ref, out_ref, low_ref, first_ref, last_ref, whole):
+def assemble_kernel(
+    fields, items, width, slots, core_ref, row_ref, plan_any, leaves_ref, mine_ref, theirs_ref, window_ref,
+    out_ref, low_ref, one_ref, two_ref, made_ref, whole, plan_ref, plan_sem,
+):
+    plan_copy = pltpu.make_async_copy(plan_any, plan_ref, plan_sem)
+    plan_copy.start()
     chips, share = mine_ref.shape[:2]
-    units, edge = out_ref.shape[0], first_ref.shape[0]
-    core = plan_ref[CORE]
+    units, edge = out_ref.shape[0], one_ref.shape[0]
+    core = core_ref[0]
     for chip in range(chips):
         whole[pl.ds((2 * chip + core) * share, share)] = mine_ref[chip]
         whole[pl.ds((2 * chip + 1 - core) * share, share)] = theirs_ref[chip]
     out_ref[...] = whole[0:units]
     low_ref[...] = whole[0:units].astype(BF16)
-    first_ref[...] = whole[0:edge].astype(BF16)
-    last_ref[...] = whole[units - edge : units].astype(BF16)
+    write_edges(
+        row_ref[0], whole[0:edge].astype(BF16), whole[units - edge : units].astype(BF16), one_ref, two_ref
+    )
+    plan_copy.wait()
+    for i in range(items):
+        place = item_place(slots, i)
+        made_ref[i] = multi_rows(
+            fields, width, plan_ref[place], plan_ref[place + 1], leaves_ref, low_ref, window_ref.at[i]
+        ).astype(BF16)
 
 
 def flat_lines(columns, fields):
@@ -325,18 +373,16 @@
     return columns[:count]
 
 
-def gram_kernel(fields, plan_ref, right_ref, image_ref, *refs):
-    out_ref = refs[-1]
-    pieces = refs[:-1]
+def gram_kernel(fields, own_ref, right_ref, image_ref, mine_ref, got_ref, out_ref):
     units = image_ref.shape[0]
-    share = pieces[0].shape[0]
+    share = mine_ref.shape[1]
     totals = None
     for k in range(share):
-        unit = plan_ref[OWN] * share + k
+        unit = own_ref[0] * share + k
         place = jnp.minimum(unit, units - 1)
         r = right_ref[:, pl.ds(pl.multiple_of(place * LANES, LANES), LANES)]
         z = image_ref[place]
-        q = tree_sum([piece[k].astype(F32) for piece in pieces])
+        q = mine_ref[0, k].astype(F32) + got_ref[0, k].astype(F32)
         r = jnp.where(unit < units, r, 0.0)
         z = jnp.where(unit < units, z, 0.0)
         (rr, ri), (zr, zi), (qr, qi) = [(v[:fields], v[fields:]) for v in (r, z, q)]
@@ -380,23 +426,12 @@
     def flat(r, g):
         return (g // columns * rows + r) * columns + g % columns
 
-    if items >= send:
-        steps = items // send
-        routes = []
-        for t in range(steps):
-            pairs = []
-            for r in range(rows):
-                for g in range(group):
-                    d = g * steps + (t + r) % steps
-                    pairs.append((flat(r, g), flat(d, r // steps)))
-            routes.append(pairs)
-        return items, steps, routes
-    pairs = []
-    for r in range(rows):
-        for g in range(group):
-            d, j = g // send, g % send
-            pairs.append((flat(r, g), flat(d, r * send + j)))
-    return items, 1, [pairs]
+    assert items * group == rows * send and (items % send == 0 or send % items == 0)
+    routes = []
+    for first in range(0, items, send):
+        numbers = [(g * items + first) // send for g in range(group)]
+        routes.append([(flat(r, g), flat((numbers[g] - r) % rows, g)) for r in range(rows) for g in range(group)])
+    return items, routes
 
 
 def local(
@@ -425,11 +460,12 @@
     edge = REACH * tile
     edge_units = edge // LANES
     width = tile // LANES + 1
-    items, steps, routes = item_route(rows, group, lax.axis_size("col"), send)
-
-    up = [(i, (i + 1) % rows) for i in range(rows)]
-    down = [(j, i) for i, j in up]
-
+    items, routes = item_route(rows, group, lax.axis_size("col"), send)
+
+    assert rows % 2 == 0
+    neighbours = [[r + 1 - 2 * (r % 2) for r in range(rows)], [(r - 1 + 2 * (r % 2)) % rows for r in range(rows)]]
+    own_place, row_place = own.reshape(1), row_here.reshape(1)
+    core_place, chip_place = lax.rem(own, 2).reshape(1), lax.div(own, 2).reshape(1)
     slots = near_tiles.shape[1]
     pad_coefs = -(-coefs // 8) * 8
     chips = group // 2
@@ -448,10 +484,11 @@
     expansions = in_hbm(expansions)
     moves = in_hbm(translations.transpose(0, 2, 1, 3))
     picks = far_pick.transpose(0, 2, 1)
-    edge_shape = jax.ShapeDtypeStruct((both, edge), F32)
-
-    plan, made, windows, leaves, right, first, last = pl.pallas_call(
-        functools.partial(begin_kernel, fields, items, width, send, edge),
+    edge_shape = jax.ShapeDtypeStruct((both, edge), BF16)
+    plan_scratch = [pltpu.SMEM(plan_shape.shape, jnp.int32), pltpu.SemaphoreType.DMA]
+
+    plan, made, windows, leaves, right, one, two = pl.pallas_call(
+        functools.partial(begin_kernel, fields, items, width, send, rows, edge),
         out_shape=(
             plan_shape,
             item_shape,
@@ -471,8 +508,8 @@
         compiler_params=params(),
         name="begin",
     )(
-        row_here.reshape(1),
-        own.reshape(1),
+        row_place,
+        own_place,
         tile_count,
         in_hbm(picks),
         in_hbm(leaf_of_panel),
@@ -484,33 +521,23 @@
         expansions,
     )
 
-    def multipoles(low):
-        return pl.pallas_call(
-            functools.partial(multi_kernel, fields, items, width, slots),
-            out_shape=item_shape,
-            in_specs=[SMEM, VMEM, VMEM, VMEM],
-            out_specs=VMEM,
-            compiler_params=params(),
-            name="multi",
-        )(plan, leaves, low, windows)
-
     def exchanged(made):
-        if items < send:
-            return lax.ppermute(made, EVERY, routes[0])
-        taken = jnp.zeros_like(made)
-        for t in range(steps):
-            outgoing = lax.dynamic_slice_in_dim(made, lax.rem(t + row_here, steps) * send, send)
-            arrived = lax.ppermute(outgoing, EVERY, routes[t])
-            place = lax.rem(row_here - t + steps, steps) * send
-            taken = lax.dynamic_update_slice_in_dim(taken, arrived, place, 0)
-        return taken
+        parts = [
+            lax.ppermute(made[k * send : k * send + min(send, items)], EVERY, route) for k, route in enumerate(routes)
+        ]
+        return parts[0] if len(parts) == 1 else jnp.concatenate(parts)
+
+    def to_neighbours(one, two):
+        return [
+            lax.ppermute(value, "row", list(enumerate(targets))) for value, targets in zip((one, two), neighbours)
+        ]
 
     image_shape = jax.ShapeDtypeStruct((units, both, LANES), F32)
     near_cost = pl.CostEstimate(
         flops=8 * fields * near_tiles.size // 2, bytes_accessed=2 * near_tiles.size, transcendentals=0
     )
 
-    def first_near(before, low, after):
+    def first_near(one, two, low):
         return pl.pallas_call(
             functools.partial(first_near_kernel, fields, items, width),
             out_shape=(
@@ -519,10 +546,11 @@
                 jax.ShapeDtypeStruct((items, 2 * pad_coefs, coefs), BF16),
                 jax.ShapeDtypeStruct((coefs, 2 * pad_coefs), BF16),
             ),
-            in_specs=[SMEM] + [HBM] * 2 + [VMEM] * 4,
+            in_specs=[SMEM, ANY] + [HBM] * 2 + [VMEM] * 4,
             out_specs=(VMEM, VMEM, VMEM, VMEM),
-            scratch_shapes=[
-                pltpu.VMEM((units + 2 * edge_units, both, LANES), low.dtype),
+            scratch_shapes=[pltpu.VMEM((units + 2 * edge_units, both, LANES), low.dtype)]
+            + plan_scratch
+            + [
                 pltpu.VMEM((items, coefs, 2, coefs), BF16),
                 pltpu.SemaphoreType.DMA((items, width)),
                 pltpu.SemaphoreType.DMA((items,)),
@@ -530,19 +558,19 @@
             compiler_params=params(24),
             cost_estimate=near_cost,
             name="first_near",
-        )(plan, expansions, moves, before, low, after, near_tiles)
-
-    def near(before, low, after):
+        )(row_place, plan, expansions, moves, one, two, low, near_tiles)
+
+    def near(one, two, low):
         return pl.pallas_call(
             functools.partial(near_kernel, fields),
             out_shape=image_shape,
-            in_specs=[SMEM, VMEM, VMEM, VMEM, VMEM],
+            in_specs=[SMEM, ANY, VMEM, VMEM, VMEM, VMEM],
             out_specs=VMEM,
-            scratch_shapes=[pltpu.VMEM((units + 2 * edge_units, both, LANES), low.dtype)],
+            scratch_shapes=[pltpu.VMEM((units + 2 * edge_units, both, LANES), low.dtype)] + plan_scratch,
             compiler_params=params(),
             cost_estimate=near_cost,
             name="near",
-        )(plan, before, low, after, near_tiles)
+        )(row_place, plan, one, two, low, near_tiles)
 
     def swapped(value, step):
         return lax.ppermute(value, GROUP, [(g, g ^ step) for g in range(group)])
@@ -552,12 +580,12 @@
         keep, give = pl.pallas_call(
             functools.partial(far_kernel, fields, items, width, slots),
             out_shape=(half_shape, half_shape),
-            in_specs=[SMEM] + [VMEM] * 6,
+            in_specs=[SMEM, ANY] + [VMEM] * 6,
             out_specs=(VMEM, VMEM),
-            scratch_shapes=[pltpu.VMEM((share * group, both, LANES), F32)],
+            scratch_shapes=[pltpu.VMEM((share * group, both, LANES), F32)] + plan_scratch,
             compiler_params=params(),
             name="far",
-        )(plan, leaves, taken, partial, moved, spread, target_windows)
+        )(core_place, plan, leaves, taken, partial, moved, spread, target_windows)
         return keep, swapped(give, 1)
 
     def whole_sum(keep, got):
@@ -582,47 +610,49 @@
         low_shape = jax.ShapeDtypeStruct((units, both, LANES), BF16)
         low_edge = jax.ShapeDtypeStruct((edge_units, both, LANES), BF16)
         return pl.pallas_call(
-            assemble_kernel,
-            out_shape=(image_shape, low_shape, low_edge, low_edge),
-            in_specs=[SMEM, VMEM, VMEM],
-            out_specs=(VMEM,) * 4,
-            scratch_shapes=[pltpu.VMEM((share * group, both, LANES), F32)],
+            functools.partial(assemble_kernel, fields, items, width, slots),
+            out_shape=(image_shape, low_shape, low_edge, low_edge, item_shape),
+            in_specs=[SMEM, SMEM, ANY] + [VMEM] * 4,
+            out_specs=(VMEM,) * 5,
+            scratch_shapes=[pltpu.VMEM((share * group, both, LANES), F32)] + plan_scratch,
             compiler_params=params(),
             name="assemble",
-        )(plan, mine, theirs)
-
-    def share_pieces(keep, got):
-        pieces = pl.pallas_call(
-            fold_kernel,
-            out_shape=(jax.ShapeDtypeStruct(part_shape, F32),)
-            + (jax.ShapeDtypeStruct(part_shape, BF16),) * (chips - 1),
-            in_specs=[SMEM, VMEM, VMEM],
-            out_specs=(VMEM,) * chips,
-            compiler_params=params(),
-            name="fold",
-        )(plan, keep, got)
-        arrived = {step: swapped(pieces[step], 2 * step) for step in steps_between}
-        return [pieces[0]] + [arrived[step] for step in range(1, chips)]
-
-    before = lax.ppermute(last, "row", up)
-    after = lax.ppermute(first, "row", down)
+        )(core_place, row_place, plan, leaves, mine, theirs, windows)
+
+    def own_share(keep, got):
+        pieces = chips
+        for level in range(chips.bit_length() - 1):
+            pieces //= 2
+            keep, give = pl.pallas_call(
+                functools.partial(halve_kernel, level),
+                out_shape=(
+                    jax.ShapeDtypeStruct((pieces, *part_shape), F32),
+                    jax.ShapeDtypeStruct((pieces, *part_shape), BF16),
+                ),
+                in_specs=[SMEM, VMEM, VMEM],
+                out_specs=(VMEM, VMEM),
+                compiler_params=params(),
+                name="halve",
+            )(chip_place, keep, got)
+            got = swapped(give, 2 << level)
+        return keep, got
+
     taken = exchanged(made)
-    partial, target_windows, moved, spread = first_near(before, right, after)
-    z_all, z_low, first, last = whole_sum(*core_parts(taken, partial, F32))
-    before = lax.ppermute(last, "row", up)
-    after = lax.ppermute(first, "row", down)
-    taken = exchanged(multipoles(z_low))
-    pieces = share_pieces(*core_parts(taken, near(before, z_low, after), BF16))
+    partial, target_windows, moved, spread = first_near(*to_neighbours(one, two), right)
+    z_all, z_low, one, two, made = whole_sum(*core_parts(taken, partial, F32))
+    taken = exchanged(made)
+    partial = near(*to_neighbours(one, two), z_low)
+    keep, got = own_share(*core_parts(taken, partial, BF16))
 
     lines = -(-9 * fields // LANES)
     sums = pl.pallas_call(
         functools.partial(gram_kernel, fields),
         out_shape=jax.ShapeDtypeStruct((group * rows, lines, LANES), F32),
-        in_specs=[SMEM] + [VMEM] * (2 + chips),
+        in_specs=[SMEM] + [VMEM] * 4,
         out_specs=VMEM,
         compiler_params=params(),
         name="gram",
-    )(plan, right, z_all, *pieces)
+    )(own_place, right, z_all, keep, got)
     sums = lax.all_to_all(sums, EVERY, 0, 0, tiled=True)
     out = pl.pallas_call(
         functools.partial(final_kernel, fields),

time: 68.1 us -> 64.7 us (0.950)
  starting transfers between devices: 27.7 us -> 17.9 us
  blocking collectives: 8.94 us -> 12.8 us
  waiting for transfers between devices: 15.8 us -> 19.3 us
  Pallas kernels: 14.4 us -> 12.6 us
  local copies, waits for them, and re-layouts: 0.01 us -> 0.87 us
    ppermute x9 -> x8, starting transfers between devices: 17.4 us -> 9.54 us  [swapped(): return lax.ppermute(value, GROUP, [(g, g ^ step) for g in range(group)])]
    ppermute x6, waiting for transfers between devices: 2.38 us -> 6.25 us  [the longest x4 6.24 us: to_neighbours(): lax.ppermute(value, 'row', list(enumerate(targets)))]
    all_to_all x1, blocking collectives: 8.94 us -> 12.8 us  [local(): sums = lax.all_to_all(sums, EVERY, 0, 0, tiled=True)]
    ppermute x6, starting transfers between devices: 10.4 us -> 8.31 us  [the longest x4 7.01 us: to_neighbours(): lax.ppermute(value, 'row', list(enumerate(targets)))]
    pallas_call x3, Pallas kernels: 2.24 us -> 1.11 us  [the longest x1 1.07 us: whole_sum(): pl.pallas_call(functools.partial(assemble_kernel, fields, items, width, s...]
    unnamed x2 -> x6, local copies, waits for them, and re-layouts: 0.01 us -> 0.87 us
    ppermute x9 -> x8, waiting for transfers between devices: 13.4 us -> 13 us  [swapped(): return lax.ppermute(value, GROUP, [(g, g ^ step) for g in range(group)])]
  transfers between devices with their start and end apart: 15 -> 14, of which waited for: 11 -> 11; matrix products, arithmetic and copies ran while one was open for 0% -> 0% of each run, Pallas kernels for 8% -> 6%
where the time goes in v4:
time: 64.7 us; the launch traced here: 64.4 us
  waiting for transfers between devices  19.3 us (30%)
  starting transfers between devices  17.9 us (28%)
  blocking collectives  12.8 us (20%)
  Pallas kernels  12.6 us (19%)
  between operations  0.97 us (1%)
  local copies, waits for them, and re-layouts  0.87 us (1%)
    ppermute x8, waiting for transfers between devices, swapped(): return lax.ppermute(value, GROUP, [(g, g ^ step) for g in range(group)])  13 us
    all_to_all x1, blocking collectives, local(): sums = lax.all_to_all(sums, EVERY, 0, 0, tiled=True)  12.8 us
    ppermute x8, starting transfers between devices, swapped(): return lax.ppermute(value, GROUP, [(g, g ^ step) for g in range(group)])  9.54 us
    ppermute x4, starting transfers between devices, to_neighbours(): lax.ppermute(value, 'row', list(enumerate(targets)))  7.01 us
    ppermute x4, waiting for transfers between devices, to_neighbours(): lax.ppermute(value, 'row', list(enumerate(targets)))  6.24 us
    pallas_call x2, Pallas kernels, core_parts(): pl.pallas_call(functools.partial(far_kernel, fields, items, width, slots)...  3.06 us
    pallas_call x1, Pallas kernels, first_near(): pl.pallas_call(functools.partial(first_near_kernel, fields, items, width)...  2.86 us
    pallas_call x1, Pallas kernels, local(): pl.pallas_call(functools.partial(begin_kernel, fields, items, width, send...  2.84 us
  transfers between devices with their start and end apart: 14, of which 11 were waited for; matrix products, arithmetic and copies ran while one was open for 0% of the time, Pallas kernels for 6%

profile of v4, /device:TPU:0, one launch (start us, length us, event | category | flops | bytes accessed | tf_op | source)
XLA Modules:
  0.0 64.4 jit_solution(9425136419784277017)
XLA Ops:
  0.8 2.8 %begin.1 = (s32[14]{0:T(128)S(1)}, bf16[1,16,896]{2,1,0:T(8,128)(2,1)S(1)}, bf16[1,3,448,2,128]{4,3,2,1,0:T(2,128)(2,1)S(1)}, s32[24,1,128]{2,1,0:T(1,128)S(1)},...) custom-call(s32[1]{0:T(128)} %bitcast.1.row_ref, s32[1]{0:T(128)} %bitcast.own_ref, ...), custom_call_target="tpu_custom_call" | custom-call | tf_op jit(solution)/shard_map/begin/pallas_call | solution.py:490
  3.7 0.9 %copy-done.1 = bf16[1,3,448,2,128]{4,3,2,1,0:T(2,128)(2,1)} copy-done((bf16[1,3,448,2,128]{4,3,2,1,0:T(2,128)(2,1)}, bf16[1,3,448,2,128]{4,3,2,1,0:T(2,128)(2,1)S(1)}, u32[]{:S(2)}) %copy-start.1) | copy-done | bytes 688152
  4.5 3.0 %collective-permute-start.1 = (bf16[32,512]{1,0:T(8,128)(2,1)S(1)}, bf16[32,512]{1,0:T(8,128)(2,1)S(1)}, u32[]{:S(2)}, u32[]{:S(2)}) collective-permute-start(bf16[32,512]{1,0:T(8,128)(2,1)S(1)} %get-tuple-element.33), channel_id=1, source_target_pairs={{0,4},{4,0},{8,12},{12,8},{1,5},{5,1},{9,13},{13,9},{2,6},{6,2},{1... | collective-permute-start | bytes 98312 | tf_op jit(solution)/shard_map/ppermute | solution.py:532
  7.5 2.5 %collective-permute-start.2 = (bf16[32,512]{1,0:T(8,128)(2,1)S(1)}, bf16[32,512]{1,0:T(8,128)(2,1)S(1)}, u32[]{:S(2)}, u32[]{:S(2)}) collective-permute-start(bf16[32,512]{1,0:T(8,128)(2,1)S(1)} %get-tuple-element.34), channel_id=1, source_target_pairs={{0,12},{4,8},{8,4},{12,0},{1,13},{5,9},{9,5},{13,1},{2,14},{6,10},... | collective-permute-start | bytes 98312 | tf_op jit(solution)/shard_map/ppermute | solution.py:532
  10.0 0.7 %collective-permute-start = (bf16[1,16,896]{2,1,0:T(8,128)(2,1)S(1)}, bf16[1,16,896]{2,1,0:T(8,128)(2,1)S(1)}, u32[]{:S(2)}, u32[]{:S(2)}) collective-permute-start(bf16[1,16,896]{2,1,0:T(8,128)(2,1)S(1)} %get-tuple-element.32), channel_id=1, source_target_pairs={{0,0},{1,1},{2,6},{3,7},{16,24},{17,25},{18,30},{19,31},{4,12},{5,... | collective-permute-start | bytes 86024 | tf_op jit(solution)/shard_map/ppermute | solution.py:526
  10.7 2.6 %collective-permute-done.2.two_ref = bf16[32,512]{1,0:T(8,128)(2,1)S(1)} collective-permute-done((bf16[32,512]{1,0:T(8,128)(2,1)S(1)}, bf16[32,512]{1,0:T(8,128)(2,1)S(1)}, u32[]{:S(2)}, u32[]{:S(2)}) %collective-permute-start.2) | collective-permute-done | bytes 32800 | tf_op jit(solution)/shard_map/ppermute | solution.py:532
  13.3 2.9 %first_near.1 = (f32[24,32,128]{2,1,0:T(8,128)S(1)}, bf16[1,3,448,2,128]{4,3,2,1,0:T(2,128)(2,1)S(1)}, bf16[1,896,441]{2,1,0:T(8,128)(2,1)S(1)}, bf16[441,896]{1,0:T(8,128)(2,1)S(1)}) custom-call(s32[1]{0:T(128)} %bitcast.1.row_ref, s32[14]{0:T(128)S(1)} %get-tuple-element.30.plan_any, bf16[441,24,2,128]{3,2,1,0:T(2,128)(2,1)} %bitcast.15, ...), custom_call_target="tpu_custom_call" | custom-call | flops 67108864 | bytes 2097152 | tf_op jit(solution)/shard_map/first_near/pallas_call | solution.py:541
  16.2 1.5 %far.2 = (f32[4,3,32,128]{3,2,1,0:T(8,128)S(1)}, f32[4,3,32,128]{3,2,1,0:T(8,128)S(1)}) custom-call(s32[1]{0:T(128)} %bitcast.8.core_ref, s32[14]{0:T(128)S(1)} %get-tuple-element.30.plan_any, s32[24,1,128]{2,1,0:T(1,128)S(1)} %get-tuple-element.31.leaves_ref, bf16[1,16,896]{2,1,0:T(8,128)(2,1)S(1)} %collective-permute-done.item_ref, ...), custom_call_target="tpu_custom_call" | custom-call | tf_op jit(solution)/shard_map/far/pallas_call | solution.py:580
  17.7 0.1 collective-permute-start.3
  17.8 1.4 %collective-permute-done.3.got_ref = f32[4,3,32,128]{3,2,1,0:T(8,128)S(1)} collective-permute-done((f32[4,3,32,128]{3,2,1,0:T(8,128)S(1)}, f32[4,3,32,128]{3,2,1,0:T(8,128)S(1)}, u32[]{:S(2)}, u32[]{:S(2)}) %collective-permute-start.3) | collective-permute-done | bytes 196640 | tf_op jit(solution)/shard_map/ppermute | solution.py:576
  19.2 3.9 %collective-permute-start.6 = (bf16[4,3,32,128]{3,2,1,0:T(8,128)(2,1)S(1)}, bf16[4,3,32,128]{3,2,1,0:T(8,128)(2,1)S(1)}, u32[]{:S(2)}, u32[]{:S(2)}) collective-permute-start(bf16[4,3,32,128]{3,2,1,0:T(8,128)(2,1)S(1)} %pair.1.refs_0_), channel_id=1, source_target_pairs={{0,18},{1,19},{2,16},{3,17},{16,2},{17,3},{18,0},{19,1},{4,22},{5,... | collective-permute-start | bytes 294920 | tf_op jit(solution)/shard_map/ppermute | solution.py:576
  23.2 0.6 collective-permute-start.4
  23.8 2.9 %collective-permute-done.6.refs_3_ = bf16[4,3,32,128]{3,2,1,0:T(8,128)(2,1)S(1)} collective-permute-done((bf16[4,3,32,128]{3,2,1,0:T(8,128)(2,1)S(1)}, bf16[4,3,32,128]{3,2,1,0:T(8,128)(2,1)S(1)}, u32[]{:S(2)}, u32[]{:S(2)}) %collective-permute-start.6) | collective-permute-done | bytes 98336 | tf_op jit(solution)/shard_map/ppermute | solution.py:576
  26.7 1.0 %collective-permute-done.5.refs_2_ = bf16[4,3,32,128]{3,2,1,0:T(8,128)(2,1)S(1)} collective-permute-done((bf16[4,3,32,128]{3,2,1,0:T(8,128)(2,1)S(1)}, bf16[4,3,32,128]{3,2,1,0:T(8,128)(2,1)S(1)}, u32[]{:S(2)}, u32[]{:S(2)}) %collective-permute-start.5) | collective-permute-done | bytes 98336 | tf_op jit(solution)/shard_map/ppermute | solution.py:576
  27.8 0.6 collective-permute-done.4.refs_1_
  28.4 0.1 collective-permute-start.7
  28.5 1.4 %collective-permute-done.7.theirs_ref = f32[4,3,32,128]{3,2,1,0:T(8,128)S(1)} collective-permute-done((f32[4,3,32,128]{3,2,1,0:T(8,128)S(1)}, f32[4,3,32,128]{3,2,1,0:T(8,128)S(1)}, u32[]{:S(2)}, u32[]{:S(2)}) %collective-permute-start.7) | collective-permute-done | bytes 196640 | tf_op jit(solution)/shard_map/ppermute | solution.py:576
  29.9 1.1 %assemble.1 = (f32[24,32,128]{2,1,0:T(8,128)S(1)}, bf16[24,32,128]{2,1,0:T(8,128)(2,1)S(1)}, bf16[4,32,128]{2,1,0:T(8,128)(2,1)S(1)}, bf16[4,32,128]{2,1,0:T(8,128)(2,1)S(1)}, bf16[1,16,896]{2,1,0:T(8,128)(2,1)S(1)}) custom-call(s32[1]{0:T(128)} %bitcast.8.core_ref, s32[1]{0:T(128)} %bitcast.1.row_ref, s32[14]{0:T(128)S(1)} %get-tuple-element.30.plan_any, ...), custom_call_target="tpu_custom_call" | custom-call | tf_op jit(solution)/shard_map/assemble/pallas_call | solution.py:612
  31.1 1.4 %collective-permute-start.10 = (bf16[4,32,128]{2,1,0:T(8,128)(2,1)S(1)}, bf16[4,32,128]{2,1,0:T(8,128)(2,1)S(1)}, u32[]{:S(2)}, u32[]{:S(2)}) collective-permute-start(bf16[4,32,128]{2,1,0:T(8,128)(2,1)S(1)} %get-tuple-element.45), channel_id=1, source_target_pairs={{0,12},{4,8},{8,4},{12,0},{1,13},{5,9},{9,5},{13,1},{2,14},{6,10},... | collective-permute-start | bytes 98312 | tf_op jit(solution)/shard_map/ppermute | solution.py:532
  32.5 0.7 %collective-permute-start.8 = (bf16[1,16,896]{2,1,0:T(8,128)(2,1)S(1)}, bf16[1,16,896]{2,1,0:T(8,128)(2,1)S(1)}, u32[]{:S(2)}, u32[]{:S(2)}) collective-permute-start(bf16[1,16,896]{2,1,0:T(8,128)(2,1)S(1)} %get-tuple-element.43), channel_id=1, source_target_pairs={{0,0},{1,1},{2,6},{3,7},{16,24},{17,25},{18,30},{19,31},{4,12},{5,... | collective-permute-start | bytes 86024 | tf_op jit(solution)/shard_map/ppermute | solution.py:526
  33.2 1.8 %collective-permute-done.9.one_ref = bf16[4,32,128]{2,1,0:T(8,128)(2,1)S(1)} collective-permute-done((bf16[4,32,128]{2,1,0:T(8,128)(2,1)S(1)}, bf16[4,32,128]{2,1,0:T(8,128)(2,1)S(1)}, u32[]{:S(2)}, u32[]{:S(2)}) %collective-permute-start.9) | collective-permute-done | bytes 32800 | tf_op jit(solution)/shard_map/ppermute | solution.py:532
  35.0 1.9 %collective-permute-done.10.two_ref = bf16[4,32,128]{2,1,0:T(8,128)(2,1)S(1)} collective-permute-done((bf16[4,32,128]{2,1,0:T(8,128)(2,1)S(1)}, bf16[4,32,128]{2,1,0:T(8,128)(2,1)S(1)}, u32[]{:S(2)}, u32[]{:S(2)}) %collective-permute-start.10) | collective-permute-done | bytes 32800 | tf_op jit(solution)/shard_map/ppermute | solution.py:532
  36.9 1.3 %near.1.partial_ref = f32[24,32,128]{2,1,0:T(8,128)S(1)} custom-call(s32[1]{0:T(128)} %bitcast.1.row_ref, s32[14]{0:T(128)S(1)} %get-tuple-element.30.plan_any, bf16[4,32,128]{2,1,0:T(8,128)(2,1)S(1)} %collective-permute-done.9.one_ref, bf16[4,32,128]{2,1,0:T(8,128)(2,1)S(1)} %collective-permute-done.10.two_ref, ...), custom_call_target="tpu_custom_call" | custom-call | flops 67108864 | bytes 2097152 | tf_op jit(solution)/shard_map/near/pallas_call | solution.py:564
  38.2 1.5 %far.3 = (bf16[4,3,32,128]{3,2,1,0:T(8,128)(2,1)S(1)}, bf16[4,3,32,128]{3,2,1,0:T(8,128)(2,1)S(1)}) custom-call(s32[1]{0:T(128)} %bitcast.8.core_ref, s32[14]{0:T(128)S(1)} %get-tuple-element.30.plan_any, s32[24,1,128]{2,1,0:T(1,128)S(1)} %get-tuple-element.31.leaves_ref, bf16[1,16,896]{2,1,0:T(8,128)(2,1)S(1)} %collective-permute-done.8.item_ref, ...), custom_call_target="tpu_custom_call" | custom-call | tf_op jit(solution)/shard_map/far/pallas_call | solution.py:580
  39.8 1.3 %collective-permute-done.11.got_ref = bf16[4,3,32,128]{3,2,1,0:T(8,128)(2,1)S(1)} collective-permute-done((bf16[4,3,32,128]{3,2,1,0:T(8,128)(2,1)S(1)}, bf16[4,3,32,128]{3,2,1,0:T(8,128)(2,1)S(1)}, u32[]{:S(2)}, u32[]{:S(2)}) %collective-permute-start.11) | collective-permute-done | bytes 98336 | tf_op jit(solution)/shard_map/ppermute | solution.py:576
  41.1 1.6 %collective-permute-start.12 = (bf16[2,3,32,128]{3,2,1,0:T(8,128)(2,1)S(1)}, bf16[2,3,32,128]{3,2,1,0:T(8,128)(2,1)S(1)}, u32[]{:S(2)}, u32[]{:S(2)}) collective-permute-start(bf16[2,3,32,128]{3,2,1,0:T(8,128)(2,1)S(1)} %get-tuple-element.50), channel_id=1, source_target_pairs={{0,2},{1,3},{2,0},{3,1},{16,18},{17,19},{18,16},{19,17},{4,6},{5,7... | collective-permute-start | bytes 147464 | tf_op jit(solution)/shard_map/ppermute | solution.py:576
  42.7 2.5 %collective-permute-done.12.got_ref = bf16[2,3,32,128]{3,2,1,0:T(8,128)(2,1)S(1)} collective-permute-done((bf16[2,3,32,128]{3,2,1,0:T(8,128)(2,1)S(1)}, bf16[2,3,32,128]{3,2,1,0:T(8,128)(2,1)S(1)}, u32[]{:S(2)}, u32[]{:S(2)}) %collective-permute-start.12) | collective-permute-done | bytes 49184 | tf_op jit(solution)/shard_map/ppermute | solution.py:576
  45.3 3.1 %collective-permute-start.13 = (bf16[1,3,32,128]{3,2,1,0:T(8,128)(2,1)S(1)}, bf16[1,3,32,128]{3,2,1,0:T(8,128)(2,1)S(1)}, u32[]{:S(2)}, u32[]{:S(2)}) collective-permute-start(bf16[1,3,32,128]{3,2,1,0:T(8,128)(2,1)S(1)} %get-tuple-element.52), channel_id=1, source_target_pairs={{0,16},{1,17},{2,18},{3,19},{16,0},{17,1},{18,2},{19,3},{4,20},{5,... | collective-permute-start | bytes 73736 | tf_op jit(solution)/shard_map/ppermute | solution.py:576
  48.4 1.8 %collective-permute-done.13.got_ref = bf16[1,3,32,128]{3,2,1,0:T(8,128)(2,1)S(1)} collective-permute-done((bf16[1,3,32,128]{3,2,1,0:T(8,128)(2,1)S(1)}, bf16[1,3,32,128]{3,2,1,0:T(8,128)(2,1)S(1)}, u32[]{:S(2)}, u32[]{:S(2)}) %collective-permute-start.13) | collective-permute-done | bytes 24608 | tf_op jit(solution)/shard_map/ppermute | solution.py:576
  50.2 0.3 gram.1
  50.5 12.8 %all_to_all.5.sums_ref = f32[32,2,128]{2,1,0:T(2,128)S(1)} all-to-all(f32[32,2,128]{2,1,0:T(2,128)S(1)} %gram.1), channel_id=1, replica_groups=mesh['grp'=2,'row'=4,'col'=4] {'grp','row','col'}, dimensions={0} | all-to-all | bytes 65536 | tf_op jit(solution)/shard_map/all_to_all | solution.py:656
  63.3 1.1 %combine.1 = f32[32,3072]{1,0:T(8,128)} custom-call(f32[32,2,128]{2,1,0:T(2,128)S(1)} %all_to_all.5.sums_ref, f32[32,3072]{1,0:T(8,128)S(1)} %get-tuple-element.29.here_ref.right_ref, f32[24,32,128]{2,1,0:T(8,128)S(1)} %get-tuple-element.42.image_ref), custom_call_target="tpu_custom_call" | custom-call | tf_op jit(solution)/shard_map/combine/pallas_call | solution.py:657
  (15 shorter events, 0.3 us)
Async XLA Ops:
  0.0 13.3 %copy-start = (bf16[2,8,256,256]{3,2,1,0:T(8,128)(2,1)S(1)}, bf16[2,8,256,256]{3,2,1,0:T(8,128)(2,1)}, u32[]{:S(2)}) copy-start(bf16[2,8,256,256]{3,2,1,0:T(8,128)(2,1)} %tiles_ref.3) | copy-start | bytes 6291460
  3.7 0.9 %copy-start.1 = (bf16[1,3,448,2,128]{4,3,2,1,0:T(2,128)(2,1)}, bf16[1,3,448,2,128]{4,3,2,1,0:T(2,128)(2,1)S(1)}, u32[]{:S(2)}) copy-start(bf16[1,3,448,2,128]{4,3,2,1,0:T(2,128)(2,1)S(1)} %get-tuple-element.41.window_ref) | copy-start | bytes 2064388
  4.5 6.2 %collective-permute-start.1 = (bf16[32,512]{1,0:T(8,128)(2,1)S(1)}, bf16[32,512]{1,0:T(8,128)(2,1)S(1)}, u32[]{:S(2)}, u32[]{:S(2)}) collective-permute-start(bf16[32,512]{1,0:T(8,128)(2,1)S(1)} %get-tuple-element.33), channel_id=1, source_target_pairs={{0,4},{4,0},{8,12},{12,8},{1,5},{5,1},{9,13},{13,9},{2,6},{6,2},{1... | collective-permute-start | bytes 98312 | tf_op jit(solution)/shard_map/ppermute | solution.py:532
  7.5 5.7 %collective-permute-start.2 = (bf16[32,512]{1,0:T(8,128)(2,1)S(1)}, bf16[32,512]{1,0:T(8,128)(2,1)S(1)}, u32[]{:S(2)}, u32[]{:S(2)}) collective-permute-start(bf16[32,512]{1,0:T(8,128)(2,1)S(1)} %get-tuple-element.34), channel_id=1, source_target_pairs={{0,12},{4,8},{8,4},{12,0},{1,13},{5,9},{9,5},{13,1},{2,14},{6,10},... | collective-permute-start | bytes 98312 | tf_op jit(solution)/shard_map/ppermute | solution.py:532
  10.0 6.1 %collective-permute-start = (bf16[1,16,896]{2,1,0:T(8,128)(2,1)S(1)}, bf16[1,16,896]{2,1,0:T(8,128)(2,1)S(1)}, u32[]{:S(2)}, u32[]{:S(2)}) collective-permute-start(bf16[1,16,896]{2,1,0:T(8,128)(2,1)S(1)} %get-tuple-element.32), channel_id=1, source_target_pairs={{0,0},{1,1},{2,6},{3,7},{16,24},{17,25},{18,30},{19,31},{4,12},{5,... | collective-permute-start | bytes 86024 | tf_op jit(solution)/shard_map/ppermute | solution.py:526
  16.1 13.8 %copy-start.2 = (bf16[1,3,448,2,128]{4,3,2,1,0:T(2,128)(2,1)S(1)}, bf16[1,3,448,2,128]{4,3,2,1,0:T(2,128)(2,1)}, u32[]{:S(2)}) copy-start(bf16[1,3,448,2,128]{4,3,2,1,0:T(2,128)(2,1)} %copy-done.1) | copy-start | bytes 2064388
  17.7 1.5 %collective-permute-start.3 = (f32[4,3,32,128]{3,2,1,0:T(8,128)S(1)}, f32[4,3,32,128]{3,2,1,0:T(8,128)S(1)}, u32[]{:S(2)}, u32[]{:S(2)}) collective-permute-start(f32[4,3,32,128]{3,2,1,0:T(8,128)S(1)} %get-tuple-element.40), channel_id=1, source_target_pairs={{0,1},{1,0},{2,3},{3,2},{16,17},{17,16},{18,19},{19,18},{4,5},{5,4... | collective-permute-start | bytes 589832 | tf_op jit(solution)/shard_map/ppermute | solution.py:576
  19.2 7.5 %collective-permute-start.6 = (bf16[4,3,32,128]{3,2,1,0:T(8,128)(2,1)S(1)}, bf16[4,3,32,128]{3,2,1,0:T(8,128)(2,1)S(1)}, u32[]{:S(2)}, u32[]{:S(2)}) collective-permute-start(bf16[4,3,32,128]{3,2,1,0:T(8,128)(2,1)S(1)} %pair.1.refs_0_), channel_id=1, source_target_pairs={{0,18},{1,19},{2,16},{3,17},{16,2},{17,3},{18,0},{19,1},{4,22},{5,... | collective-permute-start | bytes 294920 | tf_op jit(solution)/shard_map/ppermute | solution.py:576
  23.2 4.6 %collective-permute-start.5 = (bf16[4,3,32,128]{3,2,1,0:T(8,128)(2,1)S(1)}, bf16[4,3,32,128]{3,2,1,0:T(8,128)(2,1)S(1)}, u32[]{:S(2)}, u32[]{:S(2)}) collective-permute-start(bf16[4,3,32,128]{3,2,1,0:T(8,128)(2,1)S(1)} %pair.1.refs_0_), channel_id=1, source_target_pairs={{0,16},{1,17},{2,18},{3,19},{16,0},{17,1},{18,2},{19,3},{4,20},{5,... | collective-permute-start | bytes 294920 | tf_op jit(solution)/shard_map/ppermute | solution.py:576
  23.2 5.2 %collective-permute-start.4 = (bf16[4,3,32,128]{3,2,1,0:T(8,128)(2,1)S(1)}, bf16[4,3,32,128]{3,2,1,0:T(8,128)(2,1)S(1)}, u32[]{:S(2)}, u32[]{:S(2)}) collective-permute-start(bf16[4,3,32,128]{3,2,1,0:T(8,128)(2,1)S(1)} %pair.1.refs_0_), channel_id=1, source_target_pairs={{0,2},{1,3},{2,0},{3,1},{16,18},{17,19},{18,16},{19,17},{4,6},{5,7... | collective-permute-start | bytes 294920 | tf_op jit(solution)/shard_map/ppermute | solution.py:576
  28.4 1.5 %collective-permute-start.7 = (f32[4,3,32,128]{3,2,1,0:T(8,128)S(1)}, f32[4,3,32,128]{3,2,1,0:T(8,128)S(1)}, u32[]{:S(2)}, u32[]{:S(2)}) collective-permute-start(f32[4,3,32,128]{3,2,1,0:T(8,128)S(1)} %close.1.mine_ref), channel_id=1, source_target_pairs={{0,1},{1,0},{2,3},{3,2},{16,17},{17,16},{18,19},{19,18},{4,5},{5,4... | collective-permute-start | bytes 589832 | tf_op jit(solution)/shard_map/ppermute | solution.py:576
  31.0 4.0 %collective-permute-start.9 = (bf16[4,32,128]{2,1,0:T(8,128)(2,1)S(1)}, bf16[4,32,128]{2,1,0:T(8,128)(2,1)S(1)}, u32[]{:S(2)}, u32[]{:S(2)}) collective-permute-start(bf16[4,32,128]{2,1,0:T(8,128)(2,1)S(1)} %get-tuple-element.44), channel_id=1, source_target_pairs={{0,4},{4,0},{8,12},{12,8},{1,5},{5,1},{9,13},{13,9},{2,6},{6,2},{1... | collective-permute-start | bytes 98312 | tf_op jit(solution)/shard_map/ppermute | solution.py:532
  31.1 5.8 %collective-permute-start.10 = (bf16[4,32,128]{2,1,0:T(8,128)(2,1)S(1)}, bf16[4,32,128]{2,1,0:T(8,128)(2,1)S(1)}, u32[]{:S(2)}, u32[]{:S(2)}) collective-permute-start(bf16[4,32,128]{2,1,0:T(8,128)(2,1)S(1)} %get-tuple-element.45), channel_id=1, source_target_pairs={{0,12},{4,8},{8,4},{12,0},{1,13},{5,9},{9,5},{13,1},{2,14},{6,10},... | collective-permute-start | bytes 98312 | tf_op jit(solution)/shard_map/ppermute | solution.py:532
  32.5 5.6 %collective-permute-start.8 = (bf16[1,16,896]{2,1,0:T(8,128)(2,1)S(1)}, bf16[1,16,896]{2,1,0:T(8,128)(2,1)S(1)}, u32[]{:S(2)}, u32[]{:S(2)}) collective-permute-start(bf16[1,16,896]{2,1,0:T(8,128)(2,1)S(1)} %get-tuple-element.43), channel_id=1, source_target_pairs={{0,0},{1,1},{2,6},{3,7},{16,24},{17,25},{18,30},{19,31},{4,12},{5,... | collective-permute-start | bytes 86024 | tf_op jit(solution)/shard_map/ppermute | solution.py:526
  39.7 1.4 %collective-permute-start.11 = (bf16[4,3,32,128]{3,2,1,0:T(8,128)(2,1)S(1)}, bf16[4,3,32,128]{3,2,1,0:T(8,128)(2,1)S(1)}, u32[]{:S(2)}, u32[]{:S(2)}) collective-permute-start(bf16[4,3,32,128]{3,2,1,0:T(8,128)(2,1)S(1)} %get-tuple-element.48), channel_id=1, source_target_pairs={{0,1},{1,0},{2,3},{3,2},{16,17},{17,16},{18,19},{19,18},{4,5},{5,4... | collective-permute-start | bytes 294920 | tf_op jit(solution)/shard_map/ppermute | solution.py:576
  41.1 4.2 %collective-permute-start.12 = (bf16[2,3,32,128]{3,2,1,0:T(8,128)(2,1)S(1)}, bf16[2,3,32,128]{3,2,1,0:T(8,128)(2,1)S(1)}, u32[]{:S(2)}, u32[]{:S(2)}) collective-permute-start(bf16[2,3,32,128]{3,2,1,0:T(8,128)(2,1)S(1)} %get-tuple-element.50), channel_id=1, source_target_pairs={{0,2},{1,3},{2,0},{3,1},{16,18},{17,19},{18,16},{19,17},{4,6},{5,7... | collective-permute-start | bytes 147464 | tf_op jit(solution)/shard_map/ppermute | solution.py:576
  45.3 4.9 %collective-permute-start.13 = (bf16[1,3,32,128]{3,2,1,0:T(8,128)(2,1)S(1)}, bf16[1,3,32,128]{3,2,1,0:T(8,128)(2,1)S(1)}, u32[]{:S(2)}, u32[]{:S(2)}) collective-permute-start(bf16[1,3,32,128]{3,2,1,0:T(8,128)(2,1)S(1)} %get-tuple-element.52), channel_id=1, source_target_pairs={{0,16},{1,17},{2,18},{3,19},{16,0},{17,1},{18,2},{19,3},{4,20},{5,... | collective-permute-start | bytes 73736 | tf_op jit(solution)/shard_map/ppermute | solution.py:576

commit v5 on v4

--- a/solution.py
+++ b/solution.py
@@ -12,8 +12,9 @@
 LANES = 128
 EPSILON = 1e-06
 GROUP = ("grp", "col")
-COUNT, CODES = range(2)
+CODES = 0
 PER_ITEM = 5
+ITEM_REST = 2 * LANES
 EVERY = ("grp", "row", "col")
 
 F32 = jnp.float32
@@ -45,6 +46,19 @@
 
 def odd_lanes(shape):
     return lax.rem(lax.broadcasted_iota(jnp.int32, shape, 1), 2) == 1
+
+
+def twice(value, width):
+    rows = value.shape[0]
+    parts = []
+    for k in range(width // LANES):
+        first = (k // 2) * LANES
+        part = value[:, first : first + LANES]
+        if part.shape[1] < LANES:
+            part = jnp.concatenate([part, jnp.zeros((rows, LANES - part.shape[1]), part.dtype)], axis=-1)
+        lane = lax.broadcasted_iota(jnp.int32, (rows, LANES), 1)
+        parts.append(jnp.take_along_axis(part, lax.div(lane, 2) + (k % 2) * (LANES // 2), axis=1))
+    return jnp.concatenate(parts, axis=-1)
 
 
 def from_left(value):
@@ -94,11 +108,8 @@
         rows = jnp.concatenate([low_ref[unit + k] for k in range(width)], axis=-1)
     mask = window_mask(leaves_ref, leaf, unit, 2 * fields, width)
     rows = halves(jnp.where(mask, rows.astype(F32), 0.0).astype(rows.dtype))
-    total = None
-    for k in range(width):
-        part = dot_nt(rows[:, k * LANES : (k + 1) * LANES], as_rows(window_ref.at[k]))
-        total = part if total is None else total + part
-    total = joined(total, 2 * fields)
+    expansions = jnp.concatenate([as_rows(window_ref.at[k]) for k in range(width)], axis=-1)
+    total = joined(dot_nt(rows, expansions), 2 * fields)
     on_real, on_imag = total[:fields], total[fields:]
     odd = odd_lanes(on_real.shape)
     other = jnp.where(odd, from_left(on_imag), from_right(on_imag))
@@ -109,8 +120,15 @@
     return ref.reshape(ref.shape[0] * 2, ref.shape[2])[...]
 
 
-def write_edges(row, first, last, one_ref, two_ref):
-    even = lax.rem(row, 2) == 0
+def edge_kernel(row_ref, image_ref, one_ref, two_ref):
+    even = lax.rem(row_ref[0], 2) == 0
+    if len(image_ref.shape) == 2:
+        edge = one_ref.shape[1]
+        first, last = image_ref[:, :edge], image_ref[:, image_ref.shape[1] - edge :]
+    else:
+        edge = one_ref.shape[0]
+        first, last = image_ref[:edge], image_ref[image_ref.shape[0] - edge :]
+    first, last = first.astype(one_ref.dtype), last.astype(one_ref.dtype)
 
     @pl.when(even)
     def _():
@@ -122,13 +140,11 @@
 
 
 def begin_kernel(
-    fields, items, width, send, rows, edge, row_ref, own_ref, count_ref, pick_hbm, leaf_hbm, leaves_hbm,
+    fields, items, width, send, rows, row_ref, own_ref, pick_hbm, leaf_hbm, leaves_hbm,
     target_hbm, offset_hbm, pairs_hbm, right_hbm, exp_ref,
-    plan_ref, out_ref, window_ref, leaves_ref, right_ref, *edge_refs_and_scratch,
+    plan_ref, out_ref, window_ref, leaves_ref, right_ref,
+    pick_ref, leaf_ref, target_ref, offset_ref, pairs_ref, sem, window_sem,
 ):
-    edge_refs = edge_refs_and_scratch[:2]
-    pick_ref, leaf_ref, target_ref, offset_ref, pairs_ref, sem, window_sem = edge_refs_and_scratch[2:]
-    panels = right_ref.shape[1]
     loads = [
         pltpu.make_async_copy(source, place, sem.at[k])
         for k, (source, place) in enumerate(
@@ -167,9 +183,6 @@
             copy.start()
     for load in loads[2:]:
         load.wait()
-    edges = right_ref[:, :edge].astype(BF16), right_ref[:, panels - edge :].astype(BF16)
-    write_edges(row, *edges, *edge_refs)
-    plan_ref[COUNT] = count_ref[0]
     for s in range(slots):
         plan_ref[CODES + s] = pairs_ref[s]
     for i in range(items):
@@ -183,22 +196,16 @@
         leaf, unit = plan_ref[place], plan_ref[place + 1]
         for copy in window_copies(exp_ref, unit, window_ref.at[i], window_sem.at[i], width):
             copy.wait()
-        out_ref[i] = multi_rows(fields, width, leaf, unit, leaves_ref, right_ref, window_ref.at[i]).astype(BF16)
-
-
-def first_near_kernel(
-    fields, items, width, row_ref, plan_any, exp_ref, trans_ref, one_ref, two_ref, here_ref, tiles_ref,
-    out_ref, window_ref, moved_ref, spread_ref, ext, plan_ref, plan_sem, trans_buf, sem, trans_sem,
-):
+        made = multi_rows(fields, width, leaf, unit, leaves_ref, right_ref, window_ref.at[i])
+        out_ref[i, :, : made.shape[1]] = made.astype(BF16)
+
+
+def fetch_kernel(items, width, slots, plan_any, exp_ref, trans_ref, window_ref, moved_ref, plan_ref, plan_sem, trans_buf, sem, trans_sem):
     plan_copy = pltpu.make_async_copy(plan_any, plan_ref, plan_sem)
     plan_copy.start()
     coefs = trans_ref.shape[3]
-    slots = tiles_ref.shape[1]
-    shape = spread_ref.shape
-    row = lax.broadcasted_iota(jnp.int32, shape, 0)
-    column = lax.broadcasted_iota(jnp.int32, shape, 1)
-    spread_ref[...] = jnp.where(column == 2 * row, 1.0, 0.0).astype(BF16)
-    near_sources(row_ref, one_ref, two_ref, here_ref, out_ref, ext)
+    for i in range(items):
+        clear_rest(window_ref.at[i], coefs, width)
     plan_copy.wait()
 
     def trans_copy(i):
@@ -213,8 +220,6 @@
         trans_copy(i).start()
         for copy in exp_copies(i):
             copy.start()
-        clear_rest(window_ref.at[i], coefs, width)
-    near_slots(fields, plan_ref, tiles_ref, out_ref, ext)
     rest = moved_ref.shape[1] - 2 * coefs
     for i in range(items):
         trans_copy(i).wait()
@@ -224,8 +229,7 @@
             copy.wait()
 
 
-def near_sources(row_ref, one_ref, two_ref, here_ref, out_ref, ext):
-    units = out_ref.shape[0]
+def near_sources(row_ref, one_ref, two_ref, here_ref, units, ext):
     edge = (ext.shape[0] - units) // 2
     even = lax.rem(row_ref[0], 2) == 0
     one_at = jnp.where(even, edge + units, 0)
@@ -241,20 +245,24 @@
         ext[pl.ds(one_at, edge)] = one_ref[...]
         ext[pl.ds(two_at, edge)] = two_ref[...]
         ext[edge : edge + units] = here_ref[...]
-    out_ref[...] = jnp.zeros_like(out_ref)
-
-
-def near_kernel(fields, row_ref, plan_any, one_ref, two_ref, here_ref, tiles_ref, out_ref, ext, plan_ref, plan_sem):
+
+
+def near_kernel(
+    fields, units, core_ref, row_ref, count_ref, plan_any, image_ref, one_ref, two_ref, here_ref, tiles_ref,
+    keep_ref, give_ref, ext, total, plan_ref, plan_sem,
+):
     plan_copy = pltpu.make_async_copy(plan_any, plan_ref, plan_sem)
     plan_copy.start()
-    near_sources(row_ref, one_ref, two_ref, here_ref, out_ref, ext)
-    plan_copy.wait()
-    near_slots(fields, plan_ref, tiles_ref, out_ref, ext)
-
-
-def near_slots(fields, plan_ref, tiles_ref, out_ref, ext):
+    near_sources(row_ref, one_ref, two_ref, here_ref, units, ext)
+    total[...] = jnp.zeros_like(total)
     slots, tile = tiles_ref.shape[1], tiles_ref.shape[2]
     per = tile // LANES
+    plan_copy.wait()
+    items, width = image_ref.shape[:2]
+    for i in range(items):
+        unit = plan_ref[item_place(slots, i) + 3]
+        for k in range(width):
+            total[unit + k] += image_ref[i, k]
     for s in range(slots):
         code = plan_ref[CODES + s]
         target = lax.div(code, SPAN)
@@ -265,40 +273,9 @@
         value = jnp.concatenate(
             [on_real[:fields] - on_imag[fields:], on_real[fields:] + on_imag[:fields]], axis=0
         )
-        value = jnp.where(s < plan_ref[COUNT], value, 0.0)
+        value = jnp.where(s < count_ref[0], value, 0.0)
         for k in range(per):
-            out_ref[target * per + k] += value[:, k * LANES : (k + 1) * LANES]
-
-
-def far_kernel(
-    fields, items, width, slots, core_ref, plan_any, leaves_ref, item_ref, partial_ref, trans_ref, spread_ref,
-    window_ref, keep_ref, give_ref, total, plan_ref, plan_sem,
-):
-    plan_copy = pltpu.make_async_copy(plan_any, plan_ref, plan_sem)
-    plan_copy.start()
-    units = partial_ref.shape[0]
-    total[0:units] = partial_ref[...]
-    if total.shape[0] > units:
-        total[units:] = jnp.zeros((total.shape[0] - units, *total.shape[1:]), F32)
-    for i in range(items):
-        plain = item_ref[i].astype(F32)
-        odd = odd_lanes(plain.shape)
-        turned = jnp.where(odd, from_left(plain), -from_right(plain))
-        rows = jnp.concatenate([plain, turned], axis=0).astype(BF16)
-        local_field = dot_nn(rows, trans_ref[i]).astype(BF16)
-        apart = dot_nn(local_field, spread_ref[...])
-        local_real, local_imag = apart[:fields], apart[fields:]
-        rows = jnp.concatenate(
-            [local_real - from_left(local_imag), local_imag + from_left(local_real)], axis=0
-        ).astype(BF16)
-        if i == 0:
-            plan_copy.wait()
-        place = item_place(slots, i)
-        leaf, unit = plan_ref[place + 2], plan_ref[place + 3]
-        mask = window_mask(leaves_ref, leaf, unit, 2 * fields, width)
-        for k in range(width):
-            image = dot_nn(rows, as_rows(window_ref.at[i, k]))
-            total[unit + k] += jnp.where(mask[:, k * LANES : (k + 1) * LANES], image, 0.0)
+            total[target * per + k] += value[:, k * LANES : (k + 1) * LANES]
     chips, share = keep_ref.shape[:2]
     core = core_ref[0]
     for c in range(chips):
@@ -306,11 +283,38 @@
         give_ref[c] = total[pl.ds((2 * c + 1 - core) * share, share)].astype(give_ref.dtype)
 
 
-def halve_kernel(level, chip_ref, mine_ref, got_ref, keep_ref, give_ref):
-    bit = lax.rem(lax.div(chip_ref[0], 1 << level), 2)
-    for k in range(keep_ref.shape[0]):
-        for out_ref, place in ((keep_ref, 2 * k + bit), (give_ref, 2 * k + 1 - bit)):
-            out_ref[k] = (mine_ref[place].astype(F32) + got_ref[place].astype(F32)).astype(out_ref.dtype)
+def far_kernel(
+    fields, items, width, slots, plan_any, leaves_ref, item_ref, trans_ref, window_ref, image_ref, plan_ref, plan_sem
+):
+    plan_copy = pltpu.make_async_copy(plan_any, plan_ref, plan_sem)
+    plan_copy.start()
+    images = []
+    for i in range(items):
+        plain = item_ref[i, :, : trans_ref.shape[1]].astype(F32)
+        odd = odd_lanes(plain.shape)
+        turned = jnp.where(odd, from_left(plain), -from_right(plain))
+        rows = jnp.concatenate([plain, turned], axis=0).astype(BF16)
+        local_field = dot_nn(rows, trans_ref[i]).astype(BF16).astype(F32)
+        local_field = twice(local_field, plain.shape[1])
+        local_real, local_imag = local_field[:fields], local_field[fields:]
+        rows = jnp.concatenate(
+            [jnp.where(odd, -local_imag, local_real), jnp.where(odd, local_real, local_imag)], axis=0
+        ).astype(BF16)
+        expansions = jnp.concatenate([as_rows(window_ref.at[i, k]) for k in range(width)], axis=-1)
+        images.append(dot_nn(rows, expansions))
+    plan_copy.wait()
+    for i in range(items):
+        place = item_place(slots, i)
+        mask = window_mask(leaves_ref, plan_ref[place + 2], plan_ref[place + 3], 2 * fields, width)
+        image = jnp.where(mask, images[i], 0.0)
+        for k in range(width):
+            image_ref[i, k] = image[:, k * LANES : (k + 1) * LANES]
+
+
+def fold_kernel(chip_ref, keep_ref, got_ref, own_ref, *out_refs):
+    for step, out_ref in enumerate((own_ref,) + out_refs):
+        chip = lax.bitwise_xor(chip_ref[0], step)
+        out_ref[...] = (keep_ref[chip].astype(F32) + got_ref[chip].astype(F32)).astype(out_ref.dtype)
 
 
 def pair_kernel(keep_ref, got_ref, out_ref):
@@ -328,28 +332,26 @@
 
 
 def assemble_kernel(
-    fields, items, width, slots, core_ref, row_ref, plan_any, leaves_ref, mine_ref, theirs_ref, window_ref,
-    out_ref, low_ref, one_ref, two_ref, made_ref, whole, plan_ref, plan_sem,
+    fields, items, width, slots, core_ref, plan_any, leaves_ref, mine_ref, theirs_ref, window_ref,
+    out_ref, low_ref, made_ref, whole, plan_ref, plan_sem,
 ):
     plan_copy = pltpu.make_async_copy(plan_any, plan_ref, plan_sem)
     plan_copy.start()
     chips, share = mine_ref.shape[:2]
-    units, edge = out_ref.shape[0], one_ref.shape[0]
+    units = out_ref.shape[0]
     core = core_ref[0]
     for chip in range(chips):
         whole[pl.ds((2 * chip + core) * share, share)] = mine_ref[chip]
         whole[pl.ds((2 * chip + 1 - core) * share, share)] = theirs_ref[chip]
     out_ref[...] = whole[0:units]
     low_ref[...] = whole[0:units].astype(BF16)
-    write_edges(
-        row_ref[0], whole[0:edge].astype(BF16), whole[units - edge : units].astype(BF16), one_ref, two_ref
-    )
     plan_copy.wait()
     for i in range(items):
         place = item_place(slots, i)
-        made_ref[i] = multi_rows(
+        made = multi_rows(
             fields, width, plan_ref[place], plan_ref[place + 1], leaves_ref, low_ref, window_ref.at[i]
-        ).astype(BF16)
+        )
+        made_ref[i, :, : made.shape[1]] = made.astype(BF16)
 
 
 def flat_lines(columns, fields):
@@ -373,16 +375,17 @@
     return columns[:count]
 
 
-def gram_kernel(fields, own_ref, right_ref, image_ref, mine_ref, got_ref, out_ref):
+def gram_kernel(fields, own_ref, right_ref, image_ref, *pieces_and_out):
+    *pieces, out_ref = pieces_and_out
     units = image_ref.shape[0]
-    share = mine_ref.shape[1]
+    share = pieces[0].shape[0]
     totals = None
     for k in range(share):
         unit = own_ref[0] * share + k
         place = jnp.minimum(unit, units - 1)
         r = right_ref[:, pl.ds(pl.multiple_of(place * LANES, LANES), LANES)]
         z = image_ref[place]
-        q = mine_ref[0, k].astype(F32) + got_ref[0, k].astype(F32)
+        q = tree_sum([piece[k].astype(F32) for piece in pieces])
         r = jnp.where(unit < units, r, 0.0)
         z = jnp.where(unit < units, z, 0.0)
         (rr, ri), (zr, zi), (qr, qi) = [(v[:fields], v[fields:]) for v in (r, z, q)]
@@ -472,7 +475,7 @@
     steps_between = range(chips - 1, 0, -1)
     assert group == 2 * chips and chips & (chips - 1) == 0 and LANES % fields == 0
     window_shape = jax.ShapeDtypeStruct((items, width, pad_coefs, 2, LANES), BF16)
-    item_shape = jax.ShapeDtypeStruct((items, fields, 2 * pad_coefs), BF16)
+    item_shape = jax.ShapeDtypeStruct((items, fields, 2 * pad_coefs + ITEM_REST), BF16)
     plan_shape = jax.ShapeDtypeStruct((item_place(slots, items),), jnp.int32)
     part_shape = (share, both, LANES)
 
@@ -484,22 +487,19 @@
     expansions = in_hbm(expansions)
     moves = in_hbm(translations.transpose(0, 2, 1, 3))
     picks = far_pick.transpose(0, 2, 1)
-    edge_shape = jax.ShapeDtypeStruct((both, edge), BF16)
     plan_scratch = [pltpu.SMEM(plan_shape.shape, jnp.int32), pltpu.SemaphoreType.DMA]
 
-    plan, made, windows, leaves, right, one, two = pl.pallas_call(
-        functools.partial(begin_kernel, fields, items, width, send, rows, edge),
+    plan, made, windows, leaves, right = pl.pallas_call(
+        functools.partial(begin_kernel, fields, items, width, send, rows),
         out_shape=(
             plan_shape,
             item_shape,
-            window_shape,
+            pltpu.VMEM(window_shape.shape, BF16),
             jax.ShapeDtypeStruct(leaves.shape, jnp.int32),
             jax.ShapeDtypeStruct((both, panels), F32),
-            edge_shape,
-            edge_shape,
         ),
-        in_specs=[SMEM] * 3 + [HBM] * 8,
-        out_specs=(SMEM,) + (VMEM,) * 6,
+        in_specs=[SMEM] * 2 + [HBM] * 8,
+        out_specs=(SMEM,) + (VMEM,) * 4,
         scratch_shapes=[
             pltpu.SMEM(value.shape, jnp.int32)
             for value in (picks, leaf_of_panel, far_target, far_offset, tile_pairs)
@@ -510,7 +510,6 @@
     )(
         row_place,
         own_place,
-        tile_count,
         in_hbm(picks),
         in_hbm(leaf_of_panel),
         in_hbm(leaves),
@@ -527,66 +526,73 @@
         ]
         return parts[0] if len(parts) == 1 else jnp.concatenate(parts)
 
-    def to_neighbours(one, two):
+    def from_neighbours(image):
+        edge_shape = (both, edge) if image.ndim == 2 else (edge_units, both, LANES)
+        one, two = pl.pallas_call(
+            edge_kernel,
+            out_shape=(jax.ShapeDtypeStruct(edge_shape, BF16),) * 2,
+            in_specs=[SMEM, VMEM],
+            out_specs=(VMEM, VMEM),
+            compiler_params=params(),
+            name="edges",
+        )(row_place, image)
         return [
             lax.ppermute(value, "row", list(enumerate(targets))) for value, targets in zip((one, two), neighbours)
         ]
 
     image_shape = jax.ShapeDtypeStruct((units, both, LANES), F32)
-    near_cost = pl.CostEstimate(
-        flops=8 * fields * near_tiles.size // 2, bytes_accessed=2 * near_tiles.size, transcendentals=0
-    )
-
-    def first_near(one, two, low):
+    target_windows, moved = pl.pallas_call(
+        functools.partial(fetch_kernel, items, width, slots),
+        out_shape=(
+            pltpu.VMEM(window_shape.shape, BF16),
+            pltpu.VMEM((items, 2 * pad_coefs, coefs), BF16),
+        ),
+        in_specs=[ANY, HBM, HBM],
+        out_specs=(VMEM, VMEM),
+        scratch_shapes=plan_scratch
+        + [
+            pltpu.VMEM((items, coefs, 2, coefs), BF16),
+            pltpu.SemaphoreType.DMA((items, width)),
+            pltpu.SemaphoreType.DMA((items,)),
+        ],
+        compiler_params=params(24),
+        cost_estimate=pl.CostEstimate(flops=0, bytes_accessed=6 * window_shape.size, transcendentals=0),
+        name="fetch",
+    )(plan, expansions, moves)
+
+    def far(taken):
         return pl.pallas_call(
-            functools.partial(first_near_kernel, fields, items, width),
-            out_shape=(
-                image_shape,
-                window_shape,
-                jax.ShapeDtypeStruct((items, 2 * pad_coefs, coefs), BF16),
-                jax.ShapeDtypeStruct((coefs, 2 * pad_coefs), BF16),
+            functools.partial(far_kernel, fields, items, width, slots),
+            out_shape=jax.ShapeDtypeStruct((items, width, both, LANES), F32),
+            in_specs=[ANY] + [VMEM] * 4,
+            out_specs=VMEM,
+            scratch_shapes=plan_scratch,
+            compiler_params=params(),
+            name="far",
+        )(plan, leaves, taken, moved, target_windows)
+
+    def core_parts(image, one, two, low, dtype):
+        half_shape = jax.ShapeDtypeStruct((chips, *part_shape), dtype)
+        keep, give = pl.pallas_call(
+            functools.partial(near_kernel, fields, units),
+            out_shape=(half_shape, half_shape),
+            in_specs=[SMEM, SMEM, SMEM, ANY] + [VMEM] * 5,
+            out_specs=(VMEM, VMEM),
+            scratch_shapes=[
+                pltpu.VMEM((units + 2 * edge_units, both, LANES), low.dtype),
+                pltpu.VMEM((share * group, both, LANES), F32),
+            ]
+            + plan_scratch,
+            compiler_params=params(),
+            cost_estimate=pl.CostEstimate(
+                flops=8 * fields * near_tiles.size // 2, bytes_accessed=2 * near_tiles.size, transcendentals=0
             ),
-            in_specs=[SMEM, ANY] + [HBM] * 2 + [VMEM] * 4,
-            out_specs=(VMEM, VMEM, VMEM, VMEM),
-            scratch_shapes=[pltpu.VMEM((units + 2 * edge_units, both, LANES), low.dtype)]
-            + plan_scratch
-            + [
-                pltpu.VMEM((items, coefs, 2, coefs), BF16),
-                pltpu.SemaphoreType.DMA((items, width)),
-                pltpu.SemaphoreType.DMA((items,)),
-            ],
-            compiler_params=params(24),
-            cost_estimate=near_cost,
-            name="first_near",
-        )(row_place, plan, expansions, moves, one, two, low, near_tiles)
-
-    def near(one, two, low):
-        return pl.pallas_call(
-            functools.partial(near_kernel, fields),
-            out_shape=image_shape,
-            in_specs=[SMEM, ANY, VMEM, VMEM, VMEM, VMEM],
-            out_specs=VMEM,
-            scratch_shapes=[pltpu.VMEM((units + 2 * edge_units, both, LANES), low.dtype)] + plan_scratch,
-            compiler_params=params(),
-            cost_estimate=near_cost,
             name="near",
-        )(row_place, plan, one, two, low, near_tiles)
+        )(core_place, row_place, tile_count, plan, image, one, two, low, near_tiles)
+        return keep, swapped(give, 1)
 
     def swapped(value, step):
         return lax.ppermute(value, GROUP, [(g, g ^ step) for g in range(group)])
-
-    def core_parts(taken, partial, dtype):
-        half_shape = jax.ShapeDtypeStruct((chips, *part_shape), dtype)
-        keep, give = pl.pallas_call(
-            functools.partial(far_kernel, fields, items, width, slots),
-            out_shape=(half_shape, half_shape),
-            in_specs=[SMEM, ANY] + [VMEM] * 6,
-            out_specs=(VMEM, VMEM),
-            scratch_shapes=[pltpu.VMEM((share * group, both, LANES), F32)] + plan_scratch,
-            compiler_params=params(),
-            name="far",
-        )(core_place, plan, leaves, taken, partial, moved, spread, target_windows)
-        return keep, swapped(give, 1)
 
     def whole_sum(keep, got):
         pair = pl.pallas_call(
@@ -608,51 +614,43 @@
         )(pair, *[arrived[step] for step in range(1, chips)])
         theirs = swapped(mine, 1)
         low_shape = jax.ShapeDtypeStruct((units, both, LANES), BF16)
-        low_edge = jax.ShapeDtypeStruct((edge_units, both, LANES), BF16)
         return pl.pallas_call(
             functools.partial(assemble_kernel, fields, items, width, slots),
-            out_shape=(image_shape, low_shape, low_edge, low_edge, item_shape),
-            in_specs=[SMEM, SMEM, ANY] + [VMEM] * 4,
-            out_specs=(VMEM,) * 5,
+            out_shape=(image_shape, low_shape, item_shape),
+            in_specs=[SMEM, ANY] + [VMEM] * 4,
+            out_specs=(VMEM,) * 3,
             scratch_shapes=[pltpu.VMEM((share * group, both, LANES), F32)] + plan_scratch,
             compiler_params=params(),
             name="assemble",
-        )(core_place, row_place, plan, leaves, mine, theirs, windows)
-
-    def own_share(keep, got):
-        pieces = chips
-        for level in range(chips.bit_length() - 1):
-            pieces //= 2
-            keep, give = pl.pallas_call(
-                functools.partial(halve_kernel, level),
-                out_shape=(
-                    jax.ShapeDtypeStruct((pieces, *part_shape), F32),
-                    jax.ShapeDtypeStruct((pieces, *part_shape), BF16),
-                ),
-                in_specs=[SMEM, VMEM, VMEM],
-                out_specs=(VMEM, VMEM),
-                compiler_params=params(),
-                name="halve",
-            )(chip_place, keep, got)
-            got = swapped(give, 2 << level)
-        return keep, got
-
-    taken = exchanged(made)
-    partial, target_windows, moved, spread = first_near(*to_neighbours(one, two), right)
-    z_all, z_low, one, two, made = whole_sum(*core_parts(taken, partial, F32))
-    taken = exchanged(made)
-    partial = near(*to_neighbours(one, two), z_low)
-    keep, got = own_share(*core_parts(taken, partial, BF16))
+        )(core_place, plan, leaves, mine, theirs, windows)
+
+    def share_pieces(keep, got):
+        pieces = pl.pallas_call(
+            fold_kernel,
+            out_shape=(jax.ShapeDtypeStruct(part_shape, F32),)
+            + (jax.ShapeDtypeStruct(part_shape, BF16),) * (chips - 1),
+            in_specs=[SMEM, VMEM, VMEM],
+            out_specs=(VMEM,) * chips,
+            compiler_params=params(),
+            name="fold",
+        )(chip_place, keep, got)
+        arrived = {step: swapped(pieces[step], 2 * step) for step in steps_between}
+        return [pieces[0]] + [arrived[step] for step in range(1, chips)]
+
+    image = far(exchanged(made))
+    z_all, z_low, made = whole_sum(*core_parts(image, *from_neighbours(right), right, F32))
+    image = far(exchanged(made))
+    pieces = share_pieces(*core_parts(image, *from_neighbours(z_low), z_low, BF16))
 
     lines = -(-9 * fields // LANES)
     sums = pl.pallas_call(
         functools.partial(gram_kernel, fields),
         out_shape=jax.ShapeDtypeStruct((group * rows, lines, LANES), F32),
-        in_specs=[SMEM] + [VMEM] * 4,
+        in_specs=[SMEM] + [VMEM] * (2 + chips),
         out_specs=VMEM,
         compiler_params=params(),
         name="gram",
-    )(own_place, right, z_all, keep, got)
+    )(own_place, right, z_all, *pieces)
     sums = lax.all_to_all(sums, EVERY, 0, 0, tiled=True)
     out = pl.pallas_call(
         functools.partial(final_kernel, fields),

time: 64.7 us -> 60.9 us (0.941)
  blocking collectives: 12.8 us -> 9.99 us
  starting transfers between devices: 17.9 us -> 19.1 us
  Pallas kernels: 12.6 us -> 11.6 us
  local copies, waits for them, and re-layouts: 0.87 us -> 0.01 us
    ppermute x4, starting transfers between devices: 7.01 us -> 10.5 us  [from_neighbours(): lax.ppermute(value, 'row', list(enumerate(targets)))]
    all_to_all x1, blocking collectives: 12.8 us -> 9.99 us  [local(): sums = lax.all_to_all(sums, EVERY, 0, 0, tiled=True)]
    ppermute x8 -> x9, starting transfers between devices: 9.54 us -> 7.32 us  [swapped(): return lax.ppermute(value, GROUP, [(g, g ^ step) for g in range(group)])]
    ppermute x8 -> x9, waiting for transfers between devices: 13 us -> 11.8 us  [swapped(): return lax.ppermute(value, GROUP, [(g, g ^ step) for g in range(group)])]
    pallas_call x6 -> x8, Pallas kernels: 7.23 us -> 6.22 us  [the longest x2 2.66 us: core_parts(): pl.pallas_call(functools.partial(near_kernel, fields, units), out_shape=(...]
    ppermute x4, waiting for transfers between devices: 6.24 us -> 7.21 us  [from_neighbours(): lax.ppermute(value, 'row', list(enumerate(targets)))]
    unnamed x6 -> x2, local copies, waits for them, and re-layouts: 0.87 us -> 0.01 us
  transfers between devices with their start and end apart: 14 -> 15, of which waited for: 11 -> 12; matrix products, arithmetic and copies ran while one was open for 0% -> 0% of each run, Pallas kernels for 6% -> 6%
where the time goes in v5:
time: 60.9 us; the launch traced here: 60.6 us
  starting transfers between devices  19.1 us (31%)
  waiting for transfers between devices  19 us (31%)
  Pallas kernels  11.6 us (19%)
  blocking collectives  9.99 us (16%)
  between operations  0.82 us (1%)
    ppermute x9, waiting for transfers between devices, swapped(): return lax.ppermute(value, GROUP, [(g, g ^ step) for g in range(group)])  11.8 us
    ppermute x4, starting transfers between devices, from_neighbours(): lax.ppermute(value, 'row', list(enumerate(targets)))  10.5 us
    all_to_all x1, blocking collectives, local(): sums = lax.all_to_all(sums, EVERY, 0, 0, tiled=True)  9.99 us
    ppermute x9, starting transfers between devices, swapped(): return lax.ppermute(value, GROUP, [(g, g ^ step) for g in range(group)])  7.32 us
    ppermute x4, waiting for transfers between devices, from_neighbours(): lax.ppermute(value, 'row', list(enumerate(targets)))  7.21 us
    pallas_call x1, Pallas kernels, local(): pl.pallas_call(functools.partial(begin_kernel, fields, items, width, send...  2.83 us
    pallas_call x2, Pallas kernels, core_parts(): pl.pallas_call(functools.partial(near_kernel, fields, units), out_shape=(...  2.66 us
    pallas_call x1, Pallas kernels, local(): pl.pallas_call(functools.partial(fetch_kernel, items, width, slots), out_...  2.18 us
  transfers between devices with their start and end apart: 15, of which 12 were waited for; matrix products, arithmetic and copies ran while one was open for 0% of the time, Pallas kernels for 6%

profile of v5, /device:TPU:0, one launch (start us, length us, event | category | flops | bytes accessed | tf_op | source)
XLA Modules:
  0.0 60.6 jit_solution(16301717495166482691)
XLA Ops:
  0.0 2.8 %begin.1 = (s32[13]{0:T(128)S(1)}, bf16[1,16,1152]{2,1,0:T(8,128)(2,1)S(1)}, bf16[1,3,448,2,128]{4,3,2,1,0:T(2,128)(2,1)S(1)}, s32[24,1,128]{2,1,0:T(1,128)S(1)}, f32[32,3072]{1,0:T(8,128)S(1)}) custom-call(s32[1]{0:T(128)} %bitcast.1.row_ref, s32[1]{0:T(128)} %bitcast.own_ref, s32[4,2,4]{2,1,0:T(2,128)} %bitcast.19, s32[1,3072]{1,0:T(1,128)} %leaf_hbm.1, ...), custom_call_target="tpu_custom_call" | custom-call | tf_op jit(solution)/shard_map/begin/pallas_call | solution.py:492
  2.8 0.7 %collective-permute-start = (bf16[1,16,1152]{2,1,0:T(8,128)(2,1)S(1)}, bf16[1,16,1152]{2,1,0:T(8,128)(2,1)S(1)}, u32[]{:S(2)}, u32[]{:S(2)}) collective-permute-start(bf16[1,16,1152]{2,1,0:T(8,128)(2,1)S(1)} %get-tuple-element.30), channel_id=1, source_target_pairs={{0,0},{1,1},{2,6},{3,7},{16,24},{17,25},{18,30},{19,31},{4,12},{5,... | collective-permute-start | bytes 110600 | tf_op jit(solution)/shard_map/ppermute | solution.py:525
  3.5 6.9 %collective-permute-start.1 = (bf16[32,512]{1,0:T(8,128)(2,1)S(1)}, bf16[32,512]{1,0:T(8,128)(2,1)S(1)}, u32[]{:S(2)}, u32[]{:S(2)}) collective-permute-start(bf16[32,512]{1,0:T(8,128)(2,1)S(1)} %get-tuple-element.33), channel_id=1, source_target_pairs={{0,4},{4,0},{8,12},{12,8},{1,5},{5,1},{9,13},{13,9},{2,6},{6,2},{1... | collective-permute-start | bytes 98312 | tf_op jit(solution)/shard_map/ppermute | solution.py:540
  11.1 2.2 %fetch.1 = (bf16[1,3,448,2,128]{4,3,2,1,0:T(2,128)(2,1)S(1)}, bf16[1,896,441]{2,1,0:T(8,128)(2,1)S(1)}) custom-call(s32[13]{0:T(128)S(1)} %get-tuple-element.28.plan_any, bf16[441,24,2,128]{3,2,1,0:T(2,128)(2,1)} %bitcast.15, bf16[4,441,2,441]{3,2,1,0:T(2,128)(2,1)} %bitcast.16), custom_call_target="tpu_custom_call" | custom-call | bytes 2064384 | tf_op jit(solution)/shard_map/fetch/pallas_call | solution.py:544
  13.3 0.7 %far.2.image_ref = f32[1,3,32,128]{3,2,1,0:T(8,128)S(1)} custom-call(s32[13]{0:T(128)S(1)} %get-tuple-element.28.plan_any, s32[24,1,128]{2,1,0:T(1,128)S(1)} %get-tuple-element.29.leaves_ref, bf16[1,16,1152]{2,1,0:T(8,128)(2,1)S(1)} %collective-permute-done.item_ref, bf16[1,896,441]{2,1,0:T(8,128)(2,1)S(1)} %get-tuple-element.31.trans_ref, ...), custom_call_target="tpu_custom_call" | custom-call | tf_op jit(solution)/shard_map/far/pallas_call | solution.py:564
  14.0 2.2 %collective-permute-done.2.two_ref = bf16[32,512]{1,0:T(8,128)(2,1)S(1)} collective-permute-done((bf16[32,512]{1,0:T(8,128)(2,1)S(1)}, bf16[32,512]{1,0:T(8,128)(2,1)S(1)}, u32[]{:S(2)}, u32[]{:S(2)}) %collective-permute-start.2) | collective-permute-done | bytes 32800 | tf_op jit(solution)/shard_map/ppermute | solution.py:540
  16.2 1.3 %near.2 = (f32[4,3,32,128]{3,2,1,0:T(8,128)S(1)}, f32[4,3,32,128]{3,2,1,0:T(8,128)S(1)}) custom-call(s32[1]{0:T(128)} %bitcast.8.core_ref, s32[1]{0:T(128)} %bitcast.1.row_ref, s32[1]{0:T(128)S(6)} %copy.11.count_ref, s32[13]{0:T(128)S(1)} %get-tuple-element.28.plan_any, f32[1,3,32,128]{3,2,1,0:T(8,128)S(1)} %far.2.image_ref, ...), custom_call_target="tpu_custom_call" | custom-call | flops 67108864 | bytes 2097152 | tf_op jit(solution)/shard_map/near/pallas_call | solution.py:576
  17.6 1.4 %collective-permute-done.3.got_ref = f32[4,3,32,128]{3,2,1,0:T(8,128)S(1)} collective-permute-done((f32[4,3,32,128]{3,2,1,0:T(8,128)S(1)}, f32[4,3,32,128]{3,2,1,0:T(8,128)S(1)}, u32[]{:S(2)}, u32[]{:S(2)}) %collective-permute-start.3) | collective-permute-done | bytes 196640 | tf_op jit(solution)/shard_map/ppermute | solution.py:595
  19.1 2.0 %collective-permute-start.6 = (bf16[4,3,32,128]{3,2,1,0:T(8,128)(2,1)S(1)}, bf16[4,3,32,128]{3,2,1,0:T(8,128)(2,1)S(1)}, u32[]{:S(2)}, u32[]{:S(2)}) collective-permute-start(bf16[4,3,32,128]{3,2,1,0:T(8,128)(2,1)S(1)} %pair.1.refs_0_), channel_id=1, source_target_pairs={{0,18},{1,19},{2,16},{3,17},{16,2},{17,3},{18,0},{19,1},{4,22},{5,... | collective-permute-start | bytes 294920 | tf_op jit(solution)/shard_map/ppermute | solution.py:595
  21.1 0.3 collective-permute-start.5
  21.4 1.2 %collective-permute-start.4 = (bf16[4,3,32,128]{3,2,1,0:T(8,128)(2,1)S(1)}, bf16[4,3,32,128]{3,2,1,0:T(8,128)(2,1)S(1)}, u32[]{:S(2)}, u32[]{:S(2)}) collective-permute-start(bf16[4,3,32,128]{3,2,1,0:T(8,128)(2,1)S(1)} %pair.1.refs_0_), channel_id=1, source_target_pairs={{0,2},{1,3},{2,0},{3,1},{16,18},{17,19},{18,16},{19,17},{4,6},{5,7... | collective-permute-start | bytes 294920 | tf_op jit(solution)/shard_map/ppermute | solution.py:595
  22.6 3.0 %collective-permute-done.6.refs_3_ = bf16[4,3,32,128]{3,2,1,0:T(8,128)(2,1)S(1)} collective-permute-done((bf16[4,3,32,128]{3,2,1,0:T(8,128)(2,1)S(1)}, bf16[4,3,32,128]{3,2,1,0:T(8,128)(2,1)S(1)}, u32[]{:S(2)}, u32[]{:S(2)}) %collective-permute-start.6) | collective-permute-done | bytes 98336 | tf_op jit(solution)/shard_map/ppermute | solution.py:595
  25.7 0.7 %collective-permute-done.5.refs_2_ = bf16[4,3,32,128]{3,2,1,0:T(8,128)(2,1)S(1)} collective-permute-done((bf16[4,3,32,128]{3,2,1,0:T(8,128)(2,1)S(1)}, bf16[4,3,32,128]{3,2,1,0:T(8,128)(2,1)S(1)}, u32[]{:S(2)}, u32[]{:S(2)}) %collective-permute-start.5) | collective-permute-done | bytes 98336 | tf_op jit(solution)/shard_map/ppermute | solution.py:595
  26.3 0.6 %collective-permute-done.4.refs_1_ = bf16[4,3,32,128]{3,2,1,0:T(8,128)(2,1)S(1)} collective-permute-done((bf16[4,3,32,128]{3,2,1,0:T(8,128)(2,1)S(1)}, bf16[4,3,32,128]{3,2,1,0:T(8,128)(2,1)S(1)}, u32[]{:S(2)}, u32[]{:S(2)}) %collective-permute-start.4) | collective-permute-done | bytes 98336 | tf_op jit(solution)/shard_map/ppermute | solution.py:595
  27.1 1.4 %collective-permute-done.7.theirs_ref = f32[4,3,32,128]{3,2,1,0:T(8,128)S(1)} collective-permute-done((f32[4,3,32,128]{3,2,1,0:T(8,128)S(1)}, f32[4,3,32,128]{3,2,1,0:T(8,128)S(1)}, u32[]{:S(2)}, u32[]{:S(2)}) %collective-permute-start.7) | collective-permute-done | bytes 196640 | tf_op jit(solution)/shard_map/ppermute | solution.py:595
  28.5 1.1 %assemble.1 = (f32[24,32,128]{2,1,0:T(8,128)S(1)}, bf16[24,32,128]{2,1,0:T(8,128)(2,1)S(1)}, bf16[1,16,1152]{2,1,0:T(8,128)(2,1)S(1)}) custom-call(s32[1]{0:T(128)} %bitcast.8.core_ref, s32[13]{0:T(128)S(1)} %get-tuple-element.28.plan_any, s32[24,1,128]{2,1,0:T(1,128)S(1)} %get-tuple-element.29.leaves_ref, f32[4,3,32,128]{3,2,1,0:T(8,128)S(1)} %close.1.mine_ref, ...), custom_call_target="tpu_custom_call" | custom-call | tf_op jit(solution)/shard_map/assemble/pallas_call | solution.py:617
  29.6 0.7 %collective-permute-start.8 = (bf16[1,16,1152]{2,1,0:T(8,128)(2,1)S(1)}, bf16[1,16,1152]{2,1,0:T(8,128)(2,1)S(1)}, u32[]{:S(2)}, u32[]{:S(2)}) collective-permute-start(bf16[1,16,1152]{2,1,0:T(8,128)(2,1)S(1)} %get-tuple-element.39), channel_id=1, source_target_pairs={{0,0},{1,1},{2,6},{3,7},{16,24},{17,25},{18,30},{19,31},{4,12},{5,... | collective-permute-start | bytes 110600 | tf_op jit(solution)/shard_map/ppermute | solution.py:525
  30.3 3.6 %collective-permute-start.9 = (bf16[4,32,128]{2,1,0:T(8,128)(2,1)S(1)}, bf16[4,32,128]{2,1,0:T(8,128)(2,1)S(1)}, u32[]{:S(2)}, u32[]{:S(2)}) collective-permute-start(bf16[4,32,128]{2,1,0:T(8,128)(2,1)S(1)} %get-tuple-element.41), channel_id=1, source_target_pairs={{0,4},{4,0},{8,12},{12,8},{1,5},{5,1},{9,13},{13,9},{2,6},{6,2},{1... | collective-permute-start | bytes 98312 | tf_op jit(solution)/shard_map/ppermute | solution.py:540
  33.9 0.7 %far.3.image_ref = f32[1,3,32,128]{3,2,1,0:T(8,128)S(1)} custom-call(s32[13]{0:T(128)S(1)} %get-tuple-element.28.plan_any, s32[24,1,128]{2,1,0:T(1,128)S(1)} %get-tuple-element.29.leaves_ref, bf16[1,16,1152]{2,1,0:T(8,128)(2,1)S(1)} %collective-permute-done.8.item_ref, bf16[1,896,441]{2,1,0:T(8,128)(2,1)S(1)} %get-tuple-element.31.trans_ref, ...), custom_call_target="tpu_custom_call" | custom-call | tf_op jit(solution)/shard_map/far/pallas_call | solution.py:564
  34.5 1.2 %collective-permute-done.9.one_ref = bf16[4,32,128]{2,1,0:T(8,128)(2,1)S(1)} collective-permute-done((bf16[4,32,128]{2,1,0:T(8,128)(2,1)S(1)}, bf16[4,32,128]{2,1,0:T(8,128)(2,1)S(1)}, u32[]{:S(2)}, u32[]{:S(2)}) %collective-permute-start.9) | collective-permute-done | bytes 32800 | tf_op jit(solution)/shard_map/ppermute | solution.py:540
  35.8 3.8 %collective-permute-done.10.two_ref = bf16[4,32,128]{2,1,0:T(8,128)(2,1)S(1)} collective-permute-done((bf16[4,32,128]{2,1,0:T(8,128)(2,1)S(1)}, bf16[4,32,128]{2,1,0:T(8,128)(2,1)S(1)}, u32[]{:S(2)}, u32[]{:S(2)}) %collective-permute-start.10) | collective-permute-done | bytes 32800 | tf_op jit(solution)/shard_map/ppermute | solution.py:540
  39.6 1.3 %near.3 = (bf16[4,3,32,128]{3,2,1,0:T(8,128)(2,1)S(1)}, bf16[4,3,32,128]{3,2,1,0:T(8,128)(2,1)S(1)}) custom-call(s32[1]{0:T(128)} %bitcast.8.core_ref, s32[1]{0:T(128)} %bitcast.1.row_ref, s32[1]{0:T(128)S(6)} %copy.11.count_ref, s32[13]{0:T(128)S(1)} %get-tuple-element.28.plan_any, f32[1,3,32,128]{3,2,1,0:T(8,128)S(1)} %far.3.image_ref, ...), custom_call_target="tpu_custom_call" | custom-call | flops 67108864 | bytes 2097152 | tf_op jit(solution)/shard_map/near/pallas_call | solution.py:576
  41.0 1.3 %collective-permute-done.11.got_ref = bf16[4,3,32,128]{3,2,1,0:T(8,128)(2,1)S(1)} collective-permute-done((bf16[4,3,32,128]{3,2,1,0:T(8,128)(2,1)S(1)}, bf16[4,3,32,128]{3,2,1,0:T(8,128)(2,1)S(1)}, u32[]{:S(2)}, u32[]{:S(2)}) %collective-permute-start.11) | collective-permute-done | bytes 98336 | tf_op jit(solution)/shard_map/ppermute | solution.py:595
  42.3 0.7 %collective-permute-start.12 = (bf16[3,32,128]{2,1,0:T(8,128)(2,1)S(1)}, bf16[3,32,128]{2,1,0:T(8,128)(2,1)S(1)}, u32[]{:S(2)}, u32[]{:S(2)}) collective-permute-start(bf16[3,32,128]{2,1,0:T(8,128)(2,1)S(1)} %get-tuple-element.46), channel_id=1, source_target_pairs={{0,2},{1,3},{2,0},{3,1},{16,18},{17,19},{18,16},{19,17},{4,6},{5,7... | collective-permute-start | bytes 73736 | tf_op jit(solution)/shard_map/ppermute | solution.py:595
  43.0 1.5 %collective-permute-start.13 = (bf16[3,32,128]{2,1,0:T(8,128)(2,1)S(1)}, bf16[3,32,128]{2,1,0:T(8,128)(2,1)S(1)}, u32[]{:S(2)}, u32[]{:S(2)}) collective-permute-start(bf16[3,32,128]{2,1,0:T(8,128)(2,1)S(1)} %get-tuple-element.47), channel_id=1, source_target_pairs={{0,16},{1,17},{2,18},{3,19},{16,0},{17,1},{18,2},{19,3},{4,20},{5,... | collective-permute-start | bytes 73736 | tf_op jit(solution)/shard_map/ppermute | solution.py:595
  44.5 1.4 %collective-permute-start.14 = (bf16[3,32,128]{2,1,0:T(8,128)(2,1)S(1)}, bf16[3,32,128]{2,1,0:T(8,128)(2,1)S(1)}, u32[]{:S(2)}, u32[]{:S(2)}) collective-permute-start(bf16[3,32,128]{2,1,0:T(8,128)(2,1)S(1)} %get-tuple-element.48), channel_id=1, source_target_pairs={{0,18},{1,19},{2,16},{3,17},{16,2},{17,3},{18,0},{19,1},{4,22},{5,... | collective-permute-start | bytes 73736 | tf_op jit(solution)/shard_map/ppermute | solution.py:595
  45.9 0.3 collective-permute-done.12.pieces_and_out_1_
  46.2 0.8 %collective-permute-done.13.pieces_and_out_2_ = bf16[3,32,128]{2,1,0:T(8,128)(2,1)S(1)} collective-permute-done((bf16[3,32,128]{2,1,0:T(8,128)(2,1)S(1)}, bf16[3,32,128]{2,1,0:T(8,128)(2,1)S(1)}, u32[]{:S(2)}, u32[]{:S(2)}) %collective-permute-start.13) | collective-permute-done | bytes 24608 | tf_op jit(solution)/shard_map/ppermute | solution.py:595
  47.0 2.2 %collective-permute-done.14.pieces_and_out_3_ = bf16[3,32,128]{2,1,0:T(8,128)(2,1)S(1)} collective-permute-done((bf16[3,32,128]{2,1,0:T(8,128)(2,1)S(1)}, bf16[3,32,128]{2,1,0:T(8,128)(2,1)S(1)}, u32[]{:S(2)}, u32[]{:S(2)}) %collective-permute-start.14) | collective-permute-done | bytes 24608 | tf_op jit(solution)/shard_map/ppermute | solution.py:595
  49.2 0.3 gram.1
  49.5 10.0 %all_to_all.5.sums_ref = f32[32,2,128]{2,1,0:T(2,128)S(1)} all-to-all(f32[32,2,128]{2,1,0:T(2,128)S(1)} %gram.1), channel_id=1, replica_groups=mesh['grp'=2,'row'=4,'col'=4] {'grp','row','col'}, dimensions={0} | all-to-all | bytes 65536 | tf_op jit(solution)/shard_map/all_to_all | solution.py:654
  59.5 1.1 %combine.1 = f32[32,3072]{1,0:T(8,128)} custom-call(f32[32,2,128]{2,1,0:T(2,128)S(1)} %all_to_all.5.sums_ref, f32[32,3072]{1,0:T(8,128)S(1)} %get-tuple-element.27.image_ref.here_ref.right_ref, f32[24,32,128]{2,1,0:T(8,128)S(1)} %get-tuple-element.38.image_ref), custom_call_target="tpu_custom_call" | custom-call | tf_op jit(solution)/shard_map/combine/pallas_call | solution.py:655
  (15 shorter events, 0.4 us)
Async XLA Ops:
  2.8 10.5 %collective-permute-start = (bf16[1,16,1152]{2,1,0:T(8,128)(2,1)S(1)}, bf16[1,16,1152]{2,1,0:T(8,128)(2,1)S(1)}, u32[]{:S(2)}, u32[]{:S(2)}) collective-permute-start(bf16[1,16,1152]{2,1,0:T(8,128)(2,1)S(1)} %get-tuple-element.30), channel_id=1, source_target_pairs={{0,0},{1,1},{2,6},{3,7},{16,24},{17,25},{18,30},{19,31},{4,12},{5,... | collective-permute-start | bytes 110600 | tf_op jit(solution)/shard_map/ppermute | solution.py:525
  3.5 10.5 %collective-permute-start.1 = (bf16[32,512]{1,0:T(8,128)(2,1)S(1)}, bf16[32,512]{1,0:T(8,128)(2,1)S(1)}, u32[]{:S(2)}, u32[]{:S(2)}) collective-permute-start(bf16[32,512]{1,0:T(8,128)(2,1)S(1)} %get-tuple-element.33), channel_id=1, source_target_pairs={{0,4},{4,0},{8,12},{12,8},{1,5},{5,1},{9,13},{13,9},{2,6},{6,2},{1... | collective-permute-start | bytes 98312 | tf_op jit(solution)/shard_map/ppermute | solution.py:540
  10.5 5.7 %collective-permute-start.2 = (bf16[32,512]{1,0:T(8,128)(2,1)S(1)}, bf16[32,512]{1,0:T(8,128)(2,1)S(1)}, u32[]{:S(2)}, u32[]{:S(2)}) collective-permute-start(bf16[32,512]{1,0:T(8,128)(2,1)S(1)} %get-tuple-element.34), channel_id=1, source_target_pairs={{0,12},{4,8},{8,4},{12,0},{1,13},{5,9},{9,5},{13,1},{2,14},{6,10},... | collective-permute-start | bytes 98312 | tf_op jit(solution)/shard_map/ppermute | solution.py:540
  11.1 5.1 %copy-start = (bf16[2,8,256,256]{3,2,1,0:T(8,128)(2,1)S(1)}, bf16[2,8,256,256]{3,2,1,0:T(8,128)(2,1)}, u32[]{:S(2)}) copy-start(bf16[2,8,256,256]{3,2,1,0:T(8,128)(2,1)} %tiles_ref.3) | copy-start | bytes 6291460
  17.5 1.5 %collective-permute-start.3 = (f32[4,3,32,128]{3,2,1,0:T(8,128)S(1)}, f32[4,3,32,128]{3,2,1,0:T(8,128)S(1)}, u32[]{:S(2)}, u32[]{:S(2)}) collective-permute-start(f32[4,3,32,128]{3,2,1,0:T(8,128)S(1)} %get-tuple-element.36), channel_id=1, source_target_pairs={{0,1},{1,0},{2,3},{3,2},{16,17},{17,16},{18,19},{19,18},{4,5},{5,4... | collective-permute-start | bytes 589832 | tf_op jit(solution)/shard_map/ppermute | solution.py:595
  19.1 6.6 %collective-permute-start.6 = (bf16[4,3,32,128]{3,2,1,0:T(8,128)(2,1)S(1)}, bf16[4,3,32,128]{3,2,1,0:T(8,128)(2,1)S(1)}, u32[]{:S(2)}, u32[]{:S(2)}) collective-permute-start(bf16[4,3,32,128]{3,2,1,0:T(8,128)(2,1)S(1)} %pair.1.refs_0_), channel_id=1, source_target_pairs={{0,18},{1,19},{2,16},{3,17},{16,2},{17,3},{18,0},{19,1},{4,22},{5,... | collective-permute-start | bytes 294920 | tf_op jit(solution)/shard_map/ppermute | solution.py:595
  21.1 5.3 %collective-permute-start.5 = (bf16[4,3,32,128]{3,2,1,0:T(8,128)(2,1)S(1)}, bf16[4,3,32,128]{3,2,1,0:T(8,128)(2,1)S(1)}, u32[]{:S(2)}, u32[]{:S(2)}) collective-permute-start(bf16[4,3,32,128]{3,2,1,0:T(8,128)(2,1)S(1)} %pair.1.refs_0_), channel_id=1, source_target_pairs={{0,16},{1,17},{2,18},{3,19},{16,0},{17,1},{18,2},{19,3},{4,20},{5,... | collective-permute-start | bytes 294920 | tf_op jit(solution)/shard_map/ppermute | solution.py:595
  21.4 5.5 %collective-permute-start.4 = (bf16[4,3,32,128]{3,2,1,0:T(8,128)(2,1)S(1)}, bf16[4,3,32,128]{3,2,1,0:T(8,128)(2,1)S(1)}, u32[]{:S(2)}, u32[]{:S(2)}) collective-permute-start(bf16[4,3,32,128]{3,2,1,0:T(8,128)(2,1)S(1)} %pair.1.refs_0_), channel_id=1, source_target_pairs={{0,2},{1,3},{2,0},{3,1},{16,18},{17,19},{18,16},{19,17},{4,6},{5,7... | collective-permute-start | bytes 294920 | tf_op jit(solution)/shard_map/ppermute | solution.py:595
  27.0 1.5 %collective-permute-start.7 = (f32[4,3,32,128]{3,2,1,0:T(8,128)S(1)}, f32[4,3,32,128]{3,2,1,0:T(8,128)S(1)}, u32[]{:S(2)}, u32[]{:S(2)}) collective-permute-start(f32[4,3,32,128]{3,2,1,0:T(8,128)S(1)} %close.1.mine_ref), channel_id=1, source_target_pairs={{0,1},{1,0},{2,3},{3,2},{16,17},{17,16},{18,19},{19,18},{4,5},{5,4... | collective-permute-start | bytes 589832 | tf_op jit(solution)/shard_map/ppermute | solution.py:595
  29.6 4.3 %collective-permute-start.8 = (bf16[1,16,1152]{2,1,0:T(8,128)(2,1)S(1)}, bf16[1,16,1152]{2,1,0:T(8,128)(2,1)S(1)}, u32[]{:S(2)}, u32[]{:S(2)}) collective-permute-start(bf16[1,16,1152]{2,1,0:T(8,128)(2,1)S(1)} %get-tuple-element.39), channel_id=1, source_target_pairs={{0,0},{1,1},{2,6},{3,7},{16,24},{17,25},{18,30},{19,31},{4,12},{5,... | collective-permute-start | bytes 110600 | tf_op jit(solution)/shard_map/ppermute | solution.py:525
  30.3 5.4 %collective-permute-start.9 = (bf16[4,32,128]{2,1,0:T(8,128)(2,1)S(1)}, bf16[4,32,128]{2,1,0:T(8,128)(2,1)S(1)}, u32[]{:S(2)}, u32[]{:S(2)}) collective-permute-start(bf16[4,32,128]{2,1,0:T(8,128)(2,1)S(1)} %get-tuple-element.41), channel_id=1, source_target_pairs={{0,4},{4,0},{8,12},{12,8},{1,5},{5,1},{9,13},{13,9},{2,6},{6,2},{1... | collective-permute-start | bytes 98312 | tf_op jit(solution)/shard_map/ppermute | solution.py:540
  33.9 5.7 %collective-permute-start.10 = (bf16[4,32,128]{2,1,0:T(8,128)(2,1)S(1)}, bf16[4,32,128]{2,1,0:T(8,128)(2,1)S(1)}, u32[]{:S(2)}, u32[]{:S(2)}) collective-permute-start(bf16[4,32,128]{2,1,0:T(8,128)(2,1)S(1)} %get-tuple-element.42), channel_id=1, source_target_pairs={{0,12},{4,8},{8,4},{12,0},{1,13},{5,9},{9,5},{13,1},{2,14},{6,10},... | collective-permute-start | bytes 98312 | tf_op jit(solution)/shard_map/ppermute | solution.py:540
  40.9 1.4 %collective-permute-start.11 = (bf16[4,3,32,128]{3,2,1,0:T(8,128)(2,1)S(1)}, bf16[4,3,32,128]{3,2,1,0:T(8,128)(2,1)S(1)}, u32[]{:S(2)}, u32[]{:S(2)}) collective-permute-start(bf16[4,3,32,128]{3,2,1,0:T(8,128)(2,1)S(1)} %get-tuple-element.44), channel_id=1, source_target_pairs={{0,1},{1,0},{2,3},{3,2},{16,17},{17,16},{18,19},{19,18},{4,5},{5,4... | collective-permute-start | bytes 294920 | tf_op jit(solution)/shard_map/ppermute | solution.py:595
  42.3 3.9 %collective-permute-start.12 = (bf16[3,32,128]{2,1,0:T(8,128)(2,1)S(1)}, bf16[3,32,128]{2,1,0:T(8,128)(2,1)S(1)}, u32[]{:S(2)}, u32[]{:S(2)}) collective-permute-start(bf16[3,32,128]{2,1,0:T(8,128)(2,1)S(1)} %get-tuple-element.46), channel_id=1, source_target_pairs={{0,2},{1,3},{2,0},{3,1},{16,18},{17,19},{18,16},{19,17},{4,6},{5,7... | collective-permute-start | bytes 73736 | tf_op jit(solution)/shard_map/ppermute | solution.py:595
  43.0 4.0 %collective-permute-start.13 = (bf16[3,32,128]{2,1,0:T(8,128)(2,1)S(1)}, bf16[3,32,128]{2,1,0:T(8,128)(2,1)S(1)}, u32[]{:S(2)}, u32[]{:S(2)}) collective-permute-start(bf16[3,32,128]{2,1,0:T(8,128)(2,1)S(1)} %get-tuple-element.47), channel_id=1, source_target_pairs={{0,16},{1,17},{2,18},{3,19},{16,0},{17,1},{18,2},{19,3},{4,20},{5,... | collective-permute-start | bytes 73736 | tf_op jit(solution)/shard_map/ppermute | solution.py:595
  44.5 4.7 %collective-permute-start.14 = (bf16[3,32,128]{2,1,0:T(8,128)(2,1)S(1)}, bf16[3,32,128]{2,1,0:T(8,128)(2,1)S(1)}, u32[]{:S(2)}, u32[]{:S(2)}) collective-permute-start(bf16[3,32,128]{2,1,0:T(8,128)(2,1)S(1)} %get-tuple-element.48), channel_id=1, source_target_pairs={{0,18},{1,19},{2,16},{3,17},{16,2},{17,3},{18,0},{19,1},{4,22},{5,... | collective-permute-start | bytes 73736 | tf_op jit(solution)/shard_map/ppermute | solution.py:595

commit v6 on v5

--- a/solution.py
+++ b/solution.py
@@ -14,7 +14,7 @@
 GROUP = ("grp", "col")
 CODES = 0
 PER_ITEM = 5
-ITEM_REST = 2 * LANES
+PIECES = 4
 EVERY = ("grp", "row", "col")
 
 F32 = jnp.float32
@@ -22,7 +22,6 @@
 SMEM = pl.BlockSpec(memory_space=pltpu.SMEM)
 VMEM = pl.BlockSpec(memory_space=pltpu.VMEM)
 HBM = pl.BlockSpec(memory_space=pltpu.HBM)
-ANY = pl.BlockSpec(memory_space=pl.ANY)
 
 
 def dot_nn(left, right):
@@ -88,10 +87,15 @@
 
 def window_copies(exp_ref, unit, window_ref, sem, width):
     coefs = exp_ref.shape[0]
-    return [
-        pltpu.make_async_copy(exp_ref.at[:, unit + k], window_ref.at[k, pl.ds(0, coefs)], sem.at[k])
-        for k in range(width)
-    ]
+    step = -(-coefs // PIECES)
+    copies = []
+    for k in range(width):
+        for p in range(PIECES):
+            part = pl.ds(p * step, min(step, coefs - p * step))
+            copies.append(
+                pltpu.make_async_copy(exp_ref.at[part, unit + k], window_ref.at[k, part], sem.at[k, p])
+            )
+    return copies
 
 
 def clear_rest(window_ref, coefs, width):
@@ -169,12 +173,17 @@
     loads[1].wait()
     row = row_ref[0]
 
-    def partner(i):
+    def partner(i, coming):
         number = own * items + i
-        return lax.rem(lax.div(number, send) - row + rows, rows), lax.rem(number, send)
-
-    for i in range(items):
-        other, number = partner(i)
+        pair, number = lax.div(number, send), lax.rem(number, send)
+        if not is_power(rows):
+            return lax.rem(pair - row + rows, rows), number
+        if coming and items == 1 and send == 2:
+            number = jnp.where(pair == 0, 1 - number, number)
+        return lax.bitwise_xor(pair, row), number
+
+    for i in range(items):
+        other, number = partner(i, False)
         leaf = pick_ref[other, number, row]
         unit = window_start(leaf_ref, leaf, width)
         place = item_place(slots, i)
@@ -187,7 +196,7 @@
         plan_ref[CODES + s] = pairs_ref[s]
     for i in range(items):
         place = item_place(slots, i)
-        other, number = partner(i)
+        other, number = partner(i, True)
         leaf = target_ref[0, other * send + number]
         plan_ref[place + 2], plan_ref[place + 3] = leaf, window_start(leaf_ref, leaf, width)
         plan_ref[place + 4] = offset_ref[0, other * send + number]
@@ -196,17 +205,13 @@
         leaf, unit = plan_ref[place], plan_ref[place + 1]
         for copy in window_copies(exp_ref, unit, window_ref.at[i], window_sem.at[i], width):
             copy.wait()
-        made = multi_rows(fields, width, leaf, unit, leaves_ref, right_ref, window_ref.at[i])
-        out_ref[i, :, : made.shape[1]] = made.astype(BF16)
-
-
-def fetch_kernel(items, width, slots, plan_any, exp_ref, trans_ref, window_ref, moved_ref, plan_ref, plan_sem, trans_buf, sem, trans_sem):
-    plan_copy = pltpu.make_async_copy(plan_any, plan_ref, plan_sem)
-    plan_copy.start()
+        out_ref[i] = multi_rows(fields, width, leaf, unit, leaves_ref, right_ref, window_ref.at[i]).astype(BF16)
+
+
+def fetch_kernel(items, width, slots, plan_ref, exp_ref, trans_ref, window_ref, moved_ref, trans_buf, sem, trans_sem):
     coefs = trans_ref.shape[3]
     for i in range(items):
         clear_rest(window_ref.at[i], coefs, width)
-    plan_copy.wait()
 
     def trans_copy(i):
         offset = plan_ref[item_place(slots, i) + 4]
@@ -248,21 +253,12 @@
 
 
 def near_kernel(
-    fields, units, core_ref, row_ref, count_ref, plan_any, image_ref, one_ref, two_ref, here_ref, tiles_ref,
-    keep_ref, give_ref, ext, total, plan_ref, plan_sem,
+    fields, row_ref, count_ref, plan_ref, one_ref, two_ref, here_ref, tiles_ref, out_ref, ext
 ):
-    plan_copy = pltpu.make_async_copy(plan_any, plan_ref, plan_sem)
-    plan_copy.start()
-    near_sources(row_ref, one_ref, two_ref, here_ref, units, ext)
-    total[...] = jnp.zeros_like(total)
+    near_sources(row_ref, one_ref, two_ref, here_ref, out_ref.shape[0], ext)
+    out_ref[...] = jnp.zeros_like(out_ref)
     slots, tile = tiles_ref.shape[1], tiles_ref.shape[2]
     per = tile // LANES
-    plan_copy.wait()
-    items, width = image_ref.shape[:2]
-    for i in range(items):
-        unit = plan_ref[item_place(slots, i) + 3]
-        for k in range(width):
-            total[unit + k] += image_ref[i, k]
     for s in range(slots):
         code = plan_ref[CODES + s]
         target = lax.div(code, SPAN)
@@ -275,22 +271,19 @@
         )
         value = jnp.where(s < count_ref[0], value, 0.0)
         for k in range(per):
-            total[target * per + k] += value[:, k * LANES : (k + 1) * LANES]
-    chips, share = keep_ref.shape[:2]
-    core = core_ref[0]
-    for c in range(chips):
-        keep_ref[c] = total[pl.ds((2 * c + core) * share, share)].astype(keep_ref.dtype)
-        give_ref[c] = total[pl.ds((2 * c + 1 - core) * share, share)].astype(give_ref.dtype)
+            out_ref[target * per + k] += value[:, k * LANES : (k + 1) * LANES]
 
 
 def far_kernel(
-    fields, items, width, slots, plan_any, leaves_ref, item_ref, trans_ref, window_ref, image_ref, plan_ref, plan_sem
+    fields, items, width, slots, core_ref, plan_ref, leaves_ref, partial_ref, item_ref, trans_ref, window_ref,
+    keep_ref, give_ref, total,
 ):
-    plan_copy = pltpu.make_async_copy(plan_any, plan_ref, plan_sem)
-    plan_copy.start()
-    images = []
-    for i in range(items):
-        plain = item_ref[i, :, : trans_ref.shape[1]].astype(F32)
+    units = partial_ref.shape[0]
+    total[0:units] = partial_ref[...]
+    if total.shape[0] > units:
+        total[units:] = jnp.zeros((total.shape[0] - units, *total.shape[1:]), F32)
+    for i in range(items):
+        plain = item_ref[i].astype(F32)
         odd = odd_lanes(plain.shape)
         turned = jnp.where(odd, from_left(plain), -from_right(plain))
         rows = jnp.concatenate([plain, turned], axis=0).astype(BF16)
@@ -301,14 +294,17 @@
             [jnp.where(odd, -local_imag, local_real), jnp.where(odd, local_real, local_imag)], axis=0
         ).astype(BF16)
         expansions = jnp.concatenate([as_rows(window_ref.at[i, k]) for k in range(width)], axis=-1)
-        images.append(dot_nn(rows, expansions))
-    plan_copy.wait()
-    for i in range(items):
         place = item_place(slots, i)
-        mask = window_mask(leaves_ref, plan_ref[place + 2], plan_ref[place + 3], 2 * fields, width)
-        image = jnp.where(mask, images[i], 0.0)
+        leaf, unit = plan_ref[place + 2], plan_ref[place + 3]
+        mask = window_mask(leaves_ref, leaf, unit, 2 * fields, width)
+        image = jnp.where(mask, dot_nn(rows, expansions), 0.0)
         for k in range(width):
-            image_ref[i, k] = image[:, k * LANES : (k + 1) * LANES]
+            total[unit + k] += image[:, k * LANES : (k + 1) * LANES]
+    chips, share = keep_ref.shape[:2]
+    core = core_ref[0]
+    for c in range(chips):
+        keep_ref[c] = total[pl.ds((2 * c + core) * share, share)].astype(keep_ref.dtype)
+        give_ref[c] = total[pl.ds((2 * c + 1 - core) * share, share)].astype(give_ref.dtype)
 
 
 def fold_kernel(chip_ref, keep_ref, got_ref, own_ref, *out_refs):
@@ -332,11 +328,9 @@
 
 
 def assemble_kernel(
-    fields, items, width, slots, core_ref, plan_any, leaves_ref, mine_ref, theirs_ref, window_ref,
-    out_ref, low_ref, made_ref, whole, plan_ref, plan_sem,
+    fields, items, width, slots, core_ref, plan_ref, leaves_ref, mine_ref, theirs_ref, window_ref,
+    out_ref, low_ref, made_ref, whole,
 ):
-    plan_copy = pltpu.make_async_copy(plan_any, plan_ref, plan_sem)
-    plan_copy.start()
     chips, share = mine_ref.shape[:2]
     units = out_ref.shape[0]
     core = core_ref[0]
@@ -345,13 +339,11 @@
         whole[pl.ds((2 * chip + 1 - core) * share, share)] = theirs_ref[chip]
     out_ref[...] = whole[0:units]
     low_ref[...] = whole[0:units].astype(BF16)
-    plan_copy.wait()
     for i in range(items):
         place = item_place(slots, i)
-        made = multi_rows(
+        made_ref[i] = multi_rows(
             fields, width, plan_ref[place], plan_ref[place + 1], leaves_ref, low_ref, window_ref.at[i]
-        )
-        made_ref[i, :, : made.shape[1]] = made.astype(BF16)
+        ).astype(BF16)
 
 
 def flat_lines(columns, fields):
@@ -423,17 +415,26 @@
     return pltpu.CompilerParams(vmem_limit_bytes=mebibytes * 1024 * 1024)
 
 
+def is_power(count):
+    return count & (count - 1) == 0
+
+
 def item_route(rows, group, columns, send):
     items = rows * send // group
 
     def flat(r, g):
         return (g // columns * rows + r) * columns + g % columns
+
+    def target(r, g, pair):
+        if not is_power(rows):
+            return flat((pair - r) % rows, g)
+        return flat(r ^ pair, g ^ 1 if pair == 0 and items == 1 and send == 2 else g)
 
     assert items * group == rows * send and (items % send == 0 or send % items == 0)
     routes = []
     for first in range(0, items, send):
-        numbers = [(g * items + first) // send for g in range(group)]
-        routes.append([(flat(r, g), flat((numbers[g] - r) % rows, g)) for r in range(rows) for g in range(group)])
+        pairs = [(g * items + first) // send for g in range(group)]
+        routes.append([(flat(r, g), target(r, g, pairs[g])) for r in range(rows) for g in range(group)])
     return items, routes
 
 
@@ -475,8 +476,7 @@
     steps_between = range(chips - 1, 0, -1)
     assert group == 2 * chips and chips & (chips - 1) == 0 and LANES % fields == 0
     window_shape = jax.ShapeDtypeStruct((items, width, pad_coefs, 2, LANES), BF16)
-    item_shape = jax.ShapeDtypeStruct((items, fields, 2 * pad_coefs + ITEM_REST), BF16)
-    plan_shape = jax.ShapeDtypeStruct((item_place(slots, items),), jnp.int32)
+    item_shape = jax.ShapeDtypeStruct((items, fields, 2 * pad_coefs), BF16)
     part_shape = (share, both, LANES)
 
     def in_hbm(value):
@@ -487,12 +487,11 @@
     expansions = in_hbm(expansions)
     moves = in_hbm(translations.transpose(0, 2, 1, 3))
     picks = far_pick.transpose(0, 2, 1)
-    plan_scratch = [pltpu.SMEM(plan_shape.shape, jnp.int32), pltpu.SemaphoreType.DMA]
 
     plan, made, windows, leaves, right = pl.pallas_call(
         functools.partial(begin_kernel, fields, items, width, send, rows),
         out_shape=(
-            plan_shape,
+            pltpu.SMEM((item_place(slots, items),), jnp.int32),
             item_shape,
             pltpu.VMEM(window_shape.shape, BF16),
             jax.ShapeDtypeStruct(leaves.shape, jnp.int32),
@@ -504,7 +503,7 @@
             pltpu.SMEM(value.shape, jnp.int32)
             for value in (picks, leaf_of_panel, far_target, far_offset, tile_pairs)
         ]
-        + [pltpu.SemaphoreType.DMA((7,)), pltpu.SemaphoreType.DMA((items, width))],
+        + [pltpu.SemaphoreType.DMA((7,)), pltpu.SemaphoreType.DMA((items, width, PIECES))],
         compiler_params=params(),
         name="begin",
     )(
@@ -547,12 +546,11 @@
             pltpu.VMEM(window_shape.shape, BF16),
             pltpu.VMEM((items, 2 * pad_coefs, coefs), BF16),
         ),
-        in_specs=[ANY, HBM, HBM],
+        in_specs=[SMEM, HBM, HBM],
         out_specs=(VMEM, VMEM),
-        scratch_shapes=plan_scratch
-        + [
+        scratch_shapes=[
             pltpu.VMEM((items, coefs, 2, coefs), BF16),
-            pltpu.SemaphoreType.DMA((items, width)),
+            pltpu.SemaphoreType.DMA((items, width, PIECES)),
             pltpu.SemaphoreType.DMA((items,)),
         ],
         compiler_params=params(24),
@@ -560,39 +558,35 @@
         name="fetch",
     )(plan, expansions, moves)
 
-    def far(taken):
+    def swapped(value, step):
+        return lax.ppermute(value, GROUP, [(g, g ^ step) for g in range(group)])
+
+    def near(one, two, low):
         return pl.pallas_call(
-            functools.partial(far_kernel, fields, items, width, slots),
-            out_shape=jax.ShapeDtypeStruct((items, width, both, LANES), F32),
-            in_specs=[ANY] + [VMEM] * 4,
+            functools.partial(near_kernel, fields),
+            out_shape=image_shape,
+            in_specs=[SMEM] * 3 + [VMEM] * 4,
             out_specs=VMEM,
-            scratch_shapes=plan_scratch,
-            compiler_params=params(),
-            name="far",
-        )(plan, leaves, taken, moved, target_windows)
-
-    def core_parts(image, one, two, low, dtype):
-        half_shape = jax.ShapeDtypeStruct((chips, *part_shape), dtype)
-        keep, give = pl.pallas_call(
-            functools.partial(near_kernel, fields, units),
-            out_shape=(half_shape, half_shape),
-            in_specs=[SMEM, SMEM, SMEM, ANY] + [VMEM] * 5,
-            out_specs=(VMEM, VMEM),
-            scratch_shapes=[
-                pltpu.VMEM((units + 2 * edge_units, both, LANES), low.dtype),
-                pltpu.VMEM((share * group, both, LANES), F32),
-            ]
-            + plan_scratch,
+            scratch_shapes=[pltpu.VMEM((units + 2 * edge_units, both, LANES), low.dtype)],
             compiler_params=params(),
             cost_estimate=pl.CostEstimate(
                 flops=8 * fields * near_tiles.size // 2, bytes_accessed=2 * near_tiles.size, transcendentals=0
             ),
             name="near",
-        )(core_place, row_place, tile_count, plan, image, one, two, low, near_tiles)
+        )(row_place, tile_count, plan, one, two, low, near_tiles)
+
+    def core_parts(partial, taken, dtype):
+        half_shape = jax.ShapeDtypeStruct((chips, *part_shape), dtype)
+        keep, give = pl.pallas_call(
+            functools.partial(far_kernel, fields, items, width, slots),
+            out_shape=(half_shape, half_shape),
+            in_specs=[SMEM, SMEM] + [VMEM] * 5,
+            out_specs=(VMEM, VMEM),
+            scratch_shapes=[pltpu.VMEM((share * group, both, LANES), F32)],
+            compiler_params=params(),
+            name="far",
+        )(core_place, plan, leaves, partial, taken, moved, target_windows)
         return keep, swapped(give, 1)
-
-    def swapped(value, step):
-        return lax.ppermute(value, GROUP, [(g, g ^ step) for g in range(group)])
 
     def whole_sum(keep, got):
         pair = pl.pallas_call(
@@ -617,9 +611,9 @@
         return pl.pallas_call(
             functools.partial(assemble_kernel, fields, items, width, slots),
             out_shape=(image_shape, low_shape, item_shape),
-            in_specs=[SMEM, ANY] + [VMEM] * 4,
+            in_specs=[SMEM, SMEM] + [VMEM] * 4,
             out_specs=(VMEM,) * 3,
-            scratch_shapes=[pltpu.VMEM((share * group, both, LANES), F32)] + plan_scratch,
+            scratch_shapes=[pltpu.VMEM((share * group, both, LANES), F32)],
             compiler_params=params(),
             name="assemble",
         )(core_place, plan, leaves, mine, theirs, windows)
@@ -635,12 +629,12 @@
             name="fold",
         )(chip_place, keep, got)
         arrived = {step: swapped(pieces[step], 2 * step) for step in steps_between}
-        return [pieces[0]] + [arrived[step] for step in range(1, chips)]
-
-    image = far(exchanged(made))
-    z_all, z_low, made = whole_sum(*core_parts(image, *from_neighbours(right), right, F32))
-    image = far(exchanged(made))
-    pieces = share_pieces(*core_parts(image, *from_neighbours(z_low), z_low, BF16))
+        return [pieces[0]] + [arrived[step] for step in steps_between]
+
+    partial = near(*from_neighbours(right), right)
+    z_all, z_low, made = whole_sum(*core_parts(partial, exchanged(made), F32))
+    partial = near(*from_neighbours(z_low), z_low)
+    pieces = share_pieces(*core_parts(partial, exchanged(made), BF16))
 
     lines = -(-9 * fields // LANES)
     sums = pl.pallas_call(

time: 60.9 us -> 54.9 us (0.901)
  waiting for transfers between devices: 19 us -> 16.4 us
  starting transfers between devices: 19.1 us -> 16.9 us
  Pallas kernels: 11.6 us -> 9.65 us
  blocking collectives: 9.99 us -> 10.9 us
    ppermute x4, starting transfers between devices: 10.5 us -> 7.55 us  [from_neighbours(): lax.ppermute(value, 'row', list(enumerate(targets)))]
    ppermute x4, waiting for transfers between devices: 7.21 us -> 4.7 us  [from_neighbours(): lax.ppermute(value, 'row', list(enumerate(targets)))]
    ppermute x9, starting transfers between devices: 7.32 us -> 9.36 us  [swapped(): return lax.ppermute(value, GROUP, [(g, g ^ step) for g in range(group)])]
    ppermute x2, starting transfers between devices: 1.33 us -> 0.01 us  [exchanged(): lax.ppermute(made[k * send:k * send + min(send, items)], EVERY, route)]
    pallas_call x4, Pallas kernels: 3.98 us -> 2.79 us  [the longest x2 1.48 us: near(): pl.pallas_call(functools.partial(near_kernel, fields), out_shape=image_sh...]
    all_to_all x1, blocking collectives: 9.99 us -> 10.9 us  [local(): sums = lax.all_to_all(sums, EVERY, 0, 0, tiled=True)]
  transfers between devices with their start and end apart: 15 -> 15, of which waited for: 12 -> 11; matrix products, arithmetic and copies ran while one was open for 0% -> 0% of each run, Pallas kernels for 6% -> 6%
where the time goes in v6:
time: 54.9 us; the launch traced here: 54.7 us
  starting transfers between devices  16.9 us (31%)
  waiting for transfers between devices  16.4 us (30%)
  blocking collectives  10.9 us (20%)
  Pallas kernels  9.65 us (18%)
  between operations  0.8 us (1%)
    ppermute x9, waiting for transfers between devices, swapped(): return lax.ppermute(value, GROUP, [(g, g ^ step) for g in range(group)])  11.7 us
    all_to_all x1, blocking collectives, local(): sums = lax.all_to_all(sums, EVERY, 0, 0, tiled=True)  10.9 us
    ppermute x9, starting transfers between devices, swapped(): return lax.ppermute(value, GROUP, [(g, g ^ step) for g in range(group)])  9.36 us
    ppermute x4, starting transfers between devices, from_neighbours(): lax.ppermute(value, 'row', list(enumerate(targets)))  7.55 us
    ppermute x4, waiting for transfers between devices, from_neighbours(): lax.ppermute(value, 'row', list(enumerate(targets)))  4.7 us
    pallas_call x1, Pallas kernels, local(): pl.pallas_call(functools.partial(begin_kernel, fields, items, width, send...  2.79 us
    pallas_call x1, Pallas kernels, local(): pl.pallas_call(functools.partial(fetch_kernel, items, width, slots), out_...  1.94 us
    pallas_call x2, Pallas kernels, near(): pl.pallas_call(functools.partial(near_kernel, fields), out_shape=image_sh...  1.48 us
  transfers between devices with their start and end apart: 15, of which 11 were waited for; matrix products, arithmetic and copies ran while one was open for 0% of the time, Pallas kernels for 6%

profile of v6, /device:TPU:0, one launch (start us, length us, event | category | flops | bytes accessed | tf_op | source)
XLA Modules:
  0.0 54.7 jit_solution(8209988587628561586)
XLA Ops:
  0.0 2.8 %begin.1 = (s32[13]{0:T(128)S(4)}, bf16[1,16,896]{2,1,0:T(8,128)(2,1)S(1)}, bf16[1,3,448,2,128]{4,3,2,1,0:T(2,128)(2,1)S(1)}, s32[24,1,128]{2,1,0:T(1,128)S(1)}, f32[32,3072]{1,0:T(8,128)S(1)}) custom-call(s32[1]{0:T(128)} %bitcast.1.row_ref, s32[1]{0:T(128)} %bitcast.own_ref, s32[4,2,4]{2,1,0:T(2,128)} %bitcast.19, s32[1,3072]{1,0:T(1,128)} %leaf_hbm.1, ...), custom_call_target="tpu_custom_call" | custom-call | tf_op jit(solution)/shard_map/begin/pallas_call | solution.py:491
  2.8 3.1 %collective-permute-start = (bf16[32,512]{1,0:T(8,128)(2,1)S(1)}, bf16[32,512]{1,0:T(8,128)(2,1)S(1)}, u32[]{:S(2)}, u32[]{:S(2)}) collective-permute-start(bf16[32,512]{1,0:T(8,128)(2,1)S(1)} %get-tuple-element.30), channel_id=1, source_target_pairs={{0,4},{4,0},{8,12},{12,8},{1,5},{5,1},{9,13},{13,9},{2,6},{6,2},{1... | collective-permute-start | bytes 98312 | tf_op jit(solution)/shard_map/ppermute | solution.py:539
  5.9 2.5 %collective-permute-start.1 = (bf16[32,512]{1,0:T(8,128)(2,1)S(1)}, bf16[32,512]{1,0:T(8,128)(2,1)S(1)}, u32[]{:S(2)}, u32[]{:S(2)}) collective-permute-start(bf16[32,512]{1,0:T(8,128)(2,1)S(1)} %get-tuple-element.31), channel_id=1, source_target_pairs={{0,12},{4,8},{8,4},{12,0},{1,13},{5,9},{9,5},{13,1},{2,14},{6,10},... | collective-permute-start | bytes 98312 | tf_op jit(solution)/shard_map/ppermute | solution.py:539
  9.1 1.9 %fetch.1 = (bf16[1,3,448,2,128]{4,3,2,1,0:T(2,128)(2,1)S(1)}, bf16[1,896,441]{2,1,0:T(8,128)(2,1)S(1)}) custom-call(s32[13]{0:T(128)S(4)} %get-tuple-element.28.plan_ref, bf16[441,24,2,128]{3,2,1,0:T(2,128)(2,1)} %bitcast.15, bf16[4,441,2,441]{3,2,1,0:T(2,128)(2,1)} %bitcast.16), custom_call_target="tpu_custom_call" | custom-call | bytes 2064384 | tf_op jit(solution)/shard_map/fetch/pallas_call | solution.py:543
  11.0 0.6 %collective-permute-done.1.two_ref = bf16[32,512]{1,0:T(8,128)(2,1)S(1)} collective-permute-done((bf16[32,512]{1,0:T(8,128)(2,1)S(1)}, bf16[32,512]{1,0:T(8,128)(2,1)S(1)}, u32[]{:S(2)}, u32[]{:S(2)}) %collective-permute-start.1) | collective-permute-done | bytes 32800 | tf_op jit(solution)/shard_map/ppermute | solution.py:539
  11.6 0.7 %near.2.partial_ref = f32[24,32,128]{2,1,0:T(8,128)S(1)} custom-call(s32[1]{0:T(128)} %bitcast.1.row_ref, s32[1]{0:T(128)S(6)} %copy.11.count_ref, s32[13]{0:T(128)S(4)} %get-tuple-element.28.plan_ref, bf16[32,512]{1,0:T(8,128)(2,1)S(1)} %collective-permute-done.one_ref, bf16[32,512]{1,0:T(8,128)(2,1)S(1)} %collective-permute-done.1.two_ref, ...), custom_call_target="tpu_custom_call" | custom-call | flops 67108864 | bytes 2097152 | tf_op jit(solution)/shard_map/near/pallas_call | solution.py:565
  12.4 0.7 %far.2 = (f32[4,3,32,128]{3,2,1,0:T(8,128)S(1)}, f32[4,3,32,128]{3,2,1,0:T(8,128)S(1)}) custom-call(s32[1]{0:T(128)} %bitcast.8.core_ref, s32[13]{0:T(128)S(4)} %get-tuple-element.28.plan_ref, s32[24,1,128]{2,1,0:T(1,128)S(1)} %get-tuple-element.29.leaves_ref, f32[24,32,128]{2,1,0:T(8,128)S(1)} %near.2.partial_ref, ...), custom_call_target="tpu_custom_call" | custom-call | tf_op jit(solution)/shard_map/far/pallas_call | solution.py:580
  13.1 0.2 collective-permute-start.3
  13.3 1.3 %collective-permute-done.3.got_ref = f32[4,3,32,128]{3,2,1,0:T(8,128)S(1)} collective-permute-done((f32[4,3,32,128]{3,2,1,0:T(8,128)S(1)}, f32[4,3,32,128]{3,2,1,0:T(8,128)S(1)}, u32[]{:S(2)}, u32[]{:S(2)}) %collective-permute-start.3) | collective-permute-done | bytes 196640 | tf_op jit(solution)/shard_map/ppermute | solution.py:562
  14.6 4.2 %collective-permute-start.6 = (bf16[4,3,32,128]{3,2,1,0:T(8,128)(2,1)S(1)}, bf16[4,3,32,128]{3,2,1,0:T(8,128)(2,1)S(1)}, u32[]{:S(2)}, u32[]{:S(2)}) collective-permute-start(bf16[4,3,32,128]{3,2,1,0:T(8,128)(2,1)S(1)} %pair.1.refs_0_), channel_id=1, source_target_pairs={{0,18},{1,19},{2,16},{3,17},{16,2},{17,3},{18,0},{19,1},{4,22},{5,... | collective-permute-start | bytes 294920 | tf_op jit(solution)/shard_map/ppermute | solution.py:562
  18.8 0.6 %collective-permute-start.4 = (bf16[4,3,32,128]{3,2,1,0:T(8,128)(2,1)S(1)}, bf16[4,3,32,128]{3,2,1,0:T(8,128)(2,1)S(1)}, u32[]{:S(2)}, u32[]{:S(2)}) collective-permute-start(bf16[4,3,32,128]{3,2,1,0:T(8,128)(2,1)S(1)} %pair.1.refs_0_), channel_id=1, source_target_pairs={{0,2},{1,3},{2,0},{3,1},{16,18},{17,19},{18,16},{19,17},{4,6},{5,7... | collective-permute-start | bytes 294920 | tf_op jit(solution)/shard_map/ppermute | solution.py:562
  19.4 2.9 %collective-permute-done.6.refs_3_ = bf16[4,3,32,128]{3,2,1,0:T(8,128)(2,1)S(1)} collective-permute-done((bf16[4,3,32,128]{3,2,1,0:T(8,128)(2,1)S(1)}, bf16[4,3,32,128]{3,2,1,0:T(8,128)(2,1)S(1)}, u32[]{:S(2)}, u32[]{:S(2)}) %collective-permute-start.6) | collective-permute-done | bytes 98336 | tf_op jit(solution)/shard_map/ppermute | solution.py:562
  22.4 1.0 %collective-permute-done.5.refs_2_ = bf16[4,3,32,128]{3,2,1,0:T(8,128)(2,1)S(1)} collective-permute-done((bf16[4,3,32,128]{3,2,1,0:T(8,128)(2,1)S(1)}, bf16[4,3,32,128]{3,2,1,0:T(8,128)(2,1)S(1)}, u32[]{:S(2)}, u32[]{:S(2)}) %collective-permute-start.5) | collective-permute-done | bytes 98336 | tf_op jit(solution)/shard_map/ppermute | solution.py:562
  23.4 0.6 %collective-permute-done.4.refs_1_ = bf16[4,3,32,128]{3,2,1,0:T(8,128)(2,1)S(1)} collective-permute-done((bf16[4,3,32,128]{3,2,1,0:T(8,128)(2,1)S(1)}, bf16[4,3,32,128]{3,2,1,0:T(8,128)(2,1)S(1)}, u32[]{:S(2)}, u32[]{:S(2)}) %collective-permute-start.4) | collective-permute-done | bytes 98336 | tf_op jit(solution)/shard_map/ppermute | solution.py:562
  24.0 0.1 collective-permute-start.7
  24.1 1.4 %collective-permute-done.7.theirs_ref = f32[4,3,32,128]{3,2,1,0:T(8,128)S(1)} collective-permute-done((f32[4,3,32,128]{3,2,1,0:T(8,128)S(1)}, f32[4,3,32,128]{3,2,1,0:T(8,128)S(1)}, u32[]{:S(2)}, u32[]{:S(2)}) %collective-permute-start.7) | collective-permute-done | bytes 196640 | tf_op jit(solution)/shard_map/ppermute | solution.py:562
  25.5 0.6 %assemble.1 = (f32[24,32,128]{2,1,0:T(8,128)S(1)}, bf16[24,32,128]{2,1,0:T(8,128)(2,1)S(1)}, bf16[1,16,896]{2,1,0:T(8,128)(2,1)S(1)}) custom-call(s32[1]{0:T(128)} %bitcast.8.core_ref, s32[13]{0:T(128)S(4)} %get-tuple-element.28.plan_ref, s32[24,1,128]{2,1,0:T(1,128)S(1)} %get-tuple-element.29.leaves_ref, f32[4,3,32,128]{3,2,1,0:T(8,128)S(1)} %close.1.mine_ref, ...), custom_call_target="tpu_custom_call" | custom-call | tf_op jit(solution)/shard_map/assemble/pallas_call | solution.py:611
  26.1 0.4 collective-permute-start.8
  26.5 1.6 %collective-permute-start.9 = (bf16[4,32,128]{2,1,0:T(8,128)(2,1)S(1)}, bf16[4,32,128]{2,1,0:T(8,128)(2,1)S(1)}, u32[]{:S(2)}, u32[]{:S(2)}) collective-permute-start(bf16[4,32,128]{2,1,0:T(8,128)(2,1)S(1)} %get-tuple-element.41), channel_id=1, source_target_pairs={{0,12},{4,8},{8,4},{12,0},{1,13},{5,9},{9,5},{13,1},{2,14},{6,10},... | collective-permute-start | bytes 98312 | tf_op jit(solution)/shard_map/ppermute | solution.py:539
  28.1 2.0 %collective-permute-done.8.one_ref = bf16[4,32,128]{2,1,0:T(8,128)(2,1)S(1)} collective-permute-done((bf16[4,32,128]{2,1,0:T(8,128)(2,1)S(1)}, bf16[4,32,128]{2,1,0:T(8,128)(2,1)S(1)}, u32[]{:S(2)}, u32[]{:S(2)}) %collective-permute-start.8) | collective-permute-done | bytes 32800 | tf_op jit(solution)/shard_map/ppermute | solution.py:539
  30.1 2.1 %collective-permute-done.9.two_ref = bf16[4,32,128]{2,1,0:T(8,128)(2,1)S(1)} collective-permute-done((bf16[4,32,128]{2,1,0:T(8,128)(2,1)S(1)}, bf16[4,32,128]{2,1,0:T(8,128)(2,1)S(1)}, u32[]{:S(2)}, u32[]{:S(2)}) %collective-permute-start.9) | collective-permute-done | bytes 32800 | tf_op jit(solution)/shard_map/ppermute | solution.py:539
  32.2 0.7 %near.3.partial_ref = f32[24,32,128]{2,1,0:T(8,128)S(1)} custom-call(s32[1]{0:T(128)} %bitcast.1.row_ref, s32[1]{0:T(128)S(6)} %copy.11.count_ref, s32[13]{0:T(128)S(4)} %get-tuple-element.28.plan_ref, bf16[4,32,128]{2,1,0:T(8,128)(2,1)S(1)} %collective-permute-done.8.one_ref, bf16[4,32,128]{2,1,0:T(8,128)(2,1)S(1)} %collective-permute-done.9.two_ref, ...), custom_call_target="tpu_custom_call" | custom-call | flops 67108864 | bytes 2097152 | tf_op jit(solution)/shard_map/near/pallas_call | solution.py:565
  33.0 0.7 %far.3 = (bf16[4,3,32,128]{3,2,1,0:T(8,128)(2,1)S(1)}, bf16[4,3,32,128]{3,2,1,0:T(8,128)(2,1)S(1)}) custom-call(s32[1]{0:T(128)} %bitcast.8.core_ref, s32[13]{0:T(128)S(4)} %get-tuple-element.28.plan_ref, s32[24,1,128]{2,1,0:T(1,128)S(1)} %get-tuple-element.29.leaves_ref, f32[24,32,128]{2,1,0:T(8,128)S(1)} %near.3.partial_ref, ...), custom_call_target="tpu_custom_call" | custom-call | tf_op jit(solution)/shard_map/far/pallas_call | solution.py:580
  33.6 0.1 collective-permute-start.11
  33.7 1.3 %collective-permute-done.11.got_ref = bf16[4,3,32,128]{3,2,1,0:T(8,128)(2,1)S(1)} collective-permute-done((bf16[4,3,32,128]{3,2,1,0:T(8,128)(2,1)S(1)}, bf16[4,3,32,128]{3,2,1,0:T(8,128)(2,1)S(1)}, u32[]{:S(2)}, u32[]{:S(2)}) %collective-permute-start.11) | collective-permute-done | bytes 98336 | tf_op jit(solution)/shard_map/ppermute | solution.py:562
  35.0 3.5 %collective-permute-start.12 = (bf16[3,32,128]{2,1,0:T(8,128)(2,1)S(1)}, bf16[3,32,128]{2,1,0:T(8,128)(2,1)S(1)}, u32[]{:S(2)}, u32[]{:S(2)}) collective-permute-start(bf16[3,32,128]{2,1,0:T(8,128)(2,1)S(1)} %get-tuple-element.46), channel_id=1, source_target_pairs={{0,18},{1,19},{2,16},{3,17},{16,2},{17,3},{18,0},{19,1},{4,22},{5,... | collective-permute-start | bytes 73736 | tf_op jit(solution)/shard_map/ppermute | solution.py:562
  38.6 0.6 %collective-permute-start.14 = (bf16[3,32,128]{2,1,0:T(8,128)(2,1)S(1)}, bf16[3,32,128]{2,1,0:T(8,128)(2,1)S(1)}, u32[]{:S(2)}, u32[]{:S(2)}) collective-permute-start(bf16[3,32,128]{2,1,0:T(8,128)(2,1)S(1)} %get-tuple-element.48), channel_id=1, source_target_pairs={{0,2},{1,3},{2,0},{3,1},{16,18},{17,19},{18,16},{19,17},{4,6},{5,7... | collective-permute-start | bytes 73736 | tf_op jit(solution)/shard_map/ppermute | solution.py:562
  39.2 1.2 %collective-permute-done.12.pieces_and_out_1_ = bf16[3,32,128]{2,1,0:T(8,128)(2,1)S(1)} collective-permute-done((bf16[3,32,128]{2,1,0:T(8,128)(2,1)S(1)}, bf16[3,32,128]{2,1,0:T(8,128)(2,1)S(1)}, u32[]{:S(2)}, u32[]{:S(2)}) %collective-permute-start.12) | collective-permute-done | bytes 24608 | tf_op jit(solution)/shard_map/ppermute | solution.py:562
  40.4 2.0 %collective-permute-done.13.pieces_and_out_2_ = bf16[3,32,128]{2,1,0:T(8,128)(2,1)S(1)} collective-permute-done((bf16[3,32,128]{2,1,0:T(8,128)(2,1)S(1)}, bf16[3,32,128]{2,1,0:T(8,128)(2,1)S(1)}, u32[]{:S(2)}, u32[]{:S(2)}) %collective-permute-start.13) | collective-permute-done | bytes 24608 | tf_op jit(solution)/shard_map/ppermute | solution.py:562
  42.4 0.3 gram.1
  42.7 10.9 %all_to_all.5.sums_ref = f32[32,2,128]{2,1,0:T(2,128)S(1)} all-to-all(f32[32,2,128]{2,1,0:T(2,128)S(1)} %gram.1), channel_id=1, replica_groups=mesh['grp'=2,'row'=4,'col'=4] {'grp','row','col'}, dimensions={0} | all-to-all | bytes 65536 | tf_op jit(solution)/shard_map/all_to_all | solution.py:648
  53.5 1.1 %combine.1 = f32[32,3072]{1,0:T(8,128)} custom-call(f32[32,2,128]{2,1,0:T(2,128)S(1)} %all_to_all.5.sums_ref, f32[32,3072]{1,0:T(8,128)S(1)} %get-tuple-element.27.image_ref.here_ref.right_ref, f32[24,32,128]{2,1,0:T(8,128)S(1)} %get-tuple-element.38.image_ref), custom_call_target="tpu_custom_call" | custom-call | tf_op jit(solution)/shard_map/combine/pallas_call | solution.py:649
  (15 shorter events, 0.2 us)
Async XLA Ops:
  2.8 8.2 %collective-permute-start = (bf16[32,512]{1,0:T(8,128)(2,1)S(1)}, bf16[32,512]{1,0:T(8,128)(2,1)S(1)}, u32[]{:S(2)}, u32[]{:S(2)}) collective-permute-start(bf16[32,512]{1,0:T(8,128)(2,1)S(1)} %get-tuple-element.30), channel_id=1, source_target_pairs={{0,4},{4,0},{8,12},{12,8},{1,5},{5,1},{9,13},{13,9},{2,6},{6,2},{1... | collective-permute-start | bytes 98312 | tf_op jit(solution)/shard_map/ppermute | solution.py:539
  5.9 5.7 %collective-permute-start.1 = (bf16[32,512]{1,0:T(8,128)(2,1)S(1)}, bf16[32,512]{1,0:T(8,128)(2,1)S(1)}, u32[]{:S(2)}, u32[]{:S(2)}) collective-permute-start(bf16[32,512]{1,0:T(8,128)(2,1)S(1)} %get-tuple-element.31), channel_id=1, source_target_pairs={{0,12},{4,8},{8,4},{12,0},{1,13},{5,9},{9,5},{13,1},{2,14},{6,10},... | collective-permute-start | bytes 98312 | tf_op jit(solution)/shard_map/ppermute | solution.py:539
  8.4 4.0 %collective-permute-start.2 = (bf16[1,16,896]{2,1,0:T(8,128)(2,1)S(1)}, bf16[1,16,896]{2,1,0:T(8,128)(2,1)S(1)}, u32[]{:S(2)}, u32[]{:S(2)}) collective-permute-start(bf16[1,16,896]{2,1,0:T(8,128)(2,1)S(1)} %get-tuple-element.32), channel_id=1, source_target_pairs={{0,1},{1,0},{2,6},{3,7},{16,24},{17,25},{18,30},{19,31},{4,5},{5,4... | collective-permute-start | bytes 86024 | tf_op jit(solution)/shard_map/ppermute | solution.py:524
  9.1 2.6 %copy-start = (bf16[2,8,256,256]{3,2,1,0:T(8,128)(2,1)S(1)}, bf16[2,8,256,256]{3,2,1,0:T(8,128)(2,1)}, u32[]{:S(2)}) copy-start(bf16[2,8,256,256]{3,2,1,0:T(8,128)(2,1)} %tiles_ref.3) | copy-start | bytes 6291460
  13.1 1.5 %collective-permute-start.3 = (f32[4,3,32,128]{3,2,1,0:T(8,128)S(1)}, f32[4,3,32,128]{3,2,1,0:T(8,128)S(1)}, u32[]{:S(2)}, u32[]{:S(2)}) collective-permute-start(f32[4,3,32,128]{3,2,1,0:T(8,128)S(1)} %get-tuple-element.36), channel_id=1, source_target_pairs={{0,1},{1,0},{2,3},{3,2},{16,17},{17,16},{18,19},{19,18},{4,5},{5,4... | collective-permute-start | bytes 589832 | tf_op jit(solution)/shard_map/ppermute | solution.py:562
  14.6 7.7 %collective-permute-start.6 = (bf16[4,3,32,128]{3,2,1,0:T(8,128)(2,1)S(1)}, bf16[4,3,32,128]{3,2,1,0:T(8,128)(2,1)S(1)}, u32[]{:S(2)}, u32[]{:S(2)}) collective-permute-start(bf16[4,3,32,128]{3,2,1,0:T(8,128)(2,1)S(1)} %pair.1.refs_0_), channel_id=1, source_target_pairs={{0,18},{1,19},{2,16},{3,17},{16,2},{17,3},{18,0},{19,1},{4,22},{5,... | collective-permute-start | bytes 294920 | tf_op jit(solution)/shard_map/ppermute | solution.py:562
  18.8 4.6 %collective-permute-start.5 = (bf16[4,3,32,128]{3,2,1,0:T(8,128)(2,1)S(1)}, bf16[4,3,32,128]{3,2,1,0:T(8,128)(2,1)S(1)}, u32[]{:S(2)}, u32[]{:S(2)}) collective-permute-start(bf16[4,3,32,128]{3,2,1,0:T(8,128)(2,1)S(1)} %pair.1.refs_0_), channel_id=1, source_target_pairs={{0,16},{1,17},{2,18},{3,19},{16,0},{17,1},{18,2},{19,3},{4,20},{5,... | collective-permute-start | bytes 294920 | tf_op jit(solution)/shard_map/ppermute | solution.py:562
  18.8 5.2 %collective-permute-start.4 = (bf16[4,3,32,128]{3,2,1,0:T(8,128)(2,1)S(1)}, bf16[4,3,32,128]{3,2,1,0:T(8,128)(2,1)S(1)}, u32[]{:S(2)}, u32[]{:S(2)}) collective-permute-start(bf16[4,3,32,128]{3,2,1,0:T(8,128)(2,1)S(1)} %pair.1.refs_0_), channel_id=1, source_target_pairs={{0,2},{1,3},{2,0},{3,1},{16,18},{17,19},{18,16},{19,17},{4,6},{5,7... | collective-permute-start | bytes 294920 | tf_op jit(solution)/shard_map/ppermute | solution.py:562
  24.0 1.5 %collective-permute-start.7 = (f32[4,3,32,128]{3,2,1,0:T(8,128)S(1)}, f32[4,3,32,128]{3,2,1,0:T(8,128)S(1)}, u32[]{:S(2)}, u32[]{:S(2)}) collective-permute-start(f32[4,3,32,128]{3,2,1,0:T(8,128)S(1)} %close.1.mine_ref), channel_id=1, source_target_pairs={{0,1},{1,0},{2,3},{3,2},{16,17},{17,16},{18,19},{19,18},{4,5},{5,4... | collective-permute-start | bytes 589832 | tf_op jit(solution)/shard_map/ppermute | solution.py:562
  26.1 4.0 %collective-permute-start.8 = (bf16[4,32,128]{2,1,0:T(8,128)(2,1)S(1)}, bf16[4,32,128]{2,1,0:T(8,128)(2,1)S(1)}, u32[]{:S(2)}, u32[]{:S(2)}) collective-permute-start(bf16[4,32,128]{2,1,0:T(8,128)(2,1)S(1)} %get-tuple-element.40), channel_id=1, source_target_pairs={{0,4},{4,0},{8,12},{12,8},{1,5},{5,1},{9,13},{13,9},{2,6},{6,2},{1... | collective-permute-start | bytes 98312 | tf_op jit(solution)/shard_map/ppermute | solution.py:539
  26.5 5.7 %collective-permute-start.9 = (bf16[4,32,128]{2,1,0:T(8,128)(2,1)S(1)}, bf16[4,32,128]{2,1,0:T(8,128)(2,1)S(1)}, u32[]{:S(2)}, u32[]{:S(2)}) collective-permute-start(bf16[4,32,128]{2,1,0:T(8,128)(2,1)S(1)} %get-tuple-element.41), channel_id=1, source_target_pairs={{0,12},{4,8},{8,4},{12,0},{1,13},{5,9},{9,5},{13,1},{2,14},{6,10},... | collective-permute-start | bytes 98312 | tf_op jit(solution)/shard_map/ppermute | solution.py:539
  28.1 4.8 %collective-permute-start.10 = (bf16[1,16,896]{2,1,0:T(8,128)(2,1)S(1)}, bf16[1,16,896]{2,1,0:T(8,128)(2,1)S(1)}, u32[]{:S(2)}, u32[]{:S(2)}) collective-permute-start(bf16[1,16,896]{2,1,0:T(8,128)(2,1)S(1)} %get-tuple-element.42), channel_id=1, source_target_pairs={{0,1},{1,0},{2,6},{3,7},{16,24},{17,25},{18,30},{19,31},{4,5},{5,4... | collective-permute-start | bytes 86024 | tf_op jit(solution)/shard_map/ppermute | solution.py:524
  33.6 1.4 %collective-permute-start.11 = (bf16[4,3,32,128]{3,2,1,0:T(8,128)(2,1)S(1)}, bf16[4,3,32,128]{3,2,1,0:T(8,128)(2,1)S(1)}, u32[]{:S(2)}, u32[]{:S(2)}) collective-permute-start(bf16[4,3,32,128]{3,2,1,0:T(8,128)(2,1)S(1)} %get-tuple-element.44), channel_id=1, source_target_pairs={{0,1},{1,0},{2,3},{3,2},{16,17},{17,16},{18,19},{19,18},{4,5},{5,4... | collective-permute-start | bytes 294920 | tf_op jit(solution)/shard_map/ppermute | solution.py:562
  35.0 5.3 %collective-permute-start.12 = (bf16[3,32,128]{2,1,0:T(8,128)(2,1)S(1)}, bf16[3,32,128]{2,1,0:T(8,128)(2,1)S(1)}, u32[]{:S(2)}, u32[]{:S(2)}) collective-permute-start(bf16[3,32,128]{2,1,0:T(8,128)(2,1)S(1)} %get-tuple-element.46), channel_id=1, source_target_pairs={{0,18},{1,19},{2,16},{3,17},{16,2},{17,3},{18,0},{19,1},{4,22},{5,... | collective-permute-start | bytes 73736 | tf_op jit(solution)/shard_map/ppermute | solution.py:562
  38.6 3.8 %collective-permute-start.13 = (bf16[3,32,128]{2,1,0:T(8,128)(2,1)S(1)}, bf16[3,32,128]{2,1,0:T(8,128)(2,1)S(1)}, u32[]{:S(2)}, u32[]{:S(2)}) collective-permute-start(bf16[3,32,128]{2,1,0:T(8,128)(2,1)S(1)} %get-tuple-element.47), channel_id=1, source_target_pairs={{0,16},{1,17},{2,18},{3,19},{16,0},{17,1},{18,2},{19,3},{4,20},{5,... | collective-permute-start | bytes 73736 | tf_op jit(solution)/shard_map/ppermute | solution.py:562
  38.6 3.8 %collective-permute-start.14 = (bf16[3,32,128]{2,1,0:T(8,128)(2,1)S(1)}, bf16[3,32,128]{2,1,0:T(8,128)(2,1)S(1)}, u32[]{:S(2)}, u32[]{:S(2)}) collective-permute-start(bf16[3,32,128]{2,1,0:T(8,128)(2,1)S(1)} %get-tuple-element.48), channel_id=1, source_target_pairs={{0,2},{1,3},{2,0},{3,1},{16,18},{17,19},{18,16},{19,17},{4,6},{5,7... | collective-permute-start | bytes 73736 | tf_op jit(solution)/shard_map/ppermute | solution.py:562

commit v7 on v6

--- a/solution.py
+++ b/solution.py
@@ -13,7 +13,7 @@
 EPSILON = 1e-06
 GROUP = ("grp", "col")
 CODES = 0
-PER_ITEM = 5
+PER_ITEM = 4
 PIECES = 4
 EVERY = ("grp", "row", "col")
 
@@ -145,9 +145,9 @@
 
 def begin_kernel(
     fields, items, width, send, rows, row_ref, own_ref, pick_hbm, leaf_hbm, leaves_hbm,
-    target_hbm, offset_hbm, pairs_hbm, right_hbm, exp_ref,
-    plan_ref, out_ref, window_ref, leaves_ref, right_ref,
-    pick_ref, leaf_ref, target_ref, offset_ref, pairs_ref, sem, window_sem,
+    target_hbm, offset_hbm, pairs_hbm, right_hbm, exp_ref, trans_ref,
+    plan_ref, out_ref, window_ref, target_window_ref, trans_out, leaves_ref, right_ref,
+    pick_ref, leaf_ref, target_ref, offset_ref, pairs_ref, sem, window_sem, target_sem, trans_sem,
 ):
     loads = [
         pltpu.make_async_copy(source, place, sem.at[k])
@@ -176,11 +176,10 @@
     def partner(i, coming):
         number = own * items + i
         pair, number = lax.div(number, send), lax.rem(number, send)
-        if not is_power(rows):
-            return lax.rem(pair - row + rows, rows), number
-        if coming and items == 1 and send == 2:
-            number = jnp.where(pair == 0, 1 - number, number)
-        return lax.bitwise_xor(pair, row), number
+        other = source_row(row, pair, rows) if coming else target_row(row, pair, rows)
+        if coming and own_items_change_cores(rows, items, send):
+            number = jnp.where(other == row, 1 - number, number)
+        return other, number
 
     for i in range(items):
         other, number = partner(i, False)
@@ -192,6 +191,7 @@
             copy.start()
     for load in loads[2:]:
         load.wait()
+    later = []
     for s in range(slots):
         plan_ref[CODES + s] = pairs_ref[s]
     for i in range(items):
@@ -199,39 +199,29 @@
         other, number = partner(i, True)
         leaf = target_ref[0, other * send + number]
         plan_ref[place + 2], plan_ref[place + 3] = leaf, window_start(leaf_ref, leaf, width)
-        plan_ref[place + 4] = offset_ref[0, other * send + number]
+        offset = offset_ref[0, other * send + number]
+        later += window_copies(exp_ref, plan_ref[place + 3], target_window_ref.at[i], target_sem.at[i], width)
+        later.append(pltpu.make_async_copy(trans_ref.at[offset], trans_out.at[i], trans_sem.at[i]))
+    for copy in later:
+        copy.start()
+    for i in range(items):
+        clear_rest(target_window_ref.at[i], exp_ref.shape[0], width)
     for i in range(items):
         place = item_place(slots, i)
         leaf, unit = plan_ref[place], plan_ref[place + 1]
         for copy in window_copies(exp_ref, unit, window_ref.at[i], window_sem.at[i], width):
             copy.wait()
         out_ref[i] = multi_rows(fields, width, leaf, unit, leaves_ref, right_ref, window_ref.at[i]).astype(BF16)
-
-
-def fetch_kernel(items, width, slots, plan_ref, exp_ref, trans_ref, window_ref, moved_ref, trans_buf, sem, trans_sem):
-    coefs = trans_ref.shape[3]
-    for i in range(items):
-        clear_rest(window_ref.at[i], coefs, width)
-
-    def trans_copy(i):
-        offset = plan_ref[item_place(slots, i) + 4]
-        return pltpu.make_async_copy(trans_ref.at[offset], trans_buf.at[i], trans_sem.at[i])
-
-    def exp_copies(i):
-        unit = plan_ref[item_place(slots, i) + 3]
-        return window_copies(exp_ref, unit, window_ref.at[i], sem.at[i], width)
-
-    for i in range(items):
-        trans_copy(i).start()
-        for copy in exp_copies(i):
-            copy.start()
+    for copy in later:
+        copy.wait()
+
+
+def rows_kernel(trans_ref, moved_ref):
+    items, coefs = trans_ref.shape[:2]
     rest = moved_ref.shape[1] - 2 * coefs
     for i in range(items):
-        trans_copy(i).wait()
-        moved_ref[i, pl.ds(0, 2 * coefs)] = trans_buf[i].reshape(2 * coefs, coefs)
+        moved_ref[i, pl.ds(0, 2 * coefs)] = trans_ref[i].reshape(2 * coefs, coefs)
         moved_ref[i, pl.ds(2 * coefs, rest)] = jnp.zeros((rest, coefs), BF16)
-        for copy in exp_copies(i):
-            copy.wait()
 
 
 def near_sources(row_ref, one_ref, two_ref, here_ref, units, ext):
@@ -307,12 +297,6 @@
         give_ref[c] = total[pl.ds((2 * c + 1 - core) * share, share)].astype(give_ref.dtype)
 
 
-def fold_kernel(chip_ref, keep_ref, got_ref, own_ref, *out_refs):
-    for step, out_ref in enumerate((own_ref,) + out_refs):
-        chip = lax.bitwise_xor(chip_ref[0], step)
-        out_ref[...] = (keep_ref[chip].astype(F32) + got_ref[chip].astype(F32)).astype(out_ref.dtype)
-
-
 def pair_kernel(keep_ref, got_ref, out_ref):
     out_ref[...] = (keep_ref[...].astype(F32) + got_ref[...].astype(F32)).astype(out_ref.dtype)
 
@@ -367,19 +351,21 @@
     return columns[:count]
 
 
-def gram_kernel(fields, own_ref, right_ref, image_ref, *pieces_and_out):
-    *pieces, out_ref = pieces_and_out
+def gram_kernel(fields, core_ref, right_ref, image_ref, *refs):
+    *parts, out_ref = refs
     units = image_ref.shape[0]
-    share = pieces[0].shape[0]
+    chips, share = parts[0].shape[:2]
     totals = None
-    for k in range(share):
-        unit = own_ref[0] * share + k
+    for k in range(chips * share):
+        chip, within = divmod(k, share)
+        unit = (2 * chip + core_ref[0]) * share + within
         place = jnp.minimum(unit, units - 1)
         r = right_ref[:, pl.ds(pl.multiple_of(place * LANES, LANES), LANES)]
         z = image_ref[place]
-        q = tree_sum([piece[k].astype(F32) for piece in pieces])
-        r = jnp.where(unit < units, r, 0.0)
-        z = jnp.where(unit < units, z, 0.0)
+        q = tree_sum([part[chip, within].astype(F32) for part in parts])
+        if 2 * chips * share > units:
+            r = jnp.where(unit < units, r, 0.0)
+            z = jnp.where(unit < units, z, 0.0)
         (rr, ri), (zr, zi), (qr, qi) = [(v[:fields], v[fields:]) for v in (r, z, q)]
         products = [
             rr * rr + ri * ri,
@@ -394,12 +380,13 @@
         ]
         totals = products if totals is None else [t + p for t, p in zip(totals, products)]
     lines = flat_lines([jnp.sum(t, axis=1, keepdims=True) for t in totals], fields)
-    out_ref[...] = jnp.broadcast_to(lines[None], out_ref.shape)
-
-
-def final_kernel(fields, sums_ref, right_ref, image_ref, out_ref):
+    out_ref[...] = lines
+
+
+def final_kernel(fields, right_ref, image_ref, *refs):
+    *sums_refs, out_ref = refs
     units = image_ref.shape[0]
-    sums = columns_of(jnp.sum(sums_ref[...], axis=0), 9, fields)
+    sums = columns_of(tree_sum([ref[...] for ref in sums_refs]), 9, fields)
     a_real, a_imag, b_real, b_imag = [
         jnp.broadcast_to(value, (fields, LANES)) for value in krylov_coefficients(sums)
     ]
@@ -419,6 +406,27 @@
     return count & (count - 1) == 0
 
 
+def reversed_bits(value, count):
+    bits = count.bit_length() - 1
+    return sum(((value >> k) & 1) << (bits - 1 - k) for k in range(bits))
+
+
+def target_row(row, pair, rows):
+    if not is_power(rows):
+        return (pair - row + rows) % rows
+    return pair ^ reversed_bits(row, rows)
+
+
+def source_row(row, pair, rows):
+    if not is_power(rows):
+        return (pair - row + rows) % rows
+    return reversed_bits(pair ^ row, rows)
+
+
+def own_items_change_cores(rows, items, send):
+    return items == 1 and send == 2
+
+
 def item_route(rows, group, columns, send):
     items = rows * send // group
 
@@ -426,9 +434,8 @@
         return (g // columns * rows + r) * columns + g % columns
 
     def target(r, g, pair):
-        if not is_power(rows):
-            return flat((pair - r) % rows, g)
-        return flat(r ^ pair, g ^ 1 if pair == 0 and items == 1 and send == 2 else g)
+        d = target_row(r, pair, rows)
+        return flat(d, g ^ 1 if d == r and own_items_change_cores(rows, items, send) else g)
 
     assert items * group == rows * send and (items % send == 0 or send % items == 0)
     routes = []
@@ -469,11 +476,10 @@
     assert rows % 2 == 0
     neighbours = [[r + 1 - 2 * (r % 2) for r in range(rows)], [(r - 1 + 2 * (r % 2)) % rows for r in range(rows)]]
     own_place, row_place = own.reshape(1), row_here.reshape(1)
-    core_place, chip_place = lax.rem(own, 2).reshape(1), lax.div(own, 2).reshape(1)
+    core_place = lax.rem(own, 2).reshape(1)
     slots = near_tiles.shape[1]
     pad_coefs = -(-coefs // 8) * 8
     chips = group // 2
-    steps_between = range(chips - 1, 0, -1)
     assert group == 2 * chips and chips & (chips - 1) == 0 and LANES % fields == 0
     window_shape = jax.ShapeDtypeStruct((items, width, pad_coefs, 2, LANES), BF16)
     item_shape = jax.ShapeDtypeStruct((items, fields, 2 * pad_coefs), BF16)
@@ -488,23 +494,30 @@
     moves = in_hbm(translations.transpose(0, 2, 1, 3))
     picks = far_pick.transpose(0, 2, 1)
 
-    plan, made, windows, leaves, right = pl.pallas_call(
+    plan, made, windows, target_windows, moves, leaves, right = pl.pallas_call(
         functools.partial(begin_kernel, fields, items, width, send, rows),
         out_shape=(
             pltpu.SMEM((item_place(slots, items),), jnp.int32),
             item_shape,
             pltpu.VMEM(window_shape.shape, BF16),
+            pltpu.VMEM(window_shape.shape, BF16),
+            pltpu.VMEM((items, coefs, 2, coefs), BF16),
             jax.ShapeDtypeStruct(leaves.shape, jnp.int32),
             jax.ShapeDtypeStruct((both, panels), F32),
         ),
-        in_specs=[SMEM] * 2 + [HBM] * 8,
-        out_specs=(SMEM,) + (VMEM,) * 4,
+        in_specs=[SMEM] * 2 + [HBM] * 9,
+        out_specs=(SMEM,) + (VMEM,) * 6,
         scratch_shapes=[
             pltpu.SMEM(value.shape, jnp.int32)
             for value in (picks, leaf_of_panel, far_target, far_offset, tile_pairs)
         ]
-        + [pltpu.SemaphoreType.DMA((7,)), pltpu.SemaphoreType.DMA((items, width, PIECES))],
-        compiler_params=params(),
+        + [
+            pltpu.SemaphoreType.DMA((7,)),
+            pltpu.SemaphoreType.DMA((items, width, PIECES)),
+            pltpu.SemaphoreType.DMA((items, width, PIECES)),
+            pltpu.SemaphoreType.DMA((items,)),
+        ],
+        compiler_params=params(24),
         name="begin",
     )(
         row_place,
@@ -517,6 +530,7 @@
         in_hbm(tile_pairs),
         in_hbm(right_side.reshape(both, panels)),
         expansions,
+        moves,
     )
 
     def exchanged(made):
@@ -540,23 +554,15 @@
         ]
 
     image_shape = jax.ShapeDtypeStruct((units, both, LANES), F32)
-    target_windows, moved = pl.pallas_call(
-        functools.partial(fetch_kernel, items, width, slots),
-        out_shape=(
-            pltpu.VMEM(window_shape.shape, BF16),
-            pltpu.VMEM((items, 2 * pad_coefs, coefs), BF16),
-        ),
-        in_specs=[SMEM, HBM, HBM],
-        out_specs=(VMEM, VMEM),
-        scratch_shapes=[
-            pltpu.VMEM((items, coefs, 2, coefs), BF16),
-            pltpu.SemaphoreType.DMA((items, width, PIECES)),
-            pltpu.SemaphoreType.DMA((items,)),
-        ],
-        compiler_params=params(24),
+    moved = pl.pallas_call(
+        rows_kernel,
+        out_shape=pltpu.VMEM((items, 2 * pad_coefs, coefs), BF16),
+        in_specs=[VMEM],
+        out_specs=VMEM,
+        compiler_params=params(),
         cost_estimate=pl.CostEstimate(flops=0, bytes_accessed=6 * window_shape.size, transcendentals=0),
-        name="fetch",
-    )(plan, expansions, moves)
+        name="translation_rows",
+    )(moves)
 
     def swapped(value, step):
         return lax.ppermute(value, GROUP, [(g, g ^ step) for g in range(group)])
@@ -588,7 +594,7 @@
         )(core_place, plan, leaves, partial, taken, moved, target_windows)
         return keep, swapped(give, 1)
 
-    def whole_sum(keep, got):
+    def pair_sums(keep, got):
         pair = pl.pallas_call(
             pair_kernel,
             out_shape=jax.ShapeDtypeStruct(keep.shape, BF16),
@@ -597,15 +603,18 @@
             compiler_params=params(),
             name="pair",
         )(keep, got)
-        arrived = {step: swapped(pair, 2 * step) for step in steps_between}
+        arrived = {step: swapped(pair, 2 * step) for step in range(chips - 1, 0, -1)}
+        return [pair] + [arrived[step] for step in range(1, chips)]
+
+    def whole_sum(parts):
         mine = pl.pallas_call(
             close_kernel,
-            out_shape=jax.ShapeDtypeStruct(keep.shape, F32),
+            out_shape=jax.ShapeDtypeStruct((chips, *part_shape), F32),
             in_specs=[VMEM] * chips,
             out_specs=VMEM,
             compiler_params=params(),
             name="close",
-        )(pair, *[arrived[step] for step in range(1, chips)])
+        )(*parts)
         theirs = swapped(mine, 1)
         low_shape = jax.ShapeDtypeStruct((units, both, LANES), BF16)
         return pl.pallas_call(
@@ -618,42 +627,42 @@
             name="assemble",
         )(core_place, plan, leaves, mine, theirs, windows)
 
-    def share_pieces(keep, got):
-        pieces = pl.pallas_call(
-            fold_kernel,
-            out_shape=(jax.ShapeDtypeStruct(part_shape, F32),)
-            + (jax.ShapeDtypeStruct(part_shape, BF16),) * (chips - 1),
-            in_specs=[SMEM, VMEM, VMEM],
-            out_specs=(VMEM,) * chips,
+    def row_sums(lines):
+        lines = pl.pallas_call(
+            close_kernel,
+            out_shape=jax.ShapeDtypeStruct(lines.shape, F32),
+            in_specs=[VMEM] * 2,
+            out_specs=VMEM,
             compiler_params=params(),
-            name="fold",
-        )(chip_place, keep, got)
-        arrived = {step: swapped(pieces[step], 2 * step) for step in steps_between}
-        return [pieces[0]] + [arrived[step] for step in steps_between]
+            name="cores",
+        )(lines, swapped(lines, 1))
+        if rows != 4:
+            return [lax.psum(lines, "row")]
+        others = [lax.ppermute(lines, "row", [(r, r ^ step) for r in range(rows)]) for step in (3, 2, 1)]
+        return [lines] + others[::-1]
 
     partial = near(*from_neighbours(right), right)
-    z_all, z_low, made = whole_sum(*core_parts(partial, exchanged(made), F32))
+    z_all, z_low, made = whole_sum(pair_sums(*core_parts(partial, exchanged(made), F32)))
     partial = near(*from_neighbours(z_low), z_low)
-    pieces = share_pieces(*core_parts(partial, exchanged(made), BF16))
-
-    lines = -(-9 * fields // LANES)
-    sums = pl.pallas_call(
+    parts = pair_sums(*core_parts(partial, exchanged(made), BF16))
+
+    lines = pl.pallas_call(
         functools.partial(gram_kernel, fields),
-        out_shape=jax.ShapeDtypeStruct((group * rows, lines, LANES), F32),
+        out_shape=jax.ShapeDtypeStruct((-(-9 * fields // LANES), LANES), F32),
         in_specs=[SMEM] + [VMEM] * (2 + chips),
         out_specs=VMEM,
         compiler_params=params(),
         name="gram",
-    )(own_place, right, z_all, *pieces)
-    sums = lax.all_to_all(sums, EVERY, 0, 0, tiled=True)
+    )(core_place, right, z_all, *parts)
+    sums = row_sums(lines)
     out = pl.pallas_call(
         functools.partial(final_kernel, fields),
         out_shape=jax.ShapeDtypeStruct((both, panels), F32),
-        in_specs=[VMEM, VMEM, VMEM],
+        in_specs=[VMEM] * (2 + len(sums)),
         out_specs=VMEM,
         compiler_params=params(),
         name="combine",
-    )(sums, right, z_all)
+    )(right, z_all, *sums)
     return out.reshape(right_side.shape)
 
 

time: 54.9 us -> 55.4 us (level)
  blocking collectives: 10.9 us -> 0 us
  waiting for transfers between devices: 16.4 us -> 22.4 us
  starting transfers between devices: 16.9 us -> 20.7 us
  local copies, waits for them, and re-layouts: 0.01 us -> 2.99 us
  Pallas kernels: 9.65 us -> 8.3 us
    all_to_all x1 -> x0, blocking collectives: 10.9 us -> none  [local(): sums = lax.all_to_all(sums, EVERY, 0, 0, tiled=True)]
    ppermute x0 -> x3, starting transfers between devices: none -> 4.39 us  [row_sums(): lax.ppermute(lines, 'row', [(r, r ^ step) for r in range(rows)])]
    unnamed x2 -> x10, local copies, waits for them, and re-layouts: 0.01 us -> 2.99 us
    ppermute x9 -> x10, waiting for transfers between devices: 11.7 us -> 14.4 us  [swapped(): return lax.ppermute(value, GROUP, [(g, g ^ step) for g in range(group)])]
    ppermute x0 -> x3, waiting for transfers between devices: none -> 2.56 us  [row_sums(): lax.ppermute(lines, 'row', [(r, r ^ step) for r in range(rows)])]
    pallas_call x4 -> x5, Pallas kernels: 2.05 us -> 0.2 us  [the longest x1 0.09 us: local(): pl.pallas_call(rows_kernel, out_shape=pltpu.VMEM((items, 2 * pad_coefs, c...]
    ppermute x4, waiting for transfers between devices: 4.7 us -> 5.42 us  [from_neighbours(): lax.ppermute(value, 'row', list(enumerate(targets)))]
    ppermute x9 -> x10, starting transfers between devices: 9.36 us -> 8.93 us  [swapped(): return lax.ppermute(value, GROUP, [(g, g ^ step) for g in range(group)])]
  transfers between devices with their start and end apart: 15 -> 19, of which waited for: 11 -> 15; matrix products, arithmetic and copies ran while one was open for 0% -> 0% of each run, Pallas kernels for 6% -> 3%
where the time goes in v7:
time: 55.4 us; the launch traced here: 55.2 us
  waiting for transfers between devices  22.4 us (40%)
  starting transfers between devices  20.7 us (37%)
  Pallas kernels  8.3 us (15%)
  local copies, waits for them, and re-layouts  2.99 us (5%)
  between operations  0.82 us (1%)
    ppermute x10, waiting for transfers between devices, swapped(): return lax.ppermute(value, GROUP, [(g, g ^ step) for g in range(group)])  14.4 us
    ppermute x10, starting transfers between devices, swapped(): return lax.ppermute(value, GROUP, [(g, g ^ step) for g in range(group)])  8.93 us
    ppermute x4, starting transfers between devices, from_neighbours(): lax.ppermute(value, 'row', list(enumerate(targets)))  7.32 us
    ppermute x4, waiting for transfers between devices, from_neighbours(): lax.ppermute(value, 'row', list(enumerate(targets)))  5.42 us
    ppermute x3, starting transfers between devices, row_sums(): lax.ppermute(lines, 'row', [(r, r ^ step) for r in range(rows)])  4.39 us
    pallas_call x1, Pallas kernels, local(): pl.pallas_call(functools.partial(begin_kernel, fields, items, width, send...  3.21 us
    unnamed x10, local copies, waits for them, and re-layouts  2.99 us
    ppermute x3, waiting for transfers between devices, row_sums(): lax.ppermute(lines, 'row', [(r, r ^ step) for r in range(rows)])  2.56 us
  transfers between devices with their start and end apart: 19, of which 15 were waited for; matrix products, arithmetic and copies ran while one was open for 0% of the time, Pallas kernels for 3%

profile of v7, /device:TPU:0, one launch (start us, length us, event | category | flops | bytes accessed | tf_op | source)
XLA Modules:
  0.0 55.2 jit_solution(13696926484675443061)
XLA Ops:
  0.0 3.2 %begin.1 = (s32[12]{0:T(128)S(4)}, bf16[1,16,896]{2,1,0:T(8,128)(2,1)S(1)}, bf16[1,3,448,2,128]{4,3,2,1,0:T(2,128)(2,1)S(1)}, bf16[1,3,448,2,128]{4,3,2,1,0:T(2,...) custom-call(s32[1]{0:T(128)} %bitcast.row_ref, ...), custom_call_target="tpu_custom_call" | custom-call | tf_op jit(solution)/shard_map/begin/pallas_call | solution.py:497
  3.2 0.9 %copy-done.1 = bf16[1,441,2,441]{3,2,1,0:T(2,128)(2,1)} copy-done((bf16[1,441,2,441]{3,2,1,0:T(2,128)(2,1)}, bf16[1,441,2,441]{3,2,1,0:T(2,128)(2,1)S(1)}, u32[]{:S(2)}) %copy-start.1) | copy-done | bytes 777948
  4.2 0.9 %copy-done.3 = bf16[1,3,448,2,128]{4,3,2,1,0:T(2,128)(2,1)} copy-done((bf16[1,3,448,2,128]{4,3,2,1,0:T(2,128)(2,1)}, bf16[1,3,448,2,128]{4,3,2,1,0:T(2,128)(2,1)S(1)}, u32[]{:S(2)}) %copy-start.3) | copy-done | bytes 688152
  5.1 3.1 %collective-permute-start = (bf16[32,512]{1,0:T(8,128)(2,1)S(1)}, bf16[32,512]{1,0:T(8,128)(2,1)S(1)}, u32[]{:S(2)}, u32[]{:S(2)}) collective-permute-start(bf16[32,512]{1,0:T(8,128)(2,1)S(1)} %get-tuple-element.26), channel_id=1, source_target_pairs={{0,4},{4,0},{8,12},{12,8},{1,5},{5,1},{9,13},{13,9},{2,6},{6,2},{1... | collective-permute-start | bytes 98312 | tf_op jit(solution)/shard_map/ppermute | solution.py:553
  8.2 2.5 %collective-permute-start.1 = (bf16[32,512]{1,0:T(8,128)(2,1)S(1)}, bf16[32,512]{1,0:T(8,128)(2,1)S(1)}, u32[]{:S(2)}, u32[]{:S(2)}) collective-permute-start(bf16[32,512]{1,0:T(8,128)(2,1)S(1)} %get-tuple-element.27), channel_id=1, source_target_pairs={{0,12},{4,8},{8,4},{12,0},{1,13},{5,9},{9,5},{13,1},{2,14},{6,10},... | collective-permute-start | bytes 98312 | tf_op jit(solution)/shard_map/ppermute | solution.py:553
  11.3 1.2 %copy-done.2 = bf16[1,441,2,441]{3,2,1,0:T(2,128)(2,1)S(1)} copy-done((bf16[1,441,2,441]{3,2,1,0:T(2,128)(2,1)S(1)}, bf16[1,441,2,441]{3,2,1,0:T(2,128)(2,1)}, u32[]{:S(2)}) %copy-start.2) | copy-done | bytes 777948
  12.6 1.3 %collective-permute-done.1.two_ref = bf16[32,512]{1,0:T(8,128)(2,1)S(1)} collective-permute-done((bf16[32,512]{1,0:T(8,128)(2,1)S(1)}, bf16[32,512]{1,0:T(8,128)(2,1)S(1)}, u32[]{:S(2)}, u32[]{:S(2)}) %collective-permute-start.1) | collective-permute-done | bytes 32800 | tf_op jit(solution)/shard_map/ppermute | solution.py:553
  13.9 0.8 %near.2.partial_ref = f32[24,32,128]{2,1,0:T(8,128)S(1)} custom-call(s32[1]{0:T(128)} %bitcast.row_ref, s32[1]{0:T(128)S(6)} %copy.11.count_ref, s32[12]{0:T(128)S(4)} %get-tuple-element.24.plan_ref, bf16[32,512]{1,0:T(8,128)(2,1)S(1)} %collective-permute-done.one_ref, bf16[32,512]{1,0:T(8,128)(2,1)S(1)} %collective-permute-done.1.two_ref, ...), custom_call_target="tpu_custom_call" | custom-call | flops 67108864 | bytes 2097152 | tf_op jit(solution)/shard_map/near/pallas_call | solution.py:571
  14.6 0.7 %far.2 = (f32[4,3,32,128]{3,2,1,0:T(8,128)S(1)}, f32[4,3,32,128]{3,2,1,0:T(8,128)S(1)}) custom-call(s32[1]{0:T(128)} %bitcast.9.core_ref, s32[12]{0:T(128)S(4)} %get-tuple-element.24.plan_ref, s32[24,1,128]{2,1,0:T(1,128)S(1)} %get-tuple-element.25.leaves_ref, f32[24,32,128]{2,1,0:T(8,128)S(1)} %near.2.partial_ref, ...), custom_call_target="tpu_custom_call" | custom-call | tf_op jit(solution)/shard_map/far/pallas_call | solution.py:586
  15.4 1.4 %collective-permute-done.3.got_ref = f32[4,3,32,128]{3,2,1,0:T(8,128)S(1)} collective-permute-done((f32[4,3,32,128]{3,2,1,0:T(8,128)S(1)}, f32[4,3,32,128]{3,2,1,0:T(8,128)S(1)}, u32[]{:S(2)}, u32[]{:S(2)}) %collective-permute-start.3) | collective-permute-done | bytes 196640 | tf_op jit(solution)/shard_map/ppermute | solution.py:568
  16.9 4.2 %collective-permute-start.6 = (bf16[4,3,32,128]{3,2,1,0:T(8,128)(2,1)S(1)}, bf16[4,3,32,128]{3,2,1,0:T(8,128)(2,1)S(1)}, u32[]{:S(2)}, u32[]{:S(2)}) collective-permute-start(bf16[4,3,32,128]{3,2,1,0:T(8,128)(2,1)S(1)} %pair.2.refs_0_), channel_id=1, source_target_pairs={{0,18},{1,19},{2,16},{3,17},{16,2},{17,3},{18,0},{19,1},{4,22},{5,... | collective-permute-start | bytes 294920 | tf_op jit(solution)/shard_map/ppermute | solution.py:568
  21.0 0.6 %collective-permute-start.4 = (bf16[4,3,32,128]{3,2,1,0:T(8,128)(2,1)S(1)}, bf16[4,3,32,128]{3,2,1,0:T(8,128)(2,1)S(1)}, u32[]{:S(2)}, u32[]{:S(2)}) collective-permute-start(bf16[4,3,32,128]{3,2,1,0:T(8,128)(2,1)S(1)} %pair.2.refs_0_), channel_id=1, source_target_pairs={{0,2},{1,3},{2,0},{3,1},{16,18},{17,19},{18,16},{19,17},{4,6},{5,7... | collective-permute-start | bytes 294920 | tf_op jit(solution)/shard_map/ppermute | solution.py:568
  21.7 2.9 %collective-permute-done.6.refs_3_ = bf16[4,3,32,128]{3,2,1,0:T(8,128)(2,1)S(1)} collective-permute-done((bf16[4,3,32,128]{3,2,1,0:T(8,128)(2,1)S(1)}, bf16[4,3,32,128]{3,2,1,0:T(8,128)(2,1)S(1)}, u32[]{:S(2)}, u32[]{:S(2)}) %collective-permute-start.6) | collective-permute-done | bytes 98336 | tf_op jit(solution)/shard_map/ppermute | solution.py:568
  24.6 1.0 %collective-permute-done.5.refs_2_ = bf16[4,3,32,128]{3,2,1,0:T(8,128)(2,1)S(1)} collective-permute-done((bf16[4,3,32,128]{3,2,1,0:T(8,128)(2,1)S(1)}, bf16[4,3,32,128]{3,2,1,0:T(8,128)(2,1)S(1)}, u32[]{:S(2)}, u32[]{:S(2)}) %collective-permute-start.5) | collective-permute-done | bytes 98336 | tf_op jit(solution)/shard_map/ppermute | solution.py:568
  26.4 1.4 %collective-permute-done.7.theirs_ref = f32[4,3,32,128]{3,2,1,0:T(8,128)S(1)} collective-permute-done((f32[4,3,32,128]{3,2,1,0:T(8,128)S(1)}, f32[4,3,32,128]{3,2,1,0:T(8,128)S(1)}, u32[]{:S(2)}, u32[]{:S(2)}) %collective-permute-start.7) | collective-permute-done | bytes 196640 | tf_op jit(solution)/shard_map/ppermute | solution.py:568
  28.5 1.7 %collective-permute-start.9 = (bf16[4,32,128]{2,1,0:T(8,128)(2,1)S(1)}, bf16[4,32,128]{2,1,0:T(8,128)(2,1)S(1)}, u32[]{:S(2)}, u32[]{:S(2)}) collective-permute-start(bf16[4,32,128]{2,1,0:T(8,128)(2,1)S(1)} %get-tuple-element.37), channel_id=1, source_target_pairs={{0,12},{4,8},{8,4},{12,0},{1,13},{5,9},{9,5},{13,1},{2,14},{6,10},... | collective-permute-start | bytes 98312 | tf_op jit(solution)/shard_map/ppermute | solution.py:553
  30.2 2.2 %collective-permute-done.8.one_ref = bf16[4,32,128]{2,1,0:T(8,128)(2,1)S(1)} collective-permute-done((bf16[4,32,128]{2,1,0:T(8,128)(2,1)S(1)}, bf16[4,32,128]{2,1,0:T(8,128)(2,1)S(1)}, u32[]{:S(2)}, u32[]{:S(2)}) %collective-permute-start.8) | collective-permute-done | bytes 32800 | tf_op jit(solution)/shard_map/ppermute | solution.py:553
  32.4 1.9 %collective-permute-done.9.two_ref = bf16[4,32,128]{2,1,0:T(8,128)(2,1)S(1)} collective-permute-done((bf16[4,32,128]{2,1,0:T(8,128)(2,1)S(1)}, bf16[4,32,128]{2,1,0:T(8,128)(2,1)S(1)}, u32[]{:S(2)}, u32[]{:S(2)}) %collective-permute-start.9) | collective-permute-done | bytes 32800 | tf_op jit(solution)/shard_map/ppermute | solution.py:553
  34.3 0.7 %near.3.partial_ref = f32[24,32,128]{2,1,0:T(8,128)S(1)} custom-call(s32[1]{0:T(128)} %bitcast.row_ref, s32[1]{0:T(128)S(6)} %copy.11.count_ref, s32[12]{0:T(128)S(4)} %get-tuple-element.24.plan_ref, bf16[4,32,128]{2,1,0:T(8,128)(2,1)S(1)} %collective-permute-done.8.one_ref, bf16[4,32,128]{2,1,0:T(8,128)(2,1)S(1)} %collective-permute-done.9.two_ref, ...), custom_call_target="tpu_custom_call" | custom-call | flops 67108864 | bytes 2097152 | tf_op jit(solution)/shard_map/near/pallas_call | solution.py:571
  35.0 0.7 %far.3 = (bf16[4,3,32,128]{3,2,1,0:T(8,128)(2,1)S(1)}, bf16[4,3,32,128]{3,2,1,0:T(8,128)(2,1)S(1)}) custom-call(s32[1]{0:T(128)} %bitcast.9.core_ref, s32[12]{0:T(128)S(4)} %get-tuple-element.24.plan_ref, s32[24,1,128]{2,1,0:T(1,128)S(1)} %get-tuple-element.25.leaves_ref, f32[24,32,128]{2,1,0:T(8,128)S(1)} %near.3.partial_ref, ...), custom_call_target="tpu_custom_call" | custom-call | tf_op jit(solution)/shard_map/far/pallas_call | solution.py:586
  35.8 1.3 %collective-permute-done.11.got_ref = bf16[4,3,32,128]{3,2,1,0:T(8,128)(2,1)S(1)} collective-permute-done((bf16[4,3,32,128]{3,2,1,0:T(8,128)(2,1)S(1)}, bf16[4,3,32,128]{3,2,1,0:T(8,128)(2,1)S(1)}, u32[]{:S(2)}, u32[]{:S(2)}) %collective-permute-start.11) | collective-permute-done | bytes 98336 | tf_op jit(solution)/shard_map/ppermute | solution.py:568
  37.1 3.2 %collective-permute-start.14 = (bf16[4,3,32,128]{3,2,1,0:T(8,128)(2,1)S(1)}, bf16[4,3,32,128]{3,2,1,0:T(8,128)(2,1)S(1)}, u32[]{:S(2)}, u32[]{:S(2)}) collective-permute-start(bf16[4,3,32,128]{3,2,1,0:T(8,128)(2,1)S(1)} %pair.3.refs_0_), channel_id=1, source_target_pairs={{0,18},{1,19},{2,16},{3,17},{16,2},{17,3},{18,0},{19,1},{4,22},{5,... | collective-permute-start | bytes 294920 | tf_op jit(solution)/shard_map/ppermute | solution.py:568
  40.3 0.6 %collective-permute-start.12 = (bf16[4,3,32,128]{3,2,1,0:T(8,128)(2,1)S(1)}, bf16[4,3,32,128]{3,2,1,0:T(8,128)(2,1)S(1)}, u32[]{:S(2)}, u32[]{:S(2)}) collective-permute-start(bf16[4,3,32,128]{3,2,1,0:T(8,128)(2,1)S(1)} %pair.3.refs_0_), channel_id=1, source_target_pairs={{0,2},{1,3},{2,0},{3,1},{16,18},{17,19},{18,16},{19,17},{4,6},{5,7... | collective-permute-start | bytes 294920 | tf_op jit(solution)/shard_map/ppermute | solution.py:568
  40.9 2.9 %collective-permute-done.14.refs_3_ = bf16[4,3,32,128]{3,2,1,0:T(8,128)(2,1)S(1)} collective-permute-done((bf16[4,3,32,128]{3,2,1,0:T(8,128)(2,1)S(1)}, bf16[4,3,32,128]{3,2,1,0:T(8,128)(2,1)S(1)}, u32[]{:S(2)}, u32[]{:S(2)}) %collective-permute-start.14) | collective-permute-done | bytes 98336 | tf_op jit(solution)/shard_map/ppermute | solution.py:568
  43.9 1.0 %collective-permute-done.13.refs_2_ = bf16[4,3,32,128]{3,2,1,0:T(8,128)(2,1)S(1)} collective-permute-done((bf16[4,3,32,128]{3,2,1,0:T(8,128)(2,1)S(1)}, bf16[4,3,32,128]{3,2,1,0:T(8,128)(2,1)S(1)}, u32[]{:S(2)}, u32[]{:S(2)}) %collective-permute-start.13) | collective-permute-done | bytes 98336 | tf_op jit(solution)/shard_map/ppermute | solution.py:568
  44.9 0.6 %collective-permute-done.12.refs_1_ = bf16[4,3,32,128]{3,2,1,0:T(8,128)(2,1)S(1)} collective-permute-done((bf16[4,3,32,128]{3,2,1,0:T(8,128)(2,1)S(1)}, bf16[4,3,32,128]{3,2,1,0:T(8,128)(2,1)S(1)}, u32[]{:S(2)}, u32[]{:S(2)}) %collective-permute-start.12) | collective-permute-done | bytes 98336 | tf_op jit(solution)/shard_map/ppermute | solution.py:568
  46.0 1.1 %collective-permute-done.15.refs_1_ = f32[2,128]{1,0:T(2,128)S(1)} collective-permute-done((f32[2,128]{1,0:T(2,128)S(1)}, f32[2,128]{1,0:T(2,128)S(1)}, u32[]{:S(2)}, u32[]{:S(2)}) %collective-permute-start.15) | collective-permute-done | bytes 1056 | tf_op jit(solution)/shard_map/ppermute | solution.py:568
  47.1 2.5 %collective-permute-start.18 = (f32[2,128]{1,0:T(2,128)S(1)}, f32[2,128]{1,0:T(2,128)S(1)}, u32[]{:S(2)}, u32[]{:S(2)}) collective-permute-start(f32[2,128]{1,0:T(2,128)S(1)} %cores.1.refs_0_), channel_id=1, source_target_pairs={{0,12},{4,8},{8,4},{12,0},{1,13},{5,9},{9,5},{13,1},{2,14},{6,10},... | collective-permute-start | bytes 3080 | tf_op jit(solution)/shard_map/ppermute | solution.py:641
  49.6 1.9 %collective-permute-start.16 = (f32[2,128]{1,0:T(2,128)S(1)}, f32[2,128]{1,0:T(2,128)S(1)}, u32[]{:S(2)}, u32[]{:S(2)}) collective-permute-start(f32[2,128]{1,0:T(2,128)S(1)} %cores.1.refs_0_), channel_id=1, source_target_pairs={{0,4},{4,0},{8,12},{12,8},{1,5},{5,1},{9,13},{13,9},{2,6},{6,2},{1... | collective-permute-start | bytes 3080 | tf_op jit(solution)/shard_map/ppermute | solution.py:641
  51.5 1.0 %collective-permute-done.18.refs_3_ = f32[2,128]{1,0:T(2,128)S(1)} collective-permute-done((f32[2,128]{1,0:T(2,128)S(1)}, f32[2,128]{1,0:T(2,128)S(1)}, u32[]{:S(2)}, u32[]{:S(2)}) %collective-permute-start.18) | collective-permute-done | bytes 1056 | tf_op jit(solution)/shard_map/ppermute | solution.py:641
  52.5 1.6 %collective-permute-done.17.refs_2_ = f32[2,128]{1,0:T(2,128)S(1)} collective-permute-done((f32[2,128]{1,0:T(2,128)S(1)}, f32[2,128]{1,0:T(2,128)S(1)}, u32[]{:S(2)}, u32[]{:S(2)}) %collective-permute-start.17) | collective-permute-done | bytes 1056 | tf_op jit(solution)/shard_map/ppermute | solution.py:641
  54.1 1.1 %combine.1 = f32[32,3072]{1,0:T(8,128)} custom-call(f32[32,3072]{1,0:T(8,128)S(1)} %get-tuple-element.23.image_ref.here_ref.right_ref, f32[24,32,128]{2,1,0:T(8,128)S(1)} %get-tuple-element.34.image_ref, f32[2,128]{1,0:T(2,128)S(1)} %cores.1.refs_0_, f32[2,128]{1,0:T(2,128)S(1)} %collective-permute-done.16.refs_1_, ...), custom_call_target="tpu_custom_call" | custom-call | tf_op jit(solution)/shard_map/combine/pallas_call | solution.py:658
  (31 shorter events, 2.1 us)
Async XLA Ops:
  0.0 13.9 %copy-start = (bf16[2,8,256,256]{3,2,1,0:T(8,128)(2,1)S(1)}, bf16[2,8,256,256]{3,2,1,0:T(8,128)(2,1)}, u32[]{:S(2)}) copy-start(bf16[2,8,256,256]{3,2,1,0:T(8,128)(2,1)} %tiles_ref.3) | copy-start | bytes 6291460
  3.2 0.9 %copy-start.1 = (bf16[1,441,2,441]{3,2,1,0:T(2,128)(2,1)}, bf16[1,441,2,441]{3,2,1,0:T(2,128)(2,1)S(1)}, u32[]{:S(2)}) copy-start(bf16[1,441,2,441]{3,2,1,0:T(2,128)(2,1)S(1)} %get-tuple-element.29.trans_ref) | copy-start | bytes 2333776
  4.2 0.9 %copy-start.3 = (bf16[1,3,448,2,128]{4,3,2,1,0:T(2,128)(2,1)}, bf16[1,3,448,2,128]{4,3,2,1,0:T(2,128)(2,1)S(1)}, u32[]{:S(2)}) copy-start(bf16[1,3,448,2,128]{4,3,2,1,0:T(2,128)(2,1)S(1)} %get-tuple-element.33.window_ref) | copy-start | bytes 2064388
  5.1 7.5 %collective-permute-start = (bf16[32,512]{1,0:T(8,128)(2,1)S(1)}, bf16[32,512]{1,0:T(8,128)(2,1)S(1)}, u32[]{:S(2)}, u32[]{:S(2)}) collective-permute-start(bf16[32,512]{1,0:T(8,128)(2,1)S(1)} %get-tuple-element.26), channel_id=1, source_target_pairs={{0,4},{4,0},{8,12},{12,8},{1,5},{5,1},{9,13},{13,9},{2,6},{6,2},{1... | collective-permute-start | bytes 98312 | tf_op jit(solution)/shard_map/ppermute | solution.py:553
  8.2 5.7 %collective-permute-start.1 = (bf16[32,512]{1,0:T(8,128)(2,1)S(1)}, bf16[32,512]{1,0:T(8,128)(2,1)S(1)}, u32[]{:S(2)}, u32[]{:S(2)}) collective-permute-start(bf16[32,512]{1,0:T(8,128)(2,1)S(1)} %get-tuple-element.27), channel_id=1, source_target_pairs={{0,12},{4,8},{8,4},{12,0},{1,13},{5,9},{9,5},{13,1},{2,14},{6,10},... | collective-permute-start | bytes 98312 | tf_op jit(solution)/shard_map/ppermute | solution.py:553
  10.6 4.0 %collective-permute-start.2 = (bf16[1,16,896]{2,1,0:T(8,128)(2,1)S(1)}, bf16[1,16,896]{2,1,0:T(8,128)(2,1)S(1)}, u32[]{:S(2)}, u32[]{:S(2)}) collective-permute-start(bf16[1,16,896]{2,1,0:T(8,128)(2,1)S(1)} %get-tuple-element.28), channel_id=1, source_target_pairs={{0,1},{1,0},{2,6},{3,7},{16,24},{17,25},{18,30},{19,31},{4,8},{5,9... | collective-permute-start | bytes 86024 | tf_op jit(solution)/shard_map/ppermute | solution.py:538
  11.3 1.2 %copy-start.2 = (bf16[1,441,2,441]{3,2,1,0:T(2,128)(2,1)S(1)}, bf16[1,441,2,441]{3,2,1,0:T(2,128)(2,1)}, u32[]{:S(2)}) copy-start(bf16[1,441,2,441]{3,2,1,0:T(2,128)(2,1)} %copy-done.1) | copy-start | bytes 2333776
  12.5 15.3 %copy-start.4 = (bf16[1,3,448,2,128]{4,3,2,1,0:T(2,128)(2,1)S(1)}, bf16[1,3,448,2,128]{4,3,2,1,0:T(2,128)(2,1)}, u32[]{:S(2)}) copy-start(bf16[1,3,448,2,128]{4,3,2,1,0:T(2,128)(2,1)} %copy-done.3) | copy-start | bytes 2064388
  15.3 1.5 %collective-permute-start.3 = (f32[4,3,32,128]{3,2,1,0:T(8,128)S(1)}, f32[4,3,32,128]{3,2,1,0:T(8,128)S(1)}, u32[]{:S(2)}, u32[]{:S(2)}) collective-permute-start(f32[4,3,32,128]{3,2,1,0:T(8,128)S(1)} %get-tuple-element.32), channel_id=1, source_target_pairs={{0,1},{1,0},{2,3},{3,2},{16,17},{17,16},{18,19},{19,18},{4,5},{5,4... | collective-permute-start | bytes 589832 | tf_op jit(solution)/shard_map/ppermute | solution.py:568
  16.9 7.7 %collective-permute-start.6 = (bf16[4,3,32,128]{3,2,1,0:T(8,128)(2,1)S(1)}, bf16[4,3,32,128]{3,2,1,0:T(8,128)(2,1)S(1)}, u32[]{:S(2)}, u32[]{:S(2)}) collective-permute-start(bf16[4,3,32,128]{3,2,1,0:T(8,128)(2,1)S(1)} %pair.2.refs_0_), channel_id=1, source_target_pairs={{0,18},{1,19},{2,16},{3,17},{16,2},{17,3},{18,0},{19,1},{4,22},{5,... | collective-permute-start | bytes 294920 | tf_op jit(solution)/shard_map/ppermute | solution.py:568
  21.0 4.6 %collective-permute-start.5 = (bf16[4,3,32,128]{3,2,1,0:T(8,128)(2,1)S(1)}, bf16[4,3,32,128]{3,2,1,0:T(8,128)(2,1)S(1)}, u32[]{:S(2)}, u32[]{:S(2)}) collective-permute-start(bf16[4,3,32,128]{3,2,1,0:T(8,128)(2,1)S(1)} %pair.2.refs_0_), channel_id=1, source_target_pairs={{0,16},{1,17},{2,18},{3,19},{16,0},{17,1},{18,2},{19,3},{4,20},{5,... | collective-permute-start | bytes 294920 | tf_op jit(solution)/shard_map/ppermute | solution.py:568
  21.0 5.2 %collective-permute-start.4 = (bf16[4,3,32,128]{3,2,1,0:T(8,128)(2,1)S(1)}, bf16[4,3,32,128]{3,2,1,0:T(8,128)(2,1)S(1)}, u32[]{:S(2)}, u32[]{:S(2)}) collective-permute-start(bf16[4,3,32,128]{3,2,1,0:T(8,128)(2,1)S(1)} %pair.2.refs_0_), channel_id=1, source_target_pairs={{0,2},{1,3},{2,0},{3,1},{16,18},{17,19},{18,16},{19,17},{4,6},{5,7... | collective-permute-start | bytes 294920 | tf_op jit(solution)/shard_map/ppermute | solution.py:568
  26.3 1.5 %collective-permute-start.7 = (f32[4,3,32,128]{3,2,1,0:T(8,128)S(1)}, f32[4,3,32,128]{3,2,1,0:T(8,128)S(1)}, u32[]{:S(2)}, u32[]{:S(2)}) collective-permute-start(f32[4,3,32,128]{3,2,1,0:T(8,128)S(1)} %close.1.mine_ref), channel_id=1, source_target_pairs={{0,1},{1,0},{2,3},{3,2},{16,17},{17,16},{18,19},{19,18},{4,5},{5,4... | collective-permute-start | bytes 589832 | tf_op jit(solution)/shard_map/ppermute | solution.py:568
  28.4 4.0 %collective-permute-start.8 = (bf16[4,32,128]{2,1,0:T(8,128)(2,1)S(1)}, bf16[4,32,128]{2,1,0:T(8,128)(2,1)S(1)}, u32[]{:S(2)}, u32[]{:S(2)}) collective-permute-start(bf16[4,32,128]{2,1,0:T(8,128)(2,1)S(1)} %get-tuple-element.36), channel_id=1, source_target_pairs={{0,4},{4,0},{8,12},{12,8},{1,5},{5,1},{9,13},{13,9},{2,6},{6,2},{1... | collective-permute-start | bytes 98312 | tf_op jit(solution)/shard_map/ppermute | solution.py:553
  28.5 5.8 %collective-permute-start.9 = (bf16[4,32,128]{2,1,0:T(8,128)(2,1)S(1)}, bf16[4,32,128]{2,1,0:T(8,128)(2,1)S(1)}, u32[]{:S(2)}, u32[]{:S(2)}) collective-permute-start(bf16[4,32,128]{2,1,0:T(8,128)(2,1)S(1)} %get-tuple-element.37), channel_id=1, source_target_pairs={{0,12},{4,8},{8,4},{12,0},{1,13},{5,9},{9,5},{13,1},{2,14},{6,10},... | collective-permute-start | bytes 98312 | tf_op jit(solution)/shard_map/ppermute | solution.py:553
  30.2 4.9 %collective-permute-start.10 = (bf16[1,16,896]{2,1,0:T(8,128)(2,1)S(1)}, bf16[1,16,896]{2,1,0:T(8,128)(2,1)S(1)}, u32[]{:S(2)}, u32[]{:S(2)}) collective-permute-start(bf16[1,16,896]{2,1,0:T(8,128)(2,1)S(1)} %get-tuple-element.38), channel_id=1, source_target_pairs={{0,1},{1,0},{2,6},{3,7},{16,24},{17,25},{18,30},{19,31},{4,8},{5,9... | collective-permute-start | bytes 86024 | tf_op jit(solution)/shard_map/ppermute | solution.py:538
  35.7 1.4 %collective-permute-start.11 = (bf16[4,3,32,128]{3,2,1,0:T(8,128)(2,1)S(1)}, bf16[4,3,32,128]{3,2,1,0:T(8,128)(2,1)S(1)}, u32[]{:S(2)}, u32[]{:S(2)}) collective-permute-start(bf16[4,3,32,128]{3,2,1,0:T(8,128)(2,1)S(1)} %get-tuple-element.40), channel_id=1, source_target_pairs={{0,1},{1,0},{2,3},{3,2},{16,17},{17,16},{18,19},{19,18},{4,5},{5,4... | collective-permute-start | bytes 294920 | tf_op jit(solution)/shard_map/ppermute | solution.py:568
  37.1 6.8 %collective-permute-start.14 = (bf16[4,3,32,128]{3,2,1,0:T(8,128)(2,1)S(1)}, bf16[4,3,32,128]{3,2,1,0:T(8,128)(2,1)S(1)}, u32[]{:S(2)}, u32[]{:S(2)}) collective-permute-start(bf16[4,3,32,128]{3,2,1,0:T(8,128)(2,1)S(1)} %pair.3.refs_0_), channel_id=1, source_target_pairs={{0,18},{1,19},{2,16},{3,17},{16,2},{17,3},{18,0},{19,1},{4,22},{5,... | collective-permute-start | bytes 294920 | tf_op jit(solution)/shard_map/ppermute | solution.py:568
  40.3 4.6 %collective-permute-start.13 = (bf16[4,3,32,128]{3,2,1,0:T(8,128)(2,1)S(1)}, bf16[4,3,32,128]{3,2,1,0:T(8,128)(2,1)S(1)}, u32[]{:S(2)}, u32[]{:S(2)}) collective-permute-start(bf16[4,3,32,128]{3,2,1,0:T(8,128)(2,1)S(1)} %pair.3.refs_0_), channel_id=1, source_target_pairs={{0,16},{1,17},{2,18},{3,19},{16,0},{17,1},{18,2},{19,3},{4,20},{5,... | collective-permute-start | bytes 294920 | tf_op jit(solution)/shard_map/ppermute | solution.py:568
  40.3 5.2 %collective-permute-start.12 = (bf16[4,3,32,128]{3,2,1,0:T(8,128)(2,1)S(1)}, bf16[4,3,32,128]{3,2,1,0:T(8,128)(2,1)S(1)}, u32[]{:S(2)}, u32[]{:S(2)}) collective-permute-start(bf16[4,3,32,128]{3,2,1,0:T(8,128)(2,1)S(1)} %pair.3.refs_0_), channel_id=1, source_target_pairs={{0,2},{1,3},{2,0},{3,1},{16,18},{17,19},{18,16},{19,17},{4,6},{5,7... | collective-permute-start | bytes 294920 | tf_op jit(solution)/shard_map/ppermute | solution.py:568
  45.9 1.2 %collective-permute-start.15 = (f32[2,128]{1,0:T(2,128)S(1)}, f32[2,128]{1,0:T(2,128)S(1)}, u32[]{:S(2)}, u32[]{:S(2)}) collective-permute-start(f32[2,128]{1,0:T(2,128)S(1)} %gram.1.refs_0_), channel_id=1, source_target_pairs={{0,1},{1,0},{2,3},{3,2},{16,17},{17,16},{18,19},{19,18},{4,5},{5,4... | collective-permute-start | bytes 3080 | tf_op jit(solution)/shard_map/ppermute | solution.py:568
  47.1 5.4 %collective-permute-start.18 = (f32[2,128]{1,0:T(2,128)S(1)}, f32[2,128]{1,0:T(2,128)S(1)}, u32[]{:S(2)}, u32[]{:S(2)}) collective-permute-start(f32[2,128]{1,0:T(2,128)S(1)} %cores.1.refs_0_), channel_id=1, source_target_pairs={{0,12},{4,8},{8,4},{12,0},{1,13},{5,9},{9,5},{13,1},{2,14},{6,10},... | collective-permute-start | bytes 3080 | tf_op jit(solution)/shard_map/ppermute | solution.py:641
  49.6 4.5 %collective-permute-start.17 = (f32[2,128]{1,0:T(2,128)S(1)}, f32[2,128]{1,0:T(2,128)S(1)}, u32[]{:S(2)}, u32[]{:S(2)}) collective-permute-start(f32[2,128]{1,0:T(2,128)S(1)} %cores.1.refs_0_), channel_id=1, source_target_pairs={{0,8},{4,12},{8,0},{12,4},{1,9},{5,13},{9,1},{13,5},{2,10},{6,14},... | collective-permute-start | bytes 3080 | tf_op jit(solution)/shard_map/ppermute | solution.py:641
  49.6 4.5 %collective-permute-start.16 = (f32[2,128]{1,0:T(2,128)S(1)}, f32[2,128]{1,0:T(2,128)S(1)}, u32[]{:S(2)}, u32[]{:S(2)}) collective-permute-start(f32[2,128]{1,0:T(2,128)S(1)} %cores.1.refs_0_), channel_id=1, source_target_pairs={{0,4},{4,0},{8,12},{12,8},{1,5},{5,1},{9,13},{13,9},{2,6},{6,2},{1... | collective-permute-start | bytes 3080 | tf_op jit(solution)/shard_map/ppermute | solution.py:641

commit v8 on v7

--- a/solution.py
+++ b/solution.py
@@ -13,7 +13,7 @@
 EPSILON = 1e-06
 GROUP = ("grp", "col")
 CODES = 0
-PER_ITEM = 4
+PER_ITEM = 5
 PIECES = 4
 EVERY = ("grp", "row", "col")
 
@@ -145,9 +145,9 @@
 
 def begin_kernel(
     fields, items, width, send, rows, row_ref, own_ref, pick_hbm, leaf_hbm, leaves_hbm,
-    target_hbm, offset_hbm, pairs_hbm, right_hbm, exp_ref, trans_ref,
-    plan_ref, out_ref, window_ref, target_window_ref, trans_out, leaves_ref, right_ref,
-    pick_ref, leaf_ref, target_ref, offset_ref, pairs_ref, sem, window_sem, target_sem, trans_sem,
+    target_hbm, offset_hbm, pairs_hbm, right_hbm, exp_ref,
+    plan_ref, out_ref, window_ref, leaves_ref, right_ref,
+    pick_ref, leaf_ref, target_ref, offset_ref, pairs_ref, sem, window_sem,
 ):
     loads = [
         pltpu.make_async_copy(source, place, sem.at[k])
@@ -191,7 +191,6 @@
             copy.start()
     for load in loads[2:]:
         load.wait()
-    later = []
     for s in range(slots):
         plan_ref[CODES + s] = pairs_ref[s]
     for i in range(items):
@@ -199,29 +198,39 @@
         other, number = partner(i, True)
         leaf = target_ref[0, other * send + number]
         plan_ref[place + 2], plan_ref[place + 3] = leaf, window_start(leaf_ref, leaf, width)
-        offset = offset_ref[0, other * send + number]
-        later += window_copies(exp_ref, plan_ref[place + 3], target_window_ref.at[i], target_sem.at[i], width)
-        later.append(pltpu.make_async_copy(trans_ref.at[offset], trans_out.at[i], trans_sem.at[i]))
-    for copy in later:
-        copy.start()
-    for i in range(items):
-        clear_rest(target_window_ref.at[i], exp_ref.shape[0], width)
+        plan_ref[place + 4] = offset_ref[0, other * send + number]
     for i in range(items):
         place = item_place(slots, i)
         leaf, unit = plan_ref[place], plan_ref[place + 1]
         for copy in window_copies(exp_ref, unit, window_ref.at[i], window_sem.at[i], width):
             copy.wait()
         out_ref[i] = multi_rows(fields, width, leaf, unit, leaves_ref, right_ref, window_ref.at[i]).astype(BF16)
-    for copy in later:
-        copy.wait()
-
-
-def rows_kernel(trans_ref, moved_ref):
-    items, coefs = trans_ref.shape[:2]
+
+
+def fetch_kernel(items, width, slots, plan_ref, exp_ref, trans_ref, window_ref, moved_ref, trans_buf, sem, trans_sem):
+    coefs = trans_ref.shape[3]
+    for i in range(items):
+        clear_rest(window_ref.at[i], coefs, width)
+
+    def trans_copy(i):
+        offset = plan_ref[item_place(slots, i) + 4]
+        return pltpu.make_async_copy(trans_ref.at[offset], trans_buf.at[i], trans_sem.at[i])
+
+    def exp_copies(i):
+        unit = plan_ref[item_place(slots, i) + 3]
+        return window_copies(exp_ref, unit, window_ref.at[i], sem.at[i], width)
+
+    for i in range(items):
+        trans_copy(i).start()
+        for copy in exp_copies(i):
+            copy.start()
     rest = moved_ref.shape[1] - 2 * coefs
     for i in range(items):
-        moved_ref[i, pl.ds(0, 2 * coefs)] = trans_ref[i].reshape(2 * coefs, coefs)
+        trans_copy(i).wait()
+        moved_ref[i, pl.ds(0, 2 * coefs)] = trans_buf[i].reshape(2 * coefs, coefs)
         moved_ref[i, pl.ds(2 * coefs, rest)] = jnp.zeros((rest, coefs), BF16)
+        for copy in exp_copies(i):
+            copy.wait()
 
 
 def near_sources(row_ref, one_ref, two_ref, here_ref, units, ext):
@@ -330,25 +339,24 @@
         ).astype(BF16)
 
 
-def flat_lines(columns, fields):
+def flat_lines(totals, fields):
     per = LANES // fields
+    lane = lax.broadcasted_iota(jnp.int32, (fields, LANES), 1)
+    field = lax.broadcasted_iota(jnp.int32, (fields, LANES), 0)
     lines = []
-    for first in range(0, len(columns), per):
-        some = columns[first : first + per]
-        if len(some) < per:
-            some = some + [jnp.zeros(((per - len(some)) * fields, 1), F32)]
-        square = jnp.broadcast_to(jnp.concatenate(some, axis=0), (LANES, LANES))
-        lines.append(jnp.transpose(square)[:1])
+    for first in range(0, len(totals), per):
+        line = jnp.zeros((fields, LANES), F32)
+        for k, total in enumerate(totals[first : first + per]):
+            line = jnp.where(lane == field + k * fields, jnp.sum(total, axis=1, keepdims=True), line)
+        lines.append(jnp.sum(line, axis=0, keepdims=True))
     return jnp.concatenate(lines, axis=0)
 
 
-def columns_of(lines, count, fields):
-    per = LANES // fields
-    columns = []
-    for k in range(lines.shape[0]):
-        square = jnp.transpose(jnp.broadcast_to(lines[k : k + 1], (LANES, LANES)))
-        columns += [square[j * fields : (j + 1) * fields, :1] for j in range(per)]
-    return columns[:count]
+def down(line, fields):
+    shape = (fields, fields)
+    own = lax.broadcasted_iota(jnp.int32, shape, 1) == lax.broadcasted_iota(jnp.int32, shape, 0)
+    column = jnp.sum(jnp.where(own, jnp.broadcast_to(line, shape), 0.0), axis=1, keepdims=True)
+    return jnp.broadcast_to(column, (fields, LANES))
 
 
 def gram_kernel(fields, core_ref, right_ref, image_ref, *refs):
@@ -379,17 +387,16 @@
             qr * qr + qi * qi,
         ]
         totals = products if totals is None else [t + p for t, p in zip(totals, products)]
-    lines = flat_lines([jnp.sum(t, axis=1, keepdims=True) for t in totals], fields)
-    out_ref[...] = lines
+    out_ref[...] = flat_lines(totals, fields)
 
 
 def final_kernel(fields, right_ref, image_ref, *refs):
     *sums_refs, out_ref = refs
     units = image_ref.shape[0]
-    sums = columns_of(tree_sum([ref[...] for ref in sums_refs]), 9, fields)
-    a_real, a_imag, b_real, b_imag = [
-        jnp.broadcast_to(value, (fields, LANES)) for value in krylov_coefficients(sums)
-    ]
+    lines = tree_sum([ref[...] for ref in sums_refs])
+    per = LANES // fields
+    sums = [lines[k // per : k // per + 1, (k % per) * fields : (k % per + 1) * fields] for k in range(9)]
+    a_real, a_imag, b_real, b_imag = [down(value, fields) for value in krylov_coefficients(sums)]
     for k in range(units):
         lanes = slice(k * LANES, (k + 1) * LANES)
         r_real, r_imag = right_ref[:fields, lanes], right_ref[fields:, lanes]
@@ -494,19 +501,17 @@
     moves = in_hbm(translations.transpose(0, 2, 1, 3))
     picks = far_pick.transpose(0, 2, 1)
 
-    plan, made, windows, target_windows, moves, leaves, right = pl.pallas_call(
+    plan, made, windows, leaves, right = pl.pallas_call(
         functools.partial(begin_kernel, fields, items, width, send, rows),
         out_shape=(
             pltpu.SMEM((item_place(slots, items),), jnp.int32),
             item_shape,
             pltpu.VMEM(window_shape.shape, BF16),
-            pltpu.VMEM(window_shape.shape, BF16),
-            pltpu.VMEM((items, coefs, 2, coefs), BF16),
             jax.ShapeDtypeStruct(leaves.shape, jnp.int32),
             jax.ShapeDtypeStruct((both, panels), F32),
         ),
-        in_specs=[SMEM] * 2 + [HBM] * 9,
-        out_specs=(SMEM,) + (VMEM,) * 6,
+        in_specs=[SMEM] * 2 + [HBM] * 8,
+        out_specs=(SMEM,) + (VMEM,) * 4,
         scratch_shapes=[
             pltpu.SMEM(value.shape, jnp.int32)
             for value in (picks, leaf_of_panel, far_target, far_offset, tile_pairs)
@@ -514,10 +519,8 @@
         + [
             pltpu.SemaphoreType.DMA((7,)),
             pltpu.SemaphoreType.DMA((items, width, PIECES)),
-            pltpu.SemaphoreType.DMA((items, width, PIECES)),
-            pltpu.SemaphoreType.DMA((items,)),
         ],
-        compiler_params=params(24),
+        compiler_params=params(),
         name="begin",
     )(
         row_place,
@@ -530,7 +533,6 @@
         in_hbm(tile_pairs),
         in_hbm(right_side.reshape(both, panels)),
         expansions,
-        moves,
     )
 
     def exchanged(made):
@@ -554,15 +556,23 @@
         ]
 
     image_shape = jax.ShapeDtypeStruct((units, both, LANES), F32)
-    moved = pl.pallas_call(
-        rows_kernel,
-        out_shape=pltpu.VMEM((items, 2 * pad_coefs, coefs), BF16),
-        in_specs=[VMEM],
-        out_specs=VMEM,
-        compiler_params=params(),
+    target_windows, moved = pl.pallas_call(
+        functools.partial(fetch_kernel, items, width, slots),
+        out_shape=(
+            pltpu.VMEM(window_shape.shape, BF16),
+            pltpu.VMEM((items, 2 * pad_coefs, coefs), BF16),
+        ),
+        in_specs=[SMEM, HBM, HBM],
+        out_specs=(VMEM, VMEM),
+        scratch_shapes=[
+            pltpu.VMEM((items, coefs, 2, coefs), BF16),
+            pltpu.SemaphoreType.DMA((items, width, PIECES)),
+            pltpu.SemaphoreType.DMA((items,)),
+        ],
+        compiler_params=params(24),
         cost_estimate=pl.CostEstimate(flops=0, bytes_accessed=6 * window_shape.size, transcendentals=0),
-        name="translation_rows",
-    )(moves)
+        name="fetch",
+    )(plan, expansions, moves)
 
     def swapped(value, step):
         return lax.ppermute(value, GROUP, [(g, g ^ step) for g in range(group)])
@@ -628,18 +638,27 @@
         )(core_place, plan, leaves, mine, theirs, windows)
 
     def row_sums(lines):
-        lines = pl.pallas_call(
-            close_kernel,
-            out_shape=jax.ShapeDtypeStruct(lines.shape, F32),
-            in_specs=[VMEM] * 2,
-            out_specs=VMEM,
-            compiler_params=params(),
-            name="cores",
-        )(lines, swapped(lines, 1))
-        if rows != 4:
-            return [lax.psum(lines, "row")]
-        others = [lax.ppermute(lines, "row", [(r, r ^ step) for r in range(rows)]) for step in (3, 2, 1)]
-        return [lines] + others[::-1]
+        def added(*values):
+            return pl.pallas_call(
+                close_kernel,
+                out_shape=jax.ShapeDtypeStruct(lines.shape, F32),
+                in_specs=[VMEM] * 2,
+                out_specs=VMEM,
+                compiler_params=params(),
+                name="add",
+            )(*values)
+
+        lines = added(lines, swapped(lines, 1))
+        if not is_power(rows):
+            return (lax.psum(lines, "row"),)
+        step = 1
+        while step < rows:
+            other = lax.ppermute(lines, "row", [(r, r ^ step) for r in range(rows)])
+            if 2 * step == rows:
+                return lines, other
+            lines = added(lines, other)
+            step *= 2
+        return (lines,)
 
     partial = near(*from_neighbours(right), right)
     z_all, z_low, made = whole_sum(pair_sums(*core_parts(partial, exchanged(made), F32)))

time: 55.4 us -> 55 us (level)
  waiting for transfers between devices: 22.4 us -> 25.6 us
  local copies, waits for them, and re-layouts: 2.99 us -> 0.01 us
  starting transfers between devices: 20.7 us -> 18.3 us
  Pallas kernels: 8.3 us -> 10 us
    ppermute x3 -> x2, waiting for transfers between devices: 2.56 us -> 7.5 us  [row_sums(): other = lax.ppermute(lines, 'row', [(r, r ^ step) for r in range(rows)])]
    ppermute x3 -> x2, starting transfers between devices: 4.39 us -> 0.53 us  [row_sums(): other = lax.ppermute(lines, 'row', [(r, r ^ step) for r in range(rows)])]
    unnamed x10 -> x2, local copies, waits for them, and re-layouts: 2.99 us -> 0.01 us
    pallas_call x2 -> x3, Pallas kernels: 0.09 us -> 1.95 us  [the longest x1 1.94 us: local(): pl.pallas_call(functools.partial(fetch_kernel, items, width, slots), out_...]
    ppermute x4, waiting for transfers between devices: 5.42 us -> 3.89 us  [from_neighbours(): lax.ppermute(value, 'row', list(enumerate(targets)))]
    ppermute x4, starting transfers between devices: 7.32 us -> 8.29 us  [from_neighbours(): lax.ppermute(value, 'row', list(enumerate(targets)))]
    ppermute x10, starting transfers between devices: 8.93 us -> 9.5 us  [swapped(): return lax.ppermute(value, GROUP, [(g, g ^ step) for g in range(group)])]
  transfers between devices with their start and end apart: 19 -> 18, of which waited for: 15 -> 15; matrix products, arithmetic and copies ran while one was open for 0% -> 0% of each run, Pallas kernels for 3% -> 6%
where the time goes in v8:
time: 55 us; the launch traced here: 54.8 us
  waiting for transfers between devices  25.6 us (47%)
  starting transfers between devices  18.3 us (33%)
  Pallas kernels  10 us (18%)
  between operations  0.8 us (1%)
    ppermute x10, waiting for transfers between devices, swapped(): return lax.ppermute(value, GROUP, [(g, g ^ step) for g in range(group)])  14.2 us
    ppermute x10, starting transfers between devices, swapped(): return lax.ppermute(value, GROUP, [(g, g ^ step) for g in range(group)])  9.5 us
    ppermute x4, starting transfers between devices, from_neighbours(): lax.ppermute(value, 'row', list(enumerate(targets)))  8.29 us
    ppermute x2, waiting for transfers between devices, row_sums(): other = lax.ppermute(lines, 'row', [(r, r ^ step) for r in range(rows)])  7.5 us
    ppermute x4, waiting for transfers between devices, from_neighbours(): lax.ppermute(value, 'row', list(enumerate(targets)))  3.89 us
    pallas_call x1, Pallas kernels, local(): pl.pallas_call(functools.partial(begin_kernel, fields, items, width, send...  2.79 us
    pallas_call x1, Pallas kernels, local(): pl.pallas_call(functools.partial(fetch_kernel, items, width, slots), out_...  1.94 us
    pallas_call x1, Pallas kernels, local(): pl.pallas_call(functools.partial(final_kernel, fields), out_shape=jax.Sha...  1.49 us
  transfers between devices with their start and end apart: 18, of which 15 were waited for; matrix products, arithmetic and copies ran while one was open for 0% of the time, Pallas kernels for 6%

profile of v8, /device:TPU:0, one launch (start us, length us, event | category | flops | bytes accessed | tf_op | source)
XLA Modules:
  0.0 54.8 jit_solution(2286237853722538180)
XLA Ops:
  0.0 2.8 %begin.1 = (s32[13]{0:T(128)S(4)}, bf16[1,16,896]{2,1,0:T(8,128)(2,1)S(1)}, bf16[1,3,448,2,128]{4,3,2,1,0:T(2,128)(2,1)S(1)}, s32[24,1,128]{2,1,0:T(1,128)S(1)}, f32[32,3072]{1,0:T(8,128)S(1)}) custom-call(s32[1]{0:T(128)} %bitcast.row_ref, s32[1]{0:T(128)} %bitcast.1.own_ref, s32[4,2,4]{2,1,0:T(2,128)} %bitcast.18, s32[1,3072]{1,0:T(1,128)} %leaf_hbm.1, ...), custom_call_target="tpu_custom_call" | custom-call | tf_op jit(solution)/shard_map/begin/pallas_call | solution.py:504
  2.8 3.1 %collective-permute-start = (bf16[32,512]{1,0:T(8,128)(2,1)S(1)}, bf16[32,512]{1,0:T(8,128)(2,1)S(1)}, u32[]{:S(2)}, u32[]{:S(2)}) collective-permute-start(bf16[32,512]{1,0:T(8,128)(2,1)S(1)} %get-tuple-element.26), channel_id=1, source_target_pairs={{0,4},{4,0},{8,12},{12,8},{1,5},{5,1},{9,13},{13,9},{2,6},{6,2},{1... | collective-permute-start | bytes 98312 | tf_op jit(solution)/shard_map/ppermute | solution.py:555
  5.9 2.5 %collective-permute-start.1 = (bf16[32,512]{1,0:T(8,128)(2,1)S(1)}, bf16[32,512]{1,0:T(8,128)(2,1)S(1)}, u32[]{:S(2)}, u32[]{:S(2)}) collective-permute-start(bf16[32,512]{1,0:T(8,128)(2,1)S(1)} %get-tuple-element.27), channel_id=1, source_target_pairs={{0,12},{4,8},{8,4},{12,0},{1,13},{5,9},{9,5},{13,1},{2,14},{6,10},... | collective-permute-start | bytes 98312 | tf_op jit(solution)/shard_map/ppermute | solution.py:555
  9.1 1.9 %fetch.1 = (bf16[1,3,448,2,128]{4,3,2,1,0:T(2,128)(2,1)S(1)}, bf16[1,896,441]{2,1,0:T(8,128)(2,1)S(1)}) custom-call(s32[13]{0:T(128)S(4)} %get-tuple-element.24.plan_ref, bf16[441,24,2,128]{3,2,1,0:T(2,128)(2,1)} %bitcast.14, bf16[4,441,2,441]{3,2,1,0:T(2,128)(2,1)} %bitcast.15), custom_call_target="tpu_custom_call" | custom-call | bytes 2064384 | tf_op jit(solution)/shard_map/fetch/pallas_call | solution.py:559
  11.0 0.6 %collective-permute-done.1.two_ref = bf16[32,512]{1,0:T(8,128)(2,1)S(1)} collective-permute-done((bf16[32,512]{1,0:T(8,128)(2,1)S(1)}, bf16[32,512]{1,0:T(8,128)(2,1)S(1)}, u32[]{:S(2)}, u32[]{:S(2)}) %collective-permute-start.1) | collective-permute-done | bytes 32800 | tf_op jit(solution)/shard_map/ppermute | solution.py:555
  11.6 0.8 %near.2.partial_ref = f32[24,32,128]{2,1,0:T(8,128)S(1)} custom-call(s32[1]{0:T(128)} %bitcast.row_ref, s32[1]{0:T(128)S(6)} %copy.11.count_ref, s32[13]{0:T(128)S(4)} %get-tuple-element.24.plan_ref, bf16[32,512]{1,0:T(8,128)(2,1)S(1)} %collective-permute-done.one_ref, bf16[32,512]{1,0:T(8,128)(2,1)S(1)} %collective-permute-done.1.two_ref, ...), custom_call_target="tpu_custom_call" | custom-call | flops 67108864 | bytes 2097152 | tf_op jit(solution)/shard_map/near/pallas_call | solution.py:581
  12.4 0.7 %far.2 = (f32[4,3,32,128]{3,2,1,0:T(8,128)S(1)}, f32[4,3,32,128]{3,2,1,0:T(8,128)S(1)}) custom-call(s32[1]{0:T(128)} %bitcast.8.core_ref, s32[13]{0:T(128)S(4)} %get-tuple-element.24.plan_ref, s32[24,1,128]{2,1,0:T(1,128)S(1)} %get-tuple-element.25.leaves_ref, f32[24,32,128]{2,1,0:T(8,128)S(1)} %near.2.partial_ref, ...), custom_call_target="tpu_custom_call" | custom-call | tf_op jit(solution)/shard_map/far/pallas_call | solution.py:596
  13.3 1.3 %collective-permute-done.3.got_ref = f32[4,3,32,128]{3,2,1,0:T(8,128)S(1)} collective-permute-done((f32[4,3,32,128]{3,2,1,0:T(8,128)S(1)}, f32[4,3,32,128]{3,2,1,0:T(8,128)S(1)}, u32[]{:S(2)}, u32[]{:S(2)}) %collective-permute-start.3) | collective-permute-done | bytes 196640 | tf_op jit(solution)/shard_map/ppermute | solution.py:578
  14.6 4.2 %collective-permute-start.6 = (bf16[4,3,32,128]{3,2,1,0:T(8,128)(2,1)S(1)}, bf16[4,3,32,128]{3,2,1,0:T(8,128)(2,1)S(1)}, u32[]{:S(2)}, u32[]{:S(2)}) collective-permute-start(bf16[4,3,32,128]{3,2,1,0:T(8,128)(2,1)S(1)} %pair.2.refs_0_), channel_id=1, source_target_pairs={{0,18},{1,19},{2,16},{3,17},{16,2},{17,3},{18,0},{19,1},{4,22},{5,... | collective-permute-start | bytes 294920 | tf_op jit(solution)/shard_map/ppermute | solution.py:578
  18.8 0.6 %collective-permute-start.4 = (bf16[4,3,32,128]{3,2,1,0:T(8,128)(2,1)S(1)}, bf16[4,3,32,128]{3,2,1,0:T(8,128)(2,1)S(1)}, u32[]{:S(2)}, u32[]{:S(2)}) collective-permute-start(bf16[4,3,32,128]{3,2,1,0:T(8,128)(2,1)S(1)} %pair.2.refs_0_), channel_id=1, source_target_pairs={{0,2},{1,3},{2,0},{3,1},{16,18},{17,19},{18,16},{19,17},{4,6},{5,7... | collective-permute-start | bytes 294920 | tf_op jit(solution)/shard_map/ppermute | solution.py:578
  19.4 2.9 %collective-permute-done.6.refs_3_ = bf16[4,3,32,128]{3,2,1,0:T(8,128)(2,1)S(1)} collective-permute-done((bf16[4,3,32,128]{3,2,1,0:T(8,128)(2,1)S(1)}, bf16[4,3,32,128]{3,2,1,0:T(8,128)(2,1)S(1)}, u32[]{:S(2)}, u32[]{:S(2)}) %collective-permute-start.6) | collective-permute-done | bytes 98336 | tf_op jit(solution)/shard_map/ppermute | solution.py:578
  22.4 1.0 %collective-permute-done.5.refs_2_ = bf16[4,3,32,128]{3,2,1,0:T(8,128)(2,1)S(1)} collective-permute-done((bf16[4,3,32,128]{3,2,1,0:T(8,128)(2,1)S(1)}, bf16[4,3,32,128]{3,2,1,0:T(8,128)(2,1)S(1)}, u32[]{:S(2)}, u32[]{:S(2)}) %collective-permute-start.5) | collective-permute-done | bytes 98336 | tf_op jit(solution)/shard_map/ppermute | solution.py:578
  23.4 0.6 %collective-permute-done.4.refs_1_ = bf16[4,3,32,128]{3,2,1,0:T(8,128)(2,1)S(1)} collective-permute-done((bf16[4,3,32,128]{3,2,1,0:T(8,128)(2,1)S(1)}, bf16[4,3,32,128]{3,2,1,0:T(8,128)(2,1)S(1)}, u32[]{:S(2)}, u32[]{:S(2)}) %collective-permute-start.4) | collective-permute-done | bytes 98336 | tf_op jit(solution)/shard_map/ppermute | solution.py:578
  24.1 1.4 %collective-permute-done.7.theirs_ref = f32[4,3,32,128]{3,2,1,0:T(8,128)S(1)} collective-permute-done((f32[4,3,32,128]{3,2,1,0:T(8,128)S(1)}, f32[4,3,32,128]{3,2,1,0:T(8,128)S(1)}, u32[]{:S(2)}, u32[]{:S(2)}) %collective-permute-start.7) | collective-permute-done | bytes 196640 | tf_op jit(solution)/shard_map/ppermute | solution.py:578
  25.5 0.6 %assemble.1 = (f32[24,32,128]{2,1,0:T(8,128)S(1)}, bf16[24,32,128]{2,1,0:T(8,128)(2,1)S(1)}, bf16[1,16,896]{2,1,0:T(8,128)(2,1)S(1)}) custom-call(s32[1]{0:T(128)} %bitcast.8.core_ref, s32[13]{0:T(128)S(4)} %get-tuple-element.24.plan_ref, s32[24,1,128]{2,1,0:T(1,128)S(1)} %get-tuple-element.25.leaves_ref, f32[4,3,32,128]{3,2,1,0:T(8,128)S(1)} %close.1.mine_ref, ...), custom_call_target="tpu_custom_call" | custom-call | tf_op jit(solution)/shard_map/assemble/pallas_call | solution.py:630
  26.2 0.2 collective-permute-start.8
  26.4 2.5 %collective-permute-start.9 = (bf16[4,32,128]{2,1,0:T(8,128)(2,1)S(1)}, bf16[4,32,128]{2,1,0:T(8,128)(2,1)S(1)}, u32[]{:S(2)}, u32[]{:S(2)}) collective-permute-start(bf16[4,32,128]{2,1,0:T(8,128)(2,1)S(1)} %get-tuple-element.37), channel_id=1, source_target_pairs={{0,12},{4,8},{8,4},{12,0},{1,13},{5,9},{9,5},{13,1},{2,14},{6,10},... | collective-permute-start | bytes 98312 | tf_op jit(solution)/shard_map/ppermute | solution.py:555
  28.9 1.3 %collective-permute-done.8.one_ref = bf16[4,32,128]{2,1,0:T(8,128)(2,1)S(1)} collective-permute-done((bf16[4,32,128]{2,1,0:T(8,128)(2,1)S(1)}, bf16[4,32,128]{2,1,0:T(8,128)(2,1)S(1)}, u32[]{:S(2)}, u32[]{:S(2)}) %collective-permute-start.8) | collective-permute-done | bytes 32800 | tf_op jit(solution)/shard_map/ppermute | solution.py:555
  30.1 2.0 %collective-permute-done.9.two_ref = bf16[4,32,128]{2,1,0:T(8,128)(2,1)S(1)} collective-permute-done((bf16[4,32,128]{2,1,0:T(8,128)(2,1)S(1)}, bf16[4,32,128]{2,1,0:T(8,128)(2,1)S(1)}, u32[]{:S(2)}, u32[]{:S(2)}) %collective-permute-start.9) | collective-permute-done | bytes 32800 | tf_op jit(solution)/shard_map/ppermute | solution.py:555
  32.2 0.7 %near.3.partial_ref = f32[24,32,128]{2,1,0:T(8,128)S(1)} custom-call(s32[1]{0:T(128)} %bitcast.row_ref, s32[1]{0:T(128)S(6)} %copy.11.count_ref, s32[13]{0:T(128)S(4)} %get-tuple-element.24.plan_ref, bf16[4,32,128]{2,1,0:T(8,128)(2,1)S(1)} %collective-permute-done.8.one_ref, bf16[4,32,128]{2,1,0:T(8,128)(2,1)S(1)} %collective-permute-done.9.two_ref, ...), custom_call_target="tpu_custom_call" | custom-call | flops 67108864 | bytes 2097152 | tf_op jit(solution)/shard_map/near/pallas_call | solution.py:581
  32.9 0.7 %far.3 = (bf16[4,3,32,128]{3,2,1,0:T(8,128)(2,1)S(1)}, bf16[4,3,32,128]{3,2,1,0:T(8,128)(2,1)S(1)}) custom-call(s32[1]{0:T(128)} %bitcast.8.core_ref, s32[13]{0:T(128)S(4)} %get-tuple-element.24.plan_ref, s32[24,1,128]{2,1,0:T(1,128)S(1)} %get-tuple-element.25.leaves_ref, f32[24,32,128]{2,1,0:T(8,128)S(1)} %near.3.partial_ref, ...), custom_call_target="tpu_custom_call" | custom-call | tf_op jit(solution)/shard_map/far/pallas_call | solution.py:596
  33.6 1.3 %collective-permute-done.11.got_ref = bf16[4,3,32,128]{3,2,1,0:T(8,128)(2,1)S(1)} collective-permute-done((bf16[4,3,32,128]{3,2,1,0:T(8,128)(2,1)S(1)}, bf16[4,3,32,128]{3,2,1,0:T(8,128)(2,1)S(1)}, u32[]{:S(2)}, u32[]{:S(2)}) %collective-permute-start.11) | collective-permute-done | bytes 98336 | tf_op jit(solution)/shard_map/ppermute | solution.py:578
  35.0 3.6 %collective-permute-start.14 = (bf16[4,3,32,128]{3,2,1,0:T(8,128)(2,1)S(1)}, bf16[4,3,32,128]{3,2,1,0:T(8,128)(2,1)S(1)}, u32[]{:S(2)}, u32[]{:S(2)}) collective-permute-start(bf16[4,3,32,128]{3,2,1,0:T(8,128)(2,1)S(1)} %pair.3.refs_0_), channel_id=1, source_target_pairs={{0,18},{1,19},{2,16},{3,17},{16,2},{17,3},{18,0},{19,1},{4,22},{5,... | collective-permute-start | bytes 294920 | tf_op jit(solution)/shard_map/ppermute | solution.py:578
  38.7 0.5 collective-permute-start.12
  39.2 2.9 %collective-permute-done.14.refs_3_ = bf16[4,3,32,128]{3,2,1,0:T(8,128)(2,1)S(1)} collective-permute-done((bf16[4,3,32,128]{3,2,1,0:T(8,128)(2,1)S(1)}, bf16[4,3,32,128]{3,2,1,0:T(8,128)(2,1)S(1)}, u32[]{:S(2)}, u32[]{:S(2)}) %collective-permute-start.14) | collective-permute-done | bytes 98336 | tf_op jit(solution)/shard_map/ppermute | solution.py:578
  42.1 1.5 %collective-permute-done.13.refs_2_ = bf16[4,3,32,128]{3,2,1,0:T(8,128)(2,1)S(1)} collective-permute-done((bf16[4,3,32,128]{3,2,1,0:T(8,128)(2,1)S(1)}, bf16[4,3,32,128]{3,2,1,0:T(8,128)(2,1)S(1)}, u32[]{:S(2)}, u32[]{:S(2)}) %collective-permute-start.13) | collective-permute-done | bytes 98336 | tf_op jit(solution)/shard_map/ppermute | solution.py:578
  43.8 0.3 gram.1.refs_0_
  44.1 1.1 %collective-permute-done.15.refs_1_ = f32[2,128]{1,0:T(2,128)S(1)} collective-permute-done((f32[2,128]{1,0:T(2,128)S(1)}, f32[2,128]{1,0:T(2,128)S(1)}, u32[]{:S(2)}, u32[]{:S(2)}) %collective-permute-start.15) | collective-permute-done | bytes 1056 | tf_op jit(solution)/shard_map/ppermute | solution.py:578
  45.3 3.6 %collective-permute-done.16.refs_1_ = f32[2,128]{1,0:T(2,128)S(1)} collective-permute-done((f32[2,128]{1,0:T(2,128)S(1)}, f32[2,128]{1,0:T(2,128)S(1)}, u32[]{:S(2)}, u32[]{:S(2)}) %collective-permute-start.16) | collective-permute-done | bytes 1056 | tf_op jit(solution)/shard_map/ppermute | solution.py:656
  48.8 0.5 collective-permute-start.17
  49.4 3.9 %collective-permute-done.17.refs_1_ = f32[2,128]{1,0:T(2,128)S(1)} collective-permute-done((f32[2,128]{1,0:T(2,128)S(1)}, f32[2,128]{1,0:T(2,128)S(1)}, u32[]{:S(2)}, u32[]{:S(2)}) %collective-permute-start.17) | collective-permute-done | bytes 1056 | tf_op jit(solution)/shard_map/ppermute | solution.py:656
  53.3 1.5 %combine.1 = f32[32,3072]{1,0:T(8,128)} custom-call(f32[32,3072]{1,0:T(8,128)S(1)} %get-tuple-element.23.image_ref.here_ref.right_ref, f32[24,32,128]{2,1,0:T(8,128)S(1)} %get-tuple-element.34.image_ref, f32[2,128]{1,0:T(2,128)S(1)} %add.7.refs_0_, f32[2,128]{1,0:T(2,128)S(1)} %collective-permute-done.17.refs_1_), custom_call_target="tpu_custom_call" | custom-call | tf_op jit(solution)/shard_map/combine/pallas_call | solution.py:677
  (22 shorter events, 0.9 us)
Async XLA Ops:
  2.8 8.2 %collective-permute-start = (bf16[32,512]{1,0:T(8,128)(2,1)S(1)}, bf16[32,512]{1,0:T(8,128)(2,1)S(1)}, u32[]{:S(2)}, u32[]{:S(2)}) collective-permute-start(bf16[32,512]{1,0:T(8,128)(2,1)S(1)} %get-tuple-element.26), channel_id=1, source_target_pairs={{0,4},{4,0},{8,12},{12,8},{1,5},{5,1},{9,13},{13,9},{2,6},{6,2},{1... | collective-permute-start | bytes 98312 | tf_op jit(solution)/shard_map/ppermute | solution.py:555
  5.9 5.7 %collective-permute-start.1 = (bf16[32,512]{1,0:T(8,128)(2,1)S(1)}, bf16[32,512]{1,0:T(8,128)(2,1)S(1)}, u32[]{:S(2)}, u32[]{:S(2)}) collective-permute-start(bf16[32,512]{1,0:T(8,128)(2,1)S(1)} %get-tuple-element.27), channel_id=1, source_target_pairs={{0,12},{4,8},{8,4},{12,0},{1,13},{5,9},{9,5},{13,1},{2,14},{6,10},... | collective-permute-start | bytes 98312 | tf_op jit(solution)/shard_map/ppermute | solution.py:555
  8.4 4.0 %collective-permute-start.2 = (bf16[1,16,896]{2,1,0:T(8,128)(2,1)S(1)}, bf16[1,16,896]{2,1,0:T(8,128)(2,1)S(1)}, u32[]{:S(2)}, u32[]{:S(2)}) collective-permute-start(bf16[1,16,896]{2,1,0:T(8,128)(2,1)S(1)} %get-tuple-element.28), channel_id=1, source_target_pairs={{0,1},{1,0},{2,6},{3,7},{16,24},{17,25},{18,30},{19,31},{4,8},{5,9... | collective-permute-start | bytes 86024 | tf_op jit(solution)/shard_map/ppermute | solution.py:540
  9.1 2.6 %copy-start = (bf16[2,8,256,256]{3,2,1,0:T(8,128)(2,1)S(1)}, bf16[2,8,256,256]{3,2,1,0:T(8,128)(2,1)}, u32[]{:S(2)}) copy-start(bf16[2,8,256,256]{3,2,1,0:T(8,128)(2,1)} %tiles_ref.3) | copy-start | bytes 6291460
  13.1 1.5 %collective-permute-start.3 = (f32[4,3,32,128]{3,2,1,0:T(8,128)S(1)}, f32[4,3,32,128]{3,2,1,0:T(8,128)S(1)}, u32[]{:S(2)}, u32[]{:S(2)}) collective-permute-start(f32[4,3,32,128]{3,2,1,0:T(8,128)S(1)} %get-tuple-element.32), channel_id=1, source_target_pairs={{0,1},{1,0},{2,3},{3,2},{16,17},{17,16},{18,19},{19,18},{4,5},{5,4... | collective-permute-start | bytes 589832 | tf_op jit(solution)/shard_map/ppermute | solution.py:578
  14.6 7.7 %collective-permute-start.6 = (bf16[4,3,32,128]{3,2,1,0:T(8,128)(2,1)S(1)}, bf16[4,3,32,128]{3,2,1,0:T(8,128)(2,1)S(1)}, u32[]{:S(2)}, u32[]{:S(2)}) collective-permute-start(bf16[4,3,32,128]{3,2,1,0:T(8,128)(2,1)S(1)} %pair.2.refs_0_), channel_id=1, source_target_pairs={{0,18},{1,19},{2,16},{3,17},{16,2},{17,3},{18,0},{19,1},{4,22},{5,... | collective-permute-start | bytes 294920 | tf_op jit(solution)/shard_map/ppermute | solution.py:578
  18.8 4.6 %collective-permute-start.5 = (bf16[4,3,32,128]{3,2,1,0:T(8,128)(2,1)S(1)}, bf16[4,3,32,128]{3,2,1,0:T(8,128)(2,1)S(1)}, u32[]{:S(2)}, u32[]{:S(2)}) collective-permute-start(bf16[4,3,32,128]{3,2,1,0:T(8,128)(2,1)S(1)} %pair.2.refs_0_), channel_id=1, source_target_pairs={{0,16},{1,17},{2,18},{3,19},{16,0},{17,1},{18,2},{19,3},{4,20},{5,... | collective-permute-start | bytes 294920 | tf_op jit(solution)/shard_map/ppermute | solution.py:578
  18.8 5.2 %collective-permute-start.4 = (bf16[4,3,32,128]{3,2,1,0:T(8,128)(2,1)S(1)}, bf16[4,3,32,128]{3,2,1,0:T(8,128)(2,1)S(1)}, u32[]{:S(2)}, u32[]{:S(2)}) collective-permute-start(bf16[4,3,32,128]{3,2,1,0:T(8,128)(2,1)S(1)} %pair.2.refs_0_), channel_id=1, source_target_pairs={{0,2},{1,3},{2,0},{3,1},{16,18},{17,19},{18,16},{19,17},{4,6},{5,7... | collective-permute-start | bytes 294920 | tf_op jit(solution)/shard_map/ppermute | solution.py:578
  24.0 1.5 %collective-permute-start.7 = (f32[4,3,32,128]{3,2,1,0:T(8,128)S(1)}, f32[4,3,32,128]{3,2,1,0:T(8,128)S(1)}, u32[]{:S(2)}, u32[]{:S(2)}) collective-permute-start(f32[4,3,32,128]{3,2,1,0:T(8,128)S(1)} %close.1.mine_ref), channel_id=1, source_target_pairs={{0,1},{1,0},{2,3},{3,2},{16,17},{17,16},{18,19},{19,18},{4,5},{5,4... | collective-permute-start | bytes 589832 | tf_op jit(solution)/shard_map/ppermute | solution.py:578
  26.2 4.0 %collective-permute-start.8 = (bf16[4,32,128]{2,1,0:T(8,128)(2,1)S(1)}, bf16[4,32,128]{2,1,0:T(8,128)(2,1)S(1)}, u32[]{:S(2)}, u32[]{:S(2)}) collective-permute-start(bf16[4,32,128]{2,1,0:T(8,128)(2,1)S(1)} %get-tuple-element.36), channel_id=1, source_target_pairs={{0,4},{4,0},{8,12},{12,8},{1,5},{5,1},{9,13},{13,9},{2,6},{6,2},{1... | collective-permute-start | bytes 98312 | tf_op jit(solution)/shard_map/ppermute | solution.py:555
  26.4 5.8 %collective-permute-start.9 = (bf16[4,32,128]{2,1,0:T(8,128)(2,1)S(1)}, bf16[4,32,128]{2,1,0:T(8,128)(2,1)S(1)}, u32[]{:S(2)}, u32[]{:S(2)}) collective-permute-start(bf16[4,32,128]{2,1,0:T(8,128)(2,1)S(1)} %get-tuple-element.37), channel_id=1, source_target_pairs={{0,12},{4,8},{8,4},{12,0},{1,13},{5,9},{9,5},{13,1},{2,14},{6,10},... | collective-permute-start | bytes 98312 | tf_op jit(solution)/shard_map/ppermute | solution.py:555
  28.9 4.0 %collective-permute-start.10 = (bf16[1,16,896]{2,1,0:T(8,128)(2,1)S(1)}, bf16[1,16,896]{2,1,0:T(8,128)(2,1)S(1)}, u32[]{:S(2)}, u32[]{:S(2)}) collective-permute-start(bf16[1,16,896]{2,1,0:T(8,128)(2,1)S(1)} %get-tuple-element.38), channel_id=1, source_target_pairs={{0,1},{1,0},{2,6},{3,7},{16,24},{17,25},{18,30},{19,31},{4,8},{5,9... | collective-permute-start | bytes 86024 | tf_op jit(solution)/shard_map/ppermute | solution.py:540
  33.6 1.4 %collective-permute-start.11 = (bf16[4,3,32,128]{3,2,1,0:T(8,128)(2,1)S(1)}, bf16[4,3,32,128]{3,2,1,0:T(8,128)(2,1)S(1)}, u32[]{:S(2)}, u32[]{:S(2)}) collective-permute-start(bf16[4,3,32,128]{3,2,1,0:T(8,128)(2,1)S(1)} %get-tuple-element.40), channel_id=1, source_target_pairs={{0,1},{1,0},{2,3},{3,2},{16,17},{17,16},{18,19},{19,18},{4,5},{5,4... | collective-permute-start | bytes 294920 | tf_op jit(solution)/shard_map/ppermute | solution.py:578
  35.0 7.2 %collective-permute-start.14 = (bf16[4,3,32,128]{3,2,1,0:T(8,128)(2,1)S(1)}, bf16[4,3,32,128]{3,2,1,0:T(8,128)(2,1)S(1)}, u32[]{:S(2)}, u32[]{:S(2)}) collective-permute-start(bf16[4,3,32,128]{3,2,1,0:T(8,128)(2,1)S(1)} %pair.3.refs_0_), channel_id=1, source_target_pairs={{0,18},{1,19},{2,16},{3,17},{16,2},{17,3},{18,0},{19,1},{4,22},{5,... | collective-permute-start | bytes 294920 | tf_op jit(solution)/shard_map/ppermute | solution.py:578
  38.6 5.1 %collective-permute-start.13 = (bf16[4,3,32,128]{3,2,1,0:T(8,128)(2,1)S(1)}, bf16[4,3,32,128]{3,2,1,0:T(8,128)(2,1)S(1)}, u32[]{:S(2)}, u32[]{:S(2)}) collective-permute-start(bf16[4,3,32,128]{3,2,1,0:T(8,128)(2,1)S(1)} %pair.3.refs_0_), channel_id=1, source_target_pairs={{0,16},{1,17},{2,18},{3,19},{16,0},{17,1},{18,2},{19,3},{4,20},{5,... | collective-permute-start | bytes 294920 | tf_op jit(solution)/shard_map/ppermute | solution.py:578
  38.7 5.1 %collective-permute-start.12 = (bf16[4,3,32,128]{3,2,1,0:T(8,128)(2,1)S(1)}, bf16[4,3,32,128]{3,2,1,0:T(8,128)(2,1)S(1)}, u32[]{:S(2)}, u32[]{:S(2)}) collective-permute-start(bf16[4,3,32,128]{3,2,1,0:T(8,128)(2,1)S(1)} %pair.3.refs_0_), channel_id=1, source_target_pairs={{0,2},{1,3},{2,0},{3,1},{16,18},{17,19},{18,16},{19,17},{4,6},{5,7... | collective-permute-start | bytes 294920 | tf_op jit(solution)/shard_map/ppermute | solution.py:578
  44.0 1.2 %collective-permute-start.15 = (f32[2,128]{1,0:T(2,128)S(1)}, f32[2,128]{1,0:T(2,128)S(1)}, u32[]{:S(2)}, u32[]{:S(2)}) collective-permute-start(f32[2,128]{1,0:T(2,128)S(1)} %gram.1.refs_0_), channel_id=1, source_target_pairs={{0,1},{1,0},{2,3},{3,2},{16,17},{17,16},{18,19},{19,18},{4,5},{5,4... | collective-permute-start | bytes 3080 | tf_op jit(solution)/shard_map/ppermute | solution.py:578
  45.3 3.6 %collective-permute-start.16 = (f32[2,128]{1,0:T(2,128)S(1)}, f32[2,128]{1,0:T(2,128)S(1)}, u32[]{:S(2)}, u32[]{:S(2)}) collective-permute-start(f32[2,128]{1,0:T(2,128)S(1)} %add.6.refs_0_), channel_id=1, source_target_pairs={{0,4},{4,0},{8,12},{12,8},{1,5},{5,1},{9,13},{13,9},{2,6},{6,2},{1... | collective-permute-start | bytes 3080 | tf_op jit(solution)/shard_map/ppermute | solution.py:656
  48.8 4.5 %collective-permute-start.17 = (f32[2,128]{1,0:T(2,128)S(1)}, f32[2,128]{1,0:T(2,128)S(1)}, u32[]{:S(2)}, u32[]{:S(2)}) collective-permute-start(f32[2,128]{1,0:T(2,128)S(1)} %add.7.refs_0_), channel_id=1, source_target_pairs={{0,8},{4,12},{8,0},{12,4},{1,9},{5,13},{9,1},{13,5},{2,10},{6,14},... | collective-permute-start | bytes 3080 | tf_op jit(solution)/shard_map/ppermute | solution.py:656

commit v9 on v8

--- a/solution.py
+++ b/solution.py
@@ -352,11 +352,13 @@
     return jnp.concatenate(lines, axis=0)
 
 
-def down(line, fields):
-    shape = (fields, fields)
-    own = lax.broadcasted_iota(jnp.int32, shape, 1) == lax.broadcasted_iota(jnp.int32, shape, 0)
-    column = jnp.sum(jnp.where(own, jnp.broadcast_to(line, shape), 0.0), axis=1, keepdims=True)
-    return jnp.broadcast_to(column, (fields, LANES))
+def columns_of(lines, count, fields):
+    per = LANES // fields
+    columns = []
+    for k in range(lines.shape[0]):
+        square = jnp.transpose(jnp.broadcast_to(lines[k : k + 1], (LANES, LANES)))
+        columns += [square[j * fields : (j + 1) * fields, :1] for j in range(per)]
+    return columns[:count]
 
 
 def gram_kernel(fields, core_ref, right_ref, image_ref, *refs):
@@ -387,16 +389,15 @@
             qr * qr + qi * qi,
         ]
         totals = products if totals is None else [t + p for t, p in zip(totals, products)]
-    out_ref[...] = flat_lines(totals, fields)
-
-
-def final_kernel(fields, right_ref, image_ref, *refs):
-    *sums_refs, out_ref = refs
+    out_ref[...] = jnp.broadcast_to(flat_lines(totals, fields)[None], out_ref.shape)
+
+
+def final_kernel(fields, sums_ref, right_ref, image_ref, out_ref):
     units = image_ref.shape[0]
-    lines = tree_sum([ref[...] for ref in sums_refs])
-    per = LANES // fields
-    sums = [lines[k // per : k // per + 1, (k % per) * fields : (k % per + 1) * fields] for k in range(9)]
-    a_real, a_imag, b_real, b_imag = [down(value, fields) for value in krylov_coefficients(sums)]
+    sums = columns_of(jnp.sum(sums_ref[...], axis=0), 9, fields)
+    a_real, a_imag, b_real, b_imag = [
+        jnp.broadcast_to(value, (fields, LANES)) for value in krylov_coefficients(sums)
+    ]
     for k in range(units):
         lanes = slice(k * LANES, (k + 1) * LANES)
         r_real, r_imag = right_ref[:fields, lanes], right_ref[fields:, lanes]
@@ -637,29 +638,6 @@
             name="assemble",
         )(core_place, plan, leaves, mine, theirs, windows)
 
-    def row_sums(lines):
-        def added(*values):
-            return pl.pallas_call(
-                close_kernel,
-                out_shape=jax.ShapeDtypeStruct(lines.shape, F32),
-                in_specs=[VMEM] * 2,
-                out_specs=VMEM,
-                compiler_params=params(),
-                name="add",
-            )(*values)
-
-        lines = added(lines, swapped(lines, 1))
-        if not is_power(rows):
-            return (lax.psum(lines, "row"),)
-        step = 1
-        while step < rows:
-            other = lax.ppermute(lines, "row", [(r, r ^ step) for r in range(rows)])
-            if 2 * step == rows:
-                return lines, other
-            lines = added(lines, other)
-            step *= 2
-        return (lines,)
-
     partial = near(*from_neighbours(right), right)
     z_all, z_low, made = whole_sum(pair_sums(*core_parts(partial, exchanged(made), F32)))
     partial = near(*from_neighbours(z_low), z_low)
@@ -667,21 +645,26 @@
 
     lines = pl.pallas_call(
         functools.partial(gram_kernel, fields),
-        out_shape=jax.ShapeDtypeStruct((-(-9 * fields // LANES), LANES), F32),
+        out_shape=jax.ShapeDtypeStruct((2 * rows, -(-9 * fields // LANES), LANES), F32),
         in_specs=[SMEM] + [VMEM] * (2 + chips),
         out_specs=VMEM,
         compiler_params=params(),
         name="gram",
     )(core_place, right, z_all, *parts)
-    sums = row_sums(lines)
+    columns = lax.axis_size("col")
+    same_chip = [
+        [((g + k) // columns * rows + r) * columns + (g + k) % columns for r in range(rows) for k in range(2)]
+        for g in range(0, group, 2)
+    ]
+    sums = lax.all_to_all(lines, EVERY, 0, 0, axis_index_groups=same_chip, tiled=True)
     out = pl.pallas_call(
         functools.partial(final_kernel, fields),
         out_shape=jax.ShapeDtypeStruct((both, panels), F32),
-        in_specs=[VMEM] * (2 + len(sums)),
+        in_specs=[VMEM] * 3,
         out_specs=VMEM,
         compiler_params=params(),
         name="combine",
-    )(right, z_all, *sums)
+    )(sums, right, z_all)
     return out.reshape(right_side.shape)
 
 

time: 55 us -> 54.1 us (0.984)
  blocking collectives: 0 us -> 8.66 us
  waiting for transfers between devices: 25.6 us -> 17 us
  starting transfers between devices: 18.3 us -> 17.7 us
    all_to_all x0 -> x1, blocking collectives: none -> 8.66 us  [local(): lax.all_to_all(lines, EVERY, 0, 0, axis_index_groups=same_chip, tiled=True)]
    ppermute x2 -> x0, waiting for transfers between devices: 7.5 us -> none  [row_sums(): other = lax.ppermute(lines, 'row', [(r, r ^ step) for r in range(rows)])]
    ppermute x10 -> x9, waiting for transfers between devices: 14.2 us -> 13.1 us  [swapped(): return lax.ppermute(value, GROUP, [(g, g ^ step) for g in range(group)])]
    ppermute x10 -> x9, starting transfers between devices: 9.5 us -> 9.44 us  [swapped(): return lax.ppermute(value, GROUP, [(g, g ^ step) for g in range(group)])]
  transfers between devices with their start and end apart: 18 -> 15, of which waited for: 15 -> 12; matrix products, arithmetic and copies ran while one was open for 0% -> 0% of each run, Pallas kernels for 6% -> 6%
where the time goes in v9:
time: 54.1 us; the launch traced here: 53.8 us
  starting transfers between devices  17.7 us (33%)
  waiting for transfers between devices  17 us (31%)
  Pallas kernels  9.63 us (18%)
  blocking collectives  8.66 us (16%)
  between operations  0.79 us (1%)
    ppermute x9, waiting for transfers between devices, swapped(): return lax.ppermute(value, GROUP, [(g, g ^ step) for g in range(group)])  13.1 us
    ppermute x9, starting transfers between devices, swapped(): return lax.ppermute(value, GROUP, [(g, g ^ step) for g in range(group)])  9.44 us
    all_to_all x1, blocking collectives, local(): lax.all_to_all(lines, EVERY, 0, 0, axis_index_groups=same_chip, tiled=True)  8.66 us
    ppermute x4, starting transfers between devices, from_neighbours(): lax.ppermute(value, 'row', list(enumerate(targets)))  8.29 us
    ppermute x4, waiting for transfers between devices, from_neighbours(): lax.ppermute(value, 'row', list(enumerate(targets)))  3.88 us
    pallas_call x1, Pallas kernels, local(): pl.pallas_call(functools.partial(begin_kernel, fields, items, width, send...  2.79 us
    pallas_call x1, Pallas kernels, local(): pl.pallas_call(functools.partial(fetch_kernel, items, width, slots), out_...  1.94 us
    pallas_call x2, Pallas kernels, near(): pl.pallas_call(functools.partial(near_kernel, fields), out_shape=image_sh...  1.48 us
  transfers between devices with their start and end apart: 15, of which 12 were waited for; matrix products, arithmetic and copies ran while one was open for 0% of the time, Pallas kernels for 6%

profile of v9, /device:TPU:0, one launch (start us, length us, event | category | flops | bytes accessed | tf_op | source)
XLA Modules:
  0.0 53.8 jit_solution(14575545742027523338)
XLA Ops:
  0.0 2.8 %begin.1 = (s32[13]{0:T(128)S(4)}, bf16[1,16,896]{2,1,0:T(8,128)(2,1)S(1)}, bf16[1,3,448,2,128]{4,3,2,1,0:T(2,128)(2,1)S(1)}, s32[24,1,128]{2,1,0:T(1,128)S(1)}, f32[32,3072]{1,0:T(8,128)S(1)}) custom-call(s32[1]{0:T(128)} %bitcast.1.row_ref, s32[1]{0:T(128)} %bitcast.2.own_ref, s32[4,2,4]{2,1,0:T(2,128)} %bitcast.18, s32[1,3072]{1,0:T(1,128)} %leaf_hbm.1, ...), custom_call_target="tpu_custom_call" | custom-call | tf_op jit(solution)/shard_map/begin/pallas_call | solution.py:505
  2.8 3.1 %collective-permute-start = (bf16[32,512]{1,0:T(8,128)(2,1)S(1)}, bf16[32,512]{1,0:T(8,128)(2,1)S(1)}, u32[]{:S(2)}, u32[]{:S(2)}) collective-permute-start(bf16[32,512]{1,0:T(8,128)(2,1)S(1)} %get-tuple-element.26), channel_id=1, source_target_pairs={{0,4},{4,0},{8,12},{12,8},{1,5},{5,1},{9,13},{13,9},{2,6},{6,2},{1... | collective-permute-start | bytes 98312 | tf_op jit(solution)/shard_map/ppermute | solution.py:556
  5.9 2.5 %collective-permute-start.1 = (bf16[32,512]{1,0:T(8,128)(2,1)S(1)}, bf16[32,512]{1,0:T(8,128)(2,1)S(1)}, u32[]{:S(2)}, u32[]{:S(2)}) collective-permute-start(bf16[32,512]{1,0:T(8,128)(2,1)S(1)} %get-tuple-element.27), channel_id=1, source_target_pairs={{0,12},{4,8},{8,4},{12,0},{1,13},{5,9},{9,5},{13,1},{2,14},{6,10},... | collective-permute-start | bytes 98312 | tf_op jit(solution)/shard_map/ppermute | solution.py:556
  9.1 1.9 %fetch.1 = (bf16[1,3,448,2,128]{4,3,2,1,0:T(2,128)(2,1)S(1)}, bf16[1,896,441]{2,1,0:T(8,128)(2,1)S(1)}) custom-call(s32[13]{0:T(128)S(4)} %get-tuple-element.24.plan_ref, bf16[441,24,2,128]{3,2,1,0:T(2,128)(2,1)} %bitcast.14, bf16[4,441,2,441]{3,2,1,0:T(2,128)(2,1)} %bitcast.15), custom_call_target="tpu_custom_call" | custom-call | bytes 2064384 | tf_op jit(solution)/shard_map/fetch/pallas_call | solution.py:560
  11.0 0.6 %collective-permute-done.1.two_ref = bf16[32,512]{1,0:T(8,128)(2,1)S(1)} collective-permute-done((bf16[32,512]{1,0:T(8,128)(2,1)S(1)}, bf16[32,512]{1,0:T(8,128)(2,1)S(1)}, u32[]{:S(2)}, u32[]{:S(2)}) %collective-permute-start.1) | collective-permute-done | bytes 32800 | tf_op jit(solution)/shard_map/ppermute | solution.py:556
  11.6 0.8 %near.2.partial_ref = f32[24,32,128]{2,1,0:T(8,128)S(1)} custom-call(s32[1]{0:T(128)} %bitcast.1.row_ref, s32[1]{0:T(128)S(6)} %copy.11.count_ref, s32[13]{0:T(128)S(4)} %get-tuple-element.24.plan_ref, bf16[32,512]{1,0:T(8,128)(2,1)S(1)} %collective-permute-done.one_ref, bf16[32,512]{1,0:T(8,128)(2,1)S(1)} %collective-permute-done.1.two_ref, ...), custom_call_target="tpu_custom_call" | custom-call | flops 67108864 | bytes 2097152 | tf_op jit(solution)/shard_map/near/pallas_call | solution.py:582
  12.4 0.7 %far.2 = (f32[4,3,32,128]{3,2,1,0:T(8,128)S(1)}, f32[4,3,32,128]{3,2,1,0:T(8,128)S(1)}) custom-call(s32[1]{0:T(128)} %bitcast.core_ref, s32[13]{0:T(128)S(4)} %get-tuple-element.24.plan_ref, s32[24,1,128]{2,1,0:T(1,128)S(1)} %get-tuple-element.25.leaves_ref, f32[24,32,128]{2,1,0:T(8,128)S(1)} %near.2.partial_ref, ...), custom_call_target="tpu_custom_call" | custom-call | tf_op jit(solution)/shard_map/far/pallas_call | solution.py:597
  13.1 0.2 collective-permute-start.3
  13.3 1.3 %collective-permute-done.3.got_ref = f32[4,3,32,128]{3,2,1,0:T(8,128)S(1)} collective-permute-done((f32[4,3,32,128]{3,2,1,0:T(8,128)S(1)}, f32[4,3,32,128]{3,2,1,0:T(8,128)S(1)}, u32[]{:S(2)}, u32[]{:S(2)}) %collective-permute-start.3) | collective-permute-done | bytes 196640 | tf_op jit(solution)/shard_map/ppermute | solution.py:579
  14.6 4.2 %collective-permute-start.6 = (bf16[4,3,32,128]{3,2,1,0:T(8,128)(2,1)S(1)}, bf16[4,3,32,128]{3,2,1,0:T(8,128)(2,1)S(1)}, u32[]{:S(2)}, u32[]{:S(2)}) collective-permute-start(bf16[4,3,32,128]{3,2,1,0:T(8,128)(2,1)S(1)} %pair.2.refs_0_), channel_id=1, source_target_pairs={{0,18},{1,19},{2,16},{3,17},{16,2},{17,3},{18,0},{19,1},{4,22},{5,... | collective-permute-start | bytes 294920 | tf_op jit(solution)/shard_map/ppermute | solution.py:579
  18.8 0.6 %collective-permute-start.4 = (bf16[4,3,32,128]{3,2,1,0:T(8,128)(2,1)S(1)}, bf16[4,3,32,128]{3,2,1,0:T(8,128)(2,1)S(1)}, u32[]{:S(2)}, u32[]{:S(2)}) collective-permute-start(bf16[4,3,32,128]{3,2,1,0:T(8,128)(2,1)S(1)} %pair.2.refs_0_), channel_id=1, source_target_pairs={{0,2},{1,3},{2,0},{3,1},{16,18},{17,19},{18,16},{19,17},{4,6},{5,7... | collective-permute-start | bytes 294920 | tf_op jit(solution)/shard_map/ppermute | solution.py:579
  19.4 2.9 %collective-permute-done.6.refs_3_ = bf16[4,3,32,128]{3,2,1,0:T(8,128)(2,1)S(1)} collective-permute-done((bf16[4,3,32,128]{3,2,1,0:T(8,128)(2,1)S(1)}, bf16[4,3,32,128]{3,2,1,0:T(8,128)(2,1)S(1)}, u32[]{:S(2)}, u32[]{:S(2)}) %collective-permute-start.6) | collective-permute-done | bytes 98336 | tf_op jit(solution)/shard_map/ppermute | solution.py:579
  22.4 1.0 %collective-permute-done.5.refs_2_ = bf16[4,3,32,128]{3,2,1,0:T(8,128)(2,1)S(1)} collective-permute-done((bf16[4,3,32,128]{3,2,1,0:T(8,128)(2,1)S(1)}, bf16[4,3,32,128]{3,2,1,0:T(8,128)(2,1)S(1)}, u32[]{:S(2)}, u32[]{:S(2)}) %collective-permute-start.5) | collective-permute-done | bytes 98336 | tf_op jit(solution)/shard_map/ppermute | solution.py:579
  23.4 0.6 %collective-permute-done.4.refs_1_ = bf16[4,3,32,128]{3,2,1,0:T(8,128)(2,1)S(1)} collective-permute-done((bf16[4,3,32,128]{3,2,1,0:T(8,128)(2,1)S(1)}, bf16[4,3,32,128]{3,2,1,0:T(8,128)(2,1)S(1)}, u32[]{:S(2)}, u32[]{:S(2)}) %collective-permute-start.4) | collective-permute-done | bytes 98336 | tf_op jit(solution)/shard_map/ppermute | solution.py:579
  24.1 1.4 %collective-permute-done.7.theirs_ref = f32[4,3,32,128]{3,2,1,0:T(8,128)S(1)} collective-permute-done((f32[4,3,32,128]{3,2,1,0:T(8,128)S(1)}, f32[4,3,32,128]{3,2,1,0:T(8,128)S(1)}, u32[]{:S(2)}, u32[]{:S(2)}) %collective-permute-start.7) | collective-permute-done | bytes 196640 | tf_op jit(solution)/shard_map/ppermute | solution.py:579
  25.5 0.6 %assemble.1 = (f32[24,32,128]{2,1,0:T(8,128)S(1)}, bf16[24,32,128]{2,1,0:T(8,128)(2,1)S(1)}, bf16[1,16,896]{2,1,0:T(8,128)(2,1)S(1)}) custom-call(s32[1]{0:T(128)} %bitcast.core_ref, s32[13]{0:T(128)S(4)} %get-tuple-element.24.plan_ref, s32[24,1,128]{2,1,0:T(1,128)S(1)} %get-tuple-element.25.leaves_ref, f32[4,3,32,128]{3,2,1,0:T(8,128)S(1)} %close.1.mine_ref, ...), custom_call_target="tpu_custom_call" | custom-call | tf_op jit(solution)/shard_map/assemble/pallas_call | solution.py:631
  26.1 0.2 collective-permute-start.8
  26.4 2.5 %collective-permute-start.9 = (bf16[4,32,128]{2,1,0:T(8,128)(2,1)S(1)}, bf16[4,32,128]{2,1,0:T(8,128)(2,1)S(1)}, u32[]{:S(2)}, u32[]{:S(2)}) collective-permute-start(bf16[4,32,128]{2,1,0:T(8,128)(2,1)S(1)} %get-tuple-element.37), channel_id=1, source_target_pairs={{0,12},{4,8},{8,4},{12,0},{1,13},{5,9},{9,5},{13,1},{2,14},{6,10},... | collective-permute-start | bytes 98312 | tf_op jit(solution)/shard_map/ppermute | solution.py:556
  28.9 1.3 %collective-permute-done.8.one_ref = bf16[4,32,128]{2,1,0:T(8,128)(2,1)S(1)} collective-permute-done((bf16[4,32,128]{2,1,0:T(8,128)(2,1)S(1)}, bf16[4,32,128]{2,1,0:T(8,128)(2,1)S(1)}, u32[]{:S(2)}, u32[]{:S(2)}) %collective-permute-start.8) | collective-permute-done | bytes 32800 | tf_op jit(solution)/shard_map/ppermute | solution.py:556
  30.1 2.0 %collective-permute-done.9.two_ref = bf16[4,32,128]{2,1,0:T(8,128)(2,1)S(1)} collective-permute-done((bf16[4,32,128]{2,1,0:T(8,128)(2,1)S(1)}, bf16[4,32,128]{2,1,0:T(8,128)(2,1)S(1)}, u32[]{:S(2)}, u32[]{:S(2)}) %collective-permute-start.9) | collective-permute-done | bytes 32800 | tf_op jit(solution)/shard_map/ppermute | solution.py:556
  32.1 0.7 %near.3.partial_ref = f32[24,32,128]{2,1,0:T(8,128)S(1)} custom-call(s32[1]{0:T(128)} %bitcast.1.row_ref, s32[1]{0:T(128)S(6)} %copy.11.count_ref, s32[13]{0:T(128)S(4)} %get-tuple-element.24.plan_ref, bf16[4,32,128]{2,1,0:T(8,128)(2,1)S(1)} %collective-permute-done.8.one_ref, bf16[4,32,128]{2,1,0:T(8,128)(2,1)S(1)} %collective-permute-done.9.two_ref, ...), custom_call_target="tpu_custom_call" | custom-call | flops 67108864 | bytes 2097152 | tf_op jit(solution)/shard_map/near/pallas_call | solution.py:582
  32.9 0.7 %far.3 = (bf16[4,3,32,128]{3,2,1,0:T(8,128)(2,1)S(1)}, bf16[4,3,32,128]{3,2,1,0:T(8,128)(2,1)S(1)}) custom-call(s32[1]{0:T(128)} %bitcast.core_ref, s32[13]{0:T(128)S(4)} %get-tuple-element.24.plan_ref, s32[24,1,128]{2,1,0:T(1,128)S(1)} %get-tuple-element.25.leaves_ref, f32[24,32,128]{2,1,0:T(8,128)S(1)} %near.3.partial_ref, ...), custom_call_target="tpu_custom_call" | custom-call | tf_op jit(solution)/shard_map/far/pallas_call | solution.py:597
  33.6 1.3 %collective-permute-done.11.got_ref = bf16[4,3,32,128]{3,2,1,0:T(8,128)(2,1)S(1)} collective-permute-done((bf16[4,3,32,128]{3,2,1,0:T(8,128)(2,1)S(1)}, bf16[4,3,32,128]{3,2,1,0:T(8,128)(2,1)S(1)}, u32[]{:S(2)}, u32[]{:S(2)}) %collective-permute-start.11) | collective-permute-done | bytes 98336 | tf_op jit(solution)/shard_map/ppermute | solution.py:579
  35.0 3.6 %collective-permute-start.14 = (bf16[4,3,32,128]{3,2,1,0:T(8,128)(2,1)S(1)}, bf16[4,3,32,128]{3,2,1,0:T(8,128)(2,1)S(1)}, u32[]{:S(2)}, u32[]{:S(2)}) collective-permute-start(bf16[4,3,32,128]{3,2,1,0:T(8,128)(2,1)S(1)} %pair.3.refs_0_), channel_id=1, source_target_pairs={{0,18},{1,19},{2,16},{3,17},{16,2},{17,3},{18,0},{19,1},{4,22},{5,... | collective-permute-start | bytes 294920 | tf_op jit(solution)/shard_map/ppermute | solution.py:579
  38.6 0.1 collective-permute-start.13
  38.7 0.5 collective-permute-start.12
  39.2 2.9 %collective-permute-done.14.refs_3_ = bf16[4,3,32,128]{3,2,1,0:T(8,128)(2,1)S(1)} collective-permute-done((bf16[4,3,32,128]{3,2,1,0:T(8,128)(2,1)S(1)}, bf16[4,3,32,128]{3,2,1,0:T(8,128)(2,1)S(1)}, u32[]{:S(2)}, u32[]{:S(2)}) %collective-permute-start.14) | collective-permute-done | bytes 98336 | tf_op jit(solution)/shard_map/ppermute | solution.py:579
  42.1 1.5 %collective-permute-done.13.refs_2_ = bf16[4,3,32,128]{3,2,1,0:T(8,128)(2,1)S(1)} collective-permute-done((bf16[4,3,32,128]{3,2,1,0:T(8,128)(2,1)S(1)}, bf16[4,3,32,128]{3,2,1,0:T(8,128)(2,1)S(1)}, u32[]{:S(2)}, u32[]{:S(2)}) %collective-permute-start.13) | collective-permute-done | bytes 98336 | tf_op jit(solution)/shard_map/ppermute | solution.py:579
  43.6 0.2 collective-permute-done.12.refs_1_
  43.8 0.3 gram.1
  44.0 8.7 %all_to_all.5.sums_ref = f32[8,2,128]{2,1,0:T(2,128)S(1)} all-to-all(f32[8,2,128]{2,1,0:T(2,128)S(1)} %gram.1), channel_id=1, replica_groups={{0,1,4,5,8,9,12,13},{2,3,6,7,10,11,14,15},{16,17,20,21,24,25,28,29},{18..., dimensions={0} | all-to-all | bytes 16384 | tf_op jit(solution)/shard_map/all_to_all | solution.py:659
  52.7 1.1 %combine.1 = f32[32,3072]{1,0:T(8,128)} custom-call(f32[8,2,128]{2,1,0:T(2,128)S(1)} %all_to_all.5.sums_ref, f32[32,3072]{1,0:T(8,128)S(1)} %get-tuple-element.23.image_ref.here_ref.right_ref, f32[24,32,128]{2,1,0:T(8,128)S(1)} %get-tuple-element.34.image_ref), custom_call_target="tpu_custom_call" | custom-call | tf_op jit(solution)/shard_map/combine/pallas_call | solution.py:660
  (15 shorter events, 0.3 us)
Async XLA Ops:
  2.8 8.2 %collective-permute-start = (bf16[32,512]{1,0:T(8,128)(2,1)S(1)}, bf16[32,512]{1,0:T(8,128)(2,1)S(1)}, u32[]{:S(2)}, u32[]{:S(2)}) collective-permute-start(bf16[32,512]{1,0:T(8,128)(2,1)S(1)} %get-tuple-element.26), channel_id=1, source_target_pairs={{0,4},{4,0},{8,12},{12,8},{1,5},{5,1},{9,13},{13,9},{2,6},{6,2},{1... | collective-permute-start | bytes 98312 | tf_op jit(solution)/shard_map/ppermute | solution.py:556
  5.9 5.7 %collective-permute-start.1 = (bf16[32,512]{1,0:T(8,128)(2,1)S(1)}, bf16[32,512]{1,0:T(8,128)(2,1)S(1)}, u32[]{:S(2)}, u32[]{:S(2)}) collective-permute-start(bf16[32,512]{1,0:T(8,128)(2,1)S(1)} %get-tuple-element.27), channel_id=1, source_target_pairs={{0,12},{4,8},{8,4},{12,0},{1,13},{5,9},{9,5},{13,1},{2,14},{6,10},... | collective-permute-start | bytes 98312 | tf_op jit(solution)/shard_map/ppermute | solution.py:556
  8.4 4.0 %collective-permute-start.2 = (bf16[1,16,896]{2,1,0:T(8,128)(2,1)S(1)}, bf16[1,16,896]{2,1,0:T(8,128)(2,1)S(1)}, u32[]{:S(2)}, u32[]{:S(2)}) collective-permute-start(bf16[1,16,896]{2,1,0:T(8,128)(2,1)S(1)} %get-tuple-element.28), channel_id=1, source_target_pairs={{0,1},{1,0},{2,6},{3,7},{16,24},{17,25},{18,30},{19,31},{4,8},{5,9... | collective-permute-start | bytes 86024 | tf_op jit(solution)/shard_map/ppermute | solution.py:541
  9.0 2.6 %copy-start = (bf16[2,8,256,256]{3,2,1,0:T(8,128)(2,1)S(1)}, bf16[2,8,256,256]{3,2,1,0:T(8,128)(2,1)}, u32[]{:S(2)}) copy-start(bf16[2,8,256,256]{3,2,1,0:T(8,128)(2,1)} %tiles_ref.3) | copy-start | bytes 6291460
  13.1 1.5 %collective-permute-start.3 = (f32[4,3,32,128]{3,2,1,0:T(8,128)S(1)}, f32[4,3,32,128]{3,2,1,0:T(8,128)S(1)}, u32[]{:S(2)}, u32[]{:S(2)}) collective-permute-start(f32[4,3,32,128]{3,2,1,0:T(8,128)S(1)} %get-tuple-element.32), channel_id=1, source_target_pairs={{0,1},{1,0},{2,3},{3,2},{16,17},{17,16},{18,19},{19,18},{4,5},{5,4... | collective-permute-start | bytes 589832 | tf_op jit(solution)/shard_map/ppermute | solution.py:579
  14.6 7.7 %collective-permute-start.6 = (bf16[4,3,32,128]{3,2,1,0:T(8,128)(2,1)S(1)}, bf16[4,3,32,128]{3,2,1,0:T(8,128)(2,1)S(1)}, u32[]{:S(2)}, u32[]{:S(2)}) collective-permute-start(bf16[4,3,32,128]{3,2,1,0:T(8,128)(2,1)S(1)} %pair.2.refs_0_), channel_id=1, source_target_pairs={{0,18},{1,19},{2,16},{3,17},{16,2},{17,3},{18,0},{19,1},{4,22},{5,... | collective-permute-start | bytes 294920 | tf_op jit(solution)/shard_map/ppermute | solution.py:579
  18.8 4.6 %collective-permute-start.5 = (bf16[4,3,32,128]{3,2,1,0:T(8,128)(2,1)S(1)}, bf16[4,3,32,128]{3,2,1,0:T(8,128)(2,1)S(1)}, u32[]{:S(2)}, u32[]{:S(2)}) collective-permute-start(bf16[4,3,32,128]{3,2,1,0:T(8,128)(2,1)S(1)} %pair.2.refs_0_), channel_id=1, source_target_pairs={{0,16},{1,17},{2,18},{3,19},{16,0},{17,1},{18,2},{19,3},{4,20},{5,... | collective-permute-start | bytes 294920 | tf_op jit(solution)/shard_map/ppermute | solution.py:579
  18.8 5.2 %collective-permute-start.4 = (bf16[4,3,32,128]{3,2,1,0:T(8,128)(2,1)S(1)}, bf16[4,3,32,128]{3,2,1,0:T(8,128)(2,1)S(1)}, u32[]{:S(2)}, u32[]{:S(2)}) collective-permute-start(bf16[4,3,32,128]{3,2,1,0:T(8,128)(2,1)S(1)} %pair.2.refs_0_), channel_id=1, source_target_pairs={{0,2},{1,3},{2,0},{3,1},{16,18},{17,19},{18,16},{19,17},{4,6},{5,7... | collective-permute-start | bytes 294920 | tf_op jit(solution)/shard_map/ppermute | solution.py:579
  24.0 1.5 %collective-permute-start.7 = (f32[4,3,32,128]{3,2,1,0:T(8,128)S(1)}, f32[4,3,32,128]{3,2,1,0:T(8,128)S(1)}, u32[]{:S(2)}, u32[]{:S(2)}) collective-permute-start(f32[4,3,32,128]{3,2,1,0:T(8,128)S(1)} %close.1.mine_ref), channel_id=1, source_target_pairs={{0,1},{1,0},{2,3},{3,2},{16,17},{17,16},{18,19},{19,18},{4,5},{5,4... | collective-permute-start | bytes 589832 | tf_op jit(solution)/shard_map/ppermute | solution.py:579
  26.1 4.0 %collective-permute-start.8 = (bf16[4,32,128]{2,1,0:T(8,128)(2,1)S(1)}, bf16[4,32,128]{2,1,0:T(8,128)(2,1)S(1)}, u32[]{:S(2)}, u32[]{:S(2)}) collective-permute-start(bf16[4,32,128]{2,1,0:T(8,128)(2,1)S(1)} %get-tuple-element.36), channel_id=1, source_target_pairs={{0,4},{4,0},{8,12},{12,8},{1,5},{5,1},{9,13},{13,9},{2,6},{6,2},{1... | collective-permute-start | bytes 98312 | tf_op jit(solution)/shard_map/ppermute | solution.py:556
  26.4 5.8 %collective-permute-start.9 = (bf16[4,32,128]{2,1,0:T(8,128)(2,1)S(1)}, bf16[4,32,128]{2,1,0:T(8,128)(2,1)S(1)}, u32[]{:S(2)}, u32[]{:S(2)}) collective-permute-start(bf16[4,32,128]{2,1,0:T(8,128)(2,1)S(1)} %get-tuple-element.37), channel_id=1, source_target_pairs={{0,12},{4,8},{8,4},{12,0},{1,13},{5,9},{9,5},{13,1},{2,14},{6,10},... | collective-permute-start | bytes 98312 | tf_op jit(solution)/shard_map/ppermute | solution.py:556
  28.9 4.0 %collective-permute-start.10 = (bf16[1,16,896]{2,1,0:T(8,128)(2,1)S(1)}, bf16[1,16,896]{2,1,0:T(8,128)(2,1)S(1)}, u32[]{:S(2)}, u32[]{:S(2)}) collective-permute-start(bf16[1,16,896]{2,1,0:T(8,128)(2,1)S(1)} %get-tuple-element.38), channel_id=1, source_target_pairs={{0,1},{1,0},{2,6},{3,7},{16,24},{17,25},{18,30},{19,31},{4,8},{5,9... | collective-permute-start | bytes 86024 | tf_op jit(solution)/shard_map/ppermute | solution.py:541
  33.6 1.4 %collective-permute-start.11 = (bf16[4,3,32,128]{3,2,1,0:T(8,128)(2,1)S(1)}, bf16[4,3,32,128]{3,2,1,0:T(8,128)(2,1)S(1)}, u32[]{:S(2)}, u32[]{:S(2)}) collective-permute-start(bf16[4,3,32,128]{3,2,1,0:T(8,128)(2,1)S(1)} %get-tuple-element.40), channel_id=1, source_target_pairs={{0,1},{1,0},{2,3},{3,2},{16,17},{17,16},{18,19},{19,18},{4,5},{5,4... | collective-permute-start | bytes 294920 | tf_op jit(solution)/shard_map/ppermute | solution.py:579
  35.0 7.2 %collective-permute-start.14 = (bf16[4,3,32,128]{3,2,1,0:T(8,128)(2,1)S(1)}, bf16[4,3,32,128]{3,2,1,0:T(8,128)(2,1)S(1)}, u32[]{:S(2)}, u32[]{:S(2)}) collective-permute-start(bf16[4,3,32,128]{3,2,1,0:T(8,128)(2,1)S(1)} %pair.3.refs_0_), channel_id=1, source_target_pairs={{0,18},{1,19},{2,16},{3,17},{16,2},{17,3},{18,0},{19,1},{4,22},{5,... | collective-permute-start | bytes 294920 | tf_op jit(solution)/shard_map/ppermute | solution.py:579
  38.6 5.1 %collective-permute-start.13 = (bf16[4,3,32,128]{3,2,1,0:T(8,128)(2,1)S(1)}, bf16[4,3,32,128]{3,2,1,0:T(8,128)(2,1)S(1)}, u32[]{:S(2)}, u32[]{:S(2)}) collective-permute-start(bf16[4,3,32,128]{3,2,1,0:T(8,128)(2,1)S(1)} %pair.3.refs_0_), channel_id=1, source_target_pairs={{0,16},{1,17},{2,18},{3,19},{16,0},{17,1},{18,2},{19,3},{4,20},{5,... | collective-permute-start | bytes 294920 | tf_op jit(solution)/shard_map/ppermute | solution.py:579
  38.7 5.1 %collective-permute-start.12 = (bf16[4,3,32,128]{3,2,1,0:T(8,128)(2,1)S(1)}, bf16[4,3,32,128]{3,2,1,0:T(8,128)(2,1)S(1)}, u32[]{:S(2)}, u32[]{:S(2)}) collective-permute-start(bf16[4,3,32,128]{3,2,1,0:T(8,128)(2,1)S(1)} %pair.3.refs_0_), channel_id=1, source_target_pairs={{0,2},{1,3},{2,0},{3,1},{16,18},{17,19},{18,16},{19,17},{4,6},{5,7... | collective-permute-start | bytes 294920 | tf_op jit(solution)/shard_map/ppermute | solution.py:579

commit v10 on v9

--- a/solution.py
+++ b/solution.py
@@ -14,6 +14,7 @@
 GROUP = ("grp", "col")
 CODES = 0
 PER_ITEM = 5
+ITEM_REST = 2 * LANES
 PIECES = 4
 EVERY = ("grp", "row", "col")
 
@@ -22,6 +23,7 @@
 SMEM = pl.BlockSpec(memory_space=pltpu.SMEM)
 VMEM = pl.BlockSpec(memory_space=pltpu.VMEM)
 HBM = pl.BlockSpec(memory_space=pltpu.HBM)
+ANY = pl.BlockSpec(memory_space=pl.ANY)
 
 
 def dot_nn(left, right):
@@ -136,11 +138,17 @@
 
     @pl.when(even)
     def _():
-        one_ref[...], two_ref[...] = last, first
+        one_ref[...], two_ref[...] = first, last
 
     @pl.when(jnp.logical_not(even))
     def _():
-        one_ref[...], two_ref[...] = first, last
+        one_ref[...], two_ref[...] = last, first
+
+
+def join_kernel(one_ref, two_ref, after_ref, out_ref):
+    del after_ref
+    edge = one_ref.shape[0]
+    out_ref[:edge], out_ref[edge:] = one_ref[...], two_ref[...]
 
 
 def begin_kernel(
@@ -233,11 +241,11 @@
             copy.wait()
 
 
-def near_sources(row_ref, one_ref, two_ref, here_ref, units, ext):
+def near_sources(core_ref, row_ref, one_ref, two_ref, here_ref, units, ext):
     edge = (ext.shape[0] - units) // 2
     even = lax.rem(row_ref[0], 2) == 0
-    one_at = jnp.where(even, edge + units, 0)
-    two_at = jnp.where(even, 0, edge + units)
+    one_at = jnp.where(even, 0, edge + units)
+    two_at = jnp.where(even, edge + units, 0)
     if len(here_ref.shape) == 2:
         for k in range(edge):
             lanes = slice(k * LANES, (k + 1) * LANES)
@@ -245,17 +253,45 @@
             ext[two_at + k] = two_ref[:, lanes].astype(ext.dtype)
         for k in range(units):
             ext[edge + k] = here_ref[:, k * LANES : (k + 1) * LANES]
-    else:
-        ext[pl.ds(one_at, edge)] = one_ref[...]
-        ext[pl.ds(two_at, edge)] = two_ref[...]
-        ext[edge : edge + units] = here_ref[...]
+        return
+    half = edge // 2
+    for ref, core in ((one_ref, core_ref[0]), (two_ref, 1 - core_ref[0])):
+        for k in range(half):
+            ext[one_at + 2 * k + core] = ref[k]
+            ext[two_at + 2 * k + core] = ref[half + k]
+    ext[edge : edge + units] = here_ref[...]
+
+
+def part(total, core, keep_ref, give_ref):
+    for k in range(keep_ref.shape[0]):
+        keep_ref[k] = total[2 * k + core].astype(keep_ref.dtype)
+        give_ref[k] = total[2 * k + 1 - core].astype(give_ref.dtype)
 
 
 def near_kernel(
-    fields, row_ref, count_ref, plan_ref, one_ref, two_ref, here_ref, tiles_ref, out_ref, ext
+    fields, core_ref, row_ref, count_ref, plan_ref, one_ref, two_ref, here_ref, tiles_ref, out_ref, ext
 ):
-    near_sources(row_ref, one_ref, two_ref, here_ref, out_ref.shape[0], ext)
+    near_sources(core_ref, row_ref, one_ref, two_ref, here_ref, out_ref.shape[0], ext)
     out_ref[...] = jnp.zeros_like(out_ref)
+    near_slots(fields, count_ref, plan_ref, tiles_ref, out_ref, ext)
+
+
+def last_near_kernel(
+    fields, core_ref, row_ref, count_ref, plan_ref, one_ref, two_ref, here_ref, tiles_ref, image_ref,
+    keep_ref, give_ref, ext, total,
+):
+    near_sources(core_ref, row_ref, one_ref, two_ref, here_ref, total.shape[0], ext)
+    total[...] = jnp.zeros_like(total)
+    items, width = image_ref.shape[:2]
+    for i in range(items):
+        unit = plan_ref[item_place(tiles_ref.shape[1], i) + 3]
+        for k in range(width):
+            total[unit + k] += image_ref[i, k]
+    near_slots(fields, count_ref, plan_ref, tiles_ref, total, ext)
+    part(total, core_ref[0], keep_ref, give_ref)
+
+
+def near_slots(fields, count_ref, plan_ref, tiles_ref, out_ref, ext):
     slots, tile = tiles_ref.shape[1], tiles_ref.shape[2]
     per = tile // LANES
     for s in range(slots):
@@ -277,12 +313,29 @@
     fields, items, width, slots, core_ref, plan_ref, leaves_ref, partial_ref, item_ref, trans_ref, window_ref,
     keep_ref, give_ref, total,
 ):
-    units = partial_ref.shape[0]
-    total[0:units] = partial_ref[...]
-    if total.shape[0] > units:
-        total[units:] = jnp.zeros((total.shape[0] - units, *total.shape[1:]), F32)
-    for i in range(items):
-        plain = item_ref[i].astype(F32)
+    total[...] = partial_ref[...]
+
+    def add(i, unit, image):
+        for k in range(width):
+            total[unit + k] += image[:, k * LANES : (k + 1) * LANES]
+
+    far_images(fields, items, width, slots, plan_ref, leaves_ref, item_ref, trans_ref, window_ref, add)
+    part(total, core_ref[0], keep_ref, give_ref)
+
+
+def first_far_kernel(
+    fields, items, width, slots, plan_ref, leaves_ref, item_ref, trans_ref, window_ref, image_ref
+):
+    def store(i, unit, image):
+        for k in range(width):
+            image_ref[i, k] = image[:, k * LANES : (k + 1) * LANES]
+
+    far_images(fields, items, width, slots, plan_ref, leaves_ref, item_ref, trans_ref, window_ref, store)
+
+
+def far_images(fields, items, width, slots, plan_ref, leaves_ref, item_ref, trans_ref, window_ref, give):
+    for i in range(items):
+        plain = item_ref[i, :, : trans_ref.shape[1]].astype(F32)
         odd = odd_lanes(plain.shape)
         turned = jnp.where(odd, from_left(plain), -from_right(plain))
         rows = jnp.concatenate([plain, turned], axis=0).astype(BF16)
@@ -297,13 +350,7 @@
         leaf, unit = plan_ref[place + 2], plan_ref[place + 3]
         mask = window_mask(leaves_ref, leaf, unit, 2 * fields, width)
         image = jnp.where(mask, dot_nn(rows, expansions), 0.0)
-        for k in range(width):
-            total[unit + k] += image[:, k * LANES : (k + 1) * LANES]
-    chips, share = keep_ref.shape[:2]
-    core = core_ref[0]
-    for c in range(chips):
-        keep_ref[c] = total[pl.ds((2 * c + core) * share, share)].astype(keep_ref.dtype)
-        give_ref[c] = total[pl.ds((2 * c + 1 - core) * share, share)].astype(give_ref.dtype)
+        give(i, unit, image)
 
 
 def pair_kernel(keep_ref, got_ref, out_ref):
@@ -316,27 +363,29 @@
     return values[0]
 
 
+def by_step(parts):
+    return [parts[0], *reversed(parts[1:])]
+
+
 def close_kernel(*refs):
-    refs[-1][...] = tree_sum([ref[...].astype(F32) for ref in refs[:-1]])
+    refs[-1][...] = tree_sum([ref[...].astype(F32) for ref in by_step(refs[:-1])])
 
 
 def assemble_kernel(
     fields, items, width, slots, core_ref, plan_ref, leaves_ref, mine_ref, theirs_ref, window_ref,
-    out_ref, low_ref, made_ref, whole,
+    out_ref, low_ref, made_ref,
 ):
-    chips, share = mine_ref.shape[:2]
-    units = out_ref.shape[0]
     core = core_ref[0]
-    for chip in range(chips):
-        whole[pl.ds((2 * chip + core) * share, share)] = mine_ref[chip]
-        whole[pl.ds((2 * chip + 1 - core) * share, share)] = theirs_ref[chip]
-    out_ref[...] = whole[0:units]
-    low_ref[...] = whole[0:units].astype(BF16)
+    for k in range(mine_ref.shape[0]):
+        for ref, unit in ((mine_ref, 2 * k + core), (theirs_ref, 2 * k + 1 - core)):
+            out_ref[unit] = ref[k]
+            low_ref[unit] = ref[k].astype(BF16)
     for i in range(items):
         place = item_place(slots, i)
-        made_ref[i] = multi_rows(
+        made = multi_rows(
             fields, width, plan_ref[place], plan_ref[place + 1], leaves_ref, low_ref, window_ref.at[i]
-        ).astype(BF16)
+        )
+        made_ref[i, :, : made.shape[1]] = made.astype(BF16)
 
 
 def flat_lines(totals, fields):
@@ -363,19 +412,12 @@
 
 def gram_kernel(fields, core_ref, right_ref, image_ref, *refs):
     *parts, out_ref = refs
-    units = image_ref.shape[0]
-    chips, share = parts[0].shape[:2]
     totals = None
-    for k in range(chips * share):
-        chip, within = divmod(k, share)
-        unit = (2 * chip + core_ref[0]) * share + within
-        place = jnp.minimum(unit, units - 1)
-        r = right_ref[:, pl.ds(pl.multiple_of(place * LANES, LANES), LANES)]
-        z = image_ref[place]
-        q = tree_sum([part[chip, within].astype(F32) for part in parts])
-        if 2 * chips * share > units:
-            r = jnp.where(unit < units, r, 0.0)
-            z = jnp.where(unit < units, z, 0.0)
+    for k in range(parts[0].shape[0]):
+        unit = 2 * k + core_ref[0]
+        r = right_ref[:, pl.ds(pl.multiple_of(unit * LANES, LANES), LANES)]
+        z = image_ref[unit]
+        q = tree_sum([part[k].astype(F32) for part in by_step(parts)])
         (rr, ri), (zr, zi), (qr, qi) = [(v[:fields], v[fields:]) for v in (r, z, q)]
         products = [
             rr * rr + ri * ri,
@@ -475,14 +517,13 @@
     own = lax.axis_index("grp") * lax.axis_size("col") + lax.axis_index("col")
     both = 2 * fields
     units = panels // LANES
-    share = -(-units // group)
     edge = REACH * tile
     edge_units = edge // LANES
     width = tile // LANES + 1
     items, routes = item_route(rows, group, lax.axis_size("col"), send)
 
     assert rows % 2 == 0
-    neighbours = [[r + 1 - 2 * (r % 2) for r in range(rows)], [(r - 1 + 2 * (r % 2)) % rows for r in range(rows)]]
+    neighbours = [[(r - 1 + 2 * (r % 2)) % rows for r in range(rows)], [r + 1 - 2 * (r % 2) for r in range(rows)]]
     own_place, row_place = own.reshape(1), row_here.reshape(1)
     core_place = lax.rem(own, 2).reshape(1)
     slots = near_tiles.shape[1]
@@ -491,7 +532,8 @@
     assert group == 2 * chips and chips & (chips - 1) == 0 and LANES % fields == 0
     window_shape = jax.ShapeDtypeStruct((items, width, pad_coefs, 2, LANES), BF16)
     item_shape = jax.ShapeDtypeStruct((items, fields, 2 * pad_coefs), BF16)
-    part_shape = (share, both, LANES)
+    half_units = (units // 2, both, LANES)
+    assert units % 2 == 0 and edge_units % 2 == 0
 
     def in_hbm(value):
         return pltpu.with_memory_space_constraint(value, pltpu.HBM)
@@ -543,7 +585,7 @@
         return parts[0] if len(parts) == 1 else jnp.concatenate(parts)
 
     def from_neighbours(image):
-        edge_shape = (both, edge) if image.ndim == 2 else (edge_units, both, LANES)
+        edge_shape = (both, edge) if image.ndim == 2 else (edge_units // 2, both, LANES)
         one, two = pl.pallas_call(
             edge_kernel,
             out_shape=(jax.ShapeDtypeStruct(edge_shape, BF16),) * 2,
@@ -582,7 +624,7 @@
         return pl.pallas_call(
             functools.partial(near_kernel, fields),
             out_shape=image_shape,
-            in_specs=[SMEM] * 3 + [VMEM] * 4,
+            in_specs=[SMEM] * 4 + [VMEM] * 4,
             out_specs=VMEM,
             scratch_shapes=[pltpu.VMEM((units + 2 * edge_units, both, LANES), low.dtype)],
             compiler_params=params(),
@@ -590,19 +632,45 @@
                 flops=8 * fields * near_tiles.size // 2, bytes_accessed=2 * near_tiles.size, transcendentals=0
             ),
             name="near",
-        )(row_place, tile_count, plan, one, two, low, near_tiles)
-
-    def core_parts(partial, taken, dtype):
-        half_shape = jax.ShapeDtypeStruct((chips, *part_shape), dtype)
+        )(core_place, row_place, tile_count, plan, one, two, low, near_tiles)
+
+    def core_parts(partial, taken):
+        half_shape = jax.ShapeDtypeStruct(half_units, F32)
         keep, give = pl.pallas_call(
             functools.partial(far_kernel, fields, items, width, slots),
             out_shape=(half_shape, half_shape),
             in_specs=[SMEM, SMEM] + [VMEM] * 5,
             out_specs=(VMEM, VMEM),
-            scratch_shapes=[pltpu.VMEM((share * group, both, LANES), F32)],
+            scratch_shapes=[pltpu.VMEM(image_shape.shape, F32)],
             compiler_params=params(),
             name="far",
         )(core_place, plan, leaves, partial, taken, moved, target_windows)
+        return keep, swapped(give, 1)
+
+    def first_far(taken):
+        return pl.pallas_call(
+            functools.partial(first_far_kernel, fields, items, width, slots),
+            out_shape=jax.ShapeDtypeStruct((items, width, both, LANES), F32),
+            in_specs=[SMEM] + [VMEM] * 4,
+            out_specs=VMEM,
+            compiler_params=params(),
+            name="first_far",
+        )(plan, leaves, taken, moved, target_windows)
+
+    def last_core_parts(one, two, low, image):
+        half_shape = jax.ShapeDtypeStruct(half_units, BF16)
+        keep, give = pl.pallas_call(
+            functools.partial(last_near_kernel, fields),
+            out_shape=(half_shape, half_shape),
+            in_specs=[SMEM] * 4 + [VMEM] * 5,
+            out_specs=(VMEM, VMEM),
+            scratch_shapes=[
+                pltpu.VMEM((units + 2 * edge_units, both, LANES), low.dtype),
+                pltpu.VMEM(image_shape.shape, F32),
+            ],
+            compiler_params=params(),
+            name="last_near",
+        )(core_place, row_place, tile_count, plan, one, two, low, near_tiles, image)
         return keep, swapped(give, 1)
 
     def pair_sums(keep, got):
@@ -615,33 +683,50 @@
             name="pair",
         )(keep, got)
         arrived = {step: swapped(pair, 2 * step) for step in range(chips - 1, 0, -1)}
-        return [pair] + [arrived[step] for step in range(1, chips)]
-
-    def whole_sum(parts):
-        mine = pl.pallas_call(
+        return [pair] + list(arrived.values())
+
+    def half_sum(parts):
+        return pl.pallas_call(
             close_kernel,
-            out_shape=jax.ShapeDtypeStruct((chips, *part_shape), F32),
+            out_shape=jax.ShapeDtypeStruct(half_units, F32),
             in_specs=[VMEM] * chips,
             out_specs=VMEM,
             compiler_params=params(),
             name="close",
         )(*parts)
-        theirs = swapped(mine, 1)
-        low_shape = jax.ShapeDtypeStruct((units, both, LANES), BF16)
+
+    def whole(mine, theirs):
         return pl.pallas_call(
             functools.partial(assemble_kernel, fields, items, width, slots),
-            out_shape=(image_shape, low_shape, item_shape),
+            out_shape=(
+                image_shape,
+                jax.ShapeDtypeStruct(image_shape.shape, BF16),
+                jax.ShapeDtypeStruct((items, fields, 2 * pad_coefs + ITEM_REST), BF16),
+            ),
             in_specs=[SMEM, SMEM] + [VMEM] * 4,
             out_specs=(VMEM,) * 3,
-            scratch_shapes=[pltpu.VMEM((share * group, both, LANES), F32)],
             compiler_params=params(),
             name="assemble",
         )(core_place, plan, leaves, mine, theirs, windows)
 
+    def joined_edges(one, two, made):
+        return pl.pallas_call(
+            join_kernel,
+            out_shape=jax.ShapeDtypeStruct((edge_units, both, LANES), BF16),
+            in_specs=[VMEM, VMEM, ANY],
+            out_specs=VMEM,
+            compiler_params=params(),
+            name="join",
+        )(one, two, made)
+
     partial = near(*from_neighbours(right), right)
-    z_all, z_low, made = whole_sum(pair_sums(*core_parts(partial, exchanged(made), F32)))
-    partial = near(*from_neighbours(z_low), z_low)
-    parts = pair_sums(*core_parts(partial, exchanged(made), BF16))
+    mine = half_sum(pair_sums(*core_parts(partial, exchanged(made))))
+    theirs = swapped(mine, 1)
+    one, two = from_neighbours(mine)
+    z_all, z_low, made = whole(mine, theirs)
+    edges = joined_edges(one, two, made)
+    image = first_far(exchanged(made))
+    parts = pair_sums(*last_core_parts(edges, swapped(edges, 1), z_low, image))
 
     lines = pl.pallas_call(
         functools.partial(gram_kernel, fields),

time: 54.1 us -> 53 us (0.980)
  starting transfers between devices: 17.7 us -> 16.8 us
    pallas_call x2 -> x5, Pallas kernels: 0.62 us -> 1.98 us  [the longest x1 0.75 us: last_core_parts(): pl.pallas_call(functools.partial(last_near_kernel, fields), out_shape=(ha...]
    ppermute x4, starting transfers between devices: 8.29 us -> 7.15 us  [from_neighbours(): lax.ppermute(value, 'row', list(enumerate(targets)))]
    pallas_call x2 -> x1, Pallas kernels: 1.48 us -> 0.75 us  [near(): pl.pallas_call(functools.partial(near_kernel, fields), out_shape=image_sh...]
    pallas_call x2 -> x1, Pallas kernels: 1.32 us -> 0.66 us  [core_parts(): pl.pallas_call(functools.partial(far_kernel, fields, items, width, slots)...]
    ppermute x9 -> x10, waiting for transfers between devices: 13.1 us -> 12.6 us  [swapped(): return lax.ppermute(value, GROUP, [(g, g ^ step) for g in range(group)])]
    ppermute x9 -> x10, starting transfers between devices: 9.44 us -> 9.63 us  [swapped(): return lax.ppermute(value, GROUP, [(g, g ^ step) for g in range(group)])]
  transfers between devices with their start and end apart: 15 -> 16, of which waited for: 12 -> 10; matrix products, arithmetic and copies ran while one was open for 0% -> 0% of each run, Pallas kernels for 6% -> 7%
where the time goes in v10:
time: 53 us; the launch traced here: 52.7 us
  starting transfers between devices  16.8 us (32%)
  waiting for transfers between devices  16.8 us (32%)
  Pallas kernels  9.61 us (18%)
  blocking collectives  8.66 us (16%)
  between operations  0.79 us (1%)
    ppermute x10, waiting for transfers between devices, swapped(): return lax.ppermute(value, GROUP, [(g, g ^ step) for g in range(group)])  12.6 us
    ppermute x10, starting transfers between devices, swapped(): return lax.ppermute(value, GROUP, [(g, g ^ step) for g in range(group)])  9.63 us
    all_to_all x1, blocking collectives, local(): lax.all_to_all(lines, EVERY, 0, 0, axis_index_groups=same_chip, tiled=True)  8.66 us
    ppermute x4, starting transfers between devices, from_neighbours(): lax.ppermute(value, 'row', list(enumerate(targets)))  7.15 us
    ppermute x4, waiting for transfers between devices, from_neighbours(): lax.ppermute(value, 'row', list(enumerate(targets)))  4.25 us
    pallas_call x1, Pallas kernels, local(): pl.pallas_call(functools.partial(begin_kernel, fields, items, width, send...  2.79 us
    pallas_call x1, Pallas kernels, local(): pl.pallas_call(functools.partial(fetch_kernel, items, width, slots), out_...  1.94 us
    pallas_call x1, Pallas kernels, local(): pl.pallas_call(functools.partial(final_kernel, fields), out_shape=jax.Sha...  1.12 us
  transfers between devices with their start and end apart: 16, of which 10 were waited for; matrix products, arithmetic and copies ran while one was open for 0% of the time, Pallas kernels for 7%

profile of v10, /device:TPU:0, one launch (start us, length us, event | category | flops | bytes accessed | tf_op | source)
XLA Modules:
  0.0 52.7 jit_solution(4772492549020734058)
XLA Ops:
  0.0 2.8 %begin.1 = (s32[13]{0:T(128)S(4)}, bf16[1,16,896]{2,1,0:T(8,128)(2,1)S(1)}, bf16[1,3,448,2,128]{4,3,2,1,0:T(2,128)(2,1)S(1)}, s32[24,1,128]{2,1,0:T(1,128)S(1)}, f32[32,3072]{1,0:T(8,128)S(1)}) custom-call(s32[1]{0:T(128)} %bitcast.1.row_ref, s32[1]{0:T(128)} %bitcast.2.own_ref, s32[4,2,4]{2,1,0:T(2,128)} %bitcast.18, s32[1,3072]{1,0:T(1,128)} %leaf_hbm.1, ...), custom_call_target="tpu_custom_call" | custom-call | tf_op jit(solution)/shard_map/begin/pallas_call | solution.py:547
  2.8 5.1 %collective-permute-start = (bf16[32,512]{1,0:T(8,128)(2,1)S(1)}, bf16[32,512]{1,0:T(8,128)(2,1)S(1)}, u32[]{:S(2)}, u32[]{:S(2)}) collective-permute-start(bf16[32,512]{1,0:T(8,128)(2,1)S(1)} %get-tuple-element.26), channel_id=1, source_target_pairs={{0,12},{4,8},{8,4},{12,0},{1,13},{5,9},{9,5},{13,1},{2,14},{6,10},... | collective-permute-start | bytes 98312 | tf_op jit(solution)/shard_map/ppermute | solution.py:598
  8.6 1.9 %fetch.1 = (bf16[1,3,448,2,128]{4,3,2,1,0:T(2,128)(2,1)S(1)}, bf16[1,896,441]{2,1,0:T(8,128)(2,1)S(1)}) custom-call(s32[13]{0:T(128)S(4)} %get-tuple-element.24.plan_ref, bf16[441,24,2,128]{3,2,1,0:T(2,128)(2,1)} %bitcast.14, bf16[4,441,2,441]{3,2,1,0:T(2,128)(2,1)} %bitcast.15), custom_call_target="tpu_custom_call" | custom-call | bytes 2064384 | tf_op jit(solution)/shard_map/fetch/pallas_call | solution.py:602
  10.6 1.3 %collective-permute-done.1.two_ref = bf16[32,512]{1,0:T(8,128)(2,1)S(1)} collective-permute-done((bf16[32,512]{1,0:T(8,128)(2,1)S(1)}, bf16[32,512]{1,0:T(8,128)(2,1)S(1)}, u32[]{:S(2)}, u32[]{:S(2)}) %collective-permute-start.1) | collective-permute-done | bytes 32800 | tf_op jit(solution)/shard_map/ppermute | solution.py:598
  11.9 0.8 %near.1.partial_ref = f32[24,32,128]{2,1,0:T(8,128)S(1)} custom-call(s32[1]{0:T(128)} %bitcast.core_ref, s32[1]{0:T(128)} %bitcast.1.row_ref, s32[1]{0:T(128)S(6)} %copy.11.count_ref, s32[13]{0:T(128)S(4)} %get-tuple-element.24.plan_ref, bf16[32,512]{1,0:T(8,128)(2,1)S(1)} %collective-permute-done.one_ref, ...), custom_call_target="tpu_custom_call" | custom-call | flops 67108864 | bytes 2097152 | tf_op jit(solution)/shard_map/near/pallas_call | solution.py:624
  12.6 0.7 %far.1 = (f32[12,32,128]{2,1,0:T(8,128)S(1)}, f32[12,32,128]{2,1,0:T(8,128)S(1)}) custom-call(s32[1]{0:T(128)} %bitcast.core_ref, s32[13]{0:T(128)S(4)} %get-tuple-element.24.plan_ref, s32[24,1,128]{2,1,0:T(1,128)S(1)} %get-tuple-element.25.leaves_ref, f32[24,32,128]{2,1,0:T(8,128)S(1)} %near.1.partial_ref, ...), custom_call_target="tpu_custom_call" | custom-call | tf_op jit(solution)/shard_map/far/pallas_call | solution.py:639
  13.3 0.1 collective-permute-start.3
  13.4 1.4 %collective-permute-done.3.got_ref = f32[12,32,128]{2,1,0:T(8,128)S(1)} collective-permute-done((f32[12,32,128]{2,1,0:T(8,128)S(1)}, f32[12,32,128]{2,1,0:T(8,128)S(1)}, u32[]{:S(2)}, u32[]{:S(2)}) %collective-permute-start.3) | collective-permute-done | bytes 196640 | tf_op jit(solution)/shard_map/ppermute | solution.py:621
  14.8 3.5 %collective-permute-start.4 = (bf16[12,32,128]{2,1,0:T(8,128)(2,1)S(1)}, bf16[12,32,128]{2,1,0:T(8,128)(2,1)S(1)}, u32[]{:S(2)}, u32[]{:S(2)}) collective-permute-start(bf16[12,32,128]{2,1,0:T(8,128)(2,1)S(1)} %pair.2.refs_0_), channel_id=1, source_target_pairs={{0,18},{1,19},{2,16},{3,17},{16,2},{17,3},{18,0},{19,1},{4,22},{5,... | collective-permute-start | bytes 294920 | tf_op jit(solution)/shard_map/ppermute | solution.py:621
  18.3 0.6 %collective-permute-start.5 = (bf16[12,32,128]{2,1,0:T(8,128)(2,1)S(1)}, bf16[12,32,128]{2,1,0:T(8,128)(2,1)S(1)}, u32[]{:S(2)}, u32[]{:S(2)}) collective-permute-start(bf16[12,32,128]{2,1,0:T(8,128)(2,1)S(1)} %pair.2.refs_0_), channel_id=1, source_target_pairs={{0,16},{1,17},{2,18},{3,19},{16,0},{17,1},{18,2},{19,3},{4,20},{5,... | collective-permute-start | bytes 294920 | tf_op jit(solution)/shard_map/ppermute | solution.py:621
  18.9 0.1 collective-permute-start.6
  19.0 2.9 %collective-permute-done.4.refs_1_ = bf16[12,32,128]{2,1,0:T(8,128)(2,1)S(1)} collective-permute-done((bf16[12,32,128]{2,1,0:T(8,128)(2,1)S(1)}, bf16[12,32,128]{2,1,0:T(8,128)(2,1)S(1)}, u32[]{:S(2)}, u32[]{:S(2)}) %collective-permute-start.4) | collective-permute-done | bytes 98336 | tf_op jit(solution)/shard_map/ppermute | solution.py:621
  21.9 1.9 %collective-permute-done.5.refs_2_ = bf16[12,32,128]{2,1,0:T(8,128)(2,1)S(1)} collective-permute-done((bf16[12,32,128]{2,1,0:T(8,128)(2,1)S(1)}, bf16[12,32,128]{2,1,0:T(8,128)(2,1)S(1)}, u32[]{:S(2)}, u32[]{:S(2)}) %collective-permute-start.5) | collective-permute-done | bytes 98336 | tf_op jit(solution)/shard_map/ppermute | solution.py:621
  23.9 0.1 collective-permute-start.7
  24.0 1.6 %collective-permute-start.8 = (bf16[2,32,128]{2,1,0:T(8,128)(2,1)S(1)}, bf16[2,32,128]{2,1,0:T(8,128)(2,1)S(1)}, u32[]{:S(2)}, u32[]{:S(2)}) collective-permute-start(bf16[2,32,128]{2,1,0:T(8,128)(2,1)S(1)} %get-tuple-element.35), channel_id=1, source_target_pairs={{0,12},{4,8},{8,4},{12,0},{1,13},{5,9},{9,5},{13,1},{2,14},{6,10},... | collective-permute-start | bytes 49160 | tf_op jit(solution)/shard_map/ppermute | solution.py:598
  25.6 0.4 collective-permute-start.9
  26.0 0.6 %assemble.1 = (f32[24,32,128]{2,1,0:T(8,128)S(1)}, bf16[24,32,128]{2,1,0:T(8,128)(2,1)S(1)}, bf16[1,16,1152]{2,1,0:T(8,128)(2,1)S(1)}) custom-call(s32[1]{0:T(128)} %bitcast.core_ref, s32[13]{0:T(128)S(4)} %get-tuple-element.24.plan_ref, s32[24,1,128]{2,1,0:T(1,128)S(1)} %get-tuple-element.25.leaves_ref, f32[12,32,128]{2,1,0:T(8,128)S(1)} %close.1.mine_ref.image_ref, ...), custom_call_target="tpu_custom_call" | custom-call | tf_op jit(solution)/shard_map/assemble/pallas_call | solution.py:699
  26.6 0.0 collective-permute-start.11
  26.6 3.0 %collective-permute-done.8.one_ref = bf16[2,32,128]{2,1,0:T(8,128)(2,1)S(1)} collective-permute-done((bf16[2,32,128]{2,1,0:T(8,128)(2,1)S(1)}, bf16[2,32,128]{2,1,0:T(8,128)(2,1)S(1)}, u32[]{:S(2)}, u32[]{:S(2)}) %collective-permute-start.8) | collective-permute-done | bytes 16416 | tf_op jit(solution)/shard_map/ppermute | solution.py:598
  29.6 0.6 %first_far.1.image_ref = f32[1,3,32,128]{3,2,1,0:T(8,128)S(1)} custom-call(s32[13]{0:T(128)S(4)} %get-tuple-element.24.plan_ref, s32[24,1,128]{2,1,0:T(1,128)S(1)} %get-tuple-element.25.leaves_ref, bf16[1,16,1152]{2,1,0:T(8,128)(2,1)S(1)} %collective-permute-done.11.item_ref, bf16[1,896,441]{2,1,0:T(8,128)(2,1)S(1)} %get-tuple-element.29.trans_ref, ...), custom_call_target="tpu_custom_call" | custom-call | tf_op jit(solution)/shard_map/first_far/pallas_call | solution.py:651
  30.2 0.6 %collective-permute-done.10.two_ref = bf16[4,32,128]{2,1,0:T(8,128)(2,1)S(1)} collective-permute-done((bf16[4,32,128]{2,1,0:T(8,128)(2,1)S(1)}, bf16[4,32,128]{2,1,0:T(8,128)(2,1)S(1)}, u32[]{:S(2)}, u32[]{:S(2)}) %collective-permute-start.10) | collective-permute-done | bytes 32800 | tf_op jit(solution)/shard_map/ppermute | solution.py:621
  30.8 0.8 %last_near.1 = (bf16[12,32,128]{2,1,0:T(8,128)(2,1)S(1)}, bf16[12,32,128]{2,1,0:T(8,128)(2,1)S(1)}) custom-call(s32[1]{0:T(128)} %bitcast.core_ref, s32[1]{0:T(128)} %bitcast.1.row_ref, s32[1]{0:T(128)S(6)} %copy.11.count_ref, s32[13]{0:T(128)S(4)} %get-tuple-element.24.plan_ref, bf16[4,32,128]{2,1,0:T(8,128)(2,1)S(1)} %join.1.one_ref, ...), custom_call_target="tpu_custom_call" | custom-call | tf_op jit(solution)/shard_map/last_near/pallas_call | solution.py:662
  31.6 0.2 collective-permute-start.12
  31.8 1.1 %collective-permute-done.12.got_ref = bf16[12,32,128]{2,1,0:T(8,128)(2,1)S(1)} collective-permute-done((bf16[12,32,128]{2,1,0:T(8,128)(2,1)S(1)}, bf16[12,32,128]{2,1,0:T(8,128)(2,1)S(1)}, u32[]{:S(2)}, u32[]{:S(2)}) %collective-permute-start.12) | collective-permute-done | bytes 98336 | tf_op jit(solution)/shard_map/ppermute | solution.py:621
  33.0 4.5 %collective-permute-start.13 = (bf16[12,32,128]{2,1,0:T(8,128)(2,1)S(1)}, bf16[12,32,128]{2,1,0:T(8,128)(2,1)S(1)}, u32[]{:S(2)}, u32[]{:S(2)}) collective-permute-start(bf16[12,32,128]{2,1,0:T(8,128)(2,1)S(1)} %pair.3.refs_0_), channel_id=1, source_target_pairs={{0,18},{1,19},{2,16},{3,17},{16,2},{17,3},{18,0},{19,1},{4,22},{5,... | collective-permute-start | bytes 294920 | tf_op jit(solution)/shard_map/ppermute | solution.py:621
  37.5 0.6 %collective-permute-start.15 = (bf16[12,32,128]{2,1,0:T(8,128)(2,1)S(1)}, bf16[12,32,128]{2,1,0:T(8,128)(2,1)S(1)}, u32[]{:S(2)}, u32[]{:S(2)}) collective-permute-start(bf16[12,32,128]{2,1,0:T(8,128)(2,1)S(1)} %pair.3.refs_0_), channel_id=1, source_target_pairs={{0,2},{1,3},{2,0},{3,1},{16,18},{17,19},{18,16},{19,17},{4,6},{5,7... | collective-permute-start | bytes 294920 | tf_op jit(solution)/shard_map/ppermute | solution.py:621
  38.1 2.9 %collective-permute-done.13.refs_1_ = bf16[12,32,128]{2,1,0:T(8,128)(2,1)S(1)} collective-permute-done((bf16[12,32,128]{2,1,0:T(8,128)(2,1)S(1)}, bf16[12,32,128]{2,1,0:T(8,128)(2,1)S(1)}, u32[]{:S(2)}, u32[]{:S(2)}) %collective-permute-start.13) | collective-permute-done | bytes 98336 | tf_op jit(solution)/shard_map/ppermute | solution.py:621
  41.0 1.0 %collective-permute-done.14.refs_2_ = bf16[12,32,128]{2,1,0:T(8,128)(2,1)S(1)} collective-permute-done((bf16[12,32,128]{2,1,0:T(8,128)(2,1)S(1)}, bf16[12,32,128]{2,1,0:T(8,128)(2,1)S(1)}, u32[]{:S(2)}, u32[]{:S(2)}) %collective-permute-start.14) | collective-permute-done | bytes 98336 | tf_op jit(solution)/shard_map/ppermute | solution.py:621
  42.1 0.6 %collective-permute-done.15.refs_3_ = bf16[12,32,128]{2,1,0:T(8,128)(2,1)S(1)} collective-permute-done((bf16[12,32,128]{2,1,0:T(8,128)(2,1)S(1)}, bf16[12,32,128]{2,1,0:T(8,128)(2,1)S(1)}, u32[]{:S(2)}, u32[]{:S(2)}) %collective-permute-start.15) | collective-permute-done | bytes 98336 | tf_op jit(solution)/shard_map/ppermute | solution.py:621
  42.7 0.3 gram.1
  42.9 8.7 %all_to_all.5.sums_ref = f32[8,2,128]{2,1,0:T(2,128)S(1)} all-to-all(f32[8,2,128]{2,1,0:T(2,128)S(1)} %gram.1), channel_id=1, replica_groups={{0,1,4,5,8,9,12,13},{2,3,6,7,10,11,14,15},{16,17,20,21,24,25,28,29},{18..., dimensions={0} | all-to-all | bytes 16384 | tf_op jit(solution)/shard_map/all_to_all | solution.py:744
  51.6 1.1 %combine.1 = f32[32,3072]{1,0:T(8,128)} custom-call(f32[8,2,128]{2,1,0:T(2,128)S(1)} %all_to_all.5.sums_ref, f32[32,3072]{1,0:T(8,128)S(1)} %get-tuple-element.23.image_ref.here_ref.right_ref, f32[24,32,128]{2,1,0:T(8,128)S(1)} %get-tuple-element.34.image_ref), custom_call_target="tpu_custom_call" | custom-call | tf_op jit(solution)/shard_map/combine/pallas_call | solution.py:745
  (18 shorter events, 0.2 us)
Async XLA Ops:
  2.8 7.7 %collective-permute-start = (bf16[32,512]{1,0:T(8,128)(2,1)S(1)}, bf16[32,512]{1,0:T(8,128)(2,1)S(1)}, u32[]{:S(2)}, u32[]{:S(2)}) collective-permute-start(bf16[32,512]{1,0:T(8,128)(2,1)S(1)} %get-tuple-element.26), channel_id=1, source_target_pairs={{0,12},{4,8},{8,4},{12,0},{1,13},{5,9},{9,5},{13,1},{2,14},{6,10},... | collective-permute-start | bytes 98312 | tf_op jit(solution)/shard_map/ppermute | solution.py:598
  7.9 3.9 %collective-permute-start.1 = (bf16[32,512]{1,0:T(8,128)(2,1)S(1)}, bf16[32,512]{1,0:T(8,128)(2,1)S(1)}, u32[]{:S(2)}, u32[]{:S(2)}) collective-permute-start(bf16[32,512]{1,0:T(8,128)(2,1)S(1)} %get-tuple-element.27), channel_id=1, source_target_pairs={{0,4},{4,0},{8,12},{12,8},{1,5},{5,1},{9,13},{13,9},{2,6},{6,2},{1... | collective-permute-start | bytes 98312 | tf_op jit(solution)/shard_map/ppermute | solution.py:598
  7.9 4.7 %collective-permute-start.2 = (bf16[1,16,896]{2,1,0:T(8,128)(2,1)S(1)}, bf16[1,16,896]{2,1,0:T(8,128)(2,1)S(1)}, u32[]{:S(2)}, u32[]{:S(2)}) collective-permute-start(bf16[1,16,896]{2,1,0:T(8,128)(2,1)S(1)} %get-tuple-element.28), channel_id=1, source_target_pairs={{0,1},{1,0},{2,6},{3,7},{16,24},{17,25},{18,30},{19,31},{4,8},{5,9... | collective-permute-start | bytes 86024 | tf_op jit(solution)/shard_map/ppermute | solution.py:583
  8.6 3.3 %copy-start = (bf16[2,8,256,256]{3,2,1,0:T(8,128)(2,1)S(1)}, bf16[2,8,256,256]{3,2,1,0:T(8,128)(2,1)}, u32[]{:S(2)}) copy-start(bf16[2,8,256,256]{3,2,1,0:T(8,128)(2,1)} %tiles_ref.3) | copy-start | bytes 6291460
  13.3 1.5 %collective-permute-start.3 = (f32[12,32,128]{2,1,0:T(8,128)S(1)}, f32[12,32,128]{2,1,0:T(8,128)S(1)}, u32[]{:S(2)}, u32[]{:S(2)}) collective-permute-start(f32[12,32,128]{2,1,0:T(8,128)S(1)} %get-tuple-element.32), channel_id=1, source_target_pairs={{0,1},{1,0},{2,3},{3,2},{16,17},{17,16},{18,19},{19,18},{4,5},{5,4... | collective-permute-start | bytes 589832 | tf_op jit(solution)/shard_map/ppermute | solution.py:621
  14.8 7.1 %collective-permute-start.4 = (bf16[12,32,128]{2,1,0:T(8,128)(2,1)S(1)}, bf16[12,32,128]{2,1,0:T(8,128)(2,1)S(1)}, u32[]{:S(2)}, u32[]{:S(2)}) collective-permute-start(bf16[12,32,128]{2,1,0:T(8,128)(2,1)S(1)} %pair.2.refs_0_), channel_id=1, source_target_pairs={{0,18},{1,19},{2,16},{3,17},{16,2},{17,3},{18,0},{19,1},{4,22},{5,... | collective-permute-start | bytes 294920 | tf_op jit(solution)/shard_map/ppermute | solution.py:621
  18.3 5.5 %collective-permute-start.5 = (bf16[12,32,128]{2,1,0:T(8,128)(2,1)S(1)}, bf16[12,32,128]{2,1,0:T(8,128)(2,1)S(1)}, u32[]{:S(2)}, u32[]{:S(2)}) collective-permute-start(bf16[12,32,128]{2,1,0:T(8,128)(2,1)S(1)} %pair.2.refs_0_), channel_id=1, source_target_pairs={{0,16},{1,17},{2,18},{3,19},{16,0},{17,1},{18,2},{19,3},{4,20},{5,... | collective-permute-start | bytes 294920 | tf_op jit(solution)/shard_map/ppermute | solution.py:621
  18.9 4.9 %collective-permute-start.6 = (bf16[12,32,128]{2,1,0:T(8,128)(2,1)S(1)}, bf16[12,32,128]{2,1,0:T(8,128)(2,1)S(1)}, u32[]{:S(2)}, u32[]{:S(2)}) collective-permute-start(bf16[12,32,128]{2,1,0:T(8,128)(2,1)S(1)} %pair.2.refs_0_), channel_id=1, source_target_pairs={{0,2},{1,3},{2,0},{3,1},{16,18},{17,19},{18,16},{19,17},{4,6},{5,7... | collective-permute-start | bytes 294920 | tf_op jit(solution)/shard_map/ppermute | solution.py:621
  23.9 2.1 %collective-permute-start.7 = (f32[12,32,128]{2,1,0:T(8,128)S(1)}, f32[12,32,128]{2,1,0:T(8,128)S(1)}, u32[]{:S(2)}, u32[]{:S(2)}) collective-permute-start(f32[12,32,128]{2,1,0:T(8,128)S(1)} %close.1.mine_ref.image_ref), channel_id=1, source_target_pairs={{0,1},{1,0},{2,3},{3,2},{16,17},{17,16},{18,19},{19,18},{4,5},{5,4... | collective-permute-start | bytes 589832 | tf_op jit(solution)/shard_map/ppermute | solution.py:621
  24.0 5.6 %collective-permute-start.8 = (bf16[2,32,128]{2,1,0:T(8,128)(2,1)S(1)}, bf16[2,32,128]{2,1,0:T(8,128)(2,1)S(1)}, u32[]{:S(2)}, u32[]{:S(2)}) collective-permute-start(bf16[2,32,128]{2,1,0:T(8,128)(2,1)S(1)} %get-tuple-element.35), channel_id=1, source_target_pairs={{0,12},{4,8},{8,4},{12,0},{1,13},{5,9},{9,5},{13,1},{2,14},{6,10},... | collective-permute-start | bytes 49160 | tf_op jit(solution)/shard_map/ppermute | solution.py:598
  25.6 4.0 %collective-permute-start.9 = (bf16[2,32,128]{2,1,0:T(8,128)(2,1)S(1)}, bf16[2,32,128]{2,1,0:T(8,128)(2,1)S(1)}, u32[]{:S(2)}, u32[]{:S(2)}) collective-permute-start(bf16[2,32,128]{2,1,0:T(8,128)(2,1)S(1)} %get-tuple-element.36), channel_id=1, source_target_pairs={{0,4},{4,0},{8,12},{12,8},{1,5},{5,1},{9,13},{13,9},{2,6},{6,2},{1... | collective-permute-start | bytes 49160 | tf_op jit(solution)/shard_map/ppermute | solution.py:598
  26.6 3.0 %collective-permute-start.11 = (bf16[1,16,1152]{2,1,0:T(8,128)(2,1)S(1)}, bf16[1,16,1152]{2,1,0:T(8,128)(2,1)S(1)}, u32[]{:S(2)}, u32[]{:S(2)}) collective-permute-start(bf16[1,16,1152]{2,1,0:T(8,128)(2,1)S(1)} %get-tuple-element.37.after_ref), channel_id=1, source_target_pairs={{0,1},{1,0},{2,6},{3,7},{16,24},{17,25},{18,30},{19,31},{4,8},{5,9... | collective-permute-start | bytes 110600 | tf_op jit(solution)/shard_map/ppermute | solution.py:583
  29.6 1.2 %collective-permute-start.10 = (bf16[4,32,128]{2,1,0:T(8,128)(2,1)S(1)}, bf16[4,32,128]{2,1,0:T(8,128)(2,1)S(1)}, u32[]{:S(2)}, u32[]{:S(2)}) collective-permute-start(bf16[4,32,128]{2,1,0:T(8,128)(2,1)S(1)} %join.1.one_ref), channel_id=1, source_target_pairs={{0,1},{1,0},{2,3},{3,2},{16,17},{17,16},{18,19},{19,18},{4,5},{5,4... | collective-permute-start | bytes 98312 | tf_op jit(solution)/shard_map/ppermute | solution.py:621
  31.6 1.4 %collective-permute-start.12 = (bf16[12,32,128]{2,1,0:T(8,128)(2,1)S(1)}, bf16[12,32,128]{2,1,0:T(8,128)(2,1)S(1)}, u32[]{:S(2)}, u32[]{:S(2)}) collective-permute-start(bf16[12,32,128]{2,1,0:T(8,128)(2,1)S(1)} %get-tuple-element.40), channel_id=1, source_target_pairs={{0,1},{1,0},{2,3},{3,2},{16,17},{17,16},{18,19},{19,18},{4,5},{5,4... | collective-permute-start | bytes 294920 | tf_op jit(solution)/shard_map/ppermute | solution.py:621
  33.0 8.1 %collective-permute-start.13 = (bf16[12,32,128]{2,1,0:T(8,128)(2,1)S(1)}, bf16[12,32,128]{2,1,0:T(8,128)(2,1)S(1)}, u32[]{:S(2)}, u32[]{:S(2)}) collective-permute-start(bf16[12,32,128]{2,1,0:T(8,128)(2,1)S(1)} %pair.3.refs_0_), channel_id=1, source_target_pairs={{0,18},{1,19},{2,16},{3,17},{16,2},{17,3},{18,0},{19,1},{4,22},{5,... | collective-permute-start | bytes 294920 | tf_op jit(solution)/shard_map/ppermute | solution.py:621
  37.5 4.6 %collective-permute-start.14 = (bf16[12,32,128]{2,1,0:T(8,128)(2,1)S(1)}, bf16[12,32,128]{2,1,0:T(8,128)(2,1)S(1)}, u32[]{:S(2)}, u32[]{:S(2)}) collective-permute-start(bf16[12,32,128]{2,1,0:T(8,128)(2,1)S(1)} %pair.3.refs_0_), channel_id=1, source_target_pairs={{0,16},{1,17},{2,18},{3,19},{16,0},{17,1},{18,2},{19,3},{4,20},{5,... | collective-permute-start | bytes 294920 | tf_op jit(solution)/shard_map/ppermute | solution.py:621
  37.5 5.2 %collective-permute-start.15 = (bf16[12,32,128]{2,1,0:T(8,128)(2,1)S(1)}, bf16[12,32,128]{2,1,0:T(8,128)(2,1)S(1)}, u32[]{:S(2)}, u32[]{:S(2)}) collective-permute-start(bf16[12,32,128]{2,1,0:T(8,128)(2,1)S(1)} %pair.3.refs_0_), channel_id=1, source_target_pairs={{0,2},{1,3},{2,0},{3,1},{16,18},{17,19},{18,16},{19,17},{4,6},{5,7... | collective-permute-start | bytes 294920 | tf_op jit(solution)/shard_map/ppermute | solution.py:621

commit v11 on v10

--- a/solution.py
+++ b/solution.py
@@ -14,7 +14,7 @@
 GROUP = ("grp", "col")
 CODES = 0
 PER_ITEM = 5
-ITEM_REST = 2 * LANES
+ITEM_REST = LANES
 PIECES = 4
 EVERY = ("grp", "row", "col")
 
@@ -363,8 +363,14 @@
     return values[0]
 
 
+def swap_order(chips):
+    steps = list(range(chips - 1, 0, -1))
+    return [chips // 2] + [step for step in steps if step != chips // 2]
+
+
 def by_step(parts):
-    return [parts[0], *reversed(parts[1:])]
+    arrived = dict(zip(swap_order(len(parts)), parts[1:]))
+    return [parts[0]] + [arrived[step] for step in range(1, len(parts))]
 
 
 def close_kernel(*refs):
@@ -406,7 +412,7 @@
     columns = []
     for k in range(lines.shape[0]):
         square = jnp.transpose(jnp.broadcast_to(lines[k : k + 1], (LANES, LANES)))
-        columns += [square[j * fields : (j + 1) * fields, :1] for j in range(per)]
+        columns += [square[j * fields : (j + 1) * fields] for j in range(per)]
     return columns[:count]
 
 
@@ -437,9 +443,7 @@
 def final_kernel(fields, sums_ref, right_ref, image_ref, out_ref):
     units = image_ref.shape[0]
     sums = columns_of(jnp.sum(sums_ref[...], axis=0), 9, fields)
-    a_real, a_imag, b_real, b_imag = [
-        jnp.broadcast_to(value, (fields, LANES)) for value in krylov_coefficients(sums)
-    ]
+    a_real, a_imag, b_real, b_imag = krylov_coefficients(sums)
     for k in range(units):
         lanes = slice(k * LANES, (k + 1) * LANES)
         r_real, r_imag = right_ref[:fields, lanes], right_ref[fields:, lanes]
@@ -682,7 +686,7 @@
             compiler_params=params(),
             name="pair",
         )(keep, got)
-        arrived = {step: swapped(pair, 2 * step) for step in range(chips - 1, 0, -1)}
+        arrived = {step: swapped(pair, 2 * step) for step in swap_order(chips)}
         return [pair] + list(arrived.values())
 
     def half_sum(parts):

time: 53 us -> 55.1 us (1.040)
  waiting for transfers between devices: 16.8 us -> 20.1 us
  starting transfers between devices: 16.8 us -> 16 us
    ppermute x10, waiting for transfers between devices: 12.6 us -> 15.6 us  [swapped(): return lax.ppermute(value, GROUP, [(g, g ^ step) for g in range(group)])]
    ppermute x10, starting transfers between devices: 9.63 us -> 8.97 us  [swapped(): return lax.ppermute(value, GROUP, [(g, g ^ step) for g in range(group)])]
  transfers between devices with their start and end apart: 16 -> 16, of which waited for: 10 -> 11; matrix products, arithmetic and copies ran while one was open for 0% -> 0% of each run, Pallas kernels for 7% -> 7%
where the time goes in v11:
time: 55.1 us; the launch traced here: 54.8 us
  waiting for transfers between devices  20.1 us (36%)
  starting transfers between devices  16 us (29%)
  Pallas kernels  9.53 us (17%)
  blocking collectives  8.32 us (15%)
  between operations  0.79 us (1%)
    ppermute x10, waiting for transfers between devices, swapped(): return lax.ppermute(value, GROUP, [(g, g ^ step) for g in range(group)])  15.6 us
    ppermute x10, starting transfers between devices, swapped(): return lax.ppermute(value, GROUP, [(g, g ^ step) for g in range(group)])  8.97 us
    all_to_all x1, blocking collectives, local(): lax.all_to_all(lines, EVERY, 0, 0, axis_index_groups=same_chip, tiled=True)  8.32 us
    ppermute x4, starting transfers between devices, from_neighbours(): lax.ppermute(value, 'row', list(enumerate(targets)))  6.89 us
    ppermute x4, waiting for transfers between devices, from_neighbours(): lax.ppermute(value, 'row', list(enumerate(targets)))  4.46 us
    pallas_call x1, Pallas kernels, local(): pl.pallas_call(functools.partial(begin_kernel, fields, items, width, send...  2.79 us
    pallas_call x1, Pallas kernels, local(): pl.pallas_call(functools.partial(fetch_kernel, items, width, slots), out_...  1.94 us
  transfers between devices with their start and end apart: 16, of which 11 were waited for; matrix products, arithmetic and copies ran while one was open for 0% of the time, Pallas kernels for 7%

profile of v11, /device:TPU:0, one launch (start us, length us, event | category | flops | bytes accessed | tf_op | source)
XLA Modules:
  0.0 54.8 jit_solution(12493387401796803990)
XLA Ops:
  0.0 2.8 %begin.1 = (s32[13]{0:T(128)S(4)}, bf16[1,16,896]{2,1,0:T(8,128)(2,1)S(1)}, bf16[1,3,448,2,128]{4,3,2,1,0:T(2,128)(2,1)S(1)}, s32[24,1,128]{2,1,0:T(1,128)S(1)}, f32[32,3072]{1,0:T(8,128)S(1)}) custom-call(s32[1]{0:T(128)} %bitcast.1.row_ref, s32[1]{0:T(128)} %bitcast.2.own_ref, s32[4,2,4]{2,1,0:T(2,128)} %bitcast.18, s32[1,3072]{1,0:T(1,128)} %leaf_hbm.1, ...), custom_call_target="tpu_custom_call" | custom-call | tf_op jit(solution)/shard_map/begin/pallas_call | solution.py:551
  2.8 5.1 %collective-permute-start = (bf16[32,512]{1,0:T(8,128)(2,1)S(1)}, bf16[32,512]{1,0:T(8,128)(2,1)S(1)}, u32[]{:S(2)}, u32[]{:S(2)}) collective-permute-start(bf16[32,512]{1,0:T(8,128)(2,1)S(1)} %get-tuple-element.26), channel_id=1, source_target_pairs={{0,12},{4,8},{8,4},{12,0},{1,13},{5,9},{9,5},{13,1},{2,14},{6,10},... | collective-permute-start | bytes 98312 | tf_op jit(solution)/shard_map/ppermute | solution.py:602
  8.6 1.9 %fetch.1 = (bf16[1,3,448,2,128]{4,3,2,1,0:T(2,128)(2,1)S(1)}, bf16[1,896,441]{2,1,0:T(8,128)(2,1)S(1)}) custom-call(s32[13]{0:T(128)S(4)} %get-tuple-element.24.plan_ref, bf16[441,24,2,128]{3,2,1,0:T(2,128)(2,1)} %bitcast.14, bf16[4,441,2,441]{3,2,1,0:T(2,128)(2,1)} %bitcast.15), custom_call_target="tpu_custom_call" | custom-call | bytes 2064384 | tf_op jit(solution)/shard_map/fetch/pallas_call | solution.py:606
  10.6 1.3 %collective-permute-done.1.two_ref = bf16[32,512]{1,0:T(8,128)(2,1)S(1)} collective-permute-done((bf16[32,512]{1,0:T(8,128)(2,1)S(1)}, bf16[32,512]{1,0:T(8,128)(2,1)S(1)}, u32[]{:S(2)}, u32[]{:S(2)}) %collective-permute-start.1) | collective-permute-done | bytes 32800 | tf_op jit(solution)/shard_map/ppermute | solution.py:602
  11.9 0.8 %near.1.partial_ref = f32[24,32,128]{2,1,0:T(8,128)S(1)} custom-call(s32[1]{0:T(128)} %bitcast.core_ref, s32[1]{0:T(128)} %bitcast.1.row_ref, s32[1]{0:T(128)S(6)} %copy.11.count_ref, s32[13]{0:T(128)S(4)} %get-tuple-element.24.plan_ref, bf16[32,512]{1,0:T(8,128)(2,1)S(1)} %collective-permute-done.one_ref, ...), custom_call_target="tpu_custom_call" | custom-call | flops 67108864 | bytes 2097152 | tf_op jit(solution)/shard_map/near/pallas_call | solution.py:628
  12.6 0.7 %far.1 = (f32[12,32,128]{2,1,0:T(8,128)S(1)}, f32[12,32,128]{2,1,0:T(8,128)S(1)}) custom-call(s32[1]{0:T(128)} %bitcast.core_ref, s32[13]{0:T(128)S(4)} %get-tuple-element.24.plan_ref, s32[24,1,128]{2,1,0:T(1,128)S(1)} %get-tuple-element.25.leaves_ref, f32[24,32,128]{2,1,0:T(8,128)S(1)} %near.1.partial_ref, ...), custom_call_target="tpu_custom_call" | custom-call | tf_op jit(solution)/shard_map/far/pallas_call | solution.py:643
  13.3 0.1 collective-permute-start.3
  13.4 1.4 %collective-permute-done.3.got_ref = f32[12,32,128]{2,1,0:T(8,128)S(1)} collective-permute-done((f32[12,32,128]{2,1,0:T(8,128)S(1)}, f32[12,32,128]{2,1,0:T(8,128)S(1)}, u32[]{:S(2)}, u32[]{:S(2)}) %collective-permute-start.3) | collective-permute-done | bytes 196640 | tf_op jit(solution)/shard_map/ppermute | solution.py:625
  14.8 1.6 %collective-permute-start.4 = (bf16[12,32,128]{2,1,0:T(8,128)(2,1)S(1)}, bf16[12,32,128]{2,1,0:T(8,128)(2,1)S(1)}, u32[]{:S(2)}, u32[]{:S(2)}) collective-permute-start(bf16[12,32,128]{2,1,0:T(8,128)(2,1)S(1)} %pair.2.refs_0_), channel_id=1, source_target_pairs={{0,16},{1,17},{2,18},{3,19},{16,0},{17,1},{18,2},{19,3},{4,20},{5,... | collective-permute-start | bytes 294920 | tf_op jit(solution)/shard_map/ppermute | solution.py:625
  16.4 2.5 %collective-permute-start.5 = (bf16[12,32,128]{2,1,0:T(8,128)(2,1)S(1)}, bf16[12,32,128]{2,1,0:T(8,128)(2,1)S(1)}, u32[]{:S(2)}, u32[]{:S(2)}) collective-permute-start(bf16[12,32,128]{2,1,0:T(8,128)(2,1)S(1)} %pair.2.refs_0_), channel_id=1, source_target_pairs={{0,18},{1,19},{2,16},{3,17},{16,2},{17,3},{18,0},{19,1},{4,22},{5,... | collective-permute-start | bytes 294920 | tf_op jit(solution)/shard_map/ppermute | solution.py:625
  18.9 0.8 %collective-permute-done.4.refs_1_ = bf16[12,32,128]{2,1,0:T(8,128)(2,1)S(1)} collective-permute-done((bf16[12,32,128]{2,1,0:T(8,128)(2,1)S(1)}, bf16[12,32,128]{2,1,0:T(8,128)(2,1)S(1)}, u32[]{:S(2)}, u32[]{:S(2)}) %collective-permute-start.4) | collective-permute-done | bytes 98336 | tf_op jit(solution)/shard_map/ppermute | solution.py:625
  19.7 4.2 %collective-permute-done.5.refs_2_ = bf16[12,32,128]{2,1,0:T(8,128)(2,1)S(1)} collective-permute-done((bf16[12,32,128]{2,1,0:T(8,128)(2,1)S(1)}, bf16[12,32,128]{2,1,0:T(8,128)(2,1)S(1)}, u32[]{:S(2)}, u32[]{:S(2)}) %collective-permute-start.5) | collective-permute-done | bytes 98336 | tf_op jit(solution)/shard_map/ppermute | solution.py:625
  23.9 1.3 %collective-permute-done.6.refs_3_ = bf16[12,32,128]{2,1,0:T(8,128)(2,1)S(1)} collective-permute-done((bf16[12,32,128]{2,1,0:T(8,128)(2,1)S(1)}, bf16[12,32,128]{2,1,0:T(8,128)(2,1)S(1)}, u32[]{:S(2)}, u32[]{:S(2)}) %collective-permute-start.6) | collective-permute-done | bytes 98336 | tf_op jit(solution)/shard_map/ppermute | solution.py:625
  25.3 0.1 collective-permute-start.7
  25.4 1.8 %collective-permute-start.8 = (bf16[2,32,128]{2,1,0:T(8,128)(2,1)S(1)}, bf16[2,32,128]{2,1,0:T(8,128)(2,1)S(1)}, u32[]{:S(2)}, u32[]{:S(2)}) collective-permute-start(bf16[2,32,128]{2,1,0:T(8,128)(2,1)S(1)} %get-tuple-element.35), channel_id=1, source_target_pairs={{0,12},{4,8},{8,4},{12,0},{1,13},{5,9},{9,5},{13,1},{2,14},{6,10},... | collective-permute-start | bytes 49160 | tf_op jit(solution)/shard_map/ppermute | solution.py:602
  27.1 0.6 %assemble.1 = (f32[24,32,128]{2,1,0:T(8,128)S(1)}, bf16[24,32,128]{2,1,0:T(8,128)(2,1)S(1)}, bf16[1,16,1024]{2,1,0:T(8,128)(2,1)S(1)}) custom-call(s32[1]{0:T(128)} %bitcast.core_ref, s32[13]{0:T(128)S(4)} %get-tuple-element.24.plan_ref, s32[24,1,128]{2,1,0:T(1,128)S(1)} %get-tuple-element.25.leaves_ref, f32[12,32,128]{2,1,0:T(8,128)S(1)} %close.1.mine_ref.image_ref, ...), custom_call_target="tpu_custom_call" | custom-call | tf_op jit(solution)/shard_map/assemble/pallas_call | solution.py:703
  27.7 0.2 collective-permute-start.11
  27.9 3.2 %collective-permute-done.8.one_ref = bf16[2,32,128]{2,1,0:T(8,128)(2,1)S(1)} collective-permute-done((bf16[2,32,128]{2,1,0:T(8,128)(2,1)S(1)}, bf16[2,32,128]{2,1,0:T(8,128)(2,1)S(1)}, u32[]{:S(2)}, u32[]{:S(2)}) %collective-permute-start.8) | collective-permute-done | bytes 16416 | tf_op jit(solution)/shard_map/ppermute | solution.py:602
  31.1 0.6 %first_far.1.image_ref = f32[1,3,32,128]{3,2,1,0:T(8,128)S(1)} custom-call(s32[13]{0:T(128)S(4)} %get-tuple-element.24.plan_ref, s32[24,1,128]{2,1,0:T(1,128)S(1)} %get-tuple-element.25.leaves_ref, bf16[1,16,1024]{2,1,0:T(8,128)(2,1)S(1)} %collective-permute-done.11.item_ref, bf16[1,896,441]{2,1,0:T(8,128)(2,1)S(1)} %get-tuple-element.29.trans_ref, ...), custom_call_target="tpu_custom_call" | custom-call | tf_op jit(solution)/shard_map/first_far/pallas_call | solution.py:655
  31.7 0.6 %collective-permute-done.10.two_ref = bf16[4,32,128]{2,1,0:T(8,128)(2,1)S(1)} collective-permute-done((bf16[4,32,128]{2,1,0:T(8,128)(2,1)S(1)}, bf16[4,32,128]{2,1,0:T(8,128)(2,1)S(1)}, u32[]{:S(2)}, u32[]{:S(2)}) %collective-permute-start.10) | collective-permute-done | bytes 32800 | tf_op jit(solution)/shard_map/ppermute | solution.py:625
  32.3 0.7 %last_near.1 = (bf16[12,32,128]{2,1,0:T(8,128)(2,1)S(1)}, bf16[12,32,128]{2,1,0:T(8,128)(2,1)S(1)}) custom-call(s32[1]{0:T(128)} %bitcast.core_ref, s32[1]{0:T(128)} %bitcast.1.row_ref, s32[1]{0:T(128)S(6)} %copy.11.count_ref, s32[13]{0:T(128)S(4)} %get-tuple-element.24.plan_ref, bf16[4,32,128]{2,1,0:T(8,128)(2,1)S(1)} %join.1.one_ref, ...), custom_call_target="tpu_custom_call" | custom-call | tf_op jit(solution)/shard_map/last_near/pallas_call | solution.py:666
  33.0 0.2 collective-permute-start.12
  33.2 1.1 %collective-permute-done.12.got_ref = bf16[12,32,128]{2,1,0:T(8,128)(2,1)S(1)} collective-permute-done((bf16[12,32,128]{2,1,0:T(8,128)(2,1)S(1)}, bf16[12,32,128]{2,1,0:T(8,128)(2,1)S(1)}, u32[]{:S(2)}, u32[]{:S(2)}) %collective-permute-start.12) | collective-permute-done | bytes 98336 | tf_op jit(solution)/shard_map/ppermute | solution.py:625
  34.4 1.9 %collective-permute-start.13 = (bf16[12,32,128]{2,1,0:T(8,128)(2,1)S(1)}, bf16[12,32,128]{2,1,0:T(8,128)(2,1)S(1)}, u32[]{:S(2)}, u32[]{:S(2)}) collective-permute-start(bf16[12,32,128]{2,1,0:T(8,128)(2,1)S(1)} %pair.3.refs_0_), channel_id=1, source_target_pairs={{0,16},{1,17},{2,18},{3,19},{16,0},{17,1},{18,2},{19,3},{4,20},{5,... | collective-permute-start | bytes 294920 | tf_op jit(solution)/shard_map/ppermute | solution.py:625
  36.3 2.2 %collective-permute-start.14 = (bf16[12,32,128]{2,1,0:T(8,128)(2,1)S(1)}, bf16[12,32,128]{2,1,0:T(8,128)(2,1)S(1)}, u32[]{:S(2)}, u32[]{:S(2)}) collective-permute-start(bf16[12,32,128]{2,1,0:T(8,128)(2,1)S(1)} %pair.3.refs_0_), channel_id=1, source_target_pairs={{0,18},{1,19},{2,16},{3,17},{16,2},{17,3},{18,0},{19,1},{4,22},{5,... | collective-permute-start | bytes 294920 | tf_op jit(solution)/shard_map/ppermute | solution.py:625
  38.5 0.5 collective-permute-start.15
  39.0 0.5 collective-permute-done.13.refs_1_
  39.4 4.3 %collective-permute-done.14.refs_2_ = bf16[12,32,128]{2,1,0:T(8,128)(2,1)S(1)} collective-permute-done((bf16[12,32,128]{2,1,0:T(8,128)(2,1)S(1)}, bf16[12,32,128]{2,1,0:T(8,128)(2,1)S(1)}, u32[]{:S(2)}, u32[]{:S(2)}) %collective-permute-start.14) | collective-permute-done | bytes 98336 | tf_op jit(solution)/shard_map/ppermute | solution.py:625
  43.7 1.4 %collective-permute-done.15.refs_3_ = bf16[12,32,128]{2,1,0:T(8,128)(2,1)S(1)} collective-permute-done((bf16[12,32,128]{2,1,0:T(8,128)(2,1)S(1)}, bf16[12,32,128]{2,1,0:T(8,128)(2,1)S(1)}, u32[]{:S(2)}, u32[]{:S(2)}) %collective-permute-start.15) | collective-permute-done | bytes 98336 | tf_op jit(solution)/shard_map/ppermute | solution.py:625
  45.2 0.3 gram.1
  45.4 8.3 %all_to_all.5.sums_ref = f32[8,2,128]{2,1,0:T(2,128)S(1)} all-to-all(f32[8,2,128]{2,1,0:T(2,128)S(1)} %gram.1), channel_id=1, replica_groups={{0,1,4,5,8,9,12,13},{2,3,6,7,10,11,14,15},{16,17,20,21,24,25,28,29},{18..., dimensions={0} | all-to-all | bytes 16384 | tf_op jit(solution)/shard_map/all_to_all | solution.py:748
  53.7 1.0 %combine.1 = f32[32,3072]{1,0:T(8,128)} custom-call(f32[8,2,128]{2,1,0:T(2,128)S(1)} %all_to_all.5.sums_ref, f32[32,3072]{1,0:T(8,128)S(1)} %get-tuple-element.23.image_ref.here_ref.right_ref, f32[24,32,128]{2,1,0:T(8,128)S(1)} %get-tuple-element.34.image_ref), custom_call_target="tpu_custom_call" | custom-call | tf_op jit(solution)/shard_map/combine/pallas_call | solution.py:749
  (18 shorter events, 0.2 us)
Async XLA Ops:
  2.8 7.7 %collective-permute-start = (bf16[32,512]{1,0:T(8,128)(2,1)S(1)}, bf16[32,512]{1,0:T(8,128)(2,1)S(1)}, u32[]{:S(2)}, u32[]{:S(2)}) collective-permute-start(bf16[32,512]{1,0:T(8,128)(2,1)S(1)} %get-tuple-element.26), channel_id=1, source_target_pairs={{0,12},{4,8},{8,4},{12,0},{1,13},{5,9},{9,5},{13,1},{2,14},{6,10},... | collective-permute-start | bytes 98312 | tf_op jit(solution)/shard_map/ppermute | solution.py:602
  7.9 3.9 %collective-permute-start.1 = (bf16[32,512]{1,0:T(8,128)(2,1)S(1)}, bf16[32,512]{1,0:T(8,128)(2,1)S(1)}, u32[]{:S(2)}, u32[]{:S(2)}) collective-permute-start(bf16[32,512]{1,0:T(8,128)(2,1)S(1)} %get-tuple-element.27), channel_id=1, source_target_pairs={{0,4},{4,0},{8,12},{12,8},{1,5},{5,1},{9,13},{13,9},{2,6},{6,2},{1... | collective-permute-start | bytes 98312 | tf_op jit(solution)/shard_map/ppermute | solution.py:602
  7.9 4.7 %collective-permute-start.2 = (bf16[1,16,896]{2,1,0:T(8,128)(2,1)S(1)}, bf16[1,16,896]{2,1,0:T(8,128)(2,1)S(1)}, u32[]{:S(2)}, u32[]{:S(2)}) collective-permute-start(bf16[1,16,896]{2,1,0:T(8,128)(2,1)S(1)} %get-tuple-element.28), channel_id=1, source_target_pairs={{0,1},{1,0},{2,6},{3,7},{16,24},{17,25},{18,30},{19,31},{4,8},{5,9... | collective-permute-start | bytes 86024 | tf_op jit(solution)/shard_map/ppermute | solution.py:587
  8.6 3.3 %copy-start = (bf16[2,8,256,256]{3,2,1,0:T(8,128)(2,1)S(1)}, bf16[2,8,256,256]{3,2,1,0:T(8,128)(2,1)}, u32[]{:S(2)}) copy-start(bf16[2,8,256,256]{3,2,1,0:T(8,128)(2,1)} %tiles_ref.3) | copy-start | bytes 6291460
  13.3 1.5 %collective-permute-start.3 = (f32[12,32,128]{2,1,0:T(8,128)S(1)}, f32[12,32,128]{2,1,0:T(8,128)S(1)}, u32[]{:S(2)}, u32[]{:S(2)}) collective-permute-start(f32[12,32,128]{2,1,0:T(8,128)S(1)} %get-tuple-element.32), channel_id=1, source_target_pairs={{0,1},{1,0},{2,3},{3,2},{16,17},{17,16},{18,19},{19,18},{4,5},{5,4... | collective-permute-start | bytes 589832 | tf_op jit(solution)/shard_map/ppermute | solution.py:625
  14.8 4.9 %collective-permute-start.4 = (bf16[12,32,128]{2,1,0:T(8,128)(2,1)S(1)}, bf16[12,32,128]{2,1,0:T(8,128)(2,1)S(1)}, u32[]{:S(2)}, u32[]{:S(2)}) collective-permute-start(bf16[12,32,128]{2,1,0:T(8,128)(2,1)S(1)} %pair.2.refs_0_), channel_id=1, source_target_pairs={{0,16},{1,17},{2,18},{3,19},{16,0},{17,1},{18,2},{19,3},{4,20},{5,... | collective-permute-start | bytes 294920 | tf_op jit(solution)/shard_map/ppermute | solution.py:625
  16.4 7.5 %collective-permute-start.5 = (bf16[12,32,128]{2,1,0:T(8,128)(2,1)S(1)}, bf16[12,32,128]{2,1,0:T(8,128)(2,1)S(1)}, u32[]{:S(2)}, u32[]{:S(2)}) collective-permute-start(bf16[12,32,128]{2,1,0:T(8,128)(2,1)S(1)} %pair.2.refs_0_), channel_id=1, source_target_pairs={{0,18},{1,19},{2,16},{3,17},{16,2},{17,3},{18,0},{19,1},{4,22},{5,... | collective-permute-start | bytes 294920 | tf_op jit(solution)/shard_map/ppermute | solution.py:625
  18.9 6.3 %collective-permute-start.6 = (bf16[12,32,128]{2,1,0:T(8,128)(2,1)S(1)}, bf16[12,32,128]{2,1,0:T(8,128)(2,1)S(1)}, u32[]{:S(2)}, u32[]{:S(2)}) collective-permute-start(bf16[12,32,128]{2,1,0:T(8,128)(2,1)S(1)} %pair.2.refs_0_), channel_id=1, source_target_pairs={{0,2},{1,3},{2,0},{3,1},{16,18},{17,19},{18,16},{19,17},{4,6},{5,7... | collective-permute-start | bytes 294920 | tf_op jit(solution)/shard_map/ppermute | solution.py:625
  25.3 1.9 %collective-permute-start.7 = (f32[12,32,128]{2,1,0:T(8,128)S(1)}, f32[12,32,128]{2,1,0:T(8,128)S(1)}, u32[]{:S(2)}, u32[]{:S(2)}) collective-permute-start(f32[12,32,128]{2,1,0:T(8,128)S(1)} %close.1.mine_ref.image_ref), channel_id=1, source_target_pairs={{0,1},{1,0},{2,3},{3,2},{16,17},{17,16},{18,19},{19,18},{4,5},{5,4... | collective-permute-start | bytes 589832 | tf_op jit(solution)/shard_map/ppermute | solution.py:625
  25.4 5.7 %collective-permute-start.8 = (bf16[2,32,128]{2,1,0:T(8,128)(2,1)S(1)}, bf16[2,32,128]{2,1,0:T(8,128)(2,1)S(1)}, u32[]{:S(2)}, u32[]{:S(2)}) collective-permute-start(bf16[2,32,128]{2,1,0:T(8,128)(2,1)S(1)} %get-tuple-element.35), channel_id=1, source_target_pairs={{0,12},{4,8},{8,4},{12,0},{1,13},{5,9},{9,5},{13,1},{2,14},{6,10},... | collective-permute-start | bytes 49160 | tf_op jit(solution)/shard_map/ppermute | solution.py:602
  27.1 3.9 %collective-permute-start.9 = (bf16[2,32,128]{2,1,0:T(8,128)(2,1)S(1)}, bf16[2,32,128]{2,1,0:T(8,128)(2,1)S(1)}, u32[]{:S(2)}, u32[]{:S(2)}) collective-permute-start(bf16[2,32,128]{2,1,0:T(8,128)(2,1)S(1)} %get-tuple-element.36), channel_id=1, source_target_pairs={{0,4},{4,0},{8,12},{12,8},{1,5},{5,1},{9,13},{13,9},{2,6},{6,2},{1... | collective-permute-start | bytes 49160 | tf_op jit(solution)/shard_map/ppermute | solution.py:602
  27.7 3.4 %collective-permute-start.11 = (bf16[1,16,1024]{2,1,0:T(8,128)(2,1)S(1)}, bf16[1,16,1024]{2,1,0:T(8,128)(2,1)S(1)}, u32[]{:S(2)}, u32[]{:S(2)}) collective-permute-start(bf16[1,16,1024]{2,1,0:T(8,128)(2,1)S(1)} %get-tuple-element.37.after_ref), channel_id=1, source_target_pairs={{0,1},{1,0},{2,6},{3,7},{16,24},{17,25},{18,30},{19,31},{4,8},{5,9... | collective-permute-start | bytes 98312 | tf_op jit(solution)/shard_map/ppermute | solution.py:587
  31.1 1.2 %collective-permute-start.10 = (bf16[4,32,128]{2,1,0:T(8,128)(2,1)S(1)}, bf16[4,32,128]{2,1,0:T(8,128)(2,1)S(1)}, u32[]{:S(2)}, u32[]{:S(2)}) collective-permute-start(bf16[4,32,128]{2,1,0:T(8,128)(2,1)S(1)} %join.1.one_ref), channel_id=1, source_target_pairs={{0,1},{1,0},{2,3},{3,2},{16,17},{17,16},{18,19},{19,18},{4,5},{5,4... | collective-permute-start | bytes 98312 | tf_op jit(solution)/shard_map/ppermute | solution.py:625
  33.0 1.4 %collective-permute-start.12 = (bf16[12,32,128]{2,1,0:T(8,128)(2,1)S(1)}, bf16[12,32,128]{2,1,0:T(8,128)(2,1)S(1)}, u32[]{:S(2)}, u32[]{:S(2)}) collective-permute-start(bf16[12,32,128]{2,1,0:T(8,128)(2,1)S(1)} %get-tuple-element.40), channel_id=1, source_target_pairs={{0,1},{1,0},{2,3},{3,2},{16,17},{17,16},{18,19},{19,18},{4,5},{5,4... | collective-permute-start | bytes 294920 | tf_op jit(solution)/shard_map/ppermute | solution.py:625
  34.4 5.0 %collective-permute-start.13 = (bf16[12,32,128]{2,1,0:T(8,128)(2,1)S(1)}, bf16[12,32,128]{2,1,0:T(8,128)(2,1)S(1)}, u32[]{:S(2)}, u32[]{:S(2)}) collective-permute-start(bf16[12,32,128]{2,1,0:T(8,128)(2,1)S(1)} %pair.3.refs_0_), channel_id=1, source_target_pairs={{0,16},{1,17},{2,18},{3,19},{16,0},{17,1},{18,2},{19,3},{4,20},{5,... | collective-permute-start | bytes 294920 | tf_op jit(solution)/shard_map/ppermute | solution.py:625
  36.3 7.4 %collective-permute-start.14 = (bf16[12,32,128]{2,1,0:T(8,128)(2,1)S(1)}, bf16[12,32,128]{2,1,0:T(8,128)(2,1)S(1)}, u32[]{:S(2)}, u32[]{:S(2)}) collective-permute-start(bf16[12,32,128]{2,1,0:T(8,128)(2,1)S(1)} %pair.3.refs_0_), channel_id=1, source_target_pairs={{0,18},{1,19},{2,16},{3,17},{16,2},{17,3},{18,0},{19,1},{4,22},{5,... | collective-permute-start | bytes 294920 | tf_op jit(solution)/shard_map/ppermute | solution.py:625
  38.5 6.7 %collective-permute-start.15 = (bf16[12,32,128]{2,1,0:T(8,128)(2,1)S(1)}, bf16[12,32,128]{2,1,0:T(8,128)(2,1)S(1)}, u32[]{:S(2)}, u32[]{:S(2)}) collective-permute-start(bf16[12,32,128]{2,1,0:T(8,128)(2,1)S(1)} %pair.3.refs_0_), channel_id=1, source_target_pairs={{0,2},{1,3},{2,0},{3,1},{16,18},{17,19},{18,16},{19,17},{4,6},{5,7... | collective-permute-start | bytes 294920 | tf_op jit(solution)/shard_map/ppermute | solution.py:625

commit v12 on v11

--- a/solution.py
+++ b/solution.py
@@ -127,28 +127,30 @@
 
 
 def edge_kernel(row_ref, image_ref, one_ref, two_ref):
-    even = lax.rem(row_ref[0], 2) == 0
+    edge_of(row_ref, image_ref, one_ref, True)
+    edge_of(row_ref, image_ref, two_ref, False)
+
+
+def one_edge_kernel(early, row_ref, image_ref, out_ref):
+    edge_of(row_ref, image_ref, out_ref, early)
+
+
+def edge_of(row_ref, image_ref, out_ref, early):
+    first_edge = (lax.rem(row_ref[0], 2) == 0) if early else (lax.rem(row_ref[0], 2) == 1)
     if len(image_ref.shape) == 2:
-        edge = one_ref.shape[1]
+        edge = out_ref.shape[1]
         first, last = image_ref[:, :edge], image_ref[:, image_ref.shape[1] - edge :]
     else:
-        edge = one_ref.shape[0]
+        edge = out_ref.shape[0]
         first, last = image_ref[:edge], image_ref[image_ref.shape[0] - edge :]
-    first, last = first.astype(one_ref.dtype), last.astype(one_ref.dtype)
-
-    @pl.when(even)
+
+    @pl.when(first_edge)
     def _():
-        one_ref[...], two_ref[...] = first, last
-
-    @pl.when(jnp.logical_not(even))
+        out_ref[...] = first.astype(out_ref.dtype)
+
+    @pl.when(jnp.logical_not(first_edge))
     def _():
-        one_ref[...], two_ref[...] = last, first
-
-
-def join_kernel(one_ref, two_ref, after_ref, out_ref):
-    del after_ref
-    edge = one_ref.shape[0]
-    out_ref[:edge], out_ref[edge:] = one_ref[...], two_ref[...]
+        out_ref[...] = last.astype(out_ref.dtype)
 
 
 def begin_kernel(
@@ -241,25 +243,9 @@
             copy.wait()
 
 
-def near_sources(core_ref, row_ref, one_ref, two_ref, here_ref, units, ext):
-    edge = (ext.shape[0] - units) // 2
+def edge_places(row_ref, edge, units):
     even = lax.rem(row_ref[0], 2) == 0
-    one_at = jnp.where(even, 0, edge + units)
-    two_at = jnp.where(even, edge + units, 0)
-    if len(here_ref.shape) == 2:
-        for k in range(edge):
-            lanes = slice(k * LANES, (k + 1) * LANES)
-            ext[one_at + k] = one_ref[:, lanes].astype(ext.dtype)
-            ext[two_at + k] = two_ref[:, lanes].astype(ext.dtype)
-        for k in range(units):
-            ext[edge + k] = here_ref[:, k * LANES : (k + 1) * LANES]
-        return
-    half = edge // 2
-    for ref, core in ((one_ref, core_ref[0]), (two_ref, 1 - core_ref[0])):
-        for k in range(half):
-            ext[one_at + 2 * k + core] = ref[k]
-            ext[two_at + 2 * k + core] = ref[half + k]
-    ext[edge : edge + units] = here_ref[...]
+    return jnp.where(even, 0, edge + units), jnp.where(even, edge + units, 0)
 
 
 def part(total, core, keep_ref, give_ref):
@@ -268,19 +254,33 @@
         give_ref[k] = total[2 * k + 1 - core].astype(give_ref.dtype)
 
 
-def near_kernel(
-    fields, core_ref, row_ref, count_ref, plan_ref, one_ref, two_ref, here_ref, tiles_ref, out_ref, ext
-):
-    near_sources(core_ref, row_ref, one_ref, two_ref, here_ref, out_ref.shape[0], ext)
+def near_kernel(fields, row_ref, count_ref, plan_ref, one_ref, two_ref, here_ref, tiles_ref, out_ref, ext):
+    units = out_ref.shape[0]
+    edge = (ext.shape[0] - units) // 2
+    one_at, two_at = edge_places(row_ref, edge, units)
+    for k in range(edge):
+        lanes = slice(k * LANES, (k + 1) * LANES)
+        ext[one_at + k] = one_ref[:, lanes].astype(ext.dtype)
+        ext[two_at + k] = two_ref[:, lanes].astype(ext.dtype)
+    for k in range(units):
+        ext[edge + k] = here_ref[:, k * LANES : (k + 1) * LANES]
     out_ref[...] = jnp.zeros_like(out_ref)
     near_slots(fields, count_ref, plan_ref, tiles_ref, out_ref, ext)
 
 
 def last_near_kernel(
-    fields, core_ref, row_ref, count_ref, plan_ref, one_ref, two_ref, here_ref, tiles_ref, image_ref,
+    fields, core_ref, row_ref, count_ref, plan_ref, one_ref, other_one_ref, two_ref, here_ref, tiles_ref, image_ref,
     keep_ref, give_ref, ext, total,
 ):
-    near_sources(core_ref, row_ref, one_ref, two_ref, here_ref, total.shape[0], ext)
+    units = total.shape[0]
+    edge = (ext.shape[0] - units) // 2
+    core = core_ref[0]
+    one_at, two_at = edge_places(row_ref, edge, units)
+    for k in range(edge // 2):
+        ext[one_at + 2 * k + core] = one_ref[k]
+        ext[one_at + 2 * k + 1 - core] = other_one_ref[k]
+    ext[pl.ds(two_at, edge)] = two_ref[...]
+    ext[edge : edge + units] = here_ref[...]
     total[...] = jnp.zeros_like(total)
     items, width = image_ref.shape[:2]
     for i in range(items):
@@ -364,8 +364,7 @@
 
 
 def swap_order(chips):
-    steps = list(range(chips - 1, 0, -1))
-    return [chips // 2] + [step for step in steps if step != chips // 2]
+    return list(range(chips - 1, 0, -1))
 
 
 def by_step(parts):
@@ -588,19 +587,29 @@
         ]
         return parts[0] if len(parts) == 1 else jnp.concatenate(parts)
 
+    def along_row(value, which):
+        return lax.ppermute(value, "row", list(enumerate(neighbours[which])))
+
     def from_neighbours(image):
-        edge_shape = (both, edge) if image.ndim == 2 else (edge_units // 2, both, LANES)
         one, two = pl.pallas_call(
             edge_kernel,
-            out_shape=(jax.ShapeDtypeStruct(edge_shape, BF16),) * 2,
+            out_shape=(jax.ShapeDtypeStruct((both, edge), BF16),) * 2,
             in_specs=[SMEM, VMEM],
             out_specs=(VMEM, VMEM),
             compiler_params=params(),
             name="edges",
         )(row_place, image)
-        return [
-            lax.ppermute(value, "row", list(enumerate(targets))) for value, targets in zip((one, two), neighbours)
-        ]
+        return along_row(one, 0), along_row(two, 1)
+
+    def one_edge(image, edge_units, early):
+        return pl.pallas_call(
+            functools.partial(one_edge_kernel, early),
+            out_shape=jax.ShapeDtypeStruct((edge_units, both, LANES), BF16),
+            in_specs=[SMEM, VMEM],
+            out_specs=VMEM,
+            compiler_params=params(),
+            name="edge",
+        )(row_place, image)
 
     image_shape = jax.ShapeDtypeStruct((units, both, LANES), F32)
     target_windows, moved = pl.pallas_call(
@@ -628,7 +637,7 @@
         return pl.pallas_call(
             functools.partial(near_kernel, fields),
             out_shape=image_shape,
-            in_specs=[SMEM] * 4 + [VMEM] * 4,
+            in_specs=[SMEM] * 3 + [VMEM] * 4,
             out_specs=VMEM,
             scratch_shapes=[pltpu.VMEM((units + 2 * edge_units, both, LANES), low.dtype)],
             compiler_params=params(),
@@ -636,7 +645,7 @@
                 flops=8 * fields * near_tiles.size // 2, bytes_accessed=2 * near_tiles.size, transcendentals=0
             ),
             name="near",
-        )(core_place, row_place, tile_count, plan, one, two, low, near_tiles)
+        )(row_place, tile_count, plan, one, two, low, near_tiles)
 
     def core_parts(partial, taken):
         half_shape = jax.ShapeDtypeStruct(half_units, F32)
@@ -661,12 +670,12 @@
             name="first_far",
         )(plan, leaves, taken, moved, target_windows)
 
-    def last_core_parts(one, two, low, image):
+    def last_core_parts(one, other_one, two, low, image):
         half_shape = jax.ShapeDtypeStruct(half_units, BF16)
         keep, give = pl.pallas_call(
             functools.partial(last_near_kernel, fields),
             out_shape=(half_shape, half_shape),
-            in_specs=[SMEM] * 4 + [VMEM] * 5,
+            in_specs=[SMEM] * 4 + [VMEM] * 6,
             out_specs=(VMEM, VMEM),
             scratch_shapes=[
                 pltpu.VMEM((units + 2 * edge_units, both, LANES), low.dtype),
@@ -674,7 +683,7 @@
             ],
             compiler_params=params(),
             name="last_near",
-        )(core_place, row_place, tile_count, plan, one, two, low, near_tiles, image)
+        )(core_place, row_place, tile_count, plan, one, other_one, two, low, near_tiles, image)
         return keep, swapped(give, 1)
 
     def pair_sums(keep, got):
@@ -713,24 +722,14 @@
             name="assemble",
         )(core_place, plan, leaves, mine, theirs, windows)
 
-    def joined_edges(one, two, made):
-        return pl.pallas_call(
-            join_kernel,
-            out_shape=jax.ShapeDtypeStruct((edge_units, both, LANES), BF16),
-            in_specs=[VMEM, VMEM, ANY],
-            out_specs=VMEM,
-            compiler_params=params(),
-            name="join",
-        )(one, two, made)
-
     partial = near(*from_neighbours(right), right)
     mine = half_sum(pair_sums(*core_parts(partial, exchanged(made))))
     theirs = swapped(mine, 1)
-    one, two = from_neighbours(mine)
+    one = along_row(one_edge(mine, edge_units // 2, True), 0)
     z_all, z_low, made = whole(mine, theirs)
-    edges = joined_edges(one, two, made)
     image = first_far(exchanged(made))
-    parts = pair_sums(*last_core_parts(edges, swapped(edges, 1), z_low, image))
+    two = along_row(one_edge(z_low, edge_units, False), 1)
+    parts = pair_sums(*last_core_parts(one, swapped(one, 1), two, z_low, image))
 
     lines = pl.pallas_call(
         functools.partial(gram_kernel, fields),

time: 55.1 us -> 52.9 us (0.960)
  waiting for transfers between devices: 20.1 us -> 15.5 us
  starting transfers between devices: 16 us -> 18.1 us
    ppermute x10, waiting for transfers between devices: 15.6 us -> 12.6 us  [swapped(): return lax.ppermute(value, GROUP, [(g, g ^ step) for g in range(group)])]
    ppermute x4, starting transfers between devices: 6.89 us -> 8.4 us  [along_row(): return lax.ppermute(value, 'row', list(enumerate(neighbours[which])))]
    ppermute x4, waiting for transfers between devices: 4.46 us -> 2.95 us  [along_row(): return lax.ppermute(value, 'row', list(enumerate(neighbours[which])))]
    ppermute x10, starting transfers between devices: 8.97 us -> 9.53 us  [swapped(): return lax.ppermute(value, GROUP, [(g, g ^ step) for g in range(group)])]
  transfers between devices with their start and end apart: 16 -> 16, of which waited for: 11 -> 10; matrix products, arithmetic and copies ran while one was open for 0% -> 0% of each run, Pallas kernels for 7% -> 7%
where the time goes in v12:
time: 52.9 us; the launch traced here: 52.6 us
  starting transfers between devices  18.1 us (34%)
  waiting for transfers between devices  15.5 us (29%)
  Pallas kernels  9.54 us (18%)
  blocking collectives  8.67 us (16%)
  between operations  0.78 us (1%)
    ppermute x10, waiting for transfers between devices, swapped(): return lax.ppermute(value, GROUP, [(g, g ^ step) for g in range(group)])  12.6 us
    ppermute x10, starting transfers between devices, swapped(): return lax.ppermute(value, GROUP, [(g, g ^ step) for g in range(group)])  9.53 us
    all_to_all x1, blocking collectives, local(): lax.all_to_all(lines, EVERY, 0, 0, axis_index_groups=same_chip, tiled=True)  8.67 us
    ppermute x4, starting transfers between devices, along_row(): return lax.ppermute(value, 'row', list(enumerate(neighbours[which])))  8.4 us
    ppermute x4, waiting for transfers between devices, along_row(): return lax.ppermute(value, 'row', list(enumerate(neighbours[which])))  2.95 us
    pallas_call x1, Pallas kernels, local(): pl.pallas_call(functools.partial(begin_kernel, fields, items, width, send...  2.79 us
    pallas_call x1, Pallas kernels, local(): pl.pallas_call(functools.partial(fetch_kernel, items, width, slots), out_...  1.94 us
  transfers between devices with their start and end apart: 16, of which 10 were waited for; matrix products, arithmetic and copies ran while one was open for 0% of the time, Pallas kernels for 7%

profile of v12, /device:TPU:0, one launch (start us, length us, event | category | flops | bytes accessed | tf_op | source)
XLA Modules:
  0.0 52.6 jit_solution(17057992512506032163)
XLA Ops:
  0.0 2.8 %begin.1 = (s32[13]{0:T(128)S(4)}, bf16[1,16,896]{2,1,0:T(8,128)(2,1)S(1)}, bf16[1,3,448,2,128]{4,3,2,1,0:T(2,128)(2,1)S(1)}, s32[24,1,128]{2,1,0:T(1,128)S(1)}, f32[32,3072]{1,0:T(8,128)S(1)}) custom-call(s32[1]{0:T(128)} %bitcast.1.row_ref, s32[1]{0:T(128)} %bitcast.2.own_ref, s32[4,2,4]{2,1,0:T(2,128)} %bitcast.18, s32[1,3072]{1,0:T(1,128)} %leaf_hbm.1, ...), custom_call_target="tpu_custom_call" | custom-call | tf_op jit(solution)/shard_map/begin/pallas_call | solution.py:550
  2.8 5.1 %collective-permute-start = (bf16[32,512]{1,0:T(8,128)(2,1)S(1)}, bf16[32,512]{1,0:T(8,128)(2,1)S(1)}, u32[]{:S(2)}, u32[]{:S(2)}) collective-permute-start(bf16[32,512]{1,0:T(8,128)(2,1)S(1)} %get-tuple-element.24), channel_id=1, source_target_pairs={{0,12},{4,8},{8,4},{12,0},{1,13},{5,9},{9,5},{13,1},{2,14},{6,10},... | collective-permute-start | bytes 98312 | tf_op jit(solution)/shard_map/ppermute | solution.py:591
  8.6 1.9 %fetch.1 = (bf16[1,3,448,2,128]{4,3,2,1,0:T(2,128)(2,1)S(1)}, bf16[1,896,441]{2,1,0:T(8,128)(2,1)S(1)}) custom-call(s32[13]{0:T(128)S(4)} %get-tuple-element.22.plan_ref, bf16[441,24,2,128]{3,2,1,0:T(2,128)(2,1)} %bitcast.14, bf16[4,441,2,441]{3,2,1,0:T(2,128)(2,1)} %bitcast.15), custom_call_target="tpu_custom_call" | custom-call | bytes 2064384 | tf_op jit(solution)/shard_map/fetch/pallas_call | solution.py:615
  10.6 1.3 %collective-permute-done.1.two_ref = bf16[32,512]{1,0:T(8,128)(2,1)S(1)} collective-permute-done((bf16[32,512]{1,0:T(8,128)(2,1)S(1)}, bf16[32,512]{1,0:T(8,128)(2,1)S(1)}, u32[]{:S(2)}, u32[]{:S(2)}) %collective-permute-start.1) | collective-permute-done | bytes 32800 | tf_op jit(solution)/shard_map/ppermute | solution.py:591
  11.9 0.8 %near.1.partial_ref = f32[24,32,128]{2,1,0:T(8,128)S(1)} custom-call(s32[1]{0:T(128)} %bitcast.1.row_ref, s32[1]{0:T(128)S(6)} %copy.11.count_ref, s32[13]{0:T(128)S(4)} %get-tuple-element.22.plan_ref, bf16[32,512]{1,0:T(8,128)(2,1)S(1)} %collective-permute-done.one_ref, bf16[32,512]{1,0:T(8,128)(2,1)S(1)} %collective-permute-done.1.two_ref, ...), custom_call_target="tpu_custom_call" | custom-call | flops 67108864 | bytes 2097152 | tf_op jit(solution)/shard_map/near/pallas_call | solution.py:637
  12.6 0.7 %far.1 = (f32[12,32,128]{2,1,0:T(8,128)S(1)}, f32[12,32,128]{2,1,0:T(8,128)S(1)}) custom-call(s32[1]{0:T(128)} %bitcast.core_ref, s32[13]{0:T(128)S(4)} %get-tuple-element.22.plan_ref, s32[24,1,128]{2,1,0:T(1,128)S(1)} %get-tuple-element.23.leaves_ref, f32[24,32,128]{2,1,0:T(8,128)S(1)} %near.1.partial_ref, ...), custom_call_target="tpu_custom_call" | custom-call | tf_op jit(solution)/shard_map/far/pallas_call | solution.py:652
  13.3 0.1 collective-permute-start.3
  13.4 1.4 %collective-permute-done.3.got_ref = f32[12,32,128]{2,1,0:T(8,128)S(1)} collective-permute-done((f32[12,32,128]{2,1,0:T(8,128)S(1)}, f32[12,32,128]{2,1,0:T(8,128)S(1)}, u32[]{:S(2)}, u32[]{:S(2)}) %collective-permute-start.3) | collective-permute-done | bytes 196640 | tf_op jit(solution)/shard_map/ppermute | solution.py:634
  14.9 3.5 %collective-permute-start.4 = (bf16[12,32,128]{2,1,0:T(8,128)(2,1)S(1)}, bf16[12,32,128]{2,1,0:T(8,128)(2,1)S(1)}, u32[]{:S(2)}, u32[]{:S(2)}) collective-permute-start(bf16[12,32,128]{2,1,0:T(8,128)(2,1)S(1)} %pair.2.refs_0_), channel_id=1, source_target_pairs={{0,18},{1,19},{2,16},{3,17},{16,2},{17,3},{18,0},{19,1},{4,22},{5,... | collective-permute-start | bytes 294920 | tf_op jit(solution)/shard_map/ppermute | solution.py:634
  18.3 0.6 %collective-permute-start.5 = (bf16[12,32,128]{2,1,0:T(8,128)(2,1)S(1)}, bf16[12,32,128]{2,1,0:T(8,128)(2,1)S(1)}, u32[]{:S(2)}, u32[]{:S(2)}) collective-permute-start(bf16[12,32,128]{2,1,0:T(8,128)(2,1)S(1)} %pair.2.refs_0_), channel_id=1, source_target_pairs={{0,16},{1,17},{2,18},{3,19},{16,0},{17,1},{18,2},{19,3},{4,20},{5,... | collective-permute-start | bytes 294920 | tf_op jit(solution)/shard_map/ppermute | solution.py:634
  18.9 0.1 collective-permute-start.6
  19.0 2.9 %collective-permute-done.4.refs_1_ = bf16[12,32,128]{2,1,0:T(8,128)(2,1)S(1)} collective-permute-done((bf16[12,32,128]{2,1,0:T(8,128)(2,1)S(1)}, bf16[12,32,128]{2,1,0:T(8,128)(2,1)S(1)}, u32[]{:S(2)}, u32[]{:S(2)}) %collective-permute-start.4) | collective-permute-done | bytes 98336 | tf_op jit(solution)/shard_map/ppermute | solution.py:634
  21.9 1.9 %collective-permute-done.5.refs_2_ = bf16[12,32,128]{2,1,0:T(8,128)(2,1)S(1)} collective-permute-done((bf16[12,32,128]{2,1,0:T(8,128)(2,1)S(1)}, bf16[12,32,128]{2,1,0:T(8,128)(2,1)S(1)}, u32[]{:S(2)}, u32[]{:S(2)}) %collective-permute-start.5) | collective-permute-done | bytes 98336 | tf_op jit(solution)/shard_map/ppermute | solution.py:634
  23.9 0.1 collective-permute-start.7
  24.0 1.6 %collective-permute-start.8 = (bf16[2,32,128]{2,1,0:T(8,128)(2,1)S(1)}, bf16[2,32,128]{2,1,0:T(8,128)(2,1)S(1)}, u32[]{:S(2)}, u32[]{:S(2)}) collective-permute-start(bf16[2,32,128]{2,1,0:T(8,128)(2,1)S(1)} %edge.2), channel_id=1, source_target_pairs={{0,12},{4,8},{8,4},{12,0},{1,13},{5,9},{9,5},{13,1},{2,14},{6,10},... | collective-permute-start | bytes 49160 | tf_op jit(solution)/shard_map/ppermute | solution.py:591
  25.6 0.6 %assemble.1 = (f32[24,32,128]{2,1,0:T(8,128)S(1)}, bf16[24,32,128]{2,1,0:T(8,128)(2,1)S(1)}, bf16[1,16,1024]{2,1,0:T(8,128)(2,1)S(1)}) custom-call(s32[1]{0:T(128)} %bitcast.core_ref, s32[13]{0:T(128)S(4)} %get-tuple-element.22.plan_ref, s32[24,1,128]{2,1,0:T(1,128)S(1)} %get-tuple-element.23.leaves_ref, f32[12,32,128]{2,1,0:T(8,128)S(1)} %close.1.mine_ref.image_ref, ...), custom_call_target="tpu_custom_call" | custom-call | tf_op jit(solution)/shard_map/assemble/pallas_call | solution.py:712
  26.2 0.2 collective-permute-start.11
  26.4 1.7 %collective-permute-start.10 = (bf16[4,32,128]{2,1,0:T(8,128)(2,1)S(1)}, bf16[4,32,128]{2,1,0:T(8,128)(2,1)S(1)}, u32[]{:S(2)}, u32[]{:S(2)}) collective-permute-start(bf16[4,32,128]{2,1,0:T(8,128)(2,1)S(1)} %edge.3), channel_id=1, source_target_pairs={{0,4},{4,0},{8,12},{12,8},{1,5},{5,1},{9,13},{13,9},{2,6},{6,2},{1... | collective-permute-start | bytes 98312 | tf_op jit(solution)/shard_map/ppermute | solution.py:591
  28.0 1.7 %collective-permute-done.8.one_ref = bf16[2,32,128]{2,1,0:T(8,128)(2,1)S(1)} collective-permute-done((bf16[2,32,128]{2,1,0:T(8,128)(2,1)S(1)}, bf16[2,32,128]{2,1,0:T(8,128)(2,1)S(1)}, u32[]{:S(2)}, u32[]{:S(2)}) %collective-permute-start.8) | collective-permute-done | bytes 16416 | tf_op jit(solution)/shard_map/ppermute | solution.py:591
  29.7 0.6 %first_far.1.image_ref = f32[1,3,32,128]{3,2,1,0:T(8,128)S(1)} custom-call(s32[13]{0:T(128)S(4)} %get-tuple-element.22.plan_ref, s32[24,1,128]{2,1,0:T(1,128)S(1)} %get-tuple-element.23.leaves_ref, bf16[1,16,1024]{2,1,0:T(8,128)(2,1)S(1)} %collective-permute-done.11.item_ref, bf16[1,896,441]{2,1,0:T(8,128)(2,1)S(1)} %get-tuple-element.27.trans_ref, ...), custom_call_target="tpu_custom_call" | custom-call | tf_op jit(solution)/shard_map/first_far/pallas_call | solution.py:664
  30.3 0.6 %collective-permute-done.9.other_one_ref = bf16[2,32,128]{2,1,0:T(8,128)(2,1)S(1)} collective-permute-done((bf16[2,32,128]{2,1,0:T(8,128)(2,1)S(1)}, bf16[2,32,128]{2,1,0:T(8,128)(2,1)S(1)}, u32[]{:S(2)}, u32[]{:S(2)}) %collective-permute-start.9) | collective-permute-done | bytes 16416 | tf_op jit(solution)/shard_map/ppermute | solution.py:634
  30.9 0.7 %last_near.1 = (bf16[12,32,128]{2,1,0:T(8,128)(2,1)S(1)}, bf16[12,32,128]{2,1,0:T(8,128)(2,1)S(1)}) custom-call(s32[1]{0:T(128)} %bitcast.core_ref, s32[1]{0:T(128)} %bitcast.1.row_ref, s32[1]{0:T(128)S(6)} %copy.11.count_ref, s32[13]{0:T(128)S(4)} %get-tuple-element.22.plan_ref, bf16[2,32,128]{2,1,0:T(8,128)(2,1)S(1)} %collective-permute-done.8.one_ref, ...), custom_call_target="tpu_custom_call" | custom-call | tf_op jit(solution)/shard_map/last_near/pallas_call | solution.py:675
  31.7 0.2 collective-permute-start.12
  31.9 1.1 %collective-permute-done.12.got_ref = bf16[12,32,128]{2,1,0:T(8,128)(2,1)S(1)} collective-permute-done((bf16[12,32,128]{2,1,0:T(8,128)(2,1)S(1)}, bf16[12,32,128]{2,1,0:T(8,128)(2,1)S(1)}, u32[]{:S(2)}, u32[]{:S(2)}) %collective-permute-start.12) | collective-permute-done | bytes 98336 | tf_op jit(solution)/shard_map/ppermute | solution.py:634
  33.0 4.4 %collective-permute-start.13 = (bf16[12,32,128]{2,1,0:T(8,128)(2,1)S(1)}, bf16[12,32,128]{2,1,0:T(8,128)(2,1)S(1)}, u32[]{:S(2)}, u32[]{:S(2)}) collective-permute-start(bf16[12,32,128]{2,1,0:T(8,128)(2,1)S(1)} %pair.3.refs_0_), channel_id=1, source_target_pairs={{0,18},{1,19},{2,16},{3,17},{16,2},{17,3},{18,0},{19,1},{4,22},{5,... | collective-permute-start | bytes 294920 | tf_op jit(solution)/shard_map/ppermute | solution.py:634
  37.4 0.6 %collective-permute-start.15 = (bf16[12,32,128]{2,1,0:T(8,128)(2,1)S(1)}, bf16[12,32,128]{2,1,0:T(8,128)(2,1)S(1)}, u32[]{:S(2)}, u32[]{:S(2)}) collective-permute-start(bf16[12,32,128]{2,1,0:T(8,128)(2,1)S(1)} %pair.3.refs_0_), channel_id=1, source_target_pairs={{0,2},{1,3},{2,0},{3,1},{16,18},{17,19},{18,16},{19,17},{4,6},{5,7... | collective-permute-start | bytes 294920 | tf_op jit(solution)/shard_map/ppermute | solution.py:634
  38.1 2.9 %collective-permute-done.13.refs_1_ = bf16[12,32,128]{2,1,0:T(8,128)(2,1)S(1)} collective-permute-done((bf16[12,32,128]{2,1,0:T(8,128)(2,1)S(1)}, bf16[12,32,128]{2,1,0:T(8,128)(2,1)S(1)}, u32[]{:S(2)}, u32[]{:S(2)}) %collective-permute-start.13) | collective-permute-done | bytes 98336 | tf_op jit(solution)/shard_map/ppermute | solution.py:634
  41.0 1.0 %collective-permute-done.14.refs_2_ = bf16[12,32,128]{2,1,0:T(8,128)(2,1)S(1)} collective-permute-done((bf16[12,32,128]{2,1,0:T(8,128)(2,1)S(1)}, bf16[12,32,128]{2,1,0:T(8,128)(2,1)S(1)}, u32[]{:S(2)}, u32[]{:S(2)}) %collective-permute-start.14) | collective-permute-done | bytes 98336 | tf_op jit(solution)/shard_map/ppermute | solution.py:634
  42.1 0.6 %collective-permute-done.15.refs_3_ = bf16[12,32,128]{2,1,0:T(8,128)(2,1)S(1)} collective-permute-done((bf16[12,32,128]{2,1,0:T(8,128)(2,1)S(1)}, bf16[12,32,128]{2,1,0:T(8,128)(2,1)S(1)}, u32[]{:S(2)}, u32[]{:S(2)}) %collective-permute-start.15) | collective-permute-done | bytes 98336 | tf_op jit(solution)/shard_map/ppermute | solution.py:634
  42.7 0.3 gram.1
  42.9 8.7 %all_to_all.5.sums_ref = f32[8,2,128]{2,1,0:T(2,128)S(1)} all-to-all(f32[8,2,128]{2,1,0:T(2,128)S(1)} %gram.1), channel_id=1, replica_groups={{0,1,4,5,8,9,12,13},{2,3,6,7,10,11,14,15},{16,17,20,21,24,25,28,29},{18..., dimensions={0} | all-to-all | bytes 16384 | tf_op jit(solution)/shard_map/all_to_all | solution.py:747
  51.6 1.0 %combine.1 = f32[32,3072]{1,0:T(8,128)} custom-call(f32[8,2,128]{2,1,0:T(2,128)S(1)} %all_to_all.5.sums_ref, f32[32,3072]{1,0:T(8,128)S(1)} %get-tuple-element.21.image_ref.here_ref.right_ref, f32[24,32,128]{2,1,0:T(8,128)S(1)} %get-tuple-element.32.image_ref), custom_call_target="tpu_custom_call" | custom-call | tf_op jit(solution)/shard_map/combine/pallas_call | solution.py:748
  (18 shorter events, 0.2 us)
Async XLA Ops:
  2.8 7.7 %collective-permute-start = (bf16[32,512]{1,0:T(8,128)(2,1)S(1)}, bf16[32,512]{1,0:T(8,128)(2,1)S(1)}, u32[]{:S(2)}, u32[]{:S(2)}) collective-permute-start(bf16[32,512]{1,0:T(8,128)(2,1)S(1)} %get-tuple-element.24), channel_id=1, source_target_pairs={{0,12},{4,8},{8,4},{12,0},{1,13},{5,9},{9,5},{13,1},{2,14},{6,10},... | collective-permute-start | bytes 98312 | tf_op jit(solution)/shard_map/ppermute | solution.py:591
  8.0 3.9 %collective-permute-start.1 = (bf16[32,512]{1,0:T(8,128)(2,1)S(1)}, bf16[32,512]{1,0:T(8,128)(2,1)S(1)}, u32[]{:S(2)}, u32[]{:S(2)}) collective-permute-start(bf16[32,512]{1,0:T(8,128)(2,1)S(1)} %get-tuple-element.25), channel_id=1, source_target_pairs={{0,4},{4,0},{8,12},{12,8},{1,5},{5,1},{9,13},{13,9},{2,6},{6,2},{1... | collective-permute-start | bytes 98312 | tf_op jit(solution)/shard_map/ppermute | solution.py:591
  8.0 4.7 %collective-permute-start.2 = (bf16[1,16,896]{2,1,0:T(8,128)(2,1)S(1)}, bf16[1,16,896]{2,1,0:T(8,128)(2,1)S(1)}, u32[]{:S(2)}, u32[]{:S(2)}) collective-permute-start(bf16[1,16,896]{2,1,0:T(8,128)(2,1)S(1)} %get-tuple-element.26), channel_id=1, source_target_pairs={{0,1},{1,0},{2,6},{3,7},{16,24},{17,25},{18,30},{19,31},{4,8},{5,9... | collective-permute-start | bytes 86024 | tf_op jit(solution)/shard_map/ppermute | solution.py:586
  8.6 3.3 %copy-start = (bf16[2,8,256,256]{3,2,1,0:T(8,128)(2,1)S(1)}, bf16[2,8,256,256]{3,2,1,0:T(8,128)(2,1)}, u32[]{:S(2)}) copy-start(bf16[2,8,256,256]{3,2,1,0:T(8,128)(2,1)} %tiles_ref.3) | copy-start | bytes 6291460
  13.3 1.5 %collective-permute-start.3 = (f32[12,32,128]{2,1,0:T(8,128)S(1)}, f32[12,32,128]{2,1,0:T(8,128)S(1)}, u32[]{:S(2)}, u32[]{:S(2)}) collective-permute-start(f32[12,32,128]{2,1,0:T(8,128)S(1)} %get-tuple-element.30), channel_id=1, source_target_pairs={{0,1},{1,0},{2,3},{3,2},{16,17},{17,16},{18,19},{19,18},{4,5},{5,4... | collective-permute-start | bytes 589832 | tf_op jit(solution)/shard_map/ppermute | solution.py:634
  14.9 7.1 %collective-permute-start.4 = (bf16[12,32,128]{2,1,0:T(8,128)(2,1)S(1)}, bf16[12,32,128]{2,1,0:T(8,128)(2,1)S(1)}, u32[]{:S(2)}, u32[]{:S(2)}) collective-permute-start(bf16[12,32,128]{2,1,0:T(8,128)(2,1)S(1)} %pair.2.refs_0_), channel_id=1, source_target_pairs={{0,18},{1,19},{2,16},{3,17},{16,2},{17,3},{18,0},{19,1},{4,22},{5,... | collective-permute-start | bytes 294920 | tf_op jit(solution)/shard_map/ppermute | solution.py:634
  18.3 5.5 %collective-permute-start.5 = (bf16[12,32,128]{2,1,0:T(8,128)(2,1)S(1)}, bf16[12,32,128]{2,1,0:T(8,128)(2,1)S(1)}, u32[]{:S(2)}, u32[]{:S(2)}) collective-permute-start(bf16[12,32,128]{2,1,0:T(8,128)(2,1)S(1)} %pair.2.refs_0_), channel_id=1, source_target_pairs={{0,16},{1,17},{2,18},{3,19},{16,0},{17,1},{18,2},{19,3},{4,20},{5,... | collective-permute-start | bytes 294920 | tf_op jit(solution)/shard_map/ppermute | solution.py:634
  18.9 4.9 %collective-permute-start.6 = (bf16[12,32,128]{2,1,0:T(8,128)(2,1)S(1)}, bf16[12,32,128]{2,1,0:T(8,128)(2,1)S(1)}, u32[]{:S(2)}, u32[]{:S(2)}) collective-permute-start(bf16[12,32,128]{2,1,0:T(8,128)(2,1)S(1)} %pair.2.refs_0_), channel_id=1, source_target_pairs={{0,2},{1,3},{2,0},{3,1},{16,18},{17,19},{18,16},{19,17},{4,6},{5,7... | collective-permute-start | bytes 294920 | tf_op jit(solution)/shard_map/ppermute | solution.py:634
  23.9 1.7 %collective-permute-start.7 = (f32[12,32,128]{2,1,0:T(8,128)S(1)}, f32[12,32,128]{2,1,0:T(8,128)S(1)}, u32[]{:S(2)}, u32[]{:S(2)}) collective-permute-start(f32[12,32,128]{2,1,0:T(8,128)S(1)} %close.1.mine_ref.image_ref), channel_id=1, source_target_pairs={{0,1},{1,0},{2,3},{3,2},{16,17},{17,16},{18,19},{19,18},{4,5},{5,4... | collective-permute-start | bytes 589832 | tf_op jit(solution)/shard_map/ppermute | solution.py:634
  24.0 5.7 %collective-permute-start.8 = (bf16[2,32,128]{2,1,0:T(8,128)(2,1)S(1)}, bf16[2,32,128]{2,1,0:T(8,128)(2,1)S(1)}, u32[]{:S(2)}, u32[]{:S(2)}) collective-permute-start(bf16[2,32,128]{2,1,0:T(8,128)(2,1)S(1)} %edge.2), channel_id=1, source_target_pairs={{0,12},{4,8},{8,4},{12,0},{1,13},{5,9},{9,5},{13,1},{2,14},{6,10},... | collective-permute-start | bytes 49160 | tf_op jit(solution)/shard_map/ppermute | solution.py:591
  26.2 3.5 %collective-permute-start.11 = (bf16[1,16,1024]{2,1,0:T(8,128)(2,1)S(1)}, bf16[1,16,1024]{2,1,0:T(8,128)(2,1)S(1)}, u32[]{:S(2)}, u32[]{:S(2)}) collective-permute-start(bf16[1,16,1024]{2,1,0:T(8,128)(2,1)S(1)} %get-tuple-element.34), channel_id=1, source_target_pairs={{0,1},{1,0},{2,6},{3,7},{16,24},{17,25},{18,30},{19,31},{4,8},{5,9... | collective-permute-start | bytes 98312 | tf_op jit(solution)/shard_map/ppermute | solution.py:586
  26.4 4.5 %collective-permute-start.10 = (bf16[4,32,128]{2,1,0:T(8,128)(2,1)S(1)}, bf16[4,32,128]{2,1,0:T(8,128)(2,1)S(1)}, u32[]{:S(2)}, u32[]{:S(2)}) collective-permute-start(bf16[4,32,128]{2,1,0:T(8,128)(2,1)S(1)} %edge.3), channel_id=1, source_target_pairs={{0,4},{4,0},{8,12},{12,8},{1,5},{5,1},{9,13},{13,9},{2,6},{6,2},{1... | collective-permute-start | bytes 98312 | tf_op jit(solution)/shard_map/ppermute | solution.py:591
  29.7 1.2 %collective-permute-start.9 = (bf16[2,32,128]{2,1,0:T(8,128)(2,1)S(1)}, bf16[2,32,128]{2,1,0:T(8,128)(2,1)S(1)}, u32[]{:S(2)}, u32[]{:S(2)}) collective-permute-start(bf16[2,32,128]{2,1,0:T(8,128)(2,1)S(1)} %collective-permute-done.8.one_ref), channel_id=1, source_target_pairs={{0,1},{1,0},{2,3},{3,2},{16,17},{17,16},{18,19},{19,18},{4,5},{5,4... | collective-permute-start | bytes 49160 | tf_op jit(solution)/shard_map/ppermute | solution.py:634
  31.7 1.4 %collective-permute-start.12 = (bf16[12,32,128]{2,1,0:T(8,128)(2,1)S(1)}, bf16[12,32,128]{2,1,0:T(8,128)(2,1)S(1)}, u32[]{:S(2)}, u32[]{:S(2)}) collective-permute-start(bf16[12,32,128]{2,1,0:T(8,128)(2,1)S(1)} %get-tuple-element.36), channel_id=1, source_target_pairs={{0,1},{1,0},{2,3},{3,2},{16,17},{17,16},{18,19},{19,18},{4,5},{5,4... | collective-permute-start | bytes 294920 | tf_op jit(solution)/shard_map/ppermute | solution.py:634
  33.0 8.0 %collective-permute-start.13 = (bf16[12,32,128]{2,1,0:T(8,128)(2,1)S(1)}, bf16[12,32,128]{2,1,0:T(8,128)(2,1)S(1)}, u32[]{:S(2)}, u32[]{:S(2)}) collective-permute-start(bf16[12,32,128]{2,1,0:T(8,128)(2,1)S(1)} %pair.3.refs_0_), channel_id=1, source_target_pairs={{0,18},{1,19},{2,16},{3,17},{16,2},{17,3},{18,0},{19,1},{4,22},{5,... | collective-permute-start | bytes 294920 | tf_op jit(solution)/shard_map/ppermute | solution.py:634
  37.4 4.6 %collective-permute-start.14 = (bf16[12,32,128]{2,1,0:T(8,128)(2,1)S(1)}, bf16[12,32,128]{2,1,0:T(8,128)(2,1)S(1)}, u32[]{:S(2)}, u32[]{:S(2)}) collective-permute-start(bf16[12,32,128]{2,1,0:T(8,128)(2,1)S(1)} %pair.3.refs_0_), channel_id=1, source_target_pairs={{0,16},{1,17},{2,18},{3,19},{16,0},{17,1},{18,2},{19,3},{4,20},{5,... | collective-permute-start | bytes 294920 | tf_op jit(solution)/shard_map/ppermute | solution.py:634
  37.4 5.2 %collective-permute-start.15 = (bf16[12,32,128]{2,1,0:T(8,128)(2,1)S(1)}, bf16[12,32,128]{2,1,0:T(8,128)(2,1)S(1)}, u32[]{:S(2)}, u32[]{:S(2)}) collective-permute-start(bf16[12,32,128]{2,1,0:T(8,128)(2,1)S(1)} %pair.3.refs_0_), channel_id=1, source_target_pairs={{0,2},{1,3},{2,0},{3,1},{16,18},{17,19},{18,16},{19,17},{4,6},{5,7... | collective-permute-start | bytes 294920 | tf_op jit(solution)/shard_map/ppermute | solution.py:634

commit v13 on v12

--- a/solution.py
+++ b/solution.py
@@ -91,19 +91,22 @@
     coefs = exp_ref.shape[0]
     step = -(-coefs // PIECES)
     copies = []
-    for k in range(width):
-        for p in range(PIECES):
-            part = pl.ds(p * step, min(step, coefs - p * step))
-            copies.append(
-                pltpu.make_async_copy(exp_ref.at[part, unit + k], window_ref.at[k, part], sem.at[k, p])
-            )
+    for p in range(PIECES):
+        part = pl.ds(p * step, min(step, coefs - p * step))
+        copies.append(
+            pltpu.make_async_copy(exp_ref.at[part, pl.ds(unit, width)], window_ref.at[part], sem.at[p])
+        )
     return copies
 
 
-def clear_rest(window_ref, coefs, width):
-    rest = window_ref.shape[1] - coefs
-    for k in range(width):
-        window_ref[k, pl.ds(coefs, rest)] = jnp.zeros((rest, 2, LANES), BF16)
+def clear_rest(window_ref, coefs):
+    rest = window_ref.shape[0] - coefs
+    window_ref[pl.ds(coefs, rest)] = jnp.zeros((rest, *window_ref.shape[1:]), BF16)
+
+
+def window_rows(window_ref):
+    coefs, width = window_ref.shape[:2]
+    return jnp.concatenate([window_ref[:, k].reshape(2 * coefs, LANES) for k in range(width)], axis=-1)
 
 
 def multi_rows(fields, width, leaf, unit, leaves_ref, low_ref, window_ref):
@@ -114,16 +117,11 @@
         rows = jnp.concatenate([low_ref[unit + k] for k in range(width)], axis=-1)
     mask = window_mask(leaves_ref, leaf, unit, 2 * fields, width)
     rows = halves(jnp.where(mask, rows.astype(F32), 0.0).astype(rows.dtype))
-    expansions = jnp.concatenate([as_rows(window_ref.at[k]) for k in range(width)], axis=-1)
-    total = joined(dot_nt(rows, expansions), 2 * fields)
+    total = joined(dot_nt(rows, window_rows(window_ref)), 2 * fields)
     on_real, on_imag = total[:fields], total[fields:]
     odd = odd_lanes(on_real.shape)
     other = jnp.where(odd, from_left(on_imag), from_right(on_imag))
     return jnp.where(odd, -on_real, on_real) - other
-
-
-def as_rows(ref):
-    return ref.reshape(ref.shape[0] * 2, ref.shape[2])[...]
 
 
 def edge_kernel(row_ref, image_ref, one_ref, two_ref):
@@ -176,7 +174,7 @@
     for load in loads:
         load.start()
     for i in range(items):
-        clear_rest(window_ref.at[i], exp_ref.shape[0], width)
+        clear_rest(window_ref.at[i], exp_ref.shape[0])
     slots = pairs_ref.shape[0]
     own = own_ref[0]
     loads[0].wait()
@@ -220,7 +218,7 @@
 def fetch_kernel(items, width, slots, plan_ref, exp_ref, trans_ref, window_ref, moved_ref, trans_buf, sem, trans_sem):
     coefs = trans_ref.shape[3]
     for i in range(items):
-        clear_rest(window_ref.at[i], coefs, width)
+        clear_rest(window_ref.at[i], coefs)
 
     def trans_copy(i):
         offset = plan_ref[item_place(slots, i) + 4]
@@ -345,7 +343,7 @@
         rows = jnp.concatenate(
             [jnp.where(odd, -local_imag, local_real), jnp.where(odd, local_real, local_imag)], axis=0
         ).astype(BF16)
-        expansions = jnp.concatenate([as_rows(window_ref.at[i, k]) for k in range(width)], axis=-1)
+        expansions = window_rows(window_ref.at[i])
         place = item_place(slots, i)
         leaf, unit = plan_ref[place + 2], plan_ref[place + 3]
         mask = window_mask(leaves_ref, leaf, unit, 2 * fields, width)
@@ -533,7 +531,7 @@
     pad_coefs = -(-coefs // 8) * 8
     chips = group // 2
     assert group == 2 * chips and chips & (chips - 1) == 0 and LANES % fields == 0
-    window_shape = jax.ShapeDtypeStruct((items, width, pad_coefs, 2, LANES), BF16)
+    window_shape = jax.ShapeDtypeStruct((items, pad_coefs, width, 2, LANES), BF16)
     item_shape = jax.ShapeDtypeStruct((items, fields, 2 * pad_coefs), BF16)
     half_units = (units // 2, both, LANES)
     assert units % 2 == 0 and edge_units % 2 == 0
@@ -564,7 +562,7 @@
         ]
         + [
             pltpu.SemaphoreType.DMA((7,)),
-            pltpu.SemaphoreType.DMA((items, width, PIECES)),
+            pltpu.SemaphoreType.DMA((items, PIECES)),
         ],
         compiler_params=params(),
         name="begin",
@@ -622,7 +620,7 @@
         out_specs=(VMEM, VMEM),
         scratch_shapes=[
             pltpu.VMEM((items, coefs, 2, coefs), BF16),
-            pltpu.SemaphoreType.DMA((items, width, PIECES)),
+            pltpu.SemaphoreType.DMA((items, PIECES)),
             pltpu.SemaphoreType.DMA((items,)),
         ],
         compiler_params=params(24),

time: 52.9 us -> 52.8 us (level)
  no operation moved by 1% of the time
where the time goes in v13:
time: 52.8 us; the launch traced here: 52.6 us
  starting transfers between devices  18.1 us (34%)
  waiting for transfers between devices  15.7 us (30%)
  Pallas kernels  9.29 us (18%)
  blocking collectives  8.74 us (17%)
  between operations  0.78 us (1%)
    ppermute x10, waiting for transfers between devices, swapped(): return lax.ppermute(value, GROUP, [(g, g ^ step) for g in range(group)])  12.5 us
    ppermute x10, starting transfers between devices, swapped(): return lax.ppermute(value, GROUP, [(g, g ^ step) for g in range(group)])  9.52 us
    all_to_all x1, blocking collectives, local(): lax.all_to_all(lines, EVERY, 0, 0, axis_index_groups=same_chip, tiled=True)  8.74 us
    ppermute x4, starting transfers between devices, along_row(): return lax.ppermute(value, 'row', list(enumerate(neighbours[which])))  8.39 us
    ppermute x4, waiting for transfers between devices, along_row(): return lax.ppermute(value, 'row', list(enumerate(neighbours[which])))  3.17 us
    pallas_call x1, Pallas kernels, local(): pl.pallas_call(functools.partial(begin_kernel, fields, items, width, send...  2.74 us
    pallas_call x1, Pallas kernels, local(): pl.pallas_call(functools.partial(fetch_kernel, items, width, slots), out_...  1.73 us
  transfers between devices with their start and end apart: 16, of which 10 were waited for; matrix products, arithmetic and copies ran while one was open for 0% of the time, Pallas kernels for 7%

profile of v13, /device:TPU:0, one launch (start us, length us, event | category | flops | bytes accessed | tf_op | source)
XLA Modules:
  0.0 52.6 jit_solution(16494864961311777803)
XLA Ops:
  0.0 2.7 %begin.1 = (s32[13]{0:T(128)S(4)}, bf16[1,16,896]{2,1,0:T(8,128)(2,1)S(1)}, bf16[1,448,3,2,128]{4,3,2,1,0:T(2,128)(2,1)S(1)}, s32[24,1,128]{2,1,0:T(1,128)S(1)}, f32[32,3072]{1,0:T(8,128)S(1)}) custom-call(s32[1]{0:T(128)} %bitcast.1.row_ref, s32[1]{0:T(128)} %bitcast.2.own_ref, s32[4,2,4]{2,1,0:T(2,128)} %bitcast.18, s32[1,3072]{1,0:T(1,128)} %leaf_hbm.1, ...), custom_call_target="tpu_custom_call" | custom-call | tf_op jit(solution)/shard_map/begin/pallas_call | solution.py:548
  2.8 5.1 %collective-permute-start = (bf16[32,512]{1,0:T(8,128)(2,1)S(1)}, bf16[32,512]{1,0:T(8,128)(2,1)S(1)}, u32[]{:S(2)}, u32[]{:S(2)}) collective-permute-start(bf16[32,512]{1,0:T(8,128)(2,1)S(1)} %get-tuple-element.24), channel_id=1, source_target_pairs={{0,12},{4,8},{8,4},{12,0},{1,13},{5,9},{9,5},{13,1},{2,14},{6,10},... | collective-permute-start | bytes 98312 | tf_op jit(solution)/shard_map/ppermute | solution.py:589
  8.6 1.7 %fetch.1 = (bf16[1,448,3,2,128]{4,3,2,1,0:T(2,128)(2,1)S(1)}, bf16[1,896,441]{2,1,0:T(8,128)(2,1)S(1)}) custom-call(s32[13]{0:T(128)S(4)} %get-tuple-element.22.plan_ref, bf16[441,24,2,128]{3,2,1,0:T(2,128)(2,1)} %bitcast.14, bf16[4,441,2,441]{3,2,1,0:T(2,128)(2,1)} %bitcast.15), custom_call_target="tpu_custom_call" | custom-call | bytes 2064384 | tf_op jit(solution)/shard_map/fetch/pallas_call | solution.py:613
  10.3 1.5 %collective-permute-done.1.two_ref = bf16[32,512]{1,0:T(8,128)(2,1)S(1)} collective-permute-done((bf16[32,512]{1,0:T(8,128)(2,1)S(1)}, bf16[32,512]{1,0:T(8,128)(2,1)S(1)}, u32[]{:S(2)}, u32[]{:S(2)}) %collective-permute-start.1) | collective-permute-done | bytes 32800 | tf_op jit(solution)/shard_map/ppermute | solution.py:589
  11.8 0.8 %near.1.partial_ref = f32[24,32,128]{2,1,0:T(8,128)S(1)} custom-call(s32[1]{0:T(128)} %bitcast.1.row_ref, s32[1]{0:T(128)S(6)} %copy.11.count_ref, s32[13]{0:T(128)S(4)} %get-tuple-element.22.plan_ref, bf16[32,512]{1,0:T(8,128)(2,1)S(1)} %collective-permute-done.one_ref, bf16[32,512]{1,0:T(8,128)(2,1)S(1)} %collective-permute-done.1.two_ref, ...), custom_call_target="tpu_custom_call" | custom-call | flops 67108864 | bytes 2097152 | tf_op jit(solution)/shard_map/near/pallas_call | solution.py:635
  12.6 0.7 %far.1 = (f32[12,32,128]{2,1,0:T(8,128)S(1)}, f32[12,32,128]{2,1,0:T(8,128)S(1)}) custom-call(s32[1]{0:T(128)} %bitcast.core_ref, s32[13]{0:T(128)S(4)} %get-tuple-element.22.plan_ref, s32[24,1,128]{2,1,0:T(1,128)S(1)} %get-tuple-element.23.leaves_ref, f32[24,32,128]{2,1,0:T(8,128)S(1)} %near.1.partial_ref, ...), custom_call_target="tpu_custom_call" | custom-call | tf_op jit(solution)/shard_map/far/pallas_call | solution.py:650
  13.3 0.1 collective-permute-start.3
  13.3 1.4 %collective-permute-done.3.got_ref = f32[12,32,128]{2,1,0:T(8,128)S(1)} collective-permute-done((f32[12,32,128]{2,1,0:T(8,128)S(1)}, f32[12,32,128]{2,1,0:T(8,128)S(1)}, u32[]{:S(2)}, u32[]{:S(2)}) %collective-permute-start.3) | collective-permute-done | bytes 196640 | tf_op jit(solution)/shard_map/ppermute | solution.py:632
  14.8 3.5 %collective-permute-start.4 = (bf16[12,32,128]{2,1,0:T(8,128)(2,1)S(1)}, bf16[12,32,128]{2,1,0:T(8,128)(2,1)S(1)}, u32[]{:S(2)}, u32[]{:S(2)}) collective-permute-start(bf16[12,32,128]{2,1,0:T(8,128)(2,1)S(1)} %pair.2.refs_0_), channel_id=1, source_target_pairs={{0,18},{1,19},{2,16},{3,17},{16,2},{17,3},{18,0},{19,1},{4,22},{5,... | collective-permute-start | bytes 294920 | tf_op jit(solution)/shard_map/ppermute | solution.py:632
  18.3 0.5 collective-permute-start.5
  18.8 0.1 collective-permute-start.6
  18.9 2.9 %collective-permute-done.4.refs_1_ = bf16[12,32,128]{2,1,0:T(8,128)(2,1)S(1)} collective-permute-done((bf16[12,32,128]{2,1,0:T(8,128)(2,1)S(1)}, bf16[12,32,128]{2,1,0:T(8,128)(2,1)S(1)}, u32[]{:S(2)}, u32[]{:S(2)}) %collective-permute-start.4) | collective-permute-done | bytes 98336 | tf_op jit(solution)/shard_map/ppermute | solution.py:632
  21.9 1.8 %collective-permute-done.5.refs_2_ = bf16[12,32,128]{2,1,0:T(8,128)(2,1)S(1)} collective-permute-done((bf16[12,32,128]{2,1,0:T(8,128)(2,1)S(1)}, bf16[12,32,128]{2,1,0:T(8,128)(2,1)S(1)}, u32[]{:S(2)}, u32[]{:S(2)}) %collective-permute-start.5) | collective-permute-done | bytes 98336 | tf_op jit(solution)/shard_map/ppermute | solution.py:632
  23.8 0.1 collective-permute-start.7
  23.9 1.6 %collective-permute-start.8 = (bf16[2,32,128]{2,1,0:T(8,128)(2,1)S(1)}, bf16[2,32,128]{2,1,0:T(8,128)(2,1)S(1)}, u32[]{:S(2)}, u32[]{:S(2)}) collective-permute-start(bf16[2,32,128]{2,1,0:T(8,128)(2,1)S(1)} %edge.2), channel_id=1, source_target_pairs={{0,12},{4,8},{8,4},{12,0},{1,13},{5,9},{9,5},{13,1},{2,14},{6,10},... | collective-permute-start | bytes 49160 | tf_op jit(solution)/shard_map/ppermute | solution.py:589
  25.5 0.6 %assemble.1 = (f32[24,32,128]{2,1,0:T(8,128)S(1)}, bf16[24,32,128]{2,1,0:T(8,128)(2,1)S(1)}, bf16[1,16,1024]{2,1,0:T(8,128)(2,1)S(1)}) custom-call(s32[1]{0:T(128)} %bitcast.core_ref, s32[13]{0:T(128)S(4)} %get-tuple-element.22.plan_ref, s32[24,1,128]{2,1,0:T(1,128)S(1)} %get-tuple-element.23.leaves_ref, f32[12,32,128]{2,1,0:T(8,128)S(1)} %close.1.mine_ref.image_ref, ...), custom_call_target="tpu_custom_call" | custom-call | tf_op jit(solution)/shard_map/assemble/pallas_call | solution.py:710
  26.0 0.2 collective-permute-start.11
  26.2 1.7 %collective-permute-start.10 = (bf16[4,32,128]{2,1,0:T(8,128)(2,1)S(1)}, bf16[4,32,128]{2,1,0:T(8,128)(2,1)S(1)}, u32[]{:S(2)}, u32[]{:S(2)}) collective-permute-start(bf16[4,32,128]{2,1,0:T(8,128)(2,1)S(1)} %edge.3), channel_id=1, source_target_pairs={{0,4},{4,0},{8,12},{12,8},{1,5},{5,1},{9,13},{13,9},{2,6},{6,2},{1... | collective-permute-start | bytes 98312 | tf_op jit(solution)/shard_map/ppermute | solution.py:589
  27.9 1.7 %collective-permute-done.8.one_ref = bf16[2,32,128]{2,1,0:T(8,128)(2,1)S(1)} collective-permute-done((bf16[2,32,128]{2,1,0:T(8,128)(2,1)S(1)}, bf16[2,32,128]{2,1,0:T(8,128)(2,1)S(1)}, u32[]{:S(2)}, u32[]{:S(2)}) %collective-permute-start.8) | collective-permute-done | bytes 16416 | tf_op jit(solution)/shard_map/ppermute | solution.py:589
  29.6 0.6 %first_far.1.image_ref = f32[1,3,32,128]{3,2,1,0:T(8,128)S(1)} custom-call(s32[13]{0:T(128)S(4)} %get-tuple-element.22.plan_ref, s32[24,1,128]{2,1,0:T(1,128)S(1)} %get-tuple-element.23.leaves_ref, bf16[1,16,1024]{2,1,0:T(8,128)(2,1)S(1)} %collective-permute-done.11.item_ref, bf16[1,896,441]{2,1,0:T(8,128)(2,1)S(1)} %get-tuple-element.27.trans_ref, ...), custom_call_target="tpu_custom_call" | custom-call | tf_op jit(solution)/shard_map/first_far/pallas_call | solution.py:662
  30.2 0.6 %collective-permute-done.9.other_one_ref = bf16[2,32,128]{2,1,0:T(8,128)(2,1)S(1)} collective-permute-done((bf16[2,32,128]{2,1,0:T(8,128)(2,1)S(1)}, bf16[2,32,128]{2,1,0:T(8,128)(2,1)S(1)}, u32[]{:S(2)}, u32[]{:S(2)}) %collective-permute-start.9) | collective-permute-done | bytes 16416 | tf_op jit(solution)/shard_map/ppermute | solution.py:632
  30.8 0.8 %last_near.1 = (bf16[12,32,128]{2,1,0:T(8,128)(2,1)S(1)}, bf16[12,32,128]{2,1,0:T(8,128)(2,1)S(1)}) custom-call(s32[1]{0:T(128)} %bitcast.core_ref, s32[1]{0:T(128)} %bitcast.1.row_ref, s32[1]{0:T(128)S(6)} %copy.11.count_ref, s32[13]{0:T(128)S(4)} %get-tuple-element.22.plan_ref, bf16[2,32,128]{2,1,0:T(8,128)(2,1)S(1)} %collective-permute-done.8.one_ref, ...), custom_call_target="tpu_custom_call" | custom-call | tf_op jit(solution)/shard_map/last_near/pallas_call | solution.py:673
  31.5 0.2 collective-permute-start.12
  31.8 1.1 %collective-permute-done.12.got_ref = bf16[12,32,128]{2,1,0:T(8,128)(2,1)S(1)} collective-permute-done((bf16[12,32,128]{2,1,0:T(8,128)(2,1)S(1)}, bf16[12,32,128]{2,1,0:T(8,128)(2,1)S(1)}, u32[]{:S(2)}, u32[]{:S(2)}) %collective-permute-start.12) | collective-permute-done | bytes 98336 | tf_op jit(solution)/shard_map/ppermute | solution.py:632
  32.9 4.4 %collective-permute-start.13 = (bf16[12,32,128]{2,1,0:T(8,128)(2,1)S(1)}, bf16[12,32,128]{2,1,0:T(8,128)(2,1)S(1)}, u32[]{:S(2)}, u32[]{:S(2)}) collective-permute-start(bf16[12,32,128]{2,1,0:T(8,128)(2,1)S(1)} %pair.3.refs_0_), channel_id=1, source_target_pairs={{0,18},{1,19},{2,16},{3,17},{16,2},{17,3},{18,0},{19,1},{4,22},{5,... | collective-permute-start | bytes 294920 | tf_op jit(solution)/shard_map/ppermute | solution.py:632
  37.3 0.6 %collective-permute-start.15 = (bf16[12,32,128]{2,1,0:T(8,128)(2,1)S(1)}, bf16[12,32,128]{2,1,0:T(8,128)(2,1)S(1)}, u32[]{:S(2)}, u32[]{:S(2)}) collective-permute-start(bf16[12,32,128]{2,1,0:T(8,128)(2,1)S(1)} %pair.3.refs_0_), channel_id=1, source_target_pairs={{0,2},{1,3},{2,0},{3,1},{16,18},{17,19},{18,16},{19,17},{4,6},{5,7... | collective-permute-start | bytes 294920 | tf_op jit(solution)/shard_map/ppermute | solution.py:632
  38.0 2.9 %collective-permute-done.13.refs_1_ = bf16[12,32,128]{2,1,0:T(8,128)(2,1)S(1)} collective-permute-done((bf16[12,32,128]{2,1,0:T(8,128)(2,1)S(1)}, bf16[12,32,128]{2,1,0:T(8,128)(2,1)S(1)}, u32[]{:S(2)}, u32[]{:S(2)}) %collective-permute-start.13) | collective-permute-done | bytes 98336 | tf_op jit(solution)/shard_map/ppermute | solution.py:632
  40.9 1.0 %collective-permute-done.14.refs_2_ = bf16[12,32,128]{2,1,0:T(8,128)(2,1)S(1)} collective-permute-done((bf16[12,32,128]{2,1,0:T(8,128)(2,1)S(1)}, bf16[12,32,128]{2,1,0:T(8,128)(2,1)S(1)}, u32[]{:S(2)}, u32[]{:S(2)}) %collective-permute-start.14) | collective-permute-done | bytes 98336 | tf_op jit(solution)/shard_map/ppermute | solution.py:632
  41.9 0.6 %collective-permute-done.15.refs_3_ = bf16[12,32,128]{2,1,0:T(8,128)(2,1)S(1)} collective-permute-done((bf16[12,32,128]{2,1,0:T(8,128)(2,1)S(1)}, bf16[12,32,128]{2,1,0:T(8,128)(2,1)S(1)}, u32[]{:S(2)}, u32[]{:S(2)}) %collective-permute-start.15) | collective-permute-done | bytes 98336 | tf_op jit(solution)/shard_map/ppermute | solution.py:632
  42.5 0.3 gram.1
  42.8 8.7 %all_to_all.5.sums_ref = f32[8,2,128]{2,1,0:T(2,128)S(1)} all-to-all(f32[8,2,128]{2,1,0:T(2,128)S(1)} %gram.1), channel_id=1, replica_groups={{0,1,4,5,8,9,12,13},{2,3,6,7,10,11,14,15},{16,17,20,21,24,25,28,29},{18..., dimensions={0} | all-to-all | bytes 16384 | tf_op jit(solution)/shard_map/all_to_all | solution.py:745
  51.5 1.0 %combine.1 = f32[32,3072]{1,0:T(8,128)} custom-call(f32[8,2,128]{2,1,0:T(2,128)S(1)} %all_to_all.5.sums_ref, f32[32,3072]{1,0:T(8,128)S(1)} %get-tuple-element.21.image_ref.here_ref.right_ref, f32[24,32,128]{2,1,0:T(8,128)S(1)} %get-tuple-element.32.image_ref), custom_call_target="tpu_custom_call" | custom-call | tf_op jit(solution)/shard_map/combine/pallas_call | solution.py:746
  (18 shorter events, 0.2 us)
Async XLA Ops:
  2.8 7.5 %collective-permute-start = (bf16[32,512]{1,0:T(8,128)(2,1)S(1)}, bf16[32,512]{1,0:T(8,128)(2,1)S(1)}, u32[]{:S(2)}, u32[]{:S(2)}) collective-permute-start(bf16[32,512]{1,0:T(8,128)(2,1)S(1)} %get-tuple-element.24), channel_id=1, source_target_pairs={{0,12},{4,8},{8,4},{12,0},{1,13},{5,9},{9,5},{13,1},{2,14},{6,10},... | collective-permute-start | bytes 98312 | tf_op jit(solution)/shard_map/ppermute | solution.py:589
  7.9 3.9 %collective-permute-start.1 = (bf16[32,512]{1,0:T(8,128)(2,1)S(1)}, bf16[32,512]{1,0:T(8,128)(2,1)S(1)}, u32[]{:S(2)}, u32[]{:S(2)}) collective-permute-start(bf16[32,512]{1,0:T(8,128)(2,1)S(1)} %get-tuple-element.25), channel_id=1, source_target_pairs={{0,4},{4,0},{8,12},{12,8},{1,5},{5,1},{9,13},{13,9},{2,6},{6,2},{1... | collective-permute-start | bytes 98312 | tf_op jit(solution)/shard_map/ppermute | solution.py:589
  7.9 4.7 %collective-permute-start.2 = (bf16[1,16,896]{2,1,0:T(8,128)(2,1)S(1)}, bf16[1,16,896]{2,1,0:T(8,128)(2,1)S(1)}, u32[]{:S(2)}, u32[]{:S(2)}) collective-permute-start(bf16[1,16,896]{2,1,0:T(8,128)(2,1)S(1)} %get-tuple-element.26), channel_id=1, source_target_pairs={{0,1},{1,0},{2,6},{3,7},{16,24},{17,25},{18,30},{19,31},{4,8},{5,9... | collective-permute-start | bytes 86024 | tf_op jit(solution)/shard_map/ppermute | solution.py:584
  8.6 3.3 %copy-start = (bf16[2,8,256,256]{3,2,1,0:T(8,128)(2,1)S(1)}, bf16[2,8,256,256]{3,2,1,0:T(8,128)(2,1)}, u32[]{:S(2)}) copy-start(bf16[2,8,256,256]{3,2,1,0:T(8,128)(2,1)} %tiles_ref.3) | copy-start | bytes 6291460
  13.3 1.5 %collective-permute-start.3 = (f32[12,32,128]{2,1,0:T(8,128)S(1)}, f32[12,32,128]{2,1,0:T(8,128)S(1)}, u32[]{:S(2)}, u32[]{:S(2)}) collective-permute-start(f32[12,32,128]{2,1,0:T(8,128)S(1)} %get-tuple-element.30), channel_id=1, source_target_pairs={{0,1},{1,0},{2,3},{3,2},{16,17},{17,16},{18,19},{19,18},{4,5},{5,4... | collective-permute-start | bytes 589832 | tf_op jit(solution)/shard_map/ppermute | solution.py:632
  14.8 7.1 %collective-permute-start.4 = (bf16[12,32,128]{2,1,0:T(8,128)(2,1)S(1)}, bf16[12,32,128]{2,1,0:T(8,128)(2,1)S(1)}, u32[]{:S(2)}, u32[]{:S(2)}) collective-permute-start(bf16[12,32,128]{2,1,0:T(8,128)(2,1)S(1)} %pair.2.refs_0_), channel_id=1, source_target_pairs={{0,18},{1,19},{2,16},{3,17},{16,2},{17,3},{18,0},{19,1},{4,22},{5,... | collective-permute-start | bytes 294920 | tf_op jit(solution)/shard_map/ppermute | solution.py:632
  18.3 5.4 %collective-permute-start.5 = (bf16[12,32,128]{2,1,0:T(8,128)(2,1)S(1)}, bf16[12,32,128]{2,1,0:T(8,128)(2,1)S(1)}, u32[]{:S(2)}, u32[]{:S(2)}) collective-permute-start(bf16[12,32,128]{2,1,0:T(8,128)(2,1)S(1)} %pair.2.refs_0_), channel_id=1, source_target_pairs={{0,16},{1,17},{2,18},{3,19},{16,0},{17,1},{18,2},{19,3},{4,20},{5,... | collective-permute-start | bytes 294920 | tf_op jit(solution)/shard_map/ppermute | solution.py:632
  18.8 4.9 %collective-permute-start.6 = (bf16[12,32,128]{2,1,0:T(8,128)(2,1)S(1)}, bf16[12,32,128]{2,1,0:T(8,128)(2,1)S(1)}, u32[]{:S(2)}, u32[]{:S(2)}) collective-permute-start(bf16[12,32,128]{2,1,0:T(8,128)(2,1)S(1)} %pair.2.refs_0_), channel_id=1, source_target_pairs={{0,2},{1,3},{2,0},{3,1},{16,18},{17,19},{18,16},{19,17},{4,6},{5,7... | collective-permute-start | bytes 294920 | tf_op jit(solution)/shard_map/ppermute | solution.py:632
  23.8 1.7 %collective-permute-start.7 = (f32[12,32,128]{2,1,0:T(8,128)S(1)}, f32[12,32,128]{2,1,0:T(8,128)S(1)}, u32[]{:S(2)}, u32[]{:S(2)}) collective-permute-start(f32[12,32,128]{2,1,0:T(8,128)S(1)} %close.1.mine_ref.image_ref), channel_id=1, source_target_pairs={{0,1},{1,0},{2,3},{3,2},{16,17},{17,16},{18,19},{19,18},{4,5},{5,4... | collective-permute-start | bytes 589832 | tf_op jit(solution)/shard_map/ppermute | solution.py:632
  23.9 5.7 %collective-permute-start.8 = (bf16[2,32,128]{2,1,0:T(8,128)(2,1)S(1)}, bf16[2,32,128]{2,1,0:T(8,128)(2,1)S(1)}, u32[]{:S(2)}, u32[]{:S(2)}) collective-permute-start(bf16[2,32,128]{2,1,0:T(8,128)(2,1)S(1)} %edge.2), channel_id=1, source_target_pairs={{0,12},{4,8},{8,4},{12,0},{1,13},{5,9},{9,5},{13,1},{2,14},{6,10},... | collective-permute-start | bytes 49160 | tf_op jit(solution)/shard_map/ppermute | solution.py:589
  26.0 3.6 %collective-permute-start.11 = (bf16[1,16,1024]{2,1,0:T(8,128)(2,1)S(1)}, bf16[1,16,1024]{2,1,0:T(8,128)(2,1)S(1)}, u32[]{:S(2)}, u32[]{:S(2)}) collective-permute-start(bf16[1,16,1024]{2,1,0:T(8,128)(2,1)S(1)} %get-tuple-element.34), channel_id=1, source_target_pairs={{0,1},{1,0},{2,6},{3,7},{16,24},{17,25},{18,30},{19,31},{4,8},{5,9... | collective-permute-start | bytes 98312 | tf_op jit(solution)/shard_map/ppermute | solution.py:584
  26.2 4.5 %collective-permute-start.10 = (bf16[4,32,128]{2,1,0:T(8,128)(2,1)S(1)}, bf16[4,32,128]{2,1,0:T(8,128)(2,1)S(1)}, u32[]{:S(2)}, u32[]{:S(2)}) collective-permute-start(bf16[4,32,128]{2,1,0:T(8,128)(2,1)S(1)} %edge.3), channel_id=1, source_target_pairs={{0,4},{4,0},{8,12},{12,8},{1,5},{5,1},{9,13},{13,9},{2,6},{6,2},{1... | collective-permute-start | bytes 98312 | tf_op jit(solution)/shard_map/ppermute | solution.py:589
  29.6 1.2 %collective-permute-start.9 = (bf16[2,32,128]{2,1,0:T(8,128)(2,1)S(1)}, bf16[2,32,128]{2,1,0:T(8,128)(2,1)S(1)}, u32[]{:S(2)}, u32[]{:S(2)}) collective-permute-start(bf16[2,32,128]{2,1,0:T(8,128)(2,1)S(1)} %collective-permute-done.8.one_ref), channel_id=1, source_target_pairs={{0,1},{1,0},{2,3},{3,2},{16,17},{17,16},{18,19},{19,18},{4,5},{5,4... | collective-permute-start | bytes 49160 | tf_op jit(solution)/shard_map/ppermute | solution.py:632
  31.5 1.4 %collective-permute-start.12 = (bf16[12,32,128]{2,1,0:T(8,128)(2,1)S(1)}, bf16[12,32,128]{2,1,0:T(8,128)(2,1)S(1)}, u32[]{:S(2)}, u32[]{:S(2)}) collective-permute-start(bf16[12,32,128]{2,1,0:T(8,128)(2,1)S(1)} %get-tuple-element.36), channel_id=1, source_target_pairs={{0,1},{1,0},{2,3},{3,2},{16,17},{17,16},{18,19},{19,18},{4,5},{5,4... | collective-permute-start | bytes 294920 | tf_op jit(solution)/shard_map/ppermute | solution.py:632
  32.9 8.0 %collective-permute-start.13 = (bf16[12,32,128]{2,1,0:T(8,128)(2,1)S(1)}, bf16[12,32,128]{2,1,0:T(8,128)(2,1)S(1)}, u32[]{:S(2)}, u32[]{:S(2)}) collective-permute-start(bf16[12,32,128]{2,1,0:T(8,128)(2,1)S(1)} %pair.3.refs_0_), channel_id=1, source_target_pairs={{0,18},{1,19},{2,16},{3,17},{16,2},{17,3},{18,0},{19,1},{4,22},{5,... | collective-permute-start | bytes 294920 | tf_op jit(solution)/shard_map/ppermute | solution.py:632
  37.3 4.6 %collective-permute-start.14 = (bf16[12,32,128]{2,1,0:T(8,128)(2,1)S(1)}, bf16[12,32,128]{2,1,0:T(8,128)(2,1)S(1)}, u32[]{:S(2)}, u32[]{:S(2)}) collective-permute-start(bf16[12,32,128]{2,1,0:T(8,128)(2,1)S(1)} %pair.3.refs_0_), channel_id=1, source_target_pairs={{0,16},{1,17},{2,18},{3,19},{16,0},{17,1},{18,2},{19,3},{4,20},{5,... | collective-permute-start | bytes 294920 | tf_op jit(solution)/shard_map/ppermute | solution.py:632
  37.3 5.2 %collective-permute-start.15 = (bf16[12,32,128]{2,1,0:T(8,128)(2,1)S(1)}, bf16[12,32,128]{2,1,0:T(8,128)(2,1)S(1)}, u32[]{:S(2)}, u32[]{:S(2)}) collective-permute-start(bf16[12,32,128]{2,1,0:T(8,128)(2,1)S(1)} %pair.3.refs_0_), channel_id=1, source_target_pairs={{0,2},{1,3},{2,0},{3,1},{16,18},{17,19},{18,16},{19,17},{4,6},{5,7... | collective-permute-start | bytes 294920 | tf_op jit(solution)/shard_map/ppermute | solution.py:632

commit v14 on v13

--- a/solution.py
+++ b/solution.py
@@ -351,6 +351,15 @@
         give(i, unit, image)
 
 
+def fold_kernel(chip_ref, keep_ref, got_ref, own_ref, *out_refs):
+    share = own_ref.shape[0]
+    steps = [0] + swap_order(1 + len(out_refs))
+    for step, out_ref in zip(steps, (own_ref,) + out_refs):
+        for k in range(share):
+            unit = lax.bitwise_xor(chip_ref[0], step) * share + k
+            out_ref[k] = (keep_ref[unit].astype(F32) + got_ref[unit].astype(F32)).astype(out_ref.dtype)
+
+
 def pair_kernel(keep_ref, got_ref, out_ref):
     out_ref[...] = (keep_ref[...].astype(F32) + got_ref[...].astype(F32)).astype(out_ref.dtype)
 
@@ -413,11 +422,11 @@
     return columns[:count]
 
 
-def gram_kernel(fields, core_ref, right_ref, image_ref, *refs):
+def gram_kernel(fields, core_ref, first_ref, right_ref, image_ref, *refs):
     *parts, out_ref = refs
     totals = None
     for k in range(parts[0].shape[0]):
-        unit = 2 * k + core_ref[0]
+        unit = 2 * (first_ref[0] + k) + core_ref[0]
         r = right_ref[:, pl.ds(pl.multiple_of(unit * LANES, LANES), LANES)]
         z = image_ref[unit]
         q = tree_sum([part[k].astype(F32) for part in by_step(parts)])
@@ -526,7 +535,7 @@
     assert rows % 2 == 0
     neighbours = [[(r - 1 + 2 * (r % 2)) % rows for r in range(rows)], [r + 1 - 2 * (r % 2) for r in range(rows)]]
     own_place, row_place = own.reshape(1), row_here.reshape(1)
-    core_place = lax.rem(own, 2).reshape(1)
+    core_place, chip_place = lax.rem(own, 2).reshape(1), lax.div(own, 2).reshape(1)
     slots = near_tiles.shape[1]
     pad_coefs = -(-coefs // 8) * 8
     chips = group // 2
@@ -696,6 +705,18 @@
         arrived = {step: swapped(pair, 2 * step) for step in swap_order(chips)}
         return [pair] + list(arrived.values())
 
+    def own_pieces(keep, got):
+        share = (units // 2 // chips, both, LANES)
+        pieces = pl.pallas_call(
+            fold_kernel,
+            out_shape=(jax.ShapeDtypeStruct(share, F32),) + (jax.ShapeDtypeStruct(share, BF16),) * (chips - 1),
+            in_specs=[SMEM, VMEM, VMEM],
+            out_specs=(VMEM,) * chips,
+            compiler_params=params(),
+            name="fold",
+        )(chip_place, keep, got)
+        return [pieces[0]] + [swapped(piece, 2 * step) for piece, step in zip(pieces[1:], swap_order(chips))]
+
     def half_sum(parts):
         return pl.pallas_call(
             close_kernel,
@@ -727,22 +748,32 @@
     z_all, z_low, made = whole(mine, theirs)
     image = first_far(exchanged(made))
     two = along_row(one_edge(z_low, edge_units, False), 1)
-    parts = pair_sums(*last_core_parts(one, swapped(one, 1), two, z_low, image))
+    last_parts = last_core_parts(one, swapped(one, 1), two, z_low, image)
+    columns = lax.axis_size("col")
+    half = units // 2
+    if half % chips == 0:
+        first_unit = lax.div(own, 2) * (half // chips)
+        parts = own_pieces(*last_parts)
+        members = [list(range(group * rows))]
+    else:
+        first_unit = jnp.zeros_like(own)
+        parts = pair_sums(*last_parts)
+        members = [
+            [((g + k) // columns * rows + r) * columns + (g + k) % columns for r in range(rows) for k in range(2)]
+            for g in range(0, group, 2)
+        ]
 
     lines = pl.pallas_call(
         functools.partial(gram_kernel, fields),
-        out_shape=jax.ShapeDtypeStruct((2 * rows, -(-9 * fields // LANES), LANES), F32),
-        in_specs=[SMEM] + [VMEM] * (2 + chips),
+        out_shape=jax.ShapeDtypeStruct((len(members[0]), -(-9 * fields // LANES), LANES), F32),
+        in_specs=[SMEM, SMEM] + [VMEM] * (2 + chips),
         out_specs=VMEM,
         compiler_params=params(),
         name="gram",
-    )(core_place, right, z_all, *parts)
-    columns = lax.axis_size("col")
-    same_chip = [
-        [((g + k) // columns * rows + r) * columns + (g + k) % columns for r in range(rows) for k in range(2)]
-        for g in range(0, group, 2)
-    ]
-    sums = lax.all_to_all(lines, EVERY, 0, 0, axis_index_groups=same_chip, tiled=True)
+    )(core_place, first_unit.reshape(1), right, z_all, *parts)
+    sums = lax.all_to_all(
+        lines, EVERY, 0, 0, axis_index_groups=members if len(members) > 1 else None, tiled=True
+    )
     out = pl.pallas_call(
         functools.partial(final_kernel, fields),
         out_shape=jax.ShapeDtypeStruct((both, panels), F32),

time: 52.8 us -> 53.5 us (1.013)
  blocking collectives: 8.74 us -> 11 us
  waiting for transfers between devices: 15.7 us -> 14.3 us
    all_to_all x1, blocking collectives: 8.74 us -> 11 us  [local(): lax.all_to_all(lines, EVERY, 0, 0, axis_index_groups=members if len(membe...]
    ppermute x10, waiting for transfers between devices: 12.5 us -> 11.1 us  [swapped(): return lax.ppermute(value, GROUP, [(g, g ^ step) for g in range(group)])]
  transfers between devices with their start and end apart: 16 -> 16, of which waited for: 10 -> 9; matrix products, arithmetic and copies ran while one was open for 0% -> 0% of each run, Pallas kernels for 7% -> 7%
where the time goes in v14:
time: 53.5 us; the launch traced here: 53.3 us
  starting transfers between devices  18.1 us (34%)
  waiting for transfers between devices  14.3 us (27%)
  blocking collectives  11 us (21%)
  Pallas kernels  9.16 us (17%)
  between operations  0.79 us (1%)
    ppermute x10, waiting for transfers between devices, swapped(): return lax.ppermute(value, GROUP, [(g, g ^ step) for g in range(group)])  11.1 us
    all_to_all x1, blocking collectives, local(): lax.all_to_all(lines, EVERY, 0, 0, axis_index_groups=members if len(membe...  11 us
    ppermute x10, starting transfers between devices, swapped(): return lax.ppermute(value, GROUP, [(g, g ^ step) for g in range(group)])  9.52 us
    ppermute x4, starting transfers between devices, along_row(): return lax.ppermute(value, 'row', list(enumerate(neighbours[which])))  8.4 us
    ppermute x4, waiting for transfers between devices, along_row(): return lax.ppermute(value, 'row', list(enumerate(neighbours[which])))  3.16 us
    pallas_call x1, Pallas kernels, local(): pl.pallas_call(functools.partial(begin_kernel, fields, items, width, send...  2.74 us
    pallas_call x1, Pallas kernels, local(): pl.pallas_call(functools.partial(fetch_kernel, items, width, slots), out_...  1.73 us
  transfers between devices with their start and end apart: 16, of which 9 were waited for; matrix products, arithmetic and copies ran while one was open for 0% of the time, Pallas kernels for 7%

profile of v14, /device:TPU:0, one launch (start us, length us, event | category | flops | bytes accessed | tf_op | source)
XLA Modules:
  0.0 53.3 jit_solution(798800621471518571)
XLA Ops:
  0.0 2.7 %begin.1 = (s32[13]{0:T(128)S(4)}, bf16[1,16,896]{2,1,0:T(8,128)(2,1)S(1)}, bf16[1,448,3,2,128]{4,3,2,1,0:T(2,128)(2,1)S(1)}, s32[24,1,128]{2,1,0:T(1,128)S(1)}, f32[32,3072]{1,0:T(8,128)S(1)}) custom-call(s32[1]{0:T(128)} %bitcast.2.row_ref, s32[1]{0:T(128)} %bitcast.3.own_ref, s32[4,2,4]{2,1,0:T(2,128)} %bitcast.20, s32[1,3072]{1,0:T(1,128)} %leaf_hbm.1, ...), custom_call_target="tpu_custom_call" | custom-call | tf_op jit(solution)/shard_map/begin/pallas_call | solution.py:557
  2.8 5.1 %collective-permute-start = (bf16[32,512]{1,0:T(8,128)(2,1)S(1)}, bf16[32,512]{1,0:T(8,128)(2,1)S(1)}, u32[]{:S(2)}, u32[]{:S(2)}) collective-permute-start(bf16[32,512]{1,0:T(8,128)(2,1)S(1)} %get-tuple-element.28), channel_id=1, source_target_pairs={{0,12},{4,8},{8,4},{12,0},{1,13},{5,9},{9,5},{13,1},{2,14},{6,10},... | collective-permute-start | bytes 98312 | tf_op jit(solution)/shard_map/ppermute | solution.py:598
  8.6 0.0 copy-start
  8.6 1.7 %fetch.1 = (bf16[1,448,3,2,128]{4,3,2,1,0:T(2,128)(2,1)S(1)}, bf16[1,896,441]{2,1,0:T(8,128)(2,1)S(1)}) custom-call(s32[13]{0:T(128)S(4)} %get-tuple-element.26.plan_ref, bf16[441,24,2,128]{3,2,1,0:T(2,128)(2,1)} %bitcast.16, bf16[4,441,2,441]{3,2,1,0:T(2,128)(2,1)} %bitcast.17), custom_call_target="tpu_custom_call" | custom-call | bytes 2064384 | tf_op jit(solution)/shard_map/fetch/pallas_call | solution.py:622
  10.3 1.5 %collective-permute-done.1.two_ref = bf16[32,512]{1,0:T(8,128)(2,1)S(1)} collective-permute-done((bf16[32,512]{1,0:T(8,128)(2,1)S(1)}, bf16[32,512]{1,0:T(8,128)(2,1)S(1)}, u32[]{:S(2)}, u32[]{:S(2)}) %collective-permute-start.1) | collective-permute-done | bytes 32800 | tf_op jit(solution)/shard_map/ppermute | solution.py:598
  11.8 0.8 %near.1.partial_ref = f32[24,32,128]{2,1,0:T(8,128)S(1)} custom-call(s32[1]{0:T(128)} %bitcast.2.row_ref, s32[1]{0:T(128)S(6)} %copy.11.count_ref, s32[13]{0:T(128)S(4)} %get-tuple-element.26.plan_ref, bf16[32,512]{1,0:T(8,128)(2,1)S(1)} %collective-permute-done.one_ref, bf16[32,512]{1,0:T(8,128)(2,1)S(1)} %collective-permute-done.1.two_ref, ...), custom_call_target="tpu_custom_call" | custom-call | flops 67108864 | bytes 2097152 | tf_op jit(solution)/shard_map/near/pallas_call | solution.py:644
  12.6 0.7 %far.1 = (f32[12,32,128]{2,1,0:T(8,128)S(1)}, f32[12,32,128]{2,1,0:T(8,128)S(1)}) custom-call(s32[1]{0:T(128)} %bitcast.core_ref, s32[13]{0:T(128)S(4)} %get-tuple-element.26.plan_ref, s32[24,1,128]{2,1,0:T(1,128)S(1)} %get-tuple-element.27.leaves_ref, f32[24,32,128]{2,1,0:T(8,128)S(1)} %near.1.partial_ref, ...), custom_call_target="tpu_custom_call" | custom-call | tf_op jit(solution)/shard_map/far/pallas_call | solution.py:659
  13.3 0.1 collective-permute-start.3
  13.3 1.4 %collective-permute-done.3.got_ref = f32[12,32,128]{2,1,0:T(8,128)S(1)} collective-permute-done((f32[12,32,128]{2,1,0:T(8,128)S(1)}, f32[12,32,128]{2,1,0:T(8,128)S(1)}, u32[]{:S(2)}, u32[]{:S(2)}) %collective-permute-start.3) | collective-permute-done | bytes 196640 | tf_op jit(solution)/shard_map/ppermute | solution.py:641
  14.8 3.5 %collective-permute-start.4 = (bf16[12,32,128]{2,1,0:T(8,128)(2,1)S(1)}, bf16[12,32,128]{2,1,0:T(8,128)(2,1)S(1)}, u32[]{:S(2)}, u32[]{:S(2)}) collective-permute-start(bf16[12,32,128]{2,1,0:T(8,128)(2,1)S(1)} %pair.1.refs_0_), channel_id=1, source_target_pairs={{0,18},{1,19},{2,16},{3,17},{16,2},{17,3},{18,0},{19,1},{4,22},{5,... | collective-permute-start | bytes 294920 | tf_op jit(solution)/shard_map/ppermute | solution.py:641
  18.3 0.5 collective-permute-start.5
  18.8 0.1 collective-permute-start.6
  18.9 2.9 %collective-permute-done.4.refs_1_ = bf16[12,32,128]{2,1,0:T(8,128)(2,1)S(1)} collective-permute-done((bf16[12,32,128]{2,1,0:T(8,128)(2,1)S(1)}, bf16[12,32,128]{2,1,0:T(8,128)(2,1)S(1)}, u32[]{:S(2)}, u32[]{:S(2)}) %collective-permute-start.4) | collective-permute-done | bytes 98336 | tf_op jit(solution)/shard_map/ppermute | solution.py:641
  21.9 1.8 %collective-permute-done.5.refs_2_ = bf16[12,32,128]{2,1,0:T(8,128)(2,1)S(1)} collective-permute-done((bf16[12,32,128]{2,1,0:T(8,128)(2,1)S(1)}, bf16[12,32,128]{2,1,0:T(8,128)(2,1)S(1)}, u32[]{:S(2)}, u32[]{:S(2)}) %collective-permute-start.5) | collective-permute-done | bytes 98336 | tf_op jit(solution)/shard_map/ppermute | solution.py:641
  23.8 0.1 collective-permute-start.7
  23.9 1.6 %collective-permute-start.8 = (bf16[2,32,128]{2,1,0:T(8,128)(2,1)S(1)}, bf16[2,32,128]{2,1,0:T(8,128)(2,1)S(1)}, u32[]{:S(2)}, u32[]{:S(2)}) collective-permute-start(bf16[2,32,128]{2,1,0:T(8,128)(2,1)S(1)} %edge.2), channel_id=1, source_target_pairs={{0,12},{4,8},{8,4},{12,0},{1,13},{5,9},{9,5},{13,1},{2,14},{6,10},... | collective-permute-start | bytes 49160 | tf_op jit(solution)/shard_map/ppermute | solution.py:598
  25.5 0.6 %assemble.1 = (f32[24,32,128]{2,1,0:T(8,128)S(1)}, bf16[24,32,128]{2,1,0:T(8,128)(2,1)S(1)}, bf16[1,16,1024]{2,1,0:T(8,128)(2,1)S(1)}) custom-call(s32[1]{0:T(128)} %bitcast.core_ref, s32[13]{0:T(128)S(4)} %get-tuple-element.26.plan_ref, s32[24,1,128]{2,1,0:T(1,128)S(1)} %get-tuple-element.27.leaves_ref, f32[12,32,128]{2,1,0:T(8,128)S(1)} %close.1.mine_ref.image_ref, ...), custom_call_target="tpu_custom_call" | custom-call | tf_op jit(solution)/shard_map/assemble/pallas_call | solution.py:731
  26.0 0.2 collective-permute-start.11
  26.2 1.7 %collective-permute-start.10 = (bf16[4,32,128]{2,1,0:T(8,128)(2,1)S(1)}, bf16[4,32,128]{2,1,0:T(8,128)(2,1)S(1)}, u32[]{:S(2)}, u32[]{:S(2)}) collective-permute-start(bf16[4,32,128]{2,1,0:T(8,128)(2,1)S(1)} %edge.3), channel_id=1, source_target_pairs={{0,4},{4,0},{8,12},{12,8},{1,5},{5,1},{9,13},{13,9},{2,6},{6,2},{1... | collective-permute-start | bytes 98312 | tf_op jit(solution)/shard_map/ppermute | solution.py:598
  27.9 1.7 %collective-permute-done.8.one_ref = bf16[2,32,128]{2,1,0:T(8,128)(2,1)S(1)} collective-permute-done((bf16[2,32,128]{2,1,0:T(8,128)(2,1)S(1)}, bf16[2,32,128]{2,1,0:T(8,128)(2,1)S(1)}, u32[]{:S(2)}, u32[]{:S(2)}) %collective-permute-start.8) | collective-permute-done | bytes 16416 | tf_op jit(solution)/shard_map/ppermute | solution.py:598
  29.6 0.6 %first_far.1.image_ref = f32[1,3,32,128]{3,2,1,0:T(8,128)S(1)} custom-call(s32[13]{0:T(128)S(4)} %get-tuple-element.26.plan_ref, s32[24,1,128]{2,1,0:T(1,128)S(1)} %get-tuple-element.27.leaves_ref, bf16[1,16,1024]{2,1,0:T(8,128)(2,1)S(1)} %collective-permute-done.11.item_ref, bf16[1,896,441]{2,1,0:T(8,128)(2,1)S(1)} %get-tuple-element.31.trans_ref, ...), custom_call_target="tpu_custom_call" | custom-call | tf_op jit(solution)/shard_map/first_far/pallas_call | solution.py:671
  30.2 0.6 %collective-permute-done.9.other_one_ref = bf16[2,32,128]{2,1,0:T(8,128)(2,1)S(1)} collective-permute-done((bf16[2,32,128]{2,1,0:T(8,128)(2,1)S(1)}, bf16[2,32,128]{2,1,0:T(8,128)(2,1)S(1)}, u32[]{:S(2)}, u32[]{:S(2)}) %collective-permute-start.9) | collective-permute-done | bytes 16416 | tf_op jit(solution)/shard_map/ppermute | solution.py:641
  30.8 0.8 %last_near.1 = (bf16[12,32,128]{2,1,0:T(8,128)(2,1)S(1)}, bf16[12,32,128]{2,1,0:T(8,128)(2,1)S(1)}) custom-call(s32[1]{0:T(128)} %bitcast.core_ref, s32[1]{0:T(128)} %bitcast.2.row_ref, s32[1]{0:T(128)S(6)} %copy.11.count_ref, s32[13]{0:T(128)S(4)} %get-tuple-element.26.plan_ref, bf16[2,32,128]{2,1,0:T(8,128)(2,1)S(1)} %collective-permute-done.8.one_ref, ...), custom_call_target="tpu_custom_call" | custom-call | tf_op jit(solution)/shard_map/last_near/pallas_call | solution.py:682
  31.5 0.2 collective-permute-start.12
  31.8 1.1 %collective-permute-done.12.got_ref = bf16[12,32,128]{2,1,0:T(8,128)(2,1)S(1)} collective-permute-done((bf16[12,32,128]{2,1,0:T(8,128)(2,1)S(1)}, bf16[12,32,128]{2,1,0:T(8,128)(2,1)S(1)}, u32[]{:S(2)}, u32[]{:S(2)}) %collective-permute-start.12) | collective-permute-done | bytes 98336 | tf_op jit(solution)/shard_map/ppermute | solution.py:641
  32.9 4.4 %collective-permute-start.13 = (bf16[3,32,128]{2,1,0:T(8,128)(2,1)S(1)}, bf16[3,32,128]{2,1,0:T(8,128)(2,1)S(1)}, u32[]{:S(2)}, u32[]{:S(2)}) collective-permute-start(bf16[3,32,128]{2,1,0:T(8,128)(2,1)S(1)} %get-tuple-element.42), channel_id=1, source_target_pairs={{0,18},{1,19},{2,16},{3,17},{16,2},{17,3},{18,0},{19,1},{4,22},{5,... | collective-permute-start | bytes 73736 | tf_op jit(solution)/shard_map/ppermute | solution.py:641
  37.3 0.6 %collective-permute-start.15 = (bf16[3,32,128]{2,1,0:T(8,128)(2,1)S(1)}, bf16[3,32,128]{2,1,0:T(8,128)(2,1)S(1)}, u32[]{:S(2)}, u32[]{:S(2)}) collective-permute-start(bf16[3,32,128]{2,1,0:T(8,128)(2,1)S(1)} %get-tuple-element.44), channel_id=1, source_target_pairs={{0,2},{1,3},{2,0},{3,1},{16,18},{17,19},{18,16},{19,17},{4,6},{5,7... | collective-permute-start | bytes 73736 | tf_op jit(solution)/shard_map/ppermute | solution.py:641
  38.0 1.2 %collective-permute-done.13.refs_1_ = bf16[3,32,128]{2,1,0:T(8,128)(2,1)S(1)} collective-permute-done((bf16[3,32,128]{2,1,0:T(8,128)(2,1)S(1)}, bf16[3,32,128]{2,1,0:T(8,128)(2,1)S(1)}, u32[]{:S(2)}, u32[]{:S(2)}) %collective-permute-start.13) | collective-permute-done | bytes 24608 | tf_op jit(solution)/shard_map/ppermute | solution.py:641
  39.1 2.0 %collective-permute-done.14.refs_2_ = bf16[3,32,128]{2,1,0:T(8,128)(2,1)S(1)} collective-permute-done((bf16[3,32,128]{2,1,0:T(8,128)(2,1)S(1)}, bf16[3,32,128]{2,1,0:T(8,128)(2,1)S(1)}, u32[]{:S(2)}, u32[]{:S(2)}) %collective-permute-start.14) | collective-permute-done | bytes 24608 | tf_op jit(solution)/shard_map/ppermute | solution.py:641
  41.1 0.1 gram.1
  41.3 11.0 %all_to_all.5.sums_ref = f32[32,2,128]{2,1,0:T(2,128)S(1)} all-to-all(f32[32,2,128]{2,1,0:T(2,128)S(1)} %gram.1), channel_id=1, replica_groups=mesh['grp'=2,'row'=4,'col'=4] {'grp','row','col'}, dimensions={0} | all-to-all | bytes 65536 | tf_op jit(solution)/shard_map/all_to_all | solution.py:774
  52.2 1.0 %combine.1 = f32[32,3072]{1,0:T(8,128)} custom-call(f32[32,2,128]{2,1,0:T(2,128)S(1)} %all_to_all.5.sums_ref, f32[32,3072]{1,0:T(8,128)S(1)} %get-tuple-element.25.image_ref.here_ref.right_ref, f32[24,32,128]{2,1,0:T(8,128)S(1)} %get-tuple-element.36.image_ref), custom_call_target="tpu_custom_call" | custom-call | tf_op jit(solution)/shard_map/combine/pallas_call | solution.py:777
  (18 shorter events, 0.2 us)
Async XLA Ops:
  2.8 7.5 %collective-permute-start = (bf16[32,512]{1,0:T(8,128)(2,1)S(1)}, bf16[32,512]{1,0:T(8,128)(2,1)S(1)}, u32[]{:S(2)}, u32[]{:S(2)}) collective-permute-start(bf16[32,512]{1,0:T(8,128)(2,1)S(1)} %get-tuple-element.28), channel_id=1, source_target_pairs={{0,12},{4,8},{8,4},{12,0},{1,13},{5,9},{9,5},{13,1},{2,14},{6,10},... | collective-permute-start | bytes 98312 | tf_op jit(solution)/shard_map/ppermute | solution.py:598
  7.9 3.9 %collective-permute-start.1 = (bf16[32,512]{1,0:T(8,128)(2,1)S(1)}, bf16[32,512]{1,0:T(8,128)(2,1)S(1)}, u32[]{:S(2)}, u32[]{:S(2)}) collective-permute-start(bf16[32,512]{1,0:T(8,128)(2,1)S(1)} %get-tuple-element.29), channel_id=1, source_target_pairs={{0,4},{4,0},{8,12},{12,8},{1,5},{5,1},{9,13},{13,9},{2,6},{6,2},{1... | collective-permute-start | bytes 98312 | tf_op jit(solution)/shard_map/ppermute | solution.py:598
  7.9 4.7 %collective-permute-start.2 = (bf16[1,16,896]{2,1,0:T(8,128)(2,1)S(1)}, bf16[1,16,896]{2,1,0:T(8,128)(2,1)S(1)}, u32[]{:S(2)}, u32[]{:S(2)}) collective-permute-start(bf16[1,16,896]{2,1,0:T(8,128)(2,1)S(1)} %get-tuple-element.30), channel_id=1, source_target_pairs={{0,1},{1,0},{2,6},{3,7},{16,24},{17,25},{18,30},{19,31},{4,8},{5,9... | collective-permute-start | bytes 86024 | tf_op jit(solution)/shard_map/ppermute | solution.py:593
  8.6 3.3 %copy-start = (bf16[2,8,256,256]{3,2,1,0:T(8,128)(2,1)S(1)}, bf16[2,8,256,256]{3,2,1,0:T(8,128)(2,1)}, u32[]{:S(2)}) copy-start(bf16[2,8,256,256]{3,2,1,0:T(8,128)(2,1)} %tiles_ref.3) | copy-start | bytes 6291460
  13.3 1.5 %collective-permute-start.3 = (f32[12,32,128]{2,1,0:T(8,128)S(1)}, f32[12,32,128]{2,1,0:T(8,128)S(1)}, u32[]{:S(2)}, u32[]{:S(2)}) collective-permute-start(f32[12,32,128]{2,1,0:T(8,128)S(1)} %get-tuple-element.34), channel_id=1, source_target_pairs={{0,1},{1,0},{2,3},{3,2},{16,17},{17,16},{18,19},{19,18},{4,5},{5,4... | collective-permute-start | bytes 589832 | tf_op jit(solution)/shard_map/ppermute | solution.py:641
  14.8 7.1 %collective-permute-start.4 = (bf16[12,32,128]{2,1,0:T(8,128)(2,1)S(1)}, bf16[12,32,128]{2,1,0:T(8,128)(2,1)S(1)}, u32[]{:S(2)}, u32[]{:S(2)}) collective-permute-start(bf16[12,32,128]{2,1,0:T(8,128)(2,1)S(1)} %pair.1.refs_0_), channel_id=1, source_target_pairs={{0,18},{1,19},{2,16},{3,17},{16,2},{17,3},{18,0},{19,1},{4,22},{5,... | collective-permute-start | bytes 294920 | tf_op jit(solution)/shard_map/ppermute | solution.py:641
  18.3 5.4 %collective-permute-start.5 = (bf16[12,32,128]{2,1,0:T(8,128)(2,1)S(1)}, bf16[12,32,128]{2,1,0:T(8,128)(2,1)S(1)}, u32[]{:S(2)}, u32[]{:S(2)}) collective-permute-start(bf16[12,32,128]{2,1,0:T(8,128)(2,1)S(1)} %pair.1.refs_0_), channel_id=1, source_target_pairs={{0,16},{1,17},{2,18},{3,19},{16,0},{17,1},{18,2},{19,3},{4,20},{5,... | collective-permute-start | bytes 294920 | tf_op jit(solution)/shard_map/ppermute | solution.py:641
  18.8 4.9 %collective-permute-start.6 = (bf16[12,32,128]{2,1,0:T(8,128)(2,1)S(1)}, bf16[12,32,128]{2,1,0:T(8,128)(2,1)S(1)}, u32[]{:S(2)}, u32[]{:S(2)}) collective-permute-start(bf16[12,32,128]{2,1,0:T(8,128)(2,1)S(1)} %pair.1.refs_0_), channel_id=1, source_target_pairs={{0,2},{1,3},{2,0},{3,1},{16,18},{17,19},{18,16},{19,17},{4,6},{5,7... | collective-permute-start | bytes 294920 | tf_op jit(solution)/shard_map/ppermute | solution.py:641
  23.8 1.7 %collective-permute-start.7 = (f32[12,32,128]{2,1,0:T(8,128)S(1)}, f32[12,32,128]{2,1,0:T(8,128)S(1)}, u32[]{:S(2)}, u32[]{:S(2)}) collective-permute-start(f32[12,32,128]{2,1,0:T(8,128)S(1)} %close.1.mine_ref.image_ref), channel_id=1, source_target_pairs={{0,1},{1,0},{2,3},{3,2},{16,17},{17,16},{18,19},{19,18},{4,5},{5,4... | collective-permute-start | bytes 589832 | tf_op jit(solution)/shard_map/ppermute | solution.py:641
  23.9 5.7 %collective-permute-start.8 = (bf16[2,32,128]{2,1,0:T(8,128)(2,1)S(1)}, bf16[2,32,128]{2,1,0:T(8,128)(2,1)S(1)}, u32[]{:S(2)}, u32[]{:S(2)}) collective-permute-start(bf16[2,32,128]{2,1,0:T(8,128)(2,1)S(1)} %edge.2), channel_id=1, source_target_pairs={{0,12},{4,8},{8,4},{12,0},{1,13},{5,9},{9,5},{13,1},{2,14},{6,10},... | collective-permute-start | bytes 49160 | tf_op jit(solution)/shard_map/ppermute | solution.py:598
  26.0 3.5 %collective-permute-start.11 = (bf16[1,16,1024]{2,1,0:T(8,128)(2,1)S(1)}, bf16[1,16,1024]{2,1,0:T(8,128)(2,1)S(1)}, u32[]{:S(2)}, u32[]{:S(2)}) collective-permute-start(bf16[1,16,1024]{2,1,0:T(8,128)(2,1)S(1)} %get-tuple-element.38), channel_id=1, source_target_pairs={{0,1},{1,0},{2,6},{3,7},{16,24},{17,25},{18,30},{19,31},{4,8},{5,9... | collective-permute-start | bytes 98312 | tf_op jit(solution)/shard_map/ppermute | solution.py:593
  26.2 4.5 %collective-permute-start.10 = (bf16[4,32,128]{2,1,0:T(8,128)(2,1)S(1)}, bf16[4,32,128]{2,1,0:T(8,128)(2,1)S(1)}, u32[]{:S(2)}, u32[]{:S(2)}) collective-permute-start(bf16[4,32,128]{2,1,0:T(8,128)(2,1)S(1)} %edge.3), channel_id=1, source_target_pairs={{0,4},{4,0},{8,12},{12,8},{1,5},{5,1},{9,13},{13,9},{2,6},{6,2},{1... | collective-permute-start | bytes 98312 | tf_op jit(solution)/shard_map/ppermute | solution.py:598
  29.6 1.2 %collective-permute-start.9 = (bf16[2,32,128]{2,1,0:T(8,128)(2,1)S(1)}, bf16[2,32,128]{2,1,0:T(8,128)(2,1)S(1)}, u32[]{:S(2)}, u32[]{:S(2)}) collective-permute-start(bf16[2,32,128]{2,1,0:T(8,128)(2,1)S(1)} %collective-permute-done.8.one_ref), channel_id=1, source_target_pairs={{0,1},{1,0},{2,3},{3,2},{16,17},{17,16},{18,19},{19,18},{4,5},{5,4... | collective-permute-start | bytes 49160 | tf_op jit(solution)/shard_map/ppermute | solution.py:641
  31.5 1.4 %collective-permute-start.12 = (bf16[12,32,128]{2,1,0:T(8,128)(2,1)S(1)}, bf16[12,32,128]{2,1,0:T(8,128)(2,1)S(1)}, u32[]{:S(2)}, u32[]{:S(2)}) collective-permute-start(bf16[12,32,128]{2,1,0:T(8,128)(2,1)S(1)} %get-tuple-element.40), channel_id=1, source_target_pairs={{0,1},{1,0},{2,3},{3,2},{16,17},{17,16},{18,19},{19,18},{4,5},{5,4... | collective-permute-start | bytes 294920 | tf_op jit(solution)/shard_map/ppermute | solution.py:641
  32.9 6.2 %collective-permute-start.13 = (bf16[3,32,128]{2,1,0:T(8,128)(2,1)S(1)}, bf16[3,32,128]{2,1,0:T(8,128)(2,1)S(1)}, u32[]{:S(2)}, u32[]{:S(2)}) collective-permute-start(bf16[3,32,128]{2,1,0:T(8,128)(2,1)S(1)} %get-tuple-element.42), channel_id=1, source_target_pairs={{0,18},{1,19},{2,16},{3,17},{16,2},{17,3},{18,0},{19,1},{4,22},{5,... | collective-permute-start | bytes 73736 | tf_op jit(solution)/shard_map/ppermute | solution.py:641
  37.3 3.8 %collective-permute-start.14 = (bf16[3,32,128]{2,1,0:T(8,128)(2,1)S(1)}, bf16[3,32,128]{2,1,0:T(8,128)(2,1)S(1)}, u32[]{:S(2)}, u32[]{:S(2)}) collective-permute-start(bf16[3,32,128]{2,1,0:T(8,128)(2,1)S(1)} %get-tuple-element.43), channel_id=1, source_target_pairs={{0,16},{1,17},{2,18},{3,19},{16,0},{17,1},{18,2},{19,3},{4,20},{5,... | collective-permute-start | bytes 73736 | tf_op jit(solution)/shard_map/ppermute | solution.py:641
  37.3 3.8 %collective-permute-start.15 = (bf16[3,32,128]{2,1,0:T(8,128)(2,1)S(1)}, bf16[3,32,128]{2,1,0:T(8,128)(2,1)S(1)}, u32[]{:S(2)}, u32[]{:S(2)}) collective-permute-start(bf16[3,32,128]{2,1,0:T(8,128)(2,1)S(1)} %get-tuple-element.44), channel_id=1, source_target_pairs={{0,2},{1,3},{2,0},{3,1},{16,18},{17,19},{18,16},{19,17},{4,6},{5,7... | collective-permute-start | bytes 73736 | tf_op jit(solution)/shard_map/ppermute | solution.py:641

commit v15 on v13

--- a/solution.py
+++ b/solution.py
@@ -74,12 +74,11 @@
     return CODES + slots + PER_ITEM * item
 
 
-def window_start(leaf_ref, leaf, width):
-    units = leaf_ref.shape[1] // LANES
-    before = jnp.int32(0)
-    for k in range(units):
-        before = before + (leaf_ref[0, k * LANES] < leaf).astype(jnp.int32)
-    return jnp.clip(before - 1, 0, units - width)
+def window_start(leaves_ref, leaf, width):
+    leaves = leaves_ref[...]
+    first = lax.broadcasted_iota(jnp.int32, leaves.shape, 2) == 0
+    before = jnp.sum(jnp.where(jnp.logical_and(first, leaves < leaf), 1.0, 0.0)).astype(jnp.int32)
+    return jnp.clip(before - 1, 0, leaves.shape[0] - width)
 
 
 def window_mask(leaves_ref, leaf, unit, rows, width):
@@ -152,21 +151,20 @@
 
 
 def begin_kernel(
-    fields, items, width, send, rows, row_ref, own_ref, pick_hbm, leaf_hbm, leaves_hbm,
+    fields, items, width, send, rows, row_ref, own_ref, pick_hbm, leaves_hbm,
     target_hbm, offset_hbm, pairs_hbm, right_hbm, exp_ref,
     plan_ref, out_ref, window_ref, leaves_ref, right_ref,
-    pick_ref, leaf_ref, target_ref, offset_ref, pairs_ref, sem, window_sem,
+    pick_ref, target_ref, offset_ref, pairs_ref, sem, window_sem,
 ):
     loads = [
         pltpu.make_async_copy(source, place, sem.at[k])
         for k, (source, place) in enumerate(
             (
-                (leaf_hbm, leaf_ref),
+                (leaves_hbm, leaves_ref),
                 (pick_hbm, pick_ref),
                 (target_hbm, target_ref),
                 (offset_hbm, offset_ref),
                 (pairs_hbm, pairs_ref),
-                (leaves_hbm, leaves_ref),
                 (right_hbm, right_ref),
             )
         )
@@ -192,7 +190,7 @@
     for i in range(items):
         other, number = partner(i, False)
         leaf = pick_ref[other, number, row]
-        unit = window_start(leaf_ref, leaf, width)
+        unit = window_start(leaves_ref, leaf, width)
         place = item_place(slots, i)
         plan_ref[place], plan_ref[place + 1] = leaf, unit
         for copy in window_copies(exp_ref, unit, window_ref.at[i], window_sem.at[i], width):
@@ -205,14 +203,15 @@
         place = item_place(slots, i)
         other, number = partner(i, True)
         leaf = target_ref[0, other * send + number]
-        plan_ref[place + 2], plan_ref[place + 3] = leaf, window_start(leaf_ref, leaf, width)
+        plan_ref[place + 2], plan_ref[place + 3] = leaf, window_start(leaves_ref, leaf, width)
         plan_ref[place + 4] = offset_ref[0, other * send + number]
     for i in range(items):
         place = item_place(slots, i)
         leaf, unit = plan_ref[place], plan_ref[place + 1]
         for copy in window_copies(exp_ref, unit, window_ref.at[i], window_sem.at[i], width):
             copy.wait()
-        out_ref[i] = multi_rows(fields, width, leaf, unit, leaves_ref, right_ref, window_ref.at[i]).astype(BF16)
+        made = multi_rows(fields, width, leaf, unit, leaves_ref, right_ref, window_ref.at[i])
+        out_ref[i, :, : made.shape[1]] = made.astype(BF16)
 
 
 def fetch_kernel(items, width, slots, plan_ref, exp_ref, trans_ref, window_ref, moved_ref, trans_buf, sem, trans_sem):
@@ -252,33 +251,29 @@
         give_ref[k] = total[2 * k + 1 - core].astype(give_ref.dtype)
 
 
-def near_kernel(fields, row_ref, count_ref, plan_ref, one_ref, two_ref, here_ref, tiles_ref, out_ref, ext):
-    units = out_ref.shape[0]
-    edge = (ext.shape[0] - units) // 2
-    one_at, two_at = edge_places(row_ref, edge, units)
-    for k in range(edge):
-        lanes = slice(k * LANES, (k + 1) * LANES)
-        ext[one_at + k] = one_ref[:, lanes].astype(ext.dtype)
-        ext[two_at + k] = two_ref[:, lanes].astype(ext.dtype)
-    for k in range(units):
-        ext[edge + k] = here_ref[:, k * LANES : (k + 1) * LANES]
-    out_ref[...] = jnp.zeros_like(out_ref)
-    near_slots(fields, count_ref, plan_ref, tiles_ref, out_ref, ext)
-
-
-def last_near_kernel(
-    fields, core_ref, row_ref, count_ref, plan_ref, one_ref, other_one_ref, two_ref, here_ref, tiles_ref, image_ref,
-    keep_ref, give_ref, ext, total,
+def near_kernel(
+    fields, core_ref, row_ref, count_ref, plan_ref, *refs
 ):
+    *edge_refs, here_ref, tiles_ref, image_ref, keep_ref, give_ref, ext, total = refs
     units = total.shape[0]
     edge = (ext.shape[0] - units) // 2
     core = core_ref[0]
     one_at, two_at = edge_places(row_ref, edge, units)
-    for k in range(edge // 2):
-        ext[one_at + 2 * k + core] = one_ref[k]
-        ext[one_at + 2 * k + 1 - core] = other_one_ref[k]
-    ext[pl.ds(two_at, edge)] = two_ref[...]
-    ext[edge : edge + units] = here_ref[...]
+    if len(here_ref.shape) == 2:
+        one_ref, two_ref = edge_refs
+        for k in range(edge):
+            lanes = slice(k * LANES, (k + 1) * LANES)
+            ext[one_at + k] = one_ref[:, lanes].astype(ext.dtype)
+            ext[two_at + k] = two_ref[:, lanes].astype(ext.dtype)
+        for k in range(units):
+            ext[edge + k] = here_ref[:, k * LANES : (k + 1) * LANES]
+    else:
+        one_ref, other_one_ref, two_ref = edge_refs
+        for k in range(edge // 2):
+            ext[one_at + 2 * k + core] = one_ref[k]
+            ext[one_at + 2 * k + 1 - core] = other_one_ref[k]
+        ext[pl.ds(two_at, edge)] = two_ref[...]
+        ext[edge : edge + units] = here_ref[...]
     total[...] = jnp.zeros_like(total)
     items, width = image_ref.shape[:2]
     for i in range(items):
@@ -286,7 +281,7 @@
         for k in range(width):
             total[unit + k] += image_ref[i, k]
     near_slots(fields, count_ref, plan_ref, tiles_ref, total, ext)
-    part(total, core_ref[0], keep_ref, give_ref)
+    part(total, core, keep_ref, give_ref)
 
 
 def near_slots(fields, count_ref, plan_ref, tiles_ref, out_ref, ext):
@@ -308,30 +303,8 @@
 
 
 def far_kernel(
-    fields, items, width, slots, core_ref, plan_ref, leaves_ref, partial_ref, item_ref, trans_ref, window_ref,
-    keep_ref, give_ref, total,
-):
-    total[...] = partial_ref[...]
-
-    def add(i, unit, image):
-        for k in range(width):
-            total[unit + k] += image[:, k * LANES : (k + 1) * LANES]
-
-    far_images(fields, items, width, slots, plan_ref, leaves_ref, item_ref, trans_ref, window_ref, add)
-    part(total, core_ref[0], keep_ref, give_ref)
-
-
-def first_far_kernel(
     fields, items, width, slots, plan_ref, leaves_ref, item_ref, trans_ref, window_ref, image_ref
 ):
-    def store(i, unit, image):
-        for k in range(width):
-            image_ref[i, k] = image[:, k * LANES : (k + 1) * LANES]
-
-    far_images(fields, items, width, slots, plan_ref, leaves_ref, item_ref, trans_ref, window_ref, store)
-
-
-def far_images(fields, items, width, slots, plan_ref, leaves_ref, item_ref, trans_ref, window_ref, give):
     for i in range(items):
         plain = item_ref[i, :, : trans_ref.shape[1]].astype(F32)
         odd = odd_lanes(plain.shape)
@@ -348,7 +321,8 @@
         leaf, unit = plan_ref[place + 2], plan_ref[place + 3]
         mask = window_mask(leaves_ref, leaf, unit, 2 * fields, width)
         image = jnp.where(mask, dot_nn(rows, expansions), 0.0)
-        give(i, unit, image)
+        for k in range(width):
+            image_ref[i, k] = image[:, k * LANES : (k + 1) * LANES]
 
 
 def pair_kernel(keep_ref, got_ref, out_ref):
@@ -532,7 +506,7 @@
     chips = group // 2
     assert group == 2 * chips and chips & (chips - 1) == 0 and LANES % fields == 0
     window_shape = jax.ShapeDtypeStruct((items, pad_coefs, width, 2, LANES), BF16)
-    item_shape = jax.ShapeDtypeStruct((items, fields, 2 * pad_coefs), BF16)
+    item_shape = jax.ShapeDtypeStruct((items, fields, 2 * pad_coefs + ITEM_REST), BF16)
     half_units = (units // 2, both, LANES)
     assert units % 2 == 0 and edge_units % 2 == 0
 
@@ -554,14 +528,14 @@
             jax.ShapeDtypeStruct(leaves.shape, jnp.int32),
             jax.ShapeDtypeStruct((both, panels), F32),
         ),
-        in_specs=[SMEM] * 2 + [HBM] * 8,
+        in_specs=[SMEM] * 2 + [HBM] * 7,
         out_specs=(SMEM,) + (VMEM,) * 4,
         scratch_shapes=[
             pltpu.SMEM(value.shape, jnp.int32)
-            for value in (picks, leaf_of_panel, far_target, far_offset, tile_pairs)
+            for value in (picks, far_target, far_offset, tile_pairs)
         ]
         + [
-            pltpu.SemaphoreType.DMA((7,)),
+            pltpu.SemaphoreType.DMA((6,)),
             pltpu.SemaphoreType.DMA((items, PIECES)),
         ],
         compiler_params=params(),
@@ -570,7 +544,6 @@
         row_place,
         own_place,
         in_hbm(picks),
-        in_hbm(leaf_of_panel),
         in_hbm(leaves),
         in_hbm(far_target),
         in_hbm(far_offset),
@@ -631,57 +604,30 @@
     def swapped(value, step):
         return lax.ppermute(value, GROUP, [(g, g ^ step) for g in range(group)])
 
-    def near(one, two, low):
+    def far(taken):
         return pl.pallas_call(
-            functools.partial(near_kernel, fields),
-            out_shape=image_shape,
-            in_specs=[SMEM] * 3 + [VMEM] * 4,
-            out_specs=VMEM,
-            scratch_shapes=[pltpu.VMEM((units + 2 * edge_units, both, LANES), low.dtype)],
-            compiler_params=params(),
-            cost_estimate=pl.CostEstimate(
-                flops=8 * fields * near_tiles.size // 2, bytes_accessed=2 * near_tiles.size, transcendentals=0
-            ),
-            name="near",
-        )(row_place, tile_count, plan, one, two, low, near_tiles)
-
-    def core_parts(partial, taken):
-        half_shape = jax.ShapeDtypeStruct(half_units, F32)
-        keep, give = pl.pallas_call(
             functools.partial(far_kernel, fields, items, width, slots),
-            out_shape=(half_shape, half_shape),
-            in_specs=[SMEM, SMEM] + [VMEM] * 5,
-            out_specs=(VMEM, VMEM),
-            scratch_shapes=[pltpu.VMEM(image_shape.shape, F32)],
-            compiler_params=params(),
-            name="far",
-        )(core_place, plan, leaves, partial, taken, moved, target_windows)
-        return keep, swapped(give, 1)
-
-    def first_far(taken):
-        return pl.pallas_call(
-            functools.partial(first_far_kernel, fields, items, width, slots),
             out_shape=jax.ShapeDtypeStruct((items, width, both, LANES), F32),
             in_specs=[SMEM] + [VMEM] * 4,
             out_specs=VMEM,
             compiler_params=params(),
-            name="first_far",
+            name="far",
         )(plan, leaves, taken, moved, target_windows)
 
-    def last_core_parts(one, other_one, two, low, image):
-        half_shape = jax.ShapeDtypeStruct(half_units, BF16)
+    def core_parts(edges, low, image, dtype):
+        half_shape = jax.ShapeDtypeStruct(half_units, dtype)
         keep, give = pl.pallas_call(
-            functools.partial(last_near_kernel, fields),
+            functools.partial(near_kernel, fields),
             out_shape=(half_shape, half_shape),
-            in_specs=[SMEM] * 4 + [VMEM] * 6,
+            in_specs=[SMEM] * 4 + [VMEM] * (3 + len(edges)),
             out_specs=(VMEM, VMEM),
             scratch_shapes=[
                 pltpu.VMEM((units + 2 * edge_units, both, LANES), low.dtype),
                 pltpu.VMEM(image_shape.shape, F32),
             ],
             compiler_params=params(),
-            name="last_near",
-        )(core_place, row_place, tile_count, plan, one, other_one, two, low, near_tiles, image)
+            name="near",
+        )(core_place, row_place, tile_count, plan, *edges, low, near_tiles, image)
         return keep, swapped(give, 1)
 
     def pair_sums(keep, got):
@@ -712,7 +658,7 @@
             out_shape=(
                 image_shape,
                 jax.ShapeDtypeStruct(image_shape.shape, BF16),
-                jax.ShapeDtypeStruct((items, fields, 2 * pad_coefs + ITEM_REST), BF16),
+                item_shape,
             ),
             in_specs=[SMEM, SMEM] + [VMEM] * 4,
             out_specs=(VMEM,) * 3,
@@ -720,14 +666,14 @@
             name="assemble",
         )(core_place, plan, leaves, mine, theirs, windows)
 
-    partial = near(*from_neighbours(right), right)
-    mine = half_sum(pair_sums(*core_parts(partial, exchanged(made))))
+    image = far(exchanged(made))
+    mine = half_sum(pair_sums(*core_parts(from_neighbours(right), right, image, F32)))
     theirs = swapped(mine, 1)
     one = along_row(one_edge(mine, edge_units // 2, True), 0)
     z_all, z_low, made = whole(mine, theirs)
-    image = first_far(exchanged(made))
+    image = far(exchanged(made))
     two = along_row(one_edge(z_low, edge_units, False), 1)
-    parts = pair_sums(*last_core_parts(one, swapped(one, 1), two, z_low, image))
+    parts = pair_sums(*core_parts((one, swapped(one, 1), two), z_low, image, BF16))
 
     lines = pl.pallas_call(
         functools.partial(gram_kernel, fields),

time: 52.8 us -> 53.1 us (level)
  starting transfers between devices: 18.1 us -> 19.9 us
  waiting for transfers between devices: 15.7 us -> 14.4 us
    ppermute x10, starting transfers between devices: 9.52 us -> 10.9 us  [swapped(): return lax.ppermute(value, GROUP, [(g, g ^ step) for g in range(group)])]
    ppermute x4, waiting for transfers between devices: 3.17 us -> 2.15 us  [along_row(): return lax.ppermute(value, 'row', list(enumerate(neighbours[which])))]
  transfers between devices with their start and end apart: 16 -> 16, of which waited for: 10 -> 11; matrix products, arithmetic and copies ran while one was open for 0% -> 0% of each run, Pallas kernels for 7% -> 7%
where the time goes in v15:
time: 53.1 us; the launch traced here: 52.8 us
  starting transfers between devices  19.9 us (37%)
  waiting for transfers between devices  14.4 us (27%)
  Pallas kernels  9.35 us (18%)
  blocking collectives  8.44 us (16%)
  between operations  0.77 us (1%)
    ppermute x10, waiting for transfers between devices, swapped(): return lax.ppermute(value, GROUP, [(g, g ^ step) for g in range(group)])  12.3 us
    ppermute x10, starting transfers between devices, swapped(): return lax.ppermute(value, GROUP, [(g, g ^ step) for g in range(group)])  10.9 us
    all_to_all x1, blocking collectives, local(): lax.all_to_all(lines, EVERY, 0, 0, axis_index_groups=same_chip, tiled=True)  8.44 us
    ppermute x4, starting transfers between devices, along_row(): return lax.ppermute(value, 'row', list(enumerate(neighbours[which])))  8.33 us
    pallas_call x1, Pallas kernels, local(): pl.pallas_call(functools.partial(begin_kernel, fields, items, width, send...  2.82 us
    ppermute x4, waiting for transfers between devices, along_row(): return lax.ppermute(value, 'row', list(enumerate(neighbours[which])))  2.15 us
    pallas_call x1, Pallas kernels, local(): pl.pallas_call(functools.partial(fetch_kernel, items, width, slots), out_...  1.73 us
    pallas_call x2, Pallas kernels, core_parts(): pl.pallas_call(functools.partial(near_kernel, fields), out_shape=(half_sh...  1.54 us
  transfers between devices with their start and end apart: 16, of which 11 were waited for; matrix products, arithmetic and copies ran while one was open for 0% of the time, Pallas kernels for 7%

profile of v15, /device:TPU:0, one launch (start us, length us, event | category | flops | bytes accessed | tf_op | source)
XLA Modules:
  0.0 52.8 jit_solution(2151784587302046790)
XLA Ops:
  0.0 2.8 %begin.1 = (s32[13]{0:T(128)S(4)}, bf16[1,16,1024]{2,1,0:T(8,128)(2,1)S(1)}, bf16[1,448,3,2,128]{4,3,2,1,0:T(2,128)(2,1)S(1)}, s32[24,1,128]{2,1,0:T(1,128)S(1)}, f32[32,3072]{1,0:T(8,128)S(1)}) custom-call(s32[1]{0:T(128)} %bitcast.1.row_ref, s32[1]{0:T(128)} %bitcast.2.own_ref, s32[4,2,4]{2,1,0:T(2,128)} %bitcast.18, s32[24,1,128]{2,1,0:T(1,128)} %bitcast.17, ...), custom_call_target="tpu_custom_call" | custom-call | tf_op jit(solution)/shard_map/begin/pallas_call | solution.py:522
  2.8 0.5 collective-permute-start.2
  3.4 4.7 %collective-permute-start = (bf16[32,512]{1,0:T(8,128)(2,1)S(1)}, bf16[32,512]{1,0:T(8,128)(2,1)S(1)}, u32[]{:S(2)}, u32[]{:S(2)}) collective-permute-start(bf16[32,512]{1,0:T(8,128)(2,1)S(1)} %get-tuple-element.24), channel_id=1, source_target_pairs={{0,12},{4,8},{8,4},{12,0},{1,13},{5,9},{9,5},{13,1},{2,14},{6,10},... | collective-permute-start | bytes 98312 | tf_op jit(solution)/shard_map/ppermute | solution.py:562
  8.7 1.7 %fetch.1 = (bf16[1,448,3,2,128]{4,3,2,1,0:T(2,128)(2,1)S(1)}, bf16[1,896,441]{2,1,0:T(8,128)(2,1)S(1)}) custom-call(s32[13]{0:T(128)S(4)} %get-tuple-element.22.plan_ref, bf16[441,24,2,128]{3,2,1,0:T(2,128)(2,1)} %bitcast.14, bf16[4,441,2,441]{3,2,1,0:T(2,128)(2,1)} %bitcast.15), custom_call_target="tpu_custom_call" | custom-call | bytes 2064384 | tf_op jit(solution)/shard_map/fetch/pallas_call | solution.py:586
  10.5 0.6 %far.2.refs_4_ = f32[1,3,32,128]{3,2,1,0:T(8,128)S(1)} custom-call(s32[13]{0:T(128)S(4)} %get-tuple-element.22.plan_ref, s32[24,1,128]{2,1,0:T(1,128)S(1)} %get-tuple-element.23.leaves_ref, bf16[1,16,1024]{2,1,0:T(8,128)(2,1)S(1)} %collective-permute-done.2.item_ref, bf16[1,896,441]{2,1,0:T(8,128)(2,1)S(1)} %get-tuple-element.27.trans_ref, ...), custom_call_target="tpu_custom_call" | custom-call | tf_op jit(solution)/shard_map/far/pallas_call | solution.py:608
  11.1 0.9 %collective-permute-done.1.refs_1_ = bf16[32,512]{1,0:T(8,128)(2,1)S(1)} collective-permute-done((bf16[32,512]{1,0:T(8,128)(2,1)S(1)}, bf16[32,512]{1,0:T(8,128)(2,1)S(1)}, u32[]{:S(2)}, u32[]{:S(2)}) %collective-permute-start.1) | collective-permute-done | bytes 32800 | tf_op jit(solution)/shard_map/ppermute | solution.py:562
  12.0 0.8 %near.2 = (f32[12,32,128]{2,1,0:T(8,128)S(1)}, f32[12,32,128]{2,1,0:T(8,128)S(1)}) custom-call(s32[1]{0:T(128)} %bitcast.core_ref, s32[1]{0:T(128)} %bitcast.1.row_ref, s32[1]{0:T(128)S(6)} %copy.11.count_ref, s32[13]{0:T(128)S(4)} %get-tuple-element.22.plan_ref, bf16[32,512]{1,0:T(8,128)(2,1)S(1)} %collective-permute-done.refs_0_, ...), custom_call_target="tpu_custom_call" | custom-call | tf_op jit(solution)/shard_map/near/pallas_call | solution.py:619
  12.8 0.1 collective-permute-start.3
  12.8 1.4 %collective-permute-done.3.got_ref = f32[12,32,128]{2,1,0:T(8,128)S(1)} collective-permute-done((f32[12,32,128]{2,1,0:T(8,128)S(1)}, f32[12,32,128]{2,1,0:T(8,128)S(1)}, u32[]{:S(2)}, u32[]{:S(2)}) %collective-permute-start.3) | collective-permute-done | bytes 196640 | tf_op jit(solution)/shard_map/ppermute | solution.py:605
  14.3 4.3 %collective-permute-start.4 = (bf16[12,32,128]{2,1,0:T(8,128)(2,1)S(1)}, bf16[12,32,128]{2,1,0:T(8,128)(2,1)S(1)}, u32[]{:S(2)}, u32[]{:S(2)}) collective-permute-start(bf16[12,32,128]{2,1,0:T(8,128)(2,1)S(1)} %pair.2.refs_0_), channel_id=1, source_target_pairs={{0,18},{1,19},{2,16},{3,17},{16,2},{17,3},{18,0},{19,1},{4,22},{5,... | collective-permute-start | bytes 294920 | tf_op jit(solution)/shard_map/ppermute | solution.py:605
  18.6 0.6 %collective-permute-start.6 = (bf16[12,32,128]{2,1,0:T(8,128)(2,1)S(1)}, bf16[12,32,128]{2,1,0:T(8,128)(2,1)S(1)}, u32[]{:S(2)}, u32[]{:S(2)}) collective-permute-start(bf16[12,32,128]{2,1,0:T(8,128)(2,1)S(1)} %pair.2.refs_0_), channel_id=1, source_target_pairs={{0,2},{1,3},{2,0},{3,1},{16,18},{17,19},{18,16},{19,17},{4,6},{5,7... | collective-permute-start | bytes 294920 | tf_op jit(solution)/shard_map/ppermute | solution.py:605
  19.2 2.9 %collective-permute-done.4.refs_1_ = bf16[12,32,128]{2,1,0:T(8,128)(2,1)S(1)} collective-permute-done((bf16[12,32,128]{2,1,0:T(8,128)(2,1)S(1)}, bf16[12,32,128]{2,1,0:T(8,128)(2,1)S(1)}, u32[]{:S(2)}, u32[]{:S(2)}) %collective-permute-start.4) | collective-permute-done | bytes 98336 | tf_op jit(solution)/shard_map/ppermute | solution.py:605
  22.2 1.0 %collective-permute-done.5.refs_2_ = bf16[12,32,128]{2,1,0:T(8,128)(2,1)S(1)} collective-permute-done((bf16[12,32,128]{2,1,0:T(8,128)(2,1)S(1)}, bf16[12,32,128]{2,1,0:T(8,128)(2,1)S(1)}, u32[]{:S(2)}, u32[]{:S(2)}) %collective-permute-start.5) | collective-permute-done | bytes 98336 | tf_op jit(solution)/shard_map/ppermute | solution.py:605
  23.2 0.6 %collective-permute-done.6.refs_3_ = bf16[12,32,128]{2,1,0:T(8,128)(2,1)S(1)} collective-permute-done((bf16[12,32,128]{2,1,0:T(8,128)(2,1)S(1)}, bf16[12,32,128]{2,1,0:T(8,128)(2,1)S(1)}, u32[]{:S(2)}, u32[]{:S(2)}) %collective-permute-start.6) | collective-permute-done | bytes 98336 | tf_op jit(solution)/shard_map/ppermute | solution.py:605
  23.9 2.1 %collective-permute-start.8 = (bf16[2,32,128]{2,1,0:T(8,128)(2,1)S(1)}, bf16[2,32,128]{2,1,0:T(8,128)(2,1)S(1)}, u32[]{:S(2)}, u32[]{:S(2)}) collective-permute-start(bf16[2,32,128]{2,1,0:T(8,128)(2,1)S(1)} %edge.2), channel_id=1, source_target_pairs={{0,12},{4,8},{8,4},{12,0},{1,13},{5,9},{9,5},{13,1},{2,14},{6,10},... | collective-permute-start | bytes 49160 | tf_op jit(solution)/shard_map/ppermute | solution.py:562
  26.0 0.6 %assemble.1 = (f32[24,32,128]{2,1,0:T(8,128)S(1)}, bf16[24,32,128]{2,1,0:T(8,128)(2,1)S(1)}, bf16[1,16,1024]{2,1,0:T(8,128)(2,1)S(1)}) custom-call(s32[1]{0:T(128)} %bitcast.core_ref, s32[13]{0:T(128)S(4)} %get-tuple-element.22.plan_ref, s32[24,1,128]{2,1,0:T(1,128)S(1)} %get-tuple-element.23.leaves_ref, f32[12,32,128]{2,1,0:T(8,128)S(1)} %close.1.mine_ref.image_ref, ...), custom_call_target="tpu_custom_call" | custom-call | tf_op jit(solution)/shard_map/assemble/pallas_call | solution.py:656
  26.6 0.2 collective-permute-start.11
  26.8 1.5 %collective-permute-start.10 = (bf16[4,32,128]{2,1,0:T(8,128)(2,1)S(1)}, bf16[4,32,128]{2,1,0:T(8,128)(2,1)S(1)}, u32[]{:S(2)}, u32[]{:S(2)}) collective-permute-start(bf16[4,32,128]{2,1,0:T(8,128)(2,1)S(1)} %edge.3), channel_id=1, source_target_pairs={{0,4},{4,0},{8,12},{12,8},{1,5},{5,1},{9,13},{13,9},{2,6},{6,2},{1... | collective-permute-start | bytes 98312 | tf_op jit(solution)/shard_map/ppermute | solution.py:562
  28.3 1.3 %collective-permute-done.8.refs_0_ = bf16[2,32,128]{2,1,0:T(8,128)(2,1)S(1)} collective-permute-done((bf16[2,32,128]{2,1,0:T(8,128)(2,1)S(1)}, bf16[2,32,128]{2,1,0:T(8,128)(2,1)S(1)}, u32[]{:S(2)}, u32[]{:S(2)}) %collective-permute-start.8) | collective-permute-done | bytes 16416 | tf_op jit(solution)/shard_map/ppermute | solution.py:562
  29.6 0.6 %far.3.refs_5_ = f32[1,3,32,128]{3,2,1,0:T(8,128)S(1)} custom-call(s32[13]{0:T(128)S(4)} %get-tuple-element.22.plan_ref, s32[24,1,128]{2,1,0:T(1,128)S(1)} %get-tuple-element.23.leaves_ref, bf16[1,16,1024]{2,1,0:T(8,128)(2,1)S(1)} %collective-permute-done.11.item_ref, bf16[1,896,441]{2,1,0:T(8,128)(2,1)S(1)} %get-tuple-element.27.trans_ref, ...), custom_call_target="tpu_custom_call" | custom-call | tf_op jit(solution)/shard_map/far/pallas_call | solution.py:608
  30.3 0.6 %collective-permute-done.9.refs_1_ = bf16[2,32,128]{2,1,0:T(8,128)(2,1)S(1)} collective-permute-done((bf16[2,32,128]{2,1,0:T(8,128)(2,1)S(1)}, bf16[2,32,128]{2,1,0:T(8,128)(2,1)S(1)}, u32[]{:S(2)}, u32[]{:S(2)}) %collective-permute-start.9) | collective-permute-done | bytes 16416 | tf_op jit(solution)/shard_map/ppermute | solution.py:605
  30.8 0.7 %near.3 = (bf16[12,32,128]{2,1,0:T(8,128)(2,1)S(1)}, bf16[12,32,128]{2,1,0:T(8,128)(2,1)S(1)}) custom-call(s32[1]{0:T(128)} %bitcast.core_ref, s32[1]{0:T(128)} %bitcast.1.row_ref, s32[1]{0:T(128)S(6)} %copy.11.count_ref, s32[13]{0:T(128)S(4)} %get-tuple-element.22.plan_ref, bf16[2,32,128]{2,1,0:T(8,128)(2,1)S(1)} %collective-permute-done.8.refs_0_, ...), custom_call_target="tpu_custom_call" | custom-call | tf_op jit(solution)/shard_map/near/pallas_call | solution.py:619
  31.6 0.2 collective-permute-start.12
  31.8 1.1 %collective-permute-done.12.got_ref = bf16[12,32,128]{2,1,0:T(8,128)(2,1)S(1)} collective-permute-done((bf16[12,32,128]{2,1,0:T(8,128)(2,1)S(1)}, bf16[12,32,128]{2,1,0:T(8,128)(2,1)S(1)}, u32[]{:S(2)}, u32[]{:S(2)}) %collective-permute-start.12) | collective-permute-done | bytes 98336 | tf_op jit(solution)/shard_map/ppermute | solution.py:605
  33.0 4.9 %collective-permute-start.13 = (bf16[12,32,128]{2,1,0:T(8,128)(2,1)S(1)}, bf16[12,32,128]{2,1,0:T(8,128)(2,1)S(1)}, u32[]{:S(2)}, u32[]{:S(2)}) collective-permute-start(bf16[12,32,128]{2,1,0:T(8,128)(2,1)S(1)} %pair.3.refs_0_), channel_id=1, source_target_pairs={{0,18},{1,19},{2,16},{3,17},{16,2},{17,3},{18,0},{19,1},{4,22},{5,... | collective-permute-start | bytes 294920 | tf_op jit(solution)/shard_map/ppermute | solution.py:605
  37.9 0.6 %collective-permute-start.15 = (bf16[12,32,128]{2,1,0:T(8,128)(2,1)S(1)}, bf16[12,32,128]{2,1,0:T(8,128)(2,1)S(1)}, u32[]{:S(2)}, u32[]{:S(2)}) collective-permute-start(bf16[12,32,128]{2,1,0:T(8,128)(2,1)S(1)} %pair.3.refs_0_), channel_id=1, source_target_pairs={{0,2},{1,3},{2,0},{3,1},{16,18},{17,19},{18,16},{19,17},{4,6},{5,7... | collective-permute-start | bytes 294920 | tf_op jit(solution)/shard_map/ppermute | solution.py:605
  38.5 2.9 %collective-permute-done.13.refs_1_ = bf16[12,32,128]{2,1,0:T(8,128)(2,1)S(1)} collective-permute-done((bf16[12,32,128]{2,1,0:T(8,128)(2,1)S(1)}, bf16[12,32,128]{2,1,0:T(8,128)(2,1)S(1)}, u32[]{:S(2)}, u32[]{:S(2)}) %collective-permute-start.13) | collective-permute-done | bytes 98336 | tf_op jit(solution)/shard_map/ppermute | solution.py:605
  41.5 1.0 %collective-permute-done.14.refs_2_ = bf16[12,32,128]{2,1,0:T(8,128)(2,1)S(1)} collective-permute-done((bf16[12,32,128]{2,1,0:T(8,128)(2,1)S(1)}, bf16[12,32,128]{2,1,0:T(8,128)(2,1)S(1)}, u32[]{:S(2)}, u32[]{:S(2)}) %collective-permute-start.14) | collective-permute-done | bytes 98336 | tf_op jit(solution)/shard_map/ppermute | solution.py:605
  42.5 0.6 %collective-permute-done.15.refs_3_ = bf16[12,32,128]{2,1,0:T(8,128)(2,1)S(1)} collective-permute-done((bf16[12,32,128]{2,1,0:T(8,128)(2,1)S(1)}, bf16[12,32,128]{2,1,0:T(8,128)(2,1)S(1)}, u32[]{:S(2)}, u32[]{:S(2)}) %collective-permute-start.15) | collective-permute-done | bytes 98336 | tf_op jit(solution)/shard_map/ppermute | solution.py:605
  43.1 0.3 gram.1
  43.4 8.4 %all_to_all.5.sums_ref = f32[8,2,128]{2,1,0:T(2,128)S(1)} all-to-all(f32[8,2,128]{2,1,0:T(2,128)S(1)} %gram.1), channel_id=1, replica_groups={{0,1,4,5,8,9,12,13},{2,3,6,7,10,11,14,15},{16,17,20,21,24,25,28,29},{18..., dimensions={0} | all-to-all | bytes 16384 | tf_op jit(solution)/shard_map/all_to_all | solution.py:691
  51.8 1.0 %combine.1 = f32[32,3072]{1,0:T(8,128)} custom-call(f32[8,2,128]{2,1,0:T(2,128)S(1)} %all_to_all.5.sums_ref, f32[32,3072]{1,0:T(8,128)S(1)} %get-tuple-element.21.image_ref.refs_2_.right_ref, f32[24,32,128]{2,1,0:T(8,128)S(1)} %get-tuple-element.32.image_ref), custom_call_target="tpu_custom_call" | custom-call | tf_op jit(solution)/shard_map/combine/pallas_call | solution.py:692
  (18 shorter events, 0.3 us)
Async XLA Ops:
  2.8 7.6 %collective-permute-start.2 = (bf16[1,16,1024]{2,1,0:T(8,128)(2,1)S(1)}, bf16[1,16,1024]{2,1,0:T(8,128)(2,1)S(1)}, u32[]{:S(2)}, u32[]{:S(2)}) collective-permute-start(bf16[1,16,1024]{2,1,0:T(8,128)(2,1)S(1)} %get-tuple-element.26), channel_id=1, source_target_pairs={{0,1},{1,0},{2,6},{3,7},{16,24},{17,25},{18,30},{19,31},{4,8},{5,9... | collective-permute-start | bytes 98312 | tf_op jit(solution)/shard_map/ppermute | solution.py:557
  3.4 7.7 %collective-permute-start = (bf16[32,512]{1,0:T(8,128)(2,1)S(1)}, bf16[32,512]{1,0:T(8,128)(2,1)S(1)}, u32[]{:S(2)}, u32[]{:S(2)}) collective-permute-start(bf16[32,512]{1,0:T(8,128)(2,1)S(1)} %get-tuple-element.24), channel_id=1, source_target_pairs={{0,12},{4,8},{8,4},{12,0},{1,13},{5,9},{9,5},{13,1},{2,14},{6,10},... | collective-permute-start | bytes 98312 | tf_op jit(solution)/shard_map/ppermute | solution.py:562
  8.1 3.9 %collective-permute-start.1 = (bf16[32,512]{1,0:T(8,128)(2,1)S(1)}, bf16[32,512]{1,0:T(8,128)(2,1)S(1)}, u32[]{:S(2)}, u32[]{:S(2)}) collective-permute-start(bf16[32,512]{1,0:T(8,128)(2,1)S(1)} %get-tuple-element.25), channel_id=1, source_target_pairs={{0,4},{4,0},{8,12},{12,8},{1,5},{5,1},{9,13},{13,9},{2,6},{6,2},{1... | collective-permute-start | bytes 98312 | tf_op jit(solution)/shard_map/ppermute | solution.py:562
  8.7 3.3 %copy-start = (bf16[2,8,256,256]{3,2,1,0:T(8,128)(2,1)S(1)}, bf16[2,8,256,256]{3,2,1,0:T(8,128)(2,1)}, u32[]{:S(2)}) copy-start(bf16[2,8,256,256]{3,2,1,0:T(8,128)(2,1)} %refs_4_.1) | copy-start | bytes 6291460
  12.8 1.5 %collective-permute-start.3 = (f32[12,32,128]{2,1,0:T(8,128)S(1)}, f32[12,32,128]{2,1,0:T(8,128)S(1)}, u32[]{:S(2)}, u32[]{:S(2)}) collective-permute-start(f32[12,32,128]{2,1,0:T(8,128)S(1)} %get-tuple-element.30), channel_id=1, source_target_pairs={{0,1},{1,0},{2,3},{3,2},{16,17},{17,16},{18,19},{19,18},{4,5},{5,4... | collective-permute-start | bytes 589832 | tf_op jit(solution)/shard_map/ppermute | solution.py:605
  14.3 7.9 %collective-permute-start.4 = (bf16[12,32,128]{2,1,0:T(8,128)(2,1)S(1)}, bf16[12,32,128]{2,1,0:T(8,128)(2,1)S(1)}, u32[]{:S(2)}, u32[]{:S(2)}) collective-permute-start(bf16[12,32,128]{2,1,0:T(8,128)(2,1)S(1)} %pair.2.refs_0_), channel_id=1, source_target_pairs={{0,18},{1,19},{2,16},{3,17},{16,2},{17,3},{18,0},{19,1},{4,22},{5,... | collective-permute-start | bytes 294920 | tf_op jit(solution)/shard_map/ppermute | solution.py:605
  18.6 4.6 %collective-permute-start.5 = (bf16[12,32,128]{2,1,0:T(8,128)(2,1)S(1)}, bf16[12,32,128]{2,1,0:T(8,128)(2,1)S(1)}, u32[]{:S(2)}, u32[]{:S(2)}) collective-permute-start(bf16[12,32,128]{2,1,0:T(8,128)(2,1)S(1)} %pair.2.refs_0_), channel_id=1, source_target_pairs={{0,16},{1,17},{2,18},{3,19},{16,0},{17,1},{18,2},{19,3},{4,20},{5,... | collective-permute-start | bytes 294920 | tf_op jit(solution)/shard_map/ppermute | solution.py:605
  18.6 5.2 %collective-permute-start.6 = (bf16[12,32,128]{2,1,0:T(8,128)(2,1)S(1)}, bf16[12,32,128]{2,1,0:T(8,128)(2,1)S(1)}, u32[]{:S(2)}, u32[]{:S(2)}) collective-permute-start(bf16[12,32,128]{2,1,0:T(8,128)(2,1)S(1)} %pair.2.refs_0_), channel_id=1, source_target_pairs={{0,2},{1,3},{2,0},{3,1},{16,18},{17,19},{18,16},{19,17},{4,6},{5,7... | collective-permute-start | bytes 294920 | tf_op jit(solution)/shard_map/ppermute | solution.py:605
  23.8 2.2 %collective-permute-start.7 = (f32[12,32,128]{2,1,0:T(8,128)S(1)}, f32[12,32,128]{2,1,0:T(8,128)S(1)}, u32[]{:S(2)}, u32[]{:S(2)}) collective-permute-start(f32[12,32,128]{2,1,0:T(8,128)S(1)} %close.1.mine_ref.image_ref), channel_id=1, source_target_pairs={{0,1},{1,0},{2,3},{3,2},{16,17},{17,16},{18,19},{19,18},{4,5},{5,4... | collective-permute-start | bytes 589832 | tf_op jit(solution)/shard_map/ppermute | solution.py:605
  23.9 5.7 %collective-permute-start.8 = (bf16[2,32,128]{2,1,0:T(8,128)(2,1)S(1)}, bf16[2,32,128]{2,1,0:T(8,128)(2,1)S(1)}, u32[]{:S(2)}, u32[]{:S(2)}) collective-permute-start(bf16[2,32,128]{2,1,0:T(8,128)(2,1)S(1)} %edge.2), channel_id=1, source_target_pairs={{0,12},{4,8},{8,4},{12,0},{1,13},{5,9},{9,5},{13,1},{2,14},{6,10},... | collective-permute-start | bytes 49160 | tf_op jit(solution)/shard_map/ppermute | solution.py:562
  26.6 3.0 %collective-permute-start.11 = (bf16[1,16,1024]{2,1,0:T(8,128)(2,1)S(1)}, bf16[1,16,1024]{2,1,0:T(8,128)(2,1)S(1)}, u32[]{:S(2)}, u32[]{:S(2)}) collective-permute-start(bf16[1,16,1024]{2,1,0:T(8,128)(2,1)S(1)} %get-tuple-element.34), channel_id=1, source_target_pairs={{0,1},{1,0},{2,6},{3,7},{16,24},{17,25},{18,30},{19,31},{4,8},{5,9... | collective-permute-start | bytes 98312 | tf_op jit(solution)/shard_map/ppermute | solution.py:557
  26.8 4.0 %collective-permute-start.10 = (bf16[4,32,128]{2,1,0:T(8,128)(2,1)S(1)}, bf16[4,32,128]{2,1,0:T(8,128)(2,1)S(1)}, u32[]{:S(2)}, u32[]{:S(2)}) collective-permute-start(bf16[4,32,128]{2,1,0:T(8,128)(2,1)S(1)} %edge.3), channel_id=1, source_target_pairs={{0,4},{4,0},{8,12},{12,8},{1,5},{5,1},{9,13},{13,9},{2,6},{6,2},{1... | collective-permute-start | bytes 98312 | tf_op jit(solution)/shard_map/ppermute | solution.py:562
  29.6 1.2 %collective-permute-start.9 = (bf16[2,32,128]{2,1,0:T(8,128)(2,1)S(1)}, bf16[2,32,128]{2,1,0:T(8,128)(2,1)S(1)}, u32[]{:S(2)}, u32[]{:S(2)}) collective-permute-start(bf16[2,32,128]{2,1,0:T(8,128)(2,1)S(1)} %collective-permute-done.8.refs_0_), channel_id=1, source_target_pairs={{0,1},{1,0},{2,3},{3,2},{16,17},{17,16},{18,19},{19,18},{4,5},{5,4... | collective-permute-start | bytes 49160 | tf_op jit(solution)/shard_map/ppermute | solution.py:605
  31.6 1.4 %collective-permute-start.12 = (bf16[12,32,128]{2,1,0:T(8,128)(2,1)S(1)}, bf16[12,32,128]{2,1,0:T(8,128)(2,1)S(1)}, u32[]{:S(2)}, u32[]{:S(2)}) collective-permute-start(bf16[12,32,128]{2,1,0:T(8,128)(2,1)S(1)} %get-tuple-element.36), channel_id=1, source_target_pairs={{0,1},{1,0},{2,3},{3,2},{16,17},{17,16},{18,19},{19,18},{4,5},{5,4... | collective-permute-start | bytes 294920 | tf_op jit(solution)/shard_map/ppermute | solution.py:605
  33.0 8.5 %collective-permute-start.13 = (bf16[12,32,128]{2,1,0:T(8,128)(2,1)S(1)}, bf16[12,32,128]{2,1,0:T(8,128)(2,1)S(1)}, u32[]{:S(2)}, u32[]{:S(2)}) collective-permute-start(bf16[12,32,128]{2,1,0:T(8,128)(2,1)S(1)} %pair.3.refs_0_), channel_id=1, source_target_pairs={{0,18},{1,19},{2,16},{3,17},{16,2},{17,3},{18,0},{19,1},{4,22},{5,... | collective-permute-start | bytes 294920 | tf_op jit(solution)/shard_map/ppermute | solution.py:605
  37.9 4.6 %collective-permute-start.14 = (bf16[12,32,128]{2,1,0:T(8,128)(2,1)S(1)}, bf16[12,32,128]{2,1,0:T(8,128)(2,1)S(1)}, u32[]{:S(2)}, u32[]{:S(2)}) collective-permute-start(bf16[12,32,128]{2,1,0:T(8,128)(2,1)S(1)} %pair.3.refs_0_), channel_id=1, source_target_pairs={{0,16},{1,17},{2,18},{3,19},{16,0},{17,1},{18,2},{19,3},{4,20},{5,... | collective-permute-start | bytes 294920 | tf_op jit(solution)/shard_map/ppermute | solution.py:605
  37.9 5.2 %collective-permute-start.15 = (bf16[12,32,128]{2,1,0:T(8,128)(2,1)S(1)}, bf16[12,32,128]{2,1,0:T(8,128)(2,1)S(1)}, u32[]{:S(2)}, u32[]{:S(2)}) collective-permute-start(bf16[12,32,128]{2,1,0:T(8,128)(2,1)S(1)} %pair.3.refs_0_), channel_id=1, source_target_pairs={{0,2},{1,3},{2,0},{3,1},{16,18},{17,19},{18,16},{19,17},{4,6},{5,7... | collective-permute-start | bytes 294920 | tf_op jit(solution)/shard_map/ppermute | solution.py:605

commit v16 on v15

--- a/solution.py
+++ b/solution.py
@@ -12,8 +12,8 @@
 LANES = 128
 EPSILON = 1e-06
 GROUP = ("grp", "col")
-CODES = 0
-PER_ITEM = 5
+COUNT, CODES = range(2)
+PER_ITEM = 4
 ITEM_REST = LANES
 PIECES = 4
 EVERY = ("grp", "row", "col")
@@ -151,10 +151,10 @@
 
 
 def begin_kernel(
-    fields, items, width, send, rows, row_ref, own_ref, pick_hbm, leaves_hbm,
-    target_hbm, offset_hbm, pairs_hbm, right_hbm, exp_ref,
-    plan_ref, out_ref, window_ref, leaves_ref, right_ref,
-    pick_ref, target_ref, offset_ref, pairs_ref, sem, window_sem,
+    fields, items, width, send, rows, row_ref, own_ref, core_ref, count_ref, pick_hbm, leaves_hbm,
+    target_hbm, offset_hbm, pairs_hbm, right_hbm, exp_ref, trans_ref,
+    plan_ref, out_ref, window_ref, target_window_ref, moved_ref, leaves_ref, right_ref,
+    pick_ref, target_ref, offset_ref, pairs_ref, trans_buf, sem, window_sem, target_sem, trans_sem,
 ):
     loads = [
         pltpu.make_async_copy(source, place, sem.at[k])
@@ -197,6 +197,10 @@
             copy.start()
     for load in loads[2:]:
         load.wait()
+    coefs = trans_ref.shape[3]
+    later = []
+    del core_ref
+    plan_ref[COUNT] = count_ref[0]
     for s in range(slots):
         plan_ref[CODES + s] = pairs_ref[s]
     for i in range(items):
@@ -204,7 +208,13 @@
         other, number = partner(i, True)
         leaf = target_ref[0, other * send + number]
         plan_ref[place + 2], plan_ref[place + 3] = leaf, window_start(leaves_ref, leaf, width)
-        plan_ref[place + 4] = offset_ref[0, other * send + number]
+        offset = offset_ref[0, other * send + number]
+        later.append(pltpu.make_async_copy(trans_ref.at[offset], trans_buf.at[i], trans_sem.at[i]))
+        later += window_copies(exp_ref, plan_ref[place + 3], target_window_ref.at[i], target_sem.at[i], width)
+    for copy in later:
+        copy.start()
+    for i in range(items):
+        clear_rest(target_window_ref.at[i], coefs)
     for i in range(items):
         place = item_place(slots, i)
         leaf, unit = plan_ref[place], plan_ref[place + 1]
@@ -212,32 +222,12 @@
             copy.wait()
         made = multi_rows(fields, width, leaf, unit, leaves_ref, right_ref, window_ref.at[i])
         out_ref[i, :, : made.shape[1]] = made.astype(BF16)
-
-
-def fetch_kernel(items, width, slots, plan_ref, exp_ref, trans_ref, window_ref, moved_ref, trans_buf, sem, trans_sem):
-    coefs = trans_ref.shape[3]
-    for i in range(items):
-        clear_rest(window_ref.at[i], coefs)
-
-    def trans_copy(i):
-        offset = plan_ref[item_place(slots, i) + 4]
-        return pltpu.make_async_copy(trans_ref.at[offset], trans_buf.at[i], trans_sem.at[i])
-
-    def exp_copies(i):
-        unit = plan_ref[item_place(slots, i) + 3]
-        return window_copies(exp_ref, unit, window_ref.at[i], sem.at[i], width)
-
-    for i in range(items):
-        trans_copy(i).start()
-        for copy in exp_copies(i):
-            copy.start()
+    for copy in later:
+        copy.wait()
     rest = moved_ref.shape[1] - 2 * coefs
     for i in range(items):
-        trans_copy(i).wait()
         moved_ref[i, pl.ds(0, 2 * coefs)] = trans_buf[i].reshape(2 * coefs, coefs)
         moved_ref[i, pl.ds(2 * coefs, rest)] = jnp.zeros((rest, coefs), BF16)
-        for copy in exp_copies(i):
-            copy.wait()
 
 
 def edge_places(row_ref, edge, units):
@@ -252,7 +242,7 @@
 
 
 def near_kernel(
-    fields, core_ref, row_ref, count_ref, plan_ref, *refs
+    fields, core_ref, row_ref, plan_ref, *refs
 ):
     *edge_refs, here_ref, tiles_ref, image_ref, keep_ref, give_ref, ext, total = refs
     units = total.shape[0]
@@ -280,11 +270,11 @@
         unit = plan_ref[item_place(tiles_ref.shape[1], i) + 3]
         for k in range(width):
             total[unit + k] += image_ref[i, k]
-    near_slots(fields, count_ref, plan_ref, tiles_ref, total, ext)
+    near_slots(fields, plan_ref, tiles_ref, total, ext)
     part(total, core, keep_ref, give_ref)
 
 
-def near_slots(fields, count_ref, plan_ref, tiles_ref, out_ref, ext):
+def near_slots(fields, plan_ref, tiles_ref, out_ref, ext):
     slots, tile = tiles_ref.shape[1], tiles_ref.shape[2]
     per = tile // LANES
     for s in range(slots):
@@ -297,7 +287,7 @@
         value = jnp.concatenate(
             [on_real[:fields] - on_imag[fields:], on_real[fields:] + on_imag[:fields]], axis=0
         )
-        value = jnp.where(s < count_ref[0], value, 0.0)
+        value = jnp.where(s < plan_ref[COUNT], value, 0.0)
         for k in range(per):
             out_ref[target * per + k] += value[:, k * LANES : (k + 1) * LANES]
 
@@ -519,30 +509,37 @@
     moves = in_hbm(translations.transpose(0, 2, 1, 3))
     picks = far_pick.transpose(0, 2, 1)
 
-    plan, made, windows, leaves, right = pl.pallas_call(
+    plan, made, windows, target_windows, moved, leaves, right = pl.pallas_call(
         functools.partial(begin_kernel, fields, items, width, send, rows),
         out_shape=(
             pltpu.SMEM((item_place(slots, items),), jnp.int32),
             item_shape,
             pltpu.VMEM(window_shape.shape, BF16),
+            pltpu.VMEM(window_shape.shape, BF16),
+            pltpu.VMEM((items, 2 * pad_coefs, coefs), BF16),
             jax.ShapeDtypeStruct(leaves.shape, jnp.int32),
             jax.ShapeDtypeStruct((both, panels), F32),
         ),
-        in_specs=[SMEM] * 2 + [HBM] * 7,
-        out_specs=(SMEM,) + (VMEM,) * 4,
+        in_specs=[SMEM] * 4 + [HBM] * 8,
+        out_specs=(SMEM,) + (VMEM,) * 6,
         scratch_shapes=[
             pltpu.SMEM(value.shape, jnp.int32)
             for value in (picks, far_target, far_offset, tile_pairs)
         ]
         + [
+            pltpu.VMEM((items, coefs, 2, coefs), BF16),
             pltpu.SemaphoreType.DMA((6,)),
             pltpu.SemaphoreType.DMA((items, PIECES)),
+            pltpu.SemaphoreType.DMA((items, PIECES)),
+            pltpu.SemaphoreType.DMA((items,)),
         ],
-        compiler_params=params(),
+        compiler_params=params(24),
         name="begin",
     )(
         row_place,
         own_place,
+        core_place,
+        tile_count,
         in_hbm(picks),
         in_hbm(leaves),
         in_hbm(far_target),
@@ -550,6 +547,7 @@
         in_hbm(tile_pairs),
         in_hbm(right_side.reshape(both, panels)),
         expansions,
+        moves,
     )
 
     def exchanged(made):
@@ -583,24 +581,6 @@
         )(row_place, image)
 
     image_shape = jax.ShapeDtypeStruct((units, both, LANES), F32)
-    target_windows, moved = pl.pallas_call(
-        functools.partial(fetch_kernel, items, width, slots),
-        out_shape=(
-            pltpu.VMEM(window_shape.shape, BF16),
-            pltpu.VMEM((items, 2 * pad_coefs, coefs), BF16),
-        ),
-        in_specs=[SMEM, HBM, HBM],
-        out_specs=(VMEM, VMEM),
-        scratch_shapes=[
-            pltpu.VMEM((items, coefs, 2, coefs), BF16),
-            pltpu.SemaphoreType.DMA((items, PIECES)),
-            pltpu.SemaphoreType.DMA((items,)),
-        ],
-        compiler_params=params(24),
-        cost_estimate=pl.CostEstimate(flops=0, bytes_accessed=6 * window_shape.size, transcendentals=0),
-        name="fetch",
-    )(plan, expansions, moves)
-
     def swapped(value, step):
         return lax.ppermute(value, GROUP, [(g, g ^ step) for g in range(group)])
 
@@ -619,7 +599,7 @@
         keep, give = pl.pallas_call(
             functools.partial(near_kernel, fields),
             out_shape=(half_shape, half_shape),
-            in_specs=[SMEM] * 4 + [VMEM] * (3 + len(edges)),
+            in_specs=[SMEM] * 3 + [VMEM] * (3 + len(edges)),
             out_specs=(VMEM, VMEM),
             scratch_shapes=[
                 pltpu.VMEM((units + 2 * edge_units, both, LANES), low.dtype),
@@ -627,7 +607,7 @@
             ],
             compiler_params=params(),
             name="near",
-        )(core_place, row_place, tile_count, plan, *edges, low, near_tiles, image)
+        )(core_place, row_place, plan, *edges, low, near_tiles, image)
         return keep, swapped(give, 1)
 
     def pair_sums(keep, got):

time: 53.1 us -> 53.9 us (1.015)
  waiting for transfers between devices: 14.4 us -> 17.6 us
  Pallas kernels: 9.35 us -> 7.78 us
  starting transfers between devices: 19.9 us -> 19 us
    ppermute x4, waiting for transfers between devices: 2.15 us -> 5.39 us  [along_row(): return lax.ppermute(value, 'row', list(enumerate(neighbours[which])))]
    pallas_call x1 -> x0, Pallas kernels: 1.73 us -> none  [local(): pl.pallas_call(functools.partial(fetch_kernel, items, width, slots), out_...]
    ppermute x4, starting transfers between devices: 8.33 us -> 7.49 us  [along_row(): return lax.ppermute(value, 'row', list(enumerate(neighbours[which])))]
  transfers between devices with their start and end apart: 16 -> 16, of which waited for: 11 -> 12; matrix products, arithmetic and copies ran while one was open for 0% -> 0% of each run, Pallas kernels for 7% -> 3%
where the time goes in v16:
time: 53.9 us; the launch traced here: 53.7 us
  starting transfers between devices  19 us (35%)
  waiting for transfers between devices  17.6 us (33%)
  blocking collectives  8.44 us (16%)
  Pallas kernels  7.78 us (14%)
  between operations  0.74 us (1%)
    ppermute x10, waiting for transfers between devices, swapped(): return lax.ppermute(value, GROUP, [(g, g ^ step) for g in range(group)])  12.3 us
    ppermute x10, starting transfers between devices, swapped(): return lax.ppermute(value, GROUP, [(g, g ^ step) for g in range(group)])  10.9 us
    all_to_all x1, blocking collectives, local(): lax.all_to_all(lines, EVERY, 0, 0, axis_index_groups=same_chip, tiled=True)  8.44 us
    ppermute x4, starting transfers between devices, along_row(): return lax.ppermute(value, 'row', list(enumerate(neighbours[which])))  7.49 us
    ppermute x4, waiting for transfers between devices, along_row(): return lax.ppermute(value, 'row', list(enumerate(neighbours[which])))  5.39 us
    pallas_call x1, Pallas kernels, local(): pl.pallas_call(functools.partial(begin_kernel, fields, items, width, send...  2.95 us
    pallas_call x2, Pallas kernels, core_parts(): pl.pallas_call(functools.partial(near_kernel, fields), out_shape=(half_sh...  1.56 us
    pallas_call x2, Pallas kernels, far(): pl.pallas_call(functools.partial(far_kernel, fields, items, width, slots)...  1.25 us
  transfers between devices with their start and end apart: 16, of which 12 were waited for; matrix products, arithmetic and copies ran while one was open for 0% of the time, Pallas kernels for 3%

profile of v16, /device:TPU:0, one launch (start us, length us, event | category | flops | bytes accessed | tf_op | source)
XLA Modules:
  0.0 53.7 jit_solution(10296074105647139051)
XLA Ops:
  0.7 3.0 %begin.1 = (s32[13]{0:T(128)S(4)}, bf16[1,16,1024]{2,1,0:T(8,128)(2,1)S(1)}, bf16[1,448,3,2,128]{4,3,2,1,0:T(2,128)(2,1)S(1)}, bf16[1,448,3,2,128]{4,3,2,1,0:T(2...) custom-call(s32[1]{0:T(128)} %bitcast.1.row_ref, ...), custom_call_target="tpu_custom_call" | custom-call | tf_op jit(solution)/shard_map/begin/pallas_call | solution.py:512
  3.6 0.5 collective-permute-start.2
  4.2 4.7 %collective-permute-start = (bf16[32,512]{1,0:T(8,128)(2,1)S(1)}, bf16[32,512]{1,0:T(8,128)(2,1)S(1)}, u32[]{:S(2)}, u32[]{:S(2)}) collective-permute-start(bf16[32,512]{1,0:T(8,128)(2,1)S(1)} %get-tuple-element.24), channel_id=1, source_target_pairs={{0,12},{4,8},{8,4},{12,0},{1,13},{5,9},{9,5},{13,1},{2,14},{6,10},... | collective-permute-start | bytes 98312 | tf_op jit(solution)/shard_map/ppermute | solution.py:560
  8.8 0.6 %far.2.refs_4_ = f32[1,3,32,128]{3,2,1,0:T(8,128)S(1)} custom-call(s32[13]{0:T(128)S(4)} %get-tuple-element.22.plan_ref, s32[24,1,128]{2,1,0:T(1,128)S(1)} %get-tuple-element.23.leaves_ref, bf16[1,16,1024]{2,1,0:T(8,128)(2,1)S(1)} %collective-permute-done.2.item_ref, bf16[1,896,441]{2,1,0:T(8,128)(2,1)S(1)} %get-tuple-element.27.trans_ref, ...), custom_call_target="tpu_custom_call" | custom-call | tf_op jit(solution)/shard_map/far/pallas_call | solution.py:588
  9.5 1.5 %collective-permute-done.refs_0_ = bf16[32,512]{1,0:T(8,128)(2,1)S(1)} collective-permute-done((bf16[32,512]{1,0:T(8,128)(2,1)S(1)}, bf16[32,512]{1,0:T(8,128)(2,1)S(1)}, u32[]{:S(2)}, u32[]{:S(2)}) %collective-permute-start) | collective-permute-done | bytes 32800 | tf_op jit(solution)/shard_map/ppermute | solution.py:560
  11.0 1.8 %collective-permute-done.1.refs_1_ = bf16[32,512]{1,0:T(8,128)(2,1)S(1)} collective-permute-done((bf16[32,512]{1,0:T(8,128)(2,1)S(1)}, bf16[32,512]{1,0:T(8,128)(2,1)S(1)}, u32[]{:S(2)}, u32[]{:S(2)}) %collective-permute-start.1) | collective-permute-done | bytes 32800 | tf_op jit(solution)/shard_map/ppermute | solution.py:560
  12.8 0.8 %near.2 = (f32[12,32,128]{2,1,0:T(8,128)S(1)}, f32[12,32,128]{2,1,0:T(8,128)S(1)}) custom-call(s32[1]{0:T(128)} %bitcast.core_ref, s32[1]{0:T(128)} %bitcast.1.row_ref, s32[13]{0:T(128)S(4)} %get-tuple-element.22.plan_ref, bf16[32,512]{1,0:T(8,128)(2,1)S(1)} %collective-permute-done.refs_0_, bf16[32,512]{1,0:T(8,128)(2,1)S(1)} %collective-permute-done.1.refs_1_, ...), custom_call_target="tpu_custom_call" | custom-call | tf_op jit(solution)/shard_map/near/pallas_call | solution.py:599
  13.6 1.4 %collective-permute-done.3.got_ref = f32[12,32,128]{2,1,0:T(8,128)S(1)} collective-permute-done((f32[12,32,128]{2,1,0:T(8,128)S(1)}, f32[12,32,128]{2,1,0:T(8,128)S(1)}, u32[]{:S(2)}, u32[]{:S(2)}) %collective-permute-start.3) | collective-permute-done | bytes 196640 | tf_op jit(solution)/shard_map/ppermute | solution.py:585
  15.1 4.3 %collective-permute-start.4 = (bf16[12,32,128]{2,1,0:T(8,128)(2,1)S(1)}, bf16[12,32,128]{2,1,0:T(8,128)(2,1)S(1)}, u32[]{:S(2)}, u32[]{:S(2)}) collective-permute-start(bf16[12,32,128]{2,1,0:T(8,128)(2,1)S(1)} %pair.2.refs_0_), channel_id=1, source_target_pairs={{0,18},{1,19},{2,16},{3,17},{16,2},{17,3},{18,0},{19,1},{4,22},{5,... | collective-permute-start | bytes 294920 | tf_op jit(solution)/shard_map/ppermute | solution.py:585
  19.4 0.6 %collective-permute-start.6 = (bf16[12,32,128]{2,1,0:T(8,128)(2,1)S(1)}, bf16[12,32,128]{2,1,0:T(8,128)(2,1)S(1)}, u32[]{:S(2)}, u32[]{:S(2)}) collective-permute-start(bf16[12,32,128]{2,1,0:T(8,128)(2,1)S(1)} %pair.2.refs_0_), channel_id=1, source_target_pairs={{0,2},{1,3},{2,0},{3,1},{16,18},{17,19},{18,16},{19,17},{4,6},{5,7... | collective-permute-start | bytes 294920 | tf_op jit(solution)/shard_map/ppermute | solution.py:585
  20.0 2.9 %collective-permute-done.4.refs_1_ = bf16[12,32,128]{2,1,0:T(8,128)(2,1)S(1)} collective-permute-done((bf16[12,32,128]{2,1,0:T(8,128)(2,1)S(1)}, bf16[12,32,128]{2,1,0:T(8,128)(2,1)S(1)}, u32[]{:S(2)}, u32[]{:S(2)}) %collective-permute-start.4) | collective-permute-done | bytes 98336 | tf_op jit(solution)/shard_map/ppermute | solution.py:585
  23.0 1.0 %collective-permute-done.5.refs_2_ = bf16[12,32,128]{2,1,0:T(8,128)(2,1)S(1)} collective-permute-done((bf16[12,32,128]{2,1,0:T(8,128)(2,1)S(1)}, bf16[12,32,128]{2,1,0:T(8,128)(2,1)S(1)}, u32[]{:S(2)}, u32[]{:S(2)}) %collective-permute-start.5) | collective-permute-done | bytes 98336 | tf_op jit(solution)/shard_map/ppermute | solution.py:585
  24.0 0.6 %collective-permute-done.6.refs_3_ = bf16[12,32,128]{2,1,0:T(8,128)(2,1)S(1)} collective-permute-done((bf16[12,32,128]{2,1,0:T(8,128)(2,1)S(1)}, bf16[12,32,128]{2,1,0:T(8,128)(2,1)S(1)}, u32[]{:S(2)}, u32[]{:S(2)}) %collective-permute-start.6) | collective-permute-done | bytes 98336 | tf_op jit(solution)/shard_map/ppermute | solution.py:585
  24.6 0.1 collective-permute-start.7
  24.7 2.1 %collective-permute-start.8 = (bf16[2,32,128]{2,1,0:T(8,128)(2,1)S(1)}, bf16[2,32,128]{2,1,0:T(8,128)(2,1)S(1)}, u32[]{:S(2)}, u32[]{:S(2)}) collective-permute-start(bf16[2,32,128]{2,1,0:T(8,128)(2,1)S(1)} %edge.2), channel_id=1, source_target_pairs={{0,12},{4,8},{8,4},{12,0},{1,13},{5,9},{9,5},{13,1},{2,14},{6,10},... | collective-permute-start | bytes 49160 | tf_op jit(solution)/shard_map/ppermute | solution.py:560
  26.8 0.6 %assemble.1 = (f32[24,32,128]{2,1,0:T(8,128)S(1)}, bf16[24,32,128]{2,1,0:T(8,128)(2,1)S(1)}, bf16[1,16,1024]{2,1,0:T(8,128)(2,1)S(1)}) custom-call(s32[1]{0:T(128)} %bitcast.core_ref, s32[13]{0:T(128)S(4)} %get-tuple-element.22.plan_ref, s32[24,1,128]{2,1,0:T(1,128)S(1)} %get-tuple-element.23.leaves_ref, f32[12,32,128]{2,1,0:T(8,128)S(1)} %close.1.mine_ref.image_ref, ...), custom_call_target="tpu_custom_call" | custom-call | tf_op jit(solution)/shard_map/assemble/pallas_call | solution.py:636
  27.4 0.2 collective-permute-start.11
  27.6 0.7 %collective-permute-start.10 = (bf16[4,32,128]{2,1,0:T(8,128)(2,1)S(1)}, bf16[4,32,128]{2,1,0:T(8,128)(2,1)S(1)}, u32[]{:S(2)}, u32[]{:S(2)}) collective-permute-start(bf16[4,32,128]{2,1,0:T(8,128)(2,1)S(1)} %edge.3), channel_id=1, source_target_pairs={{0,4},{4,0},{8,12},{12,8},{1,5},{5,1},{9,13},{13,9},{2,6},{6,2},{1... | collective-permute-start | bytes 98312 | tf_op jit(solution)/shard_map/ppermute | solution.py:560
  28.3 2.1 %collective-permute-done.8.refs_0_ = bf16[2,32,128]{2,1,0:T(8,128)(2,1)S(1)} collective-permute-done((bf16[2,32,128]{2,1,0:T(8,128)(2,1)S(1)}, bf16[2,32,128]{2,1,0:T(8,128)(2,1)S(1)}, u32[]{:S(2)}, u32[]{:S(2)}) %collective-permute-start.8) | collective-permute-done | bytes 16416 | tf_op jit(solution)/shard_map/ppermute | solution.py:560
  30.4 0.6 %far.3.refs_5_ = f32[1,3,32,128]{3,2,1,0:T(8,128)S(1)} custom-call(s32[13]{0:T(128)S(4)} %get-tuple-element.22.plan_ref, s32[24,1,128]{2,1,0:T(1,128)S(1)} %get-tuple-element.23.leaves_ref, bf16[1,16,1024]{2,1,0:T(8,128)(2,1)S(1)} %collective-permute-done.11.item_ref, bf16[1,896,441]{2,1,0:T(8,128)(2,1)S(1)} %get-tuple-element.27.trans_ref, ...), custom_call_target="tpu_custom_call" | custom-call | tf_op jit(solution)/shard_map/far/pallas_call | solution.py:588
  31.0 0.6 %collective-permute-done.9.refs_1_ = bf16[2,32,128]{2,1,0:T(8,128)(2,1)S(1)} collective-permute-done((bf16[2,32,128]{2,1,0:T(8,128)(2,1)S(1)}, bf16[2,32,128]{2,1,0:T(8,128)(2,1)S(1)}, u32[]{:S(2)}, u32[]{:S(2)}) %collective-permute-start.9) | collective-permute-done | bytes 16416 | tf_op jit(solution)/shard_map/ppermute | solution.py:585
  31.6 0.8 %near.3 = (bf16[12,32,128]{2,1,0:T(8,128)(2,1)S(1)}, bf16[12,32,128]{2,1,0:T(8,128)(2,1)S(1)}) custom-call(s32[1]{0:T(128)} %bitcast.core_ref, s32[1]{0:T(128)} %bitcast.1.row_ref, s32[13]{0:T(128)S(4)} %get-tuple-element.22.plan_ref, bf16[2,32,128]{2,1,0:T(8,128)(2,1)S(1)} %collective-permute-done.8.refs_0_, ...), custom_call_target="tpu_custom_call" | custom-call | tf_op jit(solution)/shard_map/near/pallas_call | solution.py:599
  32.4 0.2 collective-permute-start.12
  32.6 1.1 %collective-permute-done.12.got_ref = bf16[12,32,128]{2,1,0:T(8,128)(2,1)S(1)} collective-permute-done((bf16[12,32,128]{2,1,0:T(8,128)(2,1)S(1)}, bf16[12,32,128]{2,1,0:T(8,128)(2,1)S(1)}, u32[]{:S(2)}, u32[]{:S(2)}) %collective-permute-start.12) | collective-permute-done | bytes 98336 | tf_op jit(solution)/shard_map/ppermute | solution.py:585
  33.8 4.9 %collective-permute-start.13 = (bf16[12,32,128]{2,1,0:T(8,128)(2,1)S(1)}, bf16[12,32,128]{2,1,0:T(8,128)(2,1)S(1)}, u32[]{:S(2)}, u32[]{:S(2)}) collective-permute-start(bf16[12,32,128]{2,1,0:T(8,128)(2,1)S(1)} %pair.3.refs_0_), channel_id=1, source_target_pairs={{0,18},{1,19},{2,16},{3,17},{16,2},{17,3},{18,0},{19,1},{4,22},{5,... | collective-permute-start | bytes 294920 | tf_op jit(solution)/shard_map/ppermute | solution.py:585
  38.7 0.6 %collective-permute-start.15 = (bf16[12,32,128]{2,1,0:T(8,128)(2,1)S(1)}, bf16[12,32,128]{2,1,0:T(8,128)(2,1)S(1)}, u32[]{:S(2)}, u32[]{:S(2)}) collective-permute-start(bf16[12,32,128]{2,1,0:T(8,128)(2,1)S(1)} %pair.3.refs_0_), channel_id=1, source_target_pairs={{0,2},{1,3},{2,0},{3,1},{16,18},{17,19},{18,16},{19,17},{4,6},{5,7... | collective-permute-start | bytes 294920 | tf_op jit(solution)/shard_map/ppermute | solution.py:585
  39.3 2.9 %collective-permute-done.13.refs_1_ = bf16[12,32,128]{2,1,0:T(8,128)(2,1)S(1)} collective-permute-done((bf16[12,32,128]{2,1,0:T(8,128)(2,1)S(1)}, bf16[12,32,128]{2,1,0:T(8,128)(2,1)S(1)}, u32[]{:S(2)}, u32[]{:S(2)}) %collective-permute-start.13) | collective-permute-done | bytes 98336 | tf_op jit(solution)/shard_map/ppermute | solution.py:585
  42.3 1.0 %collective-permute-done.14.refs_2_ = bf16[12,32,128]{2,1,0:T(8,128)(2,1)S(1)} collective-permute-done((bf16[12,32,128]{2,1,0:T(8,128)(2,1)S(1)}, bf16[12,32,128]{2,1,0:T(8,128)(2,1)S(1)}, u32[]{:S(2)}, u32[]{:S(2)}) %collective-permute-start.14) | collective-permute-done | bytes 98336 | tf_op jit(solution)/shard_map/ppermute | solution.py:585
  43.3 0.6 %collective-permute-done.15.refs_3_ = bf16[12,32,128]{2,1,0:T(8,128)(2,1)S(1)} collective-permute-done((bf16[12,32,128]{2,1,0:T(8,128)(2,1)S(1)}, bf16[12,32,128]{2,1,0:T(8,128)(2,1)S(1)}, u32[]{:S(2)}, u32[]{:S(2)}) %collective-permute-start.15) | collective-permute-done | bytes 98336 | tf_op jit(solution)/shard_map/ppermute | solution.py:585
  43.9 0.3 gram.1
  44.2 8.4 %all_to_all.5.sums_ref = f32[8,2,128]{2,1,0:T(2,128)S(1)} all-to-all(f32[8,2,128]{2,1,0:T(2,128)S(1)} %gram.1), channel_id=1, replica_groups={{0,1,4,5,8,9,12,13},{2,3,6,7,10,11,14,15},{16,17,20,21,24,25,28,29},{18..., dimensions={0} | all-to-all | bytes 16384 | tf_op jit(solution)/shard_map/all_to_all | solution.py:671
  52.6 1.0 %combine.1 = f32[32,3072]{1,0:T(8,128)} custom-call(f32[8,2,128]{2,1,0:T(2,128)S(1)} %all_to_all.5.sums_ref, f32[32,3072]{1,0:T(8,128)S(1)} %get-tuple-element.21.image_ref.refs_2_.right_ref, f32[24,32,128]{2,1,0:T(8,128)S(1)} %get-tuple-element.32.image_ref), custom_call_target="tpu_custom_call" | custom-call | tf_op jit(solution)/shard_map/combine/pallas_call | solution.py:672
  (17 shorter events, 0.3 us)
Async XLA Ops:
  0.7 12.1 %copy-start = (bf16[2,8,256,256]{3,2,1,0:T(8,128)(2,1)S(1)}, bf16[2,8,256,256]{3,2,1,0:T(8,128)(2,1)}, u32[]{:S(2)}) copy-start(bf16[2,8,256,256]{3,2,1,0:T(8,128)(2,1)} %refs_4_.1) | copy-start | bytes 6291460
  3.6 5.2 %collective-permute-start.2 = (bf16[1,16,1024]{2,1,0:T(8,128)(2,1)S(1)}, bf16[1,16,1024]{2,1,0:T(8,128)(2,1)S(1)}, u32[]{:S(2)}, u32[]{:S(2)}) collective-permute-start(bf16[1,16,1024]{2,1,0:T(8,128)(2,1)S(1)} %get-tuple-element.26), channel_id=1, source_target_pairs={{0,1},{1,0},{2,6},{3,7},{16,24},{17,25},{18,30},{19,31},{4,8},{5,9... | collective-permute-start | bytes 98312 | tf_op jit(solution)/shard_map/ppermute | solution.py:555
  4.2 6.8 %collective-permute-start = (bf16[32,512]{1,0:T(8,128)(2,1)S(1)}, bf16[32,512]{1,0:T(8,128)(2,1)S(1)}, u32[]{:S(2)}, u32[]{:S(2)}) collective-permute-start(bf16[32,512]{1,0:T(8,128)(2,1)S(1)} %get-tuple-element.24), channel_id=1, source_target_pairs={{0,12},{4,8},{8,4},{12,0},{1,13},{5,9},{9,5},{13,1},{2,14},{6,10},... | collective-permute-start | bytes 98312 | tf_op jit(solution)/shard_map/ppermute | solution.py:560
  8.8 3.9 %collective-permute-start.1 = (bf16[32,512]{1,0:T(8,128)(2,1)S(1)}, bf16[32,512]{1,0:T(8,128)(2,1)S(1)}, u32[]{:S(2)}, u32[]{:S(2)}) collective-permute-start(bf16[32,512]{1,0:T(8,128)(2,1)S(1)} %get-tuple-element.25), channel_id=1, source_target_pairs={{0,4},{4,0},{8,12},{12,8},{1,5},{5,1},{9,13},{13,9},{2,6},{6,2},{1... | collective-permute-start | bytes 98312 | tf_op jit(solution)/shard_map/ppermute | solution.py:560
  13.6 1.5 %collective-permute-start.3 = (f32[12,32,128]{2,1,0:T(8,128)S(1)}, f32[12,32,128]{2,1,0:T(8,128)S(1)}, u32[]{:S(2)}, u32[]{:S(2)}) collective-permute-start(f32[12,32,128]{2,1,0:T(8,128)S(1)} %get-tuple-element.30), channel_id=1, source_target_pairs={{0,1},{1,0},{2,3},{3,2},{16,17},{17,16},{18,19},{19,18},{4,5},{5,4... | collective-permute-start | bytes 589832 | tf_op jit(solution)/shard_map/ppermute | solution.py:585
  15.1 7.9 %collective-permute-start.4 = (bf16[12,32,128]{2,1,0:T(8,128)(2,1)S(1)}, bf16[12,32,128]{2,1,0:T(8,128)(2,1)S(1)}, u32[]{:S(2)}, u32[]{:S(2)}) collective-permute-start(bf16[12,32,128]{2,1,0:T(8,128)(2,1)S(1)} %pair.2.refs_0_), channel_id=1, source_target_pairs={{0,18},{1,19},{2,16},{3,17},{16,2},{17,3},{18,0},{19,1},{4,22},{5,... | collective-permute-start | bytes 294920 | tf_op jit(solution)/shard_map/ppermute | solution.py:585
  19.4 4.6 %collective-permute-start.5 = (bf16[12,32,128]{2,1,0:T(8,128)(2,1)S(1)}, bf16[12,32,128]{2,1,0:T(8,128)(2,1)S(1)}, u32[]{:S(2)}, u32[]{:S(2)}) collective-permute-start(bf16[12,32,128]{2,1,0:T(8,128)(2,1)S(1)} %pair.2.refs_0_), channel_id=1, source_target_pairs={{0,16},{1,17},{2,18},{3,19},{16,0},{17,1},{18,2},{19,3},{4,20},{5,... | collective-permute-start | bytes 294920 | tf_op jit(solution)/shard_map/ppermute | solution.py:585
  19.4 5.2 %collective-permute-start.6 = (bf16[12,32,128]{2,1,0:T(8,128)(2,1)S(1)}, bf16[12,32,128]{2,1,0:T(8,128)(2,1)S(1)}, u32[]{:S(2)}, u32[]{:S(2)}) collective-permute-start(bf16[12,32,128]{2,1,0:T(8,128)(2,1)S(1)} %pair.2.refs_0_), channel_id=1, source_target_pairs={{0,2},{1,3},{2,0},{3,1},{16,18},{17,19},{18,16},{19,17},{4,6},{5,7... | collective-permute-start | bytes 294920 | tf_op jit(solution)/shard_map/ppermute | solution.py:585
  24.6 2.2 %collective-permute-start.7 = (f32[12,32,128]{2,1,0:T(8,128)S(1)}, f32[12,32,128]{2,1,0:T(8,128)S(1)}, u32[]{:S(2)}, u32[]{:S(2)}) collective-permute-start(f32[12,32,128]{2,1,0:T(8,128)S(1)} %close.1.mine_ref.image_ref), channel_id=1, source_target_pairs={{0,1},{1,0},{2,3},{3,2},{16,17},{17,16},{18,19},{19,18},{4,5},{5,4... | collective-permute-start | bytes 589832 | tf_op jit(solution)/shard_map/ppermute | solution.py:585
  24.7 5.7 %collective-permute-start.8 = (bf16[2,32,128]{2,1,0:T(8,128)(2,1)S(1)}, bf16[2,32,128]{2,1,0:T(8,128)(2,1)S(1)}, u32[]{:S(2)}, u32[]{:S(2)}) collective-permute-start(bf16[2,32,128]{2,1,0:T(8,128)(2,1)S(1)} %edge.2), channel_id=1, source_target_pairs={{0,12},{4,8},{8,4},{12,0},{1,13},{5,9},{9,5},{13,1},{2,14},{6,10},... | collective-permute-start | bytes 49160 | tf_op jit(solution)/shard_map/ppermute | solution.py:560
  27.4 3.0 %collective-permute-start.11 = (bf16[1,16,1024]{2,1,0:T(8,128)(2,1)S(1)}, bf16[1,16,1024]{2,1,0:T(8,128)(2,1)S(1)}, u32[]{:S(2)}, u32[]{:S(2)}) collective-permute-start(bf16[1,16,1024]{2,1,0:T(8,128)(2,1)S(1)} %get-tuple-element.34), channel_id=1, source_target_pairs={{0,1},{1,0},{2,6},{3,7},{16,24},{17,25},{18,30},{19,31},{4,8},{5,9... | collective-permute-start | bytes 98312 | tf_op jit(solution)/shard_map/ppermute | solution.py:555
  27.6 4.0 %collective-permute-start.10 = (bf16[4,32,128]{2,1,0:T(8,128)(2,1)S(1)}, bf16[4,32,128]{2,1,0:T(8,128)(2,1)S(1)}, u32[]{:S(2)}, u32[]{:S(2)}) collective-permute-start(bf16[4,32,128]{2,1,0:T(8,128)(2,1)S(1)} %edge.3), channel_id=1, source_target_pairs={{0,4},{4,0},{8,12},{12,8},{1,5},{5,1},{9,13},{13,9},{2,6},{6,2},{1... | collective-permute-start | bytes 98312 | tf_op jit(solution)/shard_map/ppermute | solution.py:560
  30.4 1.2 %collective-permute-start.9 = (bf16[2,32,128]{2,1,0:T(8,128)(2,1)S(1)}, bf16[2,32,128]{2,1,0:T(8,128)(2,1)S(1)}, u32[]{:S(2)}, u32[]{:S(2)}) collective-permute-start(bf16[2,32,128]{2,1,0:T(8,128)(2,1)S(1)} %collective-permute-done.8.refs_0_), channel_id=1, source_target_pairs={{0,1},{1,0},{2,3},{3,2},{16,17},{17,16},{18,19},{19,18},{4,5},{5,4... | collective-permute-start | bytes 49160 | tf_op jit(solution)/shard_map/ppermute | solution.py:585
  32.4 1.4 %collective-permute-start.12 = (bf16[12,32,128]{2,1,0:T(8,128)(2,1)S(1)}, bf16[12,32,128]{2,1,0:T(8,128)(2,1)S(1)}, u32[]{:S(2)}, u32[]{:S(2)}) collective-permute-start(bf16[12,32,128]{2,1,0:T(8,128)(2,1)S(1)} %get-tuple-element.36), channel_id=1, source_target_pairs={{0,1},{1,0},{2,3},{3,2},{16,17},{17,16},{18,19},{19,18},{4,5},{5,4... | collective-permute-start | bytes 294920 | tf_op jit(solution)/shard_map/ppermute | solution.py:585
  33.8 8.5 %collective-permute-start.13 = (bf16[12,32,128]{2,1,0:T(8,128)(2,1)S(1)}, bf16[12,32,128]{2,1,0:T(8,128)(2,1)S(1)}, u32[]{:S(2)}, u32[]{:S(2)}) collective-permute-start(bf16[12,32,128]{2,1,0:T(8,128)(2,1)S(1)} %pair.3.refs_0_), channel_id=1, source_target_pairs={{0,18},{1,19},{2,16},{3,17},{16,2},{17,3},{18,0},{19,1},{4,22},{5,... | collective-permute-start | bytes 294920 | tf_op jit(solution)/shard_map/ppermute | solution.py:585
  38.7 4.6 %collective-permute-start.14 = (bf16[12,32,128]{2,1,0:T(8,128)(2,1)S(1)}, bf16[12,32,128]{2,1,0:T(8,128)(2,1)S(1)}, u32[]{:S(2)}, u32[]{:S(2)}) collective-permute-start(bf16[12,32,128]{2,1,0:T(8,128)(2,1)S(1)} %pair.3.refs_0_), channel_id=1, source_target_pairs={{0,16},{1,17},{2,18},{3,19},{16,0},{17,1},{18,2},{19,3},{4,20},{5,... | collective-permute-start | bytes 294920 | tf_op jit(solution)/shard_map/ppermute | solution.py:585
  38.7 5.2 %collective-permute-start.15 = (bf16[12,32,128]{2,1,0:T(8,128)(2,1)S(1)}, bf16[12,32,128]{2,1,0:T(8,128)(2,1)S(1)}, u32[]{:S(2)}, u32[]{:S(2)}) collective-permute-start(bf16[12,32,128]{2,1,0:T(8,128)(2,1)S(1)} %pair.3.refs_0_), channel_id=1, source_target_pairs={{0,2},{1,3},{2,0},{3,1},{16,18},{17,19},{18,16},{19,17},{4,6},{5,7... | collective-permute-start | bytes 294920 | tf_op jit(solution)/shard_map/ppermute | solution.py:585

commit v17 on v13

--- a/solution.py
+++ b/solution.py
@@ -646,10 +646,9 @@
         )(row_place, tile_count, plan, one, two, low, near_tiles)
 
     def core_parts(partial, taken):
-        half_shape = jax.ShapeDtypeStruct(half_units, F32)
         keep, give = pl.pallas_call(
             functools.partial(far_kernel, fields, items, width, slots),
-            out_shape=(half_shape, half_shape),
+            out_shape=(jax.ShapeDtypeStruct(half_units, F32), jax.ShapeDtypeStruct(half_units, BF16)),
             in_specs=[SMEM, SMEM] + [VMEM] * 5,
             out_specs=(VMEM, VMEM),
             scratch_shapes=[pltpu.VMEM(image_shape.shape, F32)],

time: 52.8 us -> 52.7 us (level)
  no operation moved by 1% of the time
where the time goes in v17:
time: 52.7 us; the launch traced here: 52.4 us
  starting transfers between devices  18.1 us (34%)
  waiting for transfers between devices  15.5 us (29%)
  Pallas kernels  9.27 us (18%)
  blocking collectives  8.75 us (17%)
  between operations  0.78 us (1%)
    ppermute x10, waiting for transfers between devices, swapped(): return lax.ppermute(value, GROUP, [(g, g ^ step) for g in range(group)])  12.4 us
    ppermute x10, starting transfers between devices, swapped(): return lax.ppermute(value, GROUP, [(g, g ^ step) for g in range(group)])  9.52 us
    all_to_all x1, blocking collectives, local(): lax.all_to_all(lines, EVERY, 0, 0, axis_index_groups=same_chip, tiled=True)  8.75 us
    ppermute x4, starting transfers between devices, along_row(): return lax.ppermute(value, 'row', list(enumerate(neighbours[which])))  8.4 us
    ppermute x4, waiting for transfers between devices, along_row(): return lax.ppermute(value, 'row', list(enumerate(neighbours[which])))  3.16 us
    pallas_call x1, Pallas kernels, local(): pl.pallas_call(functools.partial(begin_kernel, fields, items, width, send...  2.74 us
    pallas_call x1, Pallas kernels, local(): pl.pallas_call(functools.partial(fetch_kernel, items, width, slots), out_...  1.73 us
  transfers between devices with their start and end apart: 16, of which 10 were waited for; matrix products, arithmetic and copies ran while one was open for 0% of the time, Pallas kernels for 7%

profile of v17, /device:TPU:0, one launch (start us, length us, event | category | flops | bytes accessed | tf_op | source)
XLA Modules:
  0.0 52.4 jit_solution(17020296098075698995)
XLA Ops:
  0.0 2.7 %begin.1 = (s32[13]{0:T(128)S(4)}, bf16[1,16,896]{2,1,0:T(8,128)(2,1)S(1)}, bf16[1,448,3,2,128]{4,3,2,1,0:T(2,128)(2,1)S(1)}, s32[24,1,128]{2,1,0:T(1,128)S(1)}, f32[32,3072]{1,0:T(8,128)S(1)}) custom-call(s32[1]{0:T(128)} %bitcast.1.row_ref, s32[1]{0:T(128)} %bitcast.2.own_ref, s32[4,2,4]{2,1,0:T(2,128)} %bitcast.18, s32[1,3072]{1,0:T(1,128)} %leaf_hbm.1, ...), custom_call_target="tpu_custom_call" | custom-call | tf_op jit(solution)/shard_map/begin/pallas_call | solution.py:548
  2.8 5.1 %collective-permute-start = (bf16[32,512]{1,0:T(8,128)(2,1)S(1)}, bf16[32,512]{1,0:T(8,128)(2,1)S(1)}, u32[]{:S(2)}, u32[]{:S(2)}) collective-permute-start(bf16[32,512]{1,0:T(8,128)(2,1)S(1)} %get-tuple-element.24), channel_id=1, source_target_pairs={{0,12},{4,8},{8,4},{12,0},{1,13},{5,9},{9,5},{13,1},{2,14},{6,10},... | collective-permute-start | bytes 98312 | tf_op jit(solution)/shard_map/ppermute | solution.py:589
  8.6 1.7 %fetch.1 = (bf16[1,448,3,2,128]{4,3,2,1,0:T(2,128)(2,1)S(1)}, bf16[1,896,441]{2,1,0:T(8,128)(2,1)S(1)}) custom-call(s32[13]{0:T(128)S(4)} %get-tuple-element.22.plan_ref, bf16[441,24,2,128]{3,2,1,0:T(2,128)(2,1)} %bitcast.14, bf16[4,441,2,441]{3,2,1,0:T(2,128)(2,1)} %bitcast.15), custom_call_target="tpu_custom_call" | custom-call | bytes 2064384 | tf_op jit(solution)/shard_map/fetch/pallas_call | solution.py:613
  10.3 1.5 %collective-permute-done.1.two_ref = bf16[32,512]{1,0:T(8,128)(2,1)S(1)} collective-permute-done((bf16[32,512]{1,0:T(8,128)(2,1)S(1)}, bf16[32,512]{1,0:T(8,128)(2,1)S(1)}, u32[]{:S(2)}, u32[]{:S(2)}) %collective-permute-start.1) | collective-permute-done | bytes 32800 | tf_op jit(solution)/shard_map/ppermute | solution.py:589
  11.8 0.8 %near.1.partial_ref = f32[24,32,128]{2,1,0:T(8,128)S(1)} custom-call(s32[1]{0:T(128)} %bitcast.1.row_ref, s32[1]{0:T(128)S(6)} %copy.11.count_ref, s32[13]{0:T(128)S(4)} %get-tuple-element.22.plan_ref, bf16[32,512]{1,0:T(8,128)(2,1)S(1)} %collective-permute-done.one_ref, bf16[32,512]{1,0:T(8,128)(2,1)S(1)} %collective-permute-done.1.two_ref, ...), custom_call_target="tpu_custom_call" | custom-call | flops 67108864 | bytes 2097152 | tf_op jit(solution)/shard_map/near/pallas_call | solution.py:635
  12.6 0.7 %far.1 = (f32[12,32,128]{2,1,0:T(8,128)S(1)}, bf16[12,32,128]{2,1,0:T(8,128)(2,1)S(1)}) custom-call(s32[1]{0:T(128)} %bitcast.core_ref, s32[13]{0:T(128)S(4)} %get-tuple-element.22.plan_ref, s32[24,1,128]{2,1,0:T(1,128)S(1)} %get-tuple-element.23.leaves_ref, f32[24,32,128]{2,1,0:T(8,128)S(1)} %near.1.partial_ref, ...), custom_call_target="tpu_custom_call" | custom-call | tf_op jit(solution)/shard_map/far/pallas_call | solution.py:649
  13.3 0.1 collective-permute-start.3
  13.3 1.3 %collective-permute-done.3.got_ref = bf16[12,32,128]{2,1,0:T(8,128)(2,1)S(1)} collective-permute-done((bf16[12,32,128]{2,1,0:T(8,128)(2,1)S(1)}, bf16[12,32,128]{2,1,0:T(8,128)(2,1)S(1)}, u32[]{:S(2)}, u32[]{:S(2)}) %collective-permute-start.3) | collective-permute-done | bytes 98336 | tf_op jit(solution)/shard_map/ppermute | solution.py:632
  14.7 3.5 %collective-permute-start.4 = (bf16[12,32,128]{2,1,0:T(8,128)(2,1)S(1)}, bf16[12,32,128]{2,1,0:T(8,128)(2,1)S(1)}, u32[]{:S(2)}, u32[]{:S(2)}) collective-permute-start(bf16[12,32,128]{2,1,0:T(8,128)(2,1)S(1)} %pair.2.refs_0_), channel_id=1, source_target_pairs={{0,18},{1,19},{2,16},{3,17},{16,2},{17,3},{18,0},{19,1},{4,22},{5,... | collective-permute-start | bytes 294920 | tf_op jit(solution)/shard_map/ppermute | solution.py:632
  18.1 0.5 collective-permute-start.5
  18.7 0.1 collective-permute-start.6
  18.8 2.9 %collective-permute-done.4.refs_1_ = bf16[12,32,128]{2,1,0:T(8,128)(2,1)S(1)} collective-permute-done((bf16[12,32,128]{2,1,0:T(8,128)(2,1)S(1)}, bf16[12,32,128]{2,1,0:T(8,128)(2,1)S(1)}, u32[]{:S(2)}, u32[]{:S(2)}) %collective-permute-start.4) | collective-permute-done | bytes 98336 | tf_op jit(solution)/shard_map/ppermute | solution.py:632
  21.7 1.9 %collective-permute-done.5.refs_2_ = bf16[12,32,128]{2,1,0:T(8,128)(2,1)S(1)} collective-permute-done((bf16[12,32,128]{2,1,0:T(8,128)(2,1)S(1)}, bf16[12,32,128]{2,1,0:T(8,128)(2,1)S(1)}, u32[]{:S(2)}, u32[]{:S(2)}) %collective-permute-start.5) | collective-permute-done | bytes 98336 | tf_op jit(solution)/shard_map/ppermute | solution.py:632
  23.6 0.1 collective-permute-start.7
  23.7 1.6 %collective-permute-start.8 = (bf16[2,32,128]{2,1,0:T(8,128)(2,1)S(1)}, bf16[2,32,128]{2,1,0:T(8,128)(2,1)S(1)}, u32[]{:S(2)}, u32[]{:S(2)}) collective-permute-start(bf16[2,32,128]{2,1,0:T(8,128)(2,1)S(1)} %edge.2), channel_id=1, source_target_pairs={{0,12},{4,8},{8,4},{12,0},{1,13},{5,9},{9,5},{13,1},{2,14},{6,10},... | collective-permute-start | bytes 49160 | tf_op jit(solution)/shard_map/ppermute | solution.py:589
  25.4 0.6 %assemble.1 = (f32[24,32,128]{2,1,0:T(8,128)S(1)}, bf16[24,32,128]{2,1,0:T(8,128)(2,1)S(1)}, bf16[1,16,1024]{2,1,0:T(8,128)(2,1)S(1)}) custom-call(s32[1]{0:T(128)} %bitcast.core_ref, s32[13]{0:T(128)S(4)} %get-tuple-element.22.plan_ref, s32[24,1,128]{2,1,0:T(1,128)S(1)} %get-tuple-element.23.leaves_ref, f32[12,32,128]{2,1,0:T(8,128)S(1)} %close.1.mine_ref.image_ref, ...), custom_call_target="tpu_custom_call" | custom-call | tf_op jit(solution)/shard_map/assemble/pallas_call | solution.py:709
  25.9 0.2 collective-permute-start.11
  26.1 1.7 %collective-permute-start.10 = (bf16[4,32,128]{2,1,0:T(8,128)(2,1)S(1)}, bf16[4,32,128]{2,1,0:T(8,128)(2,1)S(1)}, u32[]{:S(2)}, u32[]{:S(2)}) collective-permute-start(bf16[4,32,128]{2,1,0:T(8,128)(2,1)S(1)} %edge.3), channel_id=1, source_target_pairs={{0,4},{4,0},{8,12},{12,8},{1,5},{5,1},{9,13},{13,9},{2,6},{6,2},{1... | collective-permute-start | bytes 98312 | tf_op jit(solution)/shard_map/ppermute | solution.py:589
  27.8 1.7 %collective-permute-done.8.one_ref = bf16[2,32,128]{2,1,0:T(8,128)(2,1)S(1)} collective-permute-done((bf16[2,32,128]{2,1,0:T(8,128)(2,1)S(1)}, bf16[2,32,128]{2,1,0:T(8,128)(2,1)S(1)}, u32[]{:S(2)}, u32[]{:S(2)}) %collective-permute-start.8) | collective-permute-done | bytes 16416 | tf_op jit(solution)/shard_map/ppermute | solution.py:589
  29.5 0.6 %first_far.1.image_ref = f32[1,3,32,128]{3,2,1,0:T(8,128)S(1)} custom-call(s32[13]{0:T(128)S(4)} %get-tuple-element.22.plan_ref, s32[24,1,128]{2,1,0:T(1,128)S(1)} %get-tuple-element.23.leaves_ref, bf16[1,16,1024]{2,1,0:T(8,128)(2,1)S(1)} %collective-permute-done.11.item_ref, bf16[1,896,441]{2,1,0:T(8,128)(2,1)S(1)} %get-tuple-element.27.trans_ref, ...), custom_call_target="tpu_custom_call" | custom-call | tf_op jit(solution)/shard_map/first_far/pallas_call | solution.py:661
  30.1 0.6 %collective-permute-done.9.other_one_ref = bf16[2,32,128]{2,1,0:T(8,128)(2,1)S(1)} collective-permute-done((bf16[2,32,128]{2,1,0:T(8,128)(2,1)S(1)}, bf16[2,32,128]{2,1,0:T(8,128)(2,1)S(1)}, u32[]{:S(2)}, u32[]{:S(2)}) %collective-permute-start.9) | collective-permute-done | bytes 16416 | tf_op jit(solution)/shard_map/ppermute | solution.py:632
  30.6 0.7 %last_near.1 = (bf16[12,32,128]{2,1,0:T(8,128)(2,1)S(1)}, bf16[12,32,128]{2,1,0:T(8,128)(2,1)S(1)}) custom-call(s32[1]{0:T(128)} %bitcast.core_ref, s32[1]{0:T(128)} %bitcast.1.row_ref, s32[1]{0:T(128)S(6)} %copy.11.count_ref, s32[13]{0:T(128)S(4)} %get-tuple-element.22.plan_ref, bf16[2,32,128]{2,1,0:T(8,128)(2,1)S(1)} %collective-permute-done.8.one_ref, ...), custom_call_target="tpu_custom_call" | custom-call | tf_op jit(solution)/shard_map/last_near/pallas_call | solution.py:672
  31.4 0.2 collective-permute-start.12
  31.6 1.1 %collective-permute-done.12.got_ref = bf16[12,32,128]{2,1,0:T(8,128)(2,1)S(1)} collective-permute-done((bf16[12,32,128]{2,1,0:T(8,128)(2,1)S(1)}, bf16[12,32,128]{2,1,0:T(8,128)(2,1)S(1)}, u32[]{:S(2)}, u32[]{:S(2)}) %collective-permute-start.12) | collective-permute-done | bytes 98336 | tf_op jit(solution)/shard_map/ppermute | solution.py:632
  32.8 4.4 %collective-permute-start.13 = (bf16[12,32,128]{2,1,0:T(8,128)(2,1)S(1)}, bf16[12,32,128]{2,1,0:T(8,128)(2,1)S(1)}, u32[]{:S(2)}, u32[]{:S(2)}) collective-permute-start(bf16[12,32,128]{2,1,0:T(8,128)(2,1)S(1)} %pair.3.refs_0_), channel_id=1, source_target_pairs={{0,18},{1,19},{2,16},{3,17},{16,2},{17,3},{18,0},{19,1},{4,22},{5,... | collective-permute-start | bytes 294920 | tf_op jit(solution)/shard_map/ppermute | solution.py:632
  37.2 0.6 %collective-permute-start.15 = (bf16[12,32,128]{2,1,0:T(8,128)(2,1)S(1)}, bf16[12,32,128]{2,1,0:T(8,128)(2,1)S(1)}, u32[]{:S(2)}, u32[]{:S(2)}) collective-permute-start(bf16[12,32,128]{2,1,0:T(8,128)(2,1)S(1)} %pair.3.refs_0_), channel_id=1, source_target_pairs={{0,2},{1,3},{2,0},{3,1},{16,18},{17,19},{18,16},{19,17},{4,6},{5,7... | collective-permute-start | bytes 294920 | tf_op jit(solution)/shard_map/ppermute | solution.py:632
  37.8 2.9 %collective-permute-done.13.refs_1_ = bf16[12,32,128]{2,1,0:T(8,128)(2,1)S(1)} collective-permute-done((bf16[12,32,128]{2,1,0:T(8,128)(2,1)S(1)}, bf16[12,32,128]{2,1,0:T(8,128)(2,1)S(1)}, u32[]{:S(2)}, u32[]{:S(2)}) %collective-permute-start.13) | collective-permute-done | bytes 98336 | tf_op jit(solution)/shard_map/ppermute | solution.py:632
  40.8 1.0 %collective-permute-done.14.refs_2_ = bf16[12,32,128]{2,1,0:T(8,128)(2,1)S(1)} collective-permute-done((bf16[12,32,128]{2,1,0:T(8,128)(2,1)S(1)}, bf16[12,32,128]{2,1,0:T(8,128)(2,1)S(1)}, u32[]{:S(2)}, u32[]{:S(2)}) %collective-permute-start.14) | collective-permute-done | bytes 98336 | tf_op jit(solution)/shard_map/ppermute | solution.py:632
  41.8 0.6 %collective-permute-done.15.refs_3_ = bf16[12,32,128]{2,1,0:T(8,128)(2,1)S(1)} collective-permute-done((bf16[12,32,128]{2,1,0:T(8,128)(2,1)S(1)}, bf16[12,32,128]{2,1,0:T(8,128)(2,1)S(1)}, u32[]{:S(2)}, u32[]{:S(2)}) %collective-permute-start.15) | collective-permute-done | bytes 98336 | tf_op jit(solution)/shard_map/ppermute | solution.py:632
  42.4 0.3 gram.1
  42.7 8.7 %all_to_all.5.sums_ref = f32[8,2,128]{2,1,0:T(2,128)S(1)} all-to-all(f32[8,2,128]{2,1,0:T(2,128)S(1)} %gram.1), channel_id=1, replica_groups={{0,1,4,5,8,9,12,13},{2,3,6,7,10,11,14,15},{16,17,20,21,24,25,28,29},{18..., dimensions={0} | all-to-all | bytes 16384 | tf_op jit(solution)/shard_map/all_to_all | solution.py:744
  51.4 1.0 %combine.1 = f32[32,3072]{1,0:T(8,128)} custom-call(f32[8,2,128]{2,1,0:T(2,128)S(1)} %all_to_all.5.sums_ref, f32[32,3072]{1,0:T(8,128)S(1)} %get-tuple-element.21.image_ref.here_ref.right_ref, f32[24,32,128]{2,1,0:T(8,128)S(1)} %get-tuple-element.32.image_ref), custom_call_target="tpu_custom_call" | custom-call | tf_op jit(solution)/shard_map/combine/pallas_call | solution.py:745
  (18 shorter events, 0.2 us)
Async XLA Ops:
  2.8 7.5 %collective-permute-start = (bf16[32,512]{1,0:T(8,128)(2,1)S(1)}, bf16[32,512]{1,0:T(8,128)(2,1)S(1)}, u32[]{:S(2)}, u32[]{:S(2)}) collective-permute-start(bf16[32,512]{1,0:T(8,128)(2,1)S(1)} %get-tuple-element.24), channel_id=1, source_target_pairs={{0,12},{4,8},{8,4},{12,0},{1,13},{5,9},{9,5},{13,1},{2,14},{6,10},... | collective-permute-start | bytes 98312 | tf_op jit(solution)/shard_map/ppermute | solution.py:589
  7.9 3.9 %collective-permute-start.1 = (bf16[32,512]{1,0:T(8,128)(2,1)S(1)}, bf16[32,512]{1,0:T(8,128)(2,1)S(1)}, u32[]{:S(2)}, u32[]{:S(2)}) collective-permute-start(bf16[32,512]{1,0:T(8,128)(2,1)S(1)} %get-tuple-element.25), channel_id=1, source_target_pairs={{0,4},{4,0},{8,12},{12,8},{1,5},{5,1},{9,13},{13,9},{2,6},{6,2},{1... | collective-permute-start | bytes 98312 | tf_op jit(solution)/shard_map/ppermute | solution.py:589
  7.9 4.7 %collective-permute-start.2 = (bf16[1,16,896]{2,1,0:T(8,128)(2,1)S(1)}, bf16[1,16,896]{2,1,0:T(8,128)(2,1)S(1)}, u32[]{:S(2)}, u32[]{:S(2)}) collective-permute-start(bf16[1,16,896]{2,1,0:T(8,128)(2,1)S(1)} %get-tuple-element.26), channel_id=1, source_target_pairs={{0,1},{1,0},{2,6},{3,7},{16,24},{17,25},{18,30},{19,31},{4,8},{5,9... | collective-permute-start | bytes 86024 | tf_op jit(solution)/shard_map/ppermute | solution.py:584
  8.6 3.3 %copy-start = (bf16[2,8,256,256]{3,2,1,0:T(8,128)(2,1)S(1)}, bf16[2,8,256,256]{3,2,1,0:T(8,128)(2,1)}, u32[]{:S(2)}) copy-start(bf16[2,8,256,256]{3,2,1,0:T(8,128)(2,1)} %tiles_ref.3) | copy-start | bytes 6291460
  13.3 1.4 %collective-permute-start.3 = (bf16[12,32,128]{2,1,0:T(8,128)(2,1)S(1)}, bf16[12,32,128]{2,1,0:T(8,128)(2,1)S(1)}, u32[]{:S(2)}, u32[]{:S(2)}) collective-permute-start(bf16[12,32,128]{2,1,0:T(8,128)(2,1)S(1)} %get-tuple-element.30), channel_id=1, source_target_pairs={{0,1},{1,0},{2,3},{3,2},{16,17},{17,16},{18,19},{19,18},{4,5},{5,4... | collective-permute-start | bytes 294920 | tf_op jit(solution)/shard_map/ppermute | solution.py:632
  14.7 7.1 %collective-permute-start.4 = (bf16[12,32,128]{2,1,0:T(8,128)(2,1)S(1)}, bf16[12,32,128]{2,1,0:T(8,128)(2,1)S(1)}, u32[]{:S(2)}, u32[]{:S(2)}) collective-permute-start(bf16[12,32,128]{2,1,0:T(8,128)(2,1)S(1)} %pair.2.refs_0_), channel_id=1, source_target_pairs={{0,18},{1,19},{2,16},{3,17},{16,2},{17,3},{18,0},{19,1},{4,22},{5,... | collective-permute-start | bytes 294920 | tf_op jit(solution)/shard_map/ppermute | solution.py:632
  18.1 5.4 %collective-permute-start.5 = (bf16[12,32,128]{2,1,0:T(8,128)(2,1)S(1)}, bf16[12,32,128]{2,1,0:T(8,128)(2,1)S(1)}, u32[]{:S(2)}, u32[]{:S(2)}) collective-permute-start(bf16[12,32,128]{2,1,0:T(8,128)(2,1)S(1)} %pair.2.refs_0_), channel_id=1, source_target_pairs={{0,16},{1,17},{2,18},{3,19},{16,0},{17,1},{18,2},{19,3},{4,20},{5,... | collective-permute-start | bytes 294920 | tf_op jit(solution)/shard_map/ppermute | solution.py:632
  18.7 4.9 %collective-permute-start.6 = (bf16[12,32,128]{2,1,0:T(8,128)(2,1)S(1)}, bf16[12,32,128]{2,1,0:T(8,128)(2,1)S(1)}, u32[]{:S(2)}, u32[]{:S(2)}) collective-permute-start(bf16[12,32,128]{2,1,0:T(8,128)(2,1)S(1)} %pair.2.refs_0_), channel_id=1, source_target_pairs={{0,2},{1,3},{2,0},{3,1},{16,18},{17,19},{18,16},{19,17},{4,6},{5,7... | collective-permute-start | bytes 294920 | tf_op jit(solution)/shard_map/ppermute | solution.py:632
  23.6 1.7 %collective-permute-start.7 = (f32[12,32,128]{2,1,0:T(8,128)S(1)}, f32[12,32,128]{2,1,0:T(8,128)S(1)}, u32[]{:S(2)}, u32[]{:S(2)}) collective-permute-start(f32[12,32,128]{2,1,0:T(8,128)S(1)} %close.1.mine_ref.image_ref), channel_id=1, source_target_pairs={{0,1},{1,0},{2,3},{3,2},{16,17},{17,16},{18,19},{19,18},{4,5},{5,4... | collective-permute-start | bytes 589832 | tf_op jit(solution)/shard_map/ppermute | solution.py:632
  23.7 5.7 %collective-permute-start.8 = (bf16[2,32,128]{2,1,0:T(8,128)(2,1)S(1)}, bf16[2,32,128]{2,1,0:T(8,128)(2,1)S(1)}, u32[]{:S(2)}, u32[]{:S(2)}) collective-permute-start(bf16[2,32,128]{2,1,0:T(8,128)(2,1)S(1)} %edge.2), channel_id=1, source_target_pairs={{0,12},{4,8},{8,4},{12,0},{1,13},{5,9},{9,5},{13,1},{2,14},{6,10},... | collective-permute-start | bytes 49160 | tf_op jit(solution)/shard_map/ppermute | solution.py:589
  25.9 3.5 %collective-permute-start.11 = (bf16[1,16,1024]{2,1,0:T(8,128)(2,1)S(1)}, bf16[1,16,1024]{2,1,0:T(8,128)(2,1)S(1)}, u32[]{:S(2)}, u32[]{:S(2)}) collective-permute-start(bf16[1,16,1024]{2,1,0:T(8,128)(2,1)S(1)} %get-tuple-element.34), channel_id=1, source_target_pairs={{0,1},{1,0},{2,6},{3,7},{16,24},{17,25},{18,30},{19,31},{4,8},{5,9... | collective-permute-start | bytes 98312 | tf_op jit(solution)/shard_map/ppermute | solution.py:584
  26.1 4.5 %collective-permute-start.10 = (bf16[4,32,128]{2,1,0:T(8,128)(2,1)S(1)}, bf16[4,32,128]{2,1,0:T(8,128)(2,1)S(1)}, u32[]{:S(2)}, u32[]{:S(2)}) collective-permute-start(bf16[4,32,128]{2,1,0:T(8,128)(2,1)S(1)} %edge.3), channel_id=1, source_target_pairs={{0,4},{4,0},{8,12},{12,8},{1,5},{5,1},{9,13},{13,9},{2,6},{6,2},{1... | collective-permute-start | bytes 98312 | tf_op jit(solution)/shard_map/ppermute | solution.py:589
  29.5 1.2 %collective-permute-start.9 = (bf16[2,32,128]{2,1,0:T(8,128)(2,1)S(1)}, bf16[2,32,128]{2,1,0:T(8,128)(2,1)S(1)}, u32[]{:S(2)}, u32[]{:S(2)}) collective-permute-start(bf16[2,32,128]{2,1,0:T(8,128)(2,1)S(1)} %collective-permute-done.8.one_ref), channel_id=1, source_target_pairs={{0,1},{1,0},{2,3},{3,2},{16,17},{17,16},{18,19},{19,18},{4,5},{5,4... | collective-permute-start | bytes 49160 | tf_op jit(solution)/shard_map/ppermute | solution.py:632
  31.4 1.4 %collective-permute-start.12 = (bf16[12,32,128]{2,1,0:T(8,128)(2,1)S(1)}, bf16[12,32,128]{2,1,0:T(8,128)(2,1)S(1)}, u32[]{:S(2)}, u32[]{:S(2)}) collective-permute-start(bf16[12,32,128]{2,1,0:T(8,128)(2,1)S(1)} %get-tuple-element.36), channel_id=1, source_target_pairs={{0,1},{1,0},{2,3},{3,2},{16,17},{17,16},{18,19},{19,18},{4,5},{5,4... | collective-permute-start | bytes 294920 | tf_op jit(solution)/shard_map/ppermute | solution.py:632
  32.8 8.0 %collective-permute-start.13 = (bf16[12,32,128]{2,1,0:T(8,128)(2,1)S(1)}, bf16[12,32,128]{2,1,0:T(8,128)(2,1)S(1)}, u32[]{:S(2)}, u32[]{:S(2)}) collective-permute-start(bf16[12,32,128]{2,1,0:T(8,128)(2,1)S(1)} %pair.3.refs_0_), channel_id=1, source_target_pairs={{0,18},{1,19},{2,16},{3,17},{16,2},{17,3},{18,0},{19,1},{4,22},{5,... | collective-permute-start | bytes 294920 | tf_op jit(solution)/shard_map/ppermute | solution.py:632
  37.2 4.6 %collective-permute-start.14 = (bf16[12,32,128]{2,1,0:T(8,128)(2,1)S(1)}, bf16[12,32,128]{2,1,0:T(8,128)(2,1)S(1)}, u32[]{:S(2)}, u32[]{:S(2)}) collective-permute-start(bf16[12,32,128]{2,1,0:T(8,128)(2,1)S(1)} %pair.3.refs_0_), channel_id=1, source_target_pairs={{0,16},{1,17},{2,18},{3,19},{16,0},{17,1},{18,2},{19,3},{4,20},{5,... | collective-permute-start | bytes 294920 | tf_op jit(solution)/shard_map/ppermute | solution.py:632
  37.2 5.2 %collective-permute-start.15 = (bf16[12,32,128]{2,1,0:T(8,128)(2,1)S(1)}, bf16[12,32,128]{2,1,0:T(8,128)(2,1)S(1)}, u32[]{:S(2)}, u32[]{:S(2)}) collective-permute-start(bf16[12,32,128]{2,1,0:T(8,128)(2,1)S(1)} %pair.3.refs_0_), channel_id=1, source_target_pairs={{0,2},{1,3},{2,0},{3,1},{16,18},{17,19},{18,16},{19,17},{4,6},{5,7... | collective-permute-start | bytes 294920 | tf_op jit(solution)/shard_map/ppermute | solution.py:632

commit v18 on v17

--- a/solution.py
+++ b/solution.py
@@ -362,7 +362,7 @@
 
 
 def swap_order(chips):
-    return list(range(chips - 1, 0, -1))
+    return [chips - 1] + list(range(1, chips - 1))
 
 
 def by_step(parts):

time: 52.7 us -> 52 us (0.987)
  starting transfers between devices: 18.1 us -> 17.4 us
where the time goes in v18:
time: 52 us; the launch traced here: 51.7 us
  starting transfers between devices  17.4 us (33%)
  waiting for transfers between devices  16 us (31%)
  Pallas kernels  9.28 us (18%)
  blocking collectives  8.29 us (16%)
  between operations  0.78 us (2%)
    ppermute x10, waiting for transfers between devices, swapped(): return lax.ppermute(value, GROUP, [(g, g ^ step) for g in range(group)])  12.4 us
    ppermute x10, starting transfers between devices, swapped(): return lax.ppermute(value, GROUP, [(g, g ^ step) for g in range(group)])  9.31 us
    all_to_all x1, blocking collectives, local(): lax.all_to_all(lines, EVERY, 0, 0, axis_index_groups=same_chip, tiled=True)  8.29 us
    ppermute x4, starting transfers between devices, along_row(): return lax.ppermute(value, 'row', list(enumerate(neighbours[which])))  7.95 us
    ppermute x4, waiting for transfers between devices, along_row(): return lax.ppermute(value, 'row', list(enumerate(neighbours[which])))  3.54 us
    pallas_call x1, Pallas kernels, local(): pl.pallas_call(functools.partial(begin_kernel, fields, items, width, send...  2.74 us
    pallas_call x1, Pallas kernels, local(): pl.pallas_call(functools.partial(fetch_kernel, items, width, slots), out_...  1.73 us
  transfers between devices with their start and end apart: 16, of which 10 were waited for; matrix products, arithmetic and copies ran while one was open for 0% of the time, Pallas kernels for 7%

profile of v18, /device:TPU:0, one launch (start us, length us, event | category | flops | bytes accessed | tf_op | source)
XLA Modules:
  0.0 51.7 jit_solution(11165458652452562662)
XLA Ops:
  0.0 2.7 %begin.1 = (s32[13]{0:T(128)S(4)}, bf16[1,16,896]{2,1,0:T(8,128)(2,1)S(1)}, bf16[1,448,3,2,128]{4,3,2,1,0:T(2,128)(2,1)S(1)}, s32[24,1,128]{2,1,0:T(1,128)S(1)}, f32[32,3072]{1,0:T(8,128)S(1)}) custom-call(s32[1]{0:T(128)} %bitcast.1.row_ref, s32[1]{0:T(128)} %bitcast.2.own_ref, s32[4,2,4]{2,1,0:T(2,128)} %bitcast.18, s32[1,3072]{1,0:T(1,128)} %leaf_hbm.1, ...), custom_call_target="tpu_custom_call" | custom-call | tf_op jit(solution)/shard_map/begin/pallas_call | solution.py:548
  2.8 5.1 %collective-permute-start = (bf16[32,512]{1,0:T(8,128)(2,1)S(1)}, bf16[32,512]{1,0:T(8,128)(2,1)S(1)}, u32[]{:S(2)}, u32[]{:S(2)}) collective-permute-start(bf16[32,512]{1,0:T(8,128)(2,1)S(1)} %get-tuple-element.24), channel_id=1, source_target_pairs={{0,12},{4,8},{8,4},{12,0},{1,13},{5,9},{9,5},{13,1},{2,14},{6,10},... | collective-permute-start | bytes 98312 | tf_op jit(solution)/shard_map/ppermute | solution.py:589
  8.6 1.7 %fetch.1 = (bf16[1,448,3,2,128]{4,3,2,1,0:T(2,128)(2,1)S(1)}, bf16[1,896,441]{2,1,0:T(8,128)(2,1)S(1)}) custom-call(s32[13]{0:T(128)S(4)} %get-tuple-element.22.plan_ref, bf16[441,24,2,128]{3,2,1,0:T(2,128)(2,1)} %bitcast.14, bf16[4,441,2,441]{3,2,1,0:T(2,128)(2,1)} %bitcast.15), custom_call_target="tpu_custom_call" | custom-call | bytes 2064384 | tf_op jit(solution)/shard_map/fetch/pallas_call | solution.py:613
  10.3 1.5 %collective-permute-done.1.two_ref = bf16[32,512]{1,0:T(8,128)(2,1)S(1)} collective-permute-done((bf16[32,512]{1,0:T(8,128)(2,1)S(1)}, bf16[32,512]{1,0:T(8,128)(2,1)S(1)}, u32[]{:S(2)}, u32[]{:S(2)}) %collective-permute-start.1) | collective-permute-done | bytes 32800 | tf_op jit(solution)/shard_map/ppermute | solution.py:589
  11.8 0.8 %near.1.partial_ref = f32[24,32,128]{2,1,0:T(8,128)S(1)} custom-call(s32[1]{0:T(128)} %bitcast.1.row_ref, s32[1]{0:T(128)S(6)} %copy.11.count_ref, s32[13]{0:T(128)S(4)} %get-tuple-element.22.plan_ref, bf16[32,512]{1,0:T(8,128)(2,1)S(1)} %collective-permute-done.one_ref, bf16[32,512]{1,0:T(8,128)(2,1)S(1)} %collective-permute-done.1.two_ref, ...), custom_call_target="tpu_custom_call" | custom-call | flops 67108864 | bytes 2097152 | tf_op jit(solution)/shard_map/near/pallas_call | solution.py:635
  12.6 0.7 %far.1 = (f32[12,32,128]{2,1,0:T(8,128)S(1)}, bf16[12,32,128]{2,1,0:T(8,128)(2,1)S(1)}) custom-call(s32[1]{0:T(128)} %bitcast.core_ref, s32[13]{0:T(128)S(4)} %get-tuple-element.22.plan_ref, s32[24,1,128]{2,1,0:T(1,128)S(1)} %get-tuple-element.23.leaves_ref, f32[24,32,128]{2,1,0:T(8,128)S(1)} %near.1.partial_ref, ...), custom_call_target="tpu_custom_call" | custom-call | tf_op jit(solution)/shard_map/far/pallas_call | solution.py:649
  13.3 0.1 collective-permute-start.3
  13.3 1.3 %collective-permute-done.3.got_ref = bf16[12,32,128]{2,1,0:T(8,128)(2,1)S(1)} collective-permute-done((bf16[12,32,128]{2,1,0:T(8,128)(2,1)S(1)}, bf16[12,32,128]{2,1,0:T(8,128)(2,1)S(1)}, u32[]{:S(2)}, u32[]{:S(2)}) %collective-permute-start.3) | collective-permute-done | bytes 98336 | tf_op jit(solution)/shard_map/ppermute | solution.py:632
  14.7 3.5 %collective-permute-start.4 = (bf16[12,32,128]{2,1,0:T(8,128)(2,1)S(1)}, bf16[12,32,128]{2,1,0:T(8,128)(2,1)S(1)}, u32[]{:S(2)}, u32[]{:S(2)}) collective-permute-start(bf16[12,32,128]{2,1,0:T(8,128)(2,1)S(1)} %pair.2.refs_0_), channel_id=1, source_target_pairs={{0,18},{1,19},{2,16},{3,17},{16,2},{17,3},{18,0},{19,1},{4,22},{5,... | collective-permute-start | bytes 294920 | tf_op jit(solution)/shard_map/ppermute | solution.py:632
  18.1 0.6 %collective-permute-start.6 = (bf16[12,32,128]{2,1,0:T(8,128)(2,1)S(1)}, bf16[12,32,128]{2,1,0:T(8,128)(2,1)S(1)}, u32[]{:S(2)}, u32[]{:S(2)}) collective-permute-start(bf16[12,32,128]{2,1,0:T(8,128)(2,1)S(1)} %pair.2.refs_0_), channel_id=1, source_target_pairs={{0,16},{1,17},{2,18},{3,19},{16,0},{17,1},{18,2},{19,3},{4,20},{5,... | collective-permute-start | bytes 294920 | tf_op jit(solution)/shard_map/ppermute | solution.py:632
  18.8 2.6 %collective-permute-done.4.refs_1_ = bf16[12,32,128]{2,1,0:T(8,128)(2,1)S(1)} collective-permute-done((bf16[12,32,128]{2,1,0:T(8,128)(2,1)S(1)}, bf16[12,32,128]{2,1,0:T(8,128)(2,1)S(1)}, u32[]{:S(2)}, u32[]{:S(2)}) %collective-permute-start.4) | collective-permute-done | bytes 98336 | tf_op jit(solution)/shard_map/ppermute | solution.py:632
  21.3 2.0 %collective-permute-done.5.refs_2_ = bf16[12,32,128]{2,1,0:T(8,128)(2,1)S(1)} collective-permute-done((bf16[12,32,128]{2,1,0:T(8,128)(2,1)S(1)}, bf16[12,32,128]{2,1,0:T(8,128)(2,1)S(1)}, u32[]{:S(2)}, u32[]{:S(2)}) %collective-permute-start.5) | collective-permute-done | bytes 98336 | tf_op jit(solution)/shard_map/ppermute | solution.py:632
  23.4 0.2 collective-permute-done.6.refs_3_
  23.6 0.1 collective-permute-start.7
  23.7 2.1 %collective-permute-start.8 = (bf16[2,32,128]{2,1,0:T(8,128)(2,1)S(1)}, bf16[2,32,128]{2,1,0:T(8,128)(2,1)S(1)}, u32[]{:S(2)}, u32[]{:S(2)}) collective-permute-start(bf16[2,32,128]{2,1,0:T(8,128)(2,1)S(1)} %edge.2), channel_id=1, source_target_pairs={{0,12},{4,8},{8,4},{12,0},{1,13},{5,9},{9,5},{13,1},{2,14},{6,10},... | collective-permute-start | bytes 49160 | tf_op jit(solution)/shard_map/ppermute | solution.py:589
  25.8 0.6 %assemble.1 = (f32[24,32,128]{2,1,0:T(8,128)S(1)}, bf16[24,32,128]{2,1,0:T(8,128)(2,1)S(1)}, bf16[1,16,1024]{2,1,0:T(8,128)(2,1)S(1)}) custom-call(s32[1]{0:T(128)} %bitcast.core_ref, s32[13]{0:T(128)S(4)} %get-tuple-element.22.plan_ref, s32[24,1,128]{2,1,0:T(1,128)S(1)} %get-tuple-element.23.leaves_ref, f32[12,32,128]{2,1,0:T(8,128)S(1)} %close.1.mine_ref.image_ref, ...), custom_call_target="tpu_custom_call" | custom-call | tf_op jit(solution)/shard_map/assemble/pallas_call | solution.py:709
  26.4 0.2 collective-permute-start.11
  26.6 0.8 %collective-permute-start.10 = (bf16[4,32,128]{2,1,0:T(8,128)(2,1)S(1)}, bf16[4,32,128]{2,1,0:T(8,128)(2,1)S(1)}, u32[]{:S(2)}, u32[]{:S(2)}) collective-permute-start(bf16[4,32,128]{2,1,0:T(8,128)(2,1)S(1)} %edge.3), channel_id=1, source_target_pairs={{0,4},{4,0},{8,12},{12,8},{1,5},{5,1},{9,13},{13,9},{2,6},{6,2},{1... | collective-permute-start | bytes 98312 | tf_op jit(solution)/shard_map/ppermute | solution.py:589
  27.3 2.0 %collective-permute-done.8.one_ref = bf16[2,32,128]{2,1,0:T(8,128)(2,1)S(1)} collective-permute-done((bf16[2,32,128]{2,1,0:T(8,128)(2,1)S(1)}, bf16[2,32,128]{2,1,0:T(8,128)(2,1)S(1)}, u32[]{:S(2)}, u32[]{:S(2)}) %collective-permute-start.8) | collective-permute-done | bytes 16416 | tf_op jit(solution)/shard_map/ppermute | solution.py:589
  29.3 0.6 %first_far.1.image_ref = f32[1,3,32,128]{3,2,1,0:T(8,128)S(1)} custom-call(s32[13]{0:T(128)S(4)} %get-tuple-element.22.plan_ref, s32[24,1,128]{2,1,0:T(1,128)S(1)} %get-tuple-element.23.leaves_ref, bf16[1,16,1024]{2,1,0:T(8,128)(2,1)S(1)} %collective-permute-done.11.item_ref, bf16[1,896,441]{2,1,0:T(8,128)(2,1)S(1)} %get-tuple-element.27.trans_ref, ...), custom_call_target="tpu_custom_call" | custom-call | tf_op jit(solution)/shard_map/first_far/pallas_call | solution.py:661
  30.0 0.6 %collective-permute-done.9.other_one_ref = bf16[2,32,128]{2,1,0:T(8,128)(2,1)S(1)} collective-permute-done((bf16[2,32,128]{2,1,0:T(8,128)(2,1)S(1)}, bf16[2,32,128]{2,1,0:T(8,128)(2,1)S(1)}, u32[]{:S(2)}, u32[]{:S(2)}) %collective-permute-start.9) | collective-permute-done | bytes 16416 | tf_op jit(solution)/shard_map/ppermute | solution.py:632
  30.5 0.0 collective-permute-done.10.two_ref
  30.6 0.8 %last_near.1 = (bf16[12,32,128]{2,1,0:T(8,128)(2,1)S(1)}, bf16[12,32,128]{2,1,0:T(8,128)(2,1)S(1)}) custom-call(s32[1]{0:T(128)} %bitcast.core_ref, s32[1]{0:T(128)} %bitcast.1.row_ref, s32[1]{0:T(128)S(6)} %copy.11.count_ref, s32[13]{0:T(128)S(4)} %get-tuple-element.22.plan_ref, bf16[2,32,128]{2,1,0:T(8,128)(2,1)S(1)} %collective-permute-done.8.one_ref, ...), custom_call_target="tpu_custom_call" | custom-call | tf_op jit(solution)/shard_map/last_near/pallas_call | solution.py:672
  31.3 0.2 collective-permute-start.12
  31.5 1.2 %collective-permute-done.12.got_ref = bf16[12,32,128]{2,1,0:T(8,128)(2,1)S(1)} collective-permute-done((bf16[12,32,128]{2,1,0:T(8,128)(2,1)S(1)}, bf16[12,32,128]{2,1,0:T(8,128)(2,1)S(1)}, u32[]{:S(2)}, u32[]{:S(2)}) %collective-permute-start.12) | collective-permute-done | bytes 98336 | tf_op jit(solution)/shard_map/ppermute | solution.py:632
  32.7 4.2 %collective-permute-start.13 = (bf16[12,32,128]{2,1,0:T(8,128)(2,1)S(1)}, bf16[12,32,128]{2,1,0:T(8,128)(2,1)S(1)}, u32[]{:S(2)}, u32[]{:S(2)}) collective-permute-start(bf16[12,32,128]{2,1,0:T(8,128)(2,1)S(1)} %pair.3.refs_0_), channel_id=1, source_target_pairs={{0,18},{1,19},{2,16},{3,17},{16,2},{17,3},{18,0},{19,1},{4,22},{5,... | collective-permute-start | bytes 294920 | tf_op jit(solution)/shard_map/ppermute | solution.py:632
  36.9 0.6 %collective-permute-start.15 = (bf16[12,32,128]{2,1,0:T(8,128)(2,1)S(1)}, bf16[12,32,128]{2,1,0:T(8,128)(2,1)S(1)}, u32[]{:S(2)}, u32[]{:S(2)}) collective-permute-start(bf16[12,32,128]{2,1,0:T(8,128)(2,1)S(1)} %pair.3.refs_0_), channel_id=1, source_target_pairs={{0,16},{1,17},{2,18},{3,19},{16,0},{17,1},{18,2},{19,3},{4,20},{5,... | collective-permute-start | bytes 294920 | tf_op jit(solution)/shard_map/ppermute | solution.py:632
  37.6 2.6 %collective-permute-done.13.refs_1_ = bf16[12,32,128]{2,1,0:T(8,128)(2,1)S(1)} collective-permute-done((bf16[12,32,128]{2,1,0:T(8,128)(2,1)S(1)}, bf16[12,32,128]{2,1,0:T(8,128)(2,1)S(1)}, u32[]{:S(2)}, u32[]{:S(2)}) %collective-permute-start.13) | collective-permute-done | bytes 98336 | tf_op jit(solution)/shard_map/ppermute | solution.py:632
  40.1 2.0 %collective-permute-done.14.refs_2_ = bf16[12,32,128]{2,1,0:T(8,128)(2,1)S(1)} collective-permute-done((bf16[12,32,128]{2,1,0:T(8,128)(2,1)S(1)}, bf16[12,32,128]{2,1,0:T(8,128)(2,1)S(1)}, u32[]{:S(2)}, u32[]{:S(2)}) %collective-permute-start.14) | collective-permute-done | bytes 98336 | tf_op jit(solution)/shard_map/ppermute | solution.py:632
  42.2 0.3 gram.1
  42.4 8.3 %all_to_all.5.sums_ref = f32[8,2,128]{2,1,0:T(2,128)S(1)} all-to-all(f32[8,2,128]{2,1,0:T(2,128)S(1)} %gram.1), channel_id=1, replica_groups={{0,1,4,5,8,9,12,13},{2,3,6,7,10,11,14,15},{16,17,20,21,24,25,28,29},{18..., dimensions={0} | all-to-all | bytes 16384 | tf_op jit(solution)/shard_map/all_to_all | solution.py:744
  50.7 1.0 %combine.1 = f32[32,3072]{1,0:T(8,128)} custom-call(f32[8,2,128]{2,1,0:T(2,128)S(1)} %all_to_all.5.sums_ref, f32[32,3072]{1,0:T(8,128)S(1)} %get-tuple-element.21.image_ref.here_ref.right_ref, f32[24,32,128]{2,1,0:T(8,128)S(1)} %get-tuple-element.32.image_ref), custom_call_target="tpu_custom_call" | custom-call | tf_op jit(solution)/shard_map/combine/pallas_call | solution.py:745
  (18 shorter events, 0.2 us)
Async XLA Ops:
  2.8 7.5 %collective-permute-start = (bf16[32,512]{1,0:T(8,128)(2,1)S(1)}, bf16[32,512]{1,0:T(8,128)(2,1)S(1)}, u32[]{:S(2)}, u32[]{:S(2)}) collective-permute-start(bf16[32,512]{1,0:T(8,128)(2,1)S(1)} %get-tuple-element.24), channel_id=1, source_target_pairs={{0,12},{4,8},{8,4},{12,0},{1,13},{5,9},{9,5},{13,1},{2,14},{6,10},... | collective-permute-start | bytes 98312 | tf_op jit(solution)/shard_map/ppermute | solution.py:589
  7.9 3.9 %collective-permute-start.1 = (bf16[32,512]{1,0:T(8,128)(2,1)S(1)}, bf16[32,512]{1,0:T(8,128)(2,1)S(1)}, u32[]{:S(2)}, u32[]{:S(2)}) collective-permute-start(bf16[32,512]{1,0:T(8,128)(2,1)S(1)} %get-tuple-element.25), channel_id=1, source_target_pairs={{0,4},{4,0},{8,12},{12,8},{1,5},{5,1},{9,13},{13,9},{2,6},{6,2},{1... | collective-permute-start | bytes 98312 | tf_op jit(solution)/shard_map/ppermute | solution.py:589
  7.9 4.7 %collective-permute-start.2 = (bf16[1,16,896]{2,1,0:T(8,128)(2,1)S(1)}, bf16[1,16,896]{2,1,0:T(8,128)(2,1)S(1)}, u32[]{:S(2)}, u32[]{:S(2)}) collective-permute-start(bf16[1,16,896]{2,1,0:T(8,128)(2,1)S(1)} %get-tuple-element.26), channel_id=1, source_target_pairs={{0,1},{1,0},{2,6},{3,7},{16,24},{17,25},{18,30},{19,31},{4,8},{5,9... | collective-permute-start | bytes 86024 | tf_op jit(solution)/shard_map/ppermute | solution.py:584
  8.6 3.3 %copy-start = (bf16[2,8,256,256]{3,2,1,0:T(8,128)(2,1)S(1)}, bf16[2,8,256,256]{3,2,1,0:T(8,128)(2,1)}, u32[]{:S(2)}) copy-start(bf16[2,8,256,256]{3,2,1,0:T(8,128)(2,1)} %tiles_ref.3) | copy-start | bytes 6291460
  13.3 1.4 %collective-permute-start.3 = (bf16[12,32,128]{2,1,0:T(8,128)(2,1)S(1)}, bf16[12,32,128]{2,1,0:T(8,128)(2,1)S(1)}, u32[]{:S(2)}, u32[]{:S(2)}) collective-permute-start(bf16[12,32,128]{2,1,0:T(8,128)(2,1)S(1)} %get-tuple-element.30), channel_id=1, source_target_pairs={{0,1},{1,0},{2,3},{3,2},{16,17},{17,16},{18,19},{19,18},{4,5},{5,4... | collective-permute-start | bytes 294920 | tf_op jit(solution)/shard_map/ppermute | solution.py:632
  14.7 6.7 %collective-permute-start.4 = (bf16[12,32,128]{2,1,0:T(8,128)(2,1)S(1)}, bf16[12,32,128]{2,1,0:T(8,128)(2,1)S(1)}, u32[]{:S(2)}, u32[]{:S(2)}) collective-permute-start(bf16[12,32,128]{2,1,0:T(8,128)(2,1)S(1)} %pair.2.refs_0_), channel_id=1, source_target_pairs={{0,18},{1,19},{2,16},{3,17},{16,2},{17,3},{18,0},{19,1},{4,22},{5,... | collective-permute-start | bytes 294920 | tf_op jit(solution)/shard_map/ppermute | solution.py:632
  18.1 5.2 %collective-permute-start.5 = (bf16[12,32,128]{2,1,0:T(8,128)(2,1)S(1)}, bf16[12,32,128]{2,1,0:T(8,128)(2,1)S(1)}, u32[]{:S(2)}, u32[]{:S(2)}) collective-permute-start(bf16[12,32,128]{2,1,0:T(8,128)(2,1)S(1)} %pair.2.refs_0_), channel_id=1, source_target_pairs={{0,2},{1,3},{2,0},{3,1},{16,18},{17,19},{18,16},{19,17},{4,6},{5,7... | collective-permute-start | bytes 294920 | tf_op jit(solution)/shard_map/ppermute | solution.py:632
  18.1 5.4 %collective-permute-start.6 = (bf16[12,32,128]{2,1,0:T(8,128)(2,1)S(1)}, bf16[12,32,128]{2,1,0:T(8,128)(2,1)S(1)}, u32[]{:S(2)}, u32[]{:S(2)}) collective-permute-start(bf16[12,32,128]{2,1,0:T(8,128)(2,1)S(1)} %pair.2.refs_0_), channel_id=1, source_target_pairs={{0,16},{1,17},{2,18},{3,19},{16,0},{17,1},{18,2},{19,3},{4,20},{5,... | collective-permute-start | bytes 294920 | tf_op jit(solution)/shard_map/ppermute | solution.py:632
  23.6 2.2 %collective-permute-start.7 = (f32[12,32,128]{2,1,0:T(8,128)S(1)}, f32[12,32,128]{2,1,0:T(8,128)S(1)}, u32[]{:S(2)}, u32[]{:S(2)}) collective-permute-start(f32[12,32,128]{2,1,0:T(8,128)S(1)} %close.1.mine_ref.image_ref), channel_id=1, source_target_pairs={{0,1},{1,0},{2,3},{3,2},{16,17},{17,16},{18,19},{19,18},{4,5},{5,4... | collective-permute-start | bytes 589832 | tf_op jit(solution)/shard_map/ppermute | solution.py:632
  23.7 5.6 %collective-permute-start.8 = (bf16[2,32,128]{2,1,0:T(8,128)(2,1)S(1)}, bf16[2,32,128]{2,1,0:T(8,128)(2,1)S(1)}, u32[]{:S(2)}, u32[]{:S(2)}) collective-permute-start(bf16[2,32,128]{2,1,0:T(8,128)(2,1)S(1)} %edge.2), channel_id=1, source_target_pairs={{0,12},{4,8},{8,4},{12,0},{1,13},{5,9},{9,5},{13,1},{2,14},{6,10},... | collective-permute-start | bytes 49160 | tf_op jit(solution)/shard_map/ppermute | solution.py:589
  26.4 3.0 %collective-permute-start.11 = (bf16[1,16,1024]{2,1,0:T(8,128)(2,1)S(1)}, bf16[1,16,1024]{2,1,0:T(8,128)(2,1)S(1)}, u32[]{:S(2)}, u32[]{:S(2)}) collective-permute-start(bf16[1,16,1024]{2,1,0:T(8,128)(2,1)S(1)} %get-tuple-element.34), channel_id=1, source_target_pairs={{0,1},{1,0},{2,6},{3,7},{16,24},{17,25},{18,30},{19,31},{4,8},{5,9... | collective-permute-start | bytes 98312 | tf_op jit(solution)/shard_map/ppermute | solution.py:584
  26.6 4.0 %collective-permute-start.10 = (bf16[4,32,128]{2,1,0:T(8,128)(2,1)S(1)}, bf16[4,32,128]{2,1,0:T(8,128)(2,1)S(1)}, u32[]{:S(2)}, u32[]{:S(2)}) collective-permute-start(bf16[4,32,128]{2,1,0:T(8,128)(2,1)S(1)} %edge.3), channel_id=1, source_target_pairs={{0,4},{4,0},{8,12},{12,8},{1,5},{5,1},{9,13},{13,9},{2,6},{6,2},{1... | collective-permute-start | bytes 98312 | tf_op jit(solution)/shard_map/ppermute | solution.py:589
  29.3 1.2 %collective-permute-start.9 = (bf16[2,32,128]{2,1,0:T(8,128)(2,1)S(1)}, bf16[2,32,128]{2,1,0:T(8,128)(2,1)S(1)}, u32[]{:S(2)}, u32[]{:S(2)}) collective-permute-start(bf16[2,32,128]{2,1,0:T(8,128)(2,1)S(1)} %collective-permute-done.8.one_ref), channel_id=1, source_target_pairs={{0,1},{1,0},{2,3},{3,2},{16,17},{17,16},{18,19},{19,18},{4,5},{5,4... | collective-permute-start | bytes 49160 | tf_op jit(solution)/shard_map/ppermute | solution.py:632
  31.3 1.4 %collective-permute-start.12 = (bf16[12,32,128]{2,1,0:T(8,128)(2,1)S(1)}, bf16[12,32,128]{2,1,0:T(8,128)(2,1)S(1)}, u32[]{:S(2)}, u32[]{:S(2)}) collective-permute-start(bf16[12,32,128]{2,1,0:T(8,128)(2,1)S(1)} %get-tuple-element.36), channel_id=1, source_target_pairs={{0,1},{1,0},{2,3},{3,2},{16,17},{17,16},{18,19},{19,18},{4,5},{5,4... | collective-permute-start | bytes 294920 | tf_op jit(solution)/shard_map/ppermute | solution.py:632
  32.7 7.4 %collective-permute-start.13 = (bf16[12,32,128]{2,1,0:T(8,128)(2,1)S(1)}, bf16[12,32,128]{2,1,0:T(8,128)(2,1)S(1)}, u32[]{:S(2)}, u32[]{:S(2)}) collective-permute-start(bf16[12,32,128]{2,1,0:T(8,128)(2,1)S(1)} %pair.3.refs_0_), channel_id=1, source_target_pairs={{0,18},{1,19},{2,16},{3,17},{16,2},{17,3},{18,0},{19,1},{4,22},{5,... | collective-permute-start | bytes 294920 | tf_op jit(solution)/shard_map/ppermute | solution.py:632
  36.9 5.2 %collective-permute-start.14 = (bf16[12,32,128]{2,1,0:T(8,128)(2,1)S(1)}, bf16[12,32,128]{2,1,0:T(8,128)(2,1)S(1)}, u32[]{:S(2)}, u32[]{:S(2)}) collective-permute-start(bf16[12,32,128]{2,1,0:T(8,128)(2,1)S(1)} %pair.3.refs_0_), channel_id=1, source_target_pairs={{0,2},{1,3},{2,0},{3,1},{16,18},{17,19},{18,16},{19,17},{4,6},{5,7... | collective-permute-start | bytes 294920 | tf_op jit(solution)/shard_map/ppermute | solution.py:632
  36.9 5.2 %collective-permute-start.15 = (bf16[12,32,128]{2,1,0:T(8,128)(2,1)S(1)}, bf16[12,32,128]{2,1,0:T(8,128)(2,1)S(1)}, u32[]{:S(2)}, u32[]{:S(2)}) collective-permute-start(bf16[12,32,128]{2,1,0:T(8,128)(2,1)S(1)} %pair.3.refs_0_), channel_id=1, source_target_pairs={{0,16},{1,17},{2,18},{3,19},{16,0},{17,1},{18,2},{19,3},{4,20},{5,... | collective-permute-start | bytes 294920 | tf_op jit(solution)/shard_map/ppermute | solution.py:632
